TPU v7x, 32 devices: a whole 2x2x4 slice. The times are simulated.
32 devices in a mesh: pipe: 2 (over core), dp: 4 (over z), tensor: 4 (over y, x).
Axes of the slice: x: 2, y: 2, z: 4, core: 2. Of those that a mesh axis runs over, the one named last changes fastest.
Arguments:
- tokens: bfloat16 [2, 4, 256, 768], P(None, 'dp', 'tensor'), may hold values from -6 to 6
- conditions: bfloat16 [2, 4, 768], P(None, 'dp', 'tensor'), may hold values from -6 to 6
- cotangent: bfloat16 [2, 4, 256, 768], P(None, 'dp', 'tensor'), may hold values from -6 to 6
- modulation_weight: bfloat16 [2, 768, 4608], P('pipe', 'tensor', 'dp'), may hold values from -0.21875 to 0.21875
- modulation_bias: float32 [2, 4608], P('pipe'), may hold values from -3 to 3
- joint_weight: bfloat16 [2, 768, 3, 768], P('pipe', 'dp', None, 'tensor'), may hold values from -0.21875 to 0.21875
- joint_bias: float32 [2, 2, 768], P('pipe', None, 'tensor'), may hold values from -3 to 3
- output_weight: bfloat16 [2, 768, 768], P('pipe', 'tensor', 'dp'), may hold values from -0.875 to 0.875
- output_bias: float32 [2, 768], P('pipe'), may hold values from -3 to 3
- expand_weight: bfloat16 [2, 768, 3072], P('pipe', 'dp', 'tensor'), may hold values from -0.21875 to 0.21875
- expand_bias: float32 [2, 3072], P('pipe', 'tensor'), may hold values from -3 to 3
- shrink_weight: bfloat16 [2, 3072, 768], P('pipe', 'tensor', 'dp'), may hold values from -0.109375 to 0.109375
- shrink_bias: float32 [2, 768], P('pipe'), may hold values from -3 to 3
Outputs:
- layer_outputs: bfloat16 [2, 2, 4, 256, 768], P('pipe', None, 'dp', 'tensor')
- input_grads: bfloat16 [2, 2, 4, 256, 768], P('pipe', None, 'dp', 'tensor')
- condition_grads: float32 [2, 2, 4, 768], P('pipe', None, 'dp', 'tensor')
- modulation_weight_grad: float32 [2, 768, 4608], P('pipe', 'tensor', 'dp')
- modulation_bias_grad: float32 [2, 4608], P('pipe')
- joint_weight_grad: float32 [2, 768, 3, 768], P('pipe', 'dp', None, 'tensor')
- joint_bias_grad: float32 [2, 2, 768], P('pipe', None, 'tensor')
- output_weight_grad: float32 [2, 768, 768], P('pipe', 'tensor', 'dp')
- output_bias_grad: float32 [2, 768], P('pipe')
- expand_weight_grad: float32 [2, 768, 3072], P('pipe', 'dp', 'tensor')
- expand_bias_grad: float32 [2, 3072], P('pipe', 'tensor')
- shrink_weight_grad: float32 [2, 3072, 768], P('pipe', 'tensor', 'dp')
- shrink_bias_grad: float32 [2, 768], P('pipe')
All inputs are finite; a program needn't handle non-finite values.
Results may differ from a plain program's by a relative error of at most 0.025.
Values may be sent and summed in bfloat16 or wider, within the bound.
No kernel may reach another device: no remote copies, remote signals or barrier semaphores. Data moves between devices by JAX's collectives and lax.ppermute only.
A program may use at most 128 MiB of HBM per device.

v0:
```python
import jax
import jax.numpy as jnp
from jax import lax
from jax.sharding import PartitionSpec as P

HEAD = 64


def from_partner(value, axis, distance):
    mask = 2**distance
    pairs = [(source, source ^ mask) for source in range(lax.axis_size(axis))]
    return lax.ppermute(value, axis, pairs)


def layer_norm(values):
    centre = jnp.mean(values, axis=-1, keepdims=True)
    centred = values - centre
    spread = jnp.mean(centred * centred, axis=-1, keepdims=True)
    return centred * lax.rsqrt(spread + 1e-06)


def modulate_norm(values, shift_part, scale_part):
    return layer_norm(values) * (1.0 + scale_part) + shift_part


def tanh_gelu(values):
    return jax.nn.gelu(values, approximate=True)


def section_pass(outgoing):
    return from_partner(outgoing, "pipe", 0)


def select_index(stacked, position):
    return jax.tree.map(
        lambda member: lax.dynamic_index_in_dim(member, position, 0, keepdims=False), stacked
    )


def split_modulation(mod_now, model_width):
    return [
        mod_now[:, part_index * model_width : (part_index + 1) * model_width]
        for part_index in range(6)
    ]


def scatter_grads(ada_grad, joint_grad, output_grad, expand_grad, shrink_grad):
    return (
        lax.psum_scatter(
            ada_grad.astype(jnp.bfloat16), "dp", scatter_dimension=1, tiled=True
        ).astype(jnp.float32),
        lax.psum_scatter(
            joint_grad.astype(jnp.bfloat16), "dp", scatter_dimension=0, tiled=True
        ).astype(jnp.float32),
        lax.psum_scatter(
            output_grad.astype(jnp.bfloat16), "dp", scatter_dimension=1, tiled=True
        ).astype(jnp.float32),
        lax.psum_scatter(
            expand_grad.astype(jnp.bfloat16), "dp", scatter_dimension=0, tiled=True
        ).astype(jnp.float32),
        lax.psum_scatter(
            shrink_grad.astype(jnp.bfloat16), "dp", scatter_dimension=1, tiled=True
        ).astype(jnp.float32),
    )


def weight_products(row_pairs):
    flat_in, joint_grad, mixed_heads, attended_rows, mlp_rows, pre_grad, hidden, shrunk_rows = (
        row_pairs
    )
    joint_w_grad = jnp.einsum(
        "rd,rce->dce", flat_in, joint_grad, preferred_element_type=jnp.float32
    )
    output_w_grad = jnp.einsum(
        "re,rd->ed", mixed_heads, attended_rows, preferred_element_type=jnp.float32
    )
    expand_w_grad = jnp.einsum("rd,rf->df", mlp_rows, pre_grad, preferred_element_type=jnp.float32)
    shrink_w_grad = jnp.einsum("rf,rd->fd", hidden, shrunk_rows, preferred_element_type=jnp.float32)
    return (joint_w_grad, output_w_grad, expand_w_grad, shrink_w_grad)


def modulation_back(mod_grad_part, cond_part, ada_rows):
    mod_grad = lax.psum(mod_grad_part, "tensor").astype(jnp.bfloat16)
    activated = jax.nn.silu(cond_part).astype(jnp.bfloat16)
    ada_grad = jnp.einsum("mlr,mlf->rf", activated, mod_grad, preferred_element_type=jnp.float32)
    ada_bias_grad = jnp.sum(mod_grad.astype(jnp.float32), axis=(0, 1))
    act_grad = jnp.einsum("mlf,rf->mlr", mod_grad, ada_rows, preferred_element_type=jnp.float32)
    _, silu_back = jax.vjp(jax.nn.silu, cond_part)
    return (ada_grad, ada_bias_grad, silu_back(act_grad)[0])


def layer_forward(layer_input, mod_now, weights, biases):
    ada_rows, combined_weight, final_output_weight, widen_weight, narrow_weight = weights
    combined_bias, final_output_bias, widen_bias, narrow_bias = biases
    own_tokens, latents, model_width = layer_input.shape
    shift_attn, scale_attn, gate_attn, shift_mlp, scale_mlp, gate_mlp = split_modulation(
        mod_now, model_width
    )
    attn_in = modulate_norm(layer_input, shift_attn, scale_attn).astype(jnp.bfloat16)
    attn_rows = lax.all_gather(attn_in, "tensor", axis=0, tiled=True)
    seq_len = attn_rows.shape[0]
    flat_in = attn_rows.reshape(seq_len * latents, model_width)
    joint_out = jnp.einsum(
        "rd,dce->rce", flat_in, combined_weight, preferred_element_type=jnp.float32
    )
    head_count = combined_weight.shape[2] // HEAD
    head_shape = (seq_len, latents, head_count, HEAD)
    query_block = (joint_out[:, 0] + combined_bias[0]).astype(jnp.bfloat16).reshape(head_shape)
    key_block = joint_out[:, 1].astype(jnp.bfloat16).reshape(head_shape)
    value_block = (joint_out[:, 2] + combined_bias[1]).astype(jnp.bfloat16).reshape(head_shape)
    score_scale = HEAD ** (-0.5)
    scores = (
        jnp.einsum("qlhe,klhe->lhqk", query_block, key_block, preferred_element_type=jnp.float32)
        * score_scale
    )
    row_max = jnp.max(scores, axis=-1, keepdims=True)
    weights_exp = jnp.exp(scores - row_max)
    denominator = jnp.sum(weights_exp, axis=-1, keepdims=True)
    attn_probs = (weights_exp / denominator).astype(jnp.bfloat16)
    log_total = row_max + jnp.log(denominator)
    mixed_heads = jnp.einsum(
        "lhqk,klhe->qlhe", attn_probs, value_block, preferred_element_type=jnp.float32
    )
    mixed_heads = mixed_heads.astype(jnp.bfloat16).reshape(seq_len * latents, head_count * HEAD)
    piece_rows = mixed_heads
    attended = (
        lax.psum_scatter(
            jnp.dot(piece_rows, final_output_weight, preferred_element_type=jnp.float32).astype(
                jnp.bfloat16
            ),
            "tensor",
            scatter_dimension=0,
            tiled=True,
        )
        .astype(jnp.float32)
        .reshape(own_tokens, latents, model_width)
        + final_output_bias
    )
    middle = layer_input + gate_attn * attended
    mlp_in = modulate_norm(middle, shift_mlp, scale_mlp).astype(jnp.bfloat16)
    mlp_rows = lax.all_gather(mlp_in, "tensor", axis=0, tiled=True).reshape(
        seq_len * latents, model_width
    )
    pre_act = jnp.dot(mlp_rows, widen_weight, preferred_element_type=jnp.float32) + widen_bias
    hidden = tanh_gelu(pre_act).astype(jnp.bfloat16)
    piece_rows = hidden
    shrunk = (
        lax.psum_scatter(
            jnp.dot(piece_rows, narrow_weight, preferred_element_type=jnp.float32).astype(
                jnp.bfloat16
            ),
            "tensor",
            scatter_dimension=0,
            tiled=True,
        )
        .astype(jnp.float32)
        .reshape(own_tokens, latents, model_width)
        + narrow_bias
    )
    layer_out = middle + gate_mlp * shrunk
    kept_values = (
        layer_input,
        flat_in,
        query_block,
        key_block,
        value_block,
        log_total,
        mixed_heads,
        attended,
        middle,
        mlp_rows,
        pre_act,
        hidden,
        shrunk,
    )
    return (layer_out, kept_values)


def layer_backward(grad_out, kept_values, mod_now, weights):
    ada_rows, combined_weight, final_output_weight, widen_weight, narrow_weight = weights
    (
        layer_input,
        flat_in,
        query_block,
        key_block,
        value_block,
        log_total,
        mixed_heads,
        attended,
        middle,
        mlp_rows,
        pre_act,
        hidden,
        shrunk,
    ) = kept_values
    own_tokens, latents, model_width = layer_input.shape
    seq_len = query_block.shape[0]
    head_count = query_block.shape[2]
    score_scale = HEAD ** (-0.5)
    shift_attn, scale_attn, gate_attn, shift_mlp, scale_mlp, gate_mlp = split_modulation(
        mod_now, model_width
    )
    gate_mlp_grad = jnp.sum(grad_out * shrunk, axis=0)
    shrunk_grad = (gate_mlp * grad_out).astype(jnp.bfloat16)
    shrunk_rows = lax.all_gather(shrunk_grad, "tensor", axis=0, tiled=True).reshape(
        seq_len * latents, model_width
    )
    shrink_bias_grad = jnp.sum(shrunk_rows.astype(jnp.float32), axis=0)
    hidden_grad = jnp.einsum(
        "rd,fd->rf", shrunk_rows, narrow_weight, preferred_element_type=jnp.float32
    )
    _, gelu_back = jax.vjp(tanh_gelu, pre_act)
    pre_grad = gelu_back(hidden_grad)[0].astype(jnp.bfloat16)
    expand_bias_grad = jnp.sum(pre_grad.astype(jnp.float32), axis=0)
    piece_rows = pre_grad
    mlp_in_grad = (
        lax.psum_scatter(
            jnp.einsum(
                "rf,df->rd", piece_rows, widen_weight, preferred_element_type=jnp.float32
            ).astype(jnp.bfloat16),
            "tensor",
            scatter_dimension=0,
            tiled=True,
        )
        .astype(jnp.float32)
        .reshape(own_tokens, latents, model_width)
    )
    _, mlp_norm_back = jax.vjp(modulate_norm, middle, shift_mlp, scale_mlp)
    middle_grad, shift_mlp_grad, scale_mlp_grad = mlp_norm_back(mlp_in_grad)
    middle_grad = middle_grad + grad_out
    gate_attn_grad = jnp.sum(middle_grad * attended, axis=0)
    attended_grad = (gate_attn * middle_grad).astype(jnp.bfloat16)
    attended_rows = lax.all_gather(attended_grad, "tensor", axis=0, tiled=True).reshape(
        seq_len * latents, model_width
    )
    output_bias_grad = jnp.sum(attended_rows.astype(jnp.float32), axis=0)
    mixed_grad = jnp.einsum(
        "rd,ed->re", attended_rows, final_output_weight, preferred_element_type=jnp.float32
    )
    mixed_grad = mixed_grad.astype(jnp.bfloat16).reshape(seq_len, latents, head_count, HEAD)
    scores = (
        jnp.einsum("qlhe,klhe->lhqk", query_block, key_block, preferred_element_type=jnp.float32)
        * score_scale
    )
    attn_probs = jnp.exp(scores - log_total)
    probs_grad = jnp.einsum(
        "qlhe,klhe->lhqk", mixed_grad, value_block, preferred_element_type=jnp.float32
    )
    row_dot = jnp.sum(attn_probs * probs_grad, axis=-1, keepdims=True)
    scores_grad = (attn_probs * (probs_grad - row_dot)).astype(jnp.bfloat16)
    value_grad = jnp.einsum(
        "lhqk,qlhe->klhe",
        attn_probs.astype(jnp.bfloat16),
        mixed_grad,
        preferred_element_type=jnp.float32,
    )
    query_grad = (
        jnp.einsum("lhqk,klhe->qlhe", scores_grad, key_block, preferred_element_type=jnp.float32)
        * score_scale
    )
    key_grad = (
        jnp.einsum("lhqk,qlhe->klhe", scores_grad, query_block, preferred_element_type=jnp.float32)
        * score_scale
    )
    joint_grad = jnp.stack([query_grad, key_grad, value_grad], axis=2).astype(jnp.bfloat16)
    joint_grad = joint_grad.reshape(seq_len * latents, 3, head_count * HEAD)
    joint_bias_grad = jnp.sum(joint_grad[:, 0::2].astype(jnp.float32), axis=0)
    piece_rows = joint_grad
    attn_in_grad = (
        lax.psum_scatter(
            jnp.einsum(
                "rce,dce->rd", piece_rows, combined_weight, preferred_element_type=jnp.float32
            ).astype(jnp.bfloat16),
            "tensor",
            scatter_dimension=0,
            tiled=True,
        )
        .astype(jnp.float32)
        .reshape(own_tokens, latents, model_width)
    )
    _, attn_norm_back = jax.vjp(modulate_norm, layer_input, shift_attn, scale_attn)
    input_grad, shift_attn_grad, scale_attn_grad = attn_norm_back(attn_in_grad)
    input_grad = input_grad + middle_grad
    mod_grad = jnp.concatenate(
        [
            shift_attn_grad,
            scale_attn_grad,
            gate_attn_grad,
            shift_mlp_grad,
            scale_mlp_grad,
            gate_mlp_grad,
        ],
        axis=-1,
    )
    row_pairs = (
        flat_in,
        joint_grad,
        mixed_heads,
        attended_rows,
        mlp_rows,
        pre_grad,
        hidden,
        shrunk_rows,
    )
    bias_grads = (joint_bias_grad, output_bias_grad, expand_bias_grad, shrink_bias_grad)
    return (input_grad, mod_grad, row_pairs, bias_grads)


def on_device(
    tokens,
    conditions,
    cotangent,
    modulation_weight,
    modulation_bias,
    joint_weight,
    joint_bias,
    output_weight,
    output_bias,
    expand_weight,
    expand_bias,
    shrink_weight,
    shrink_bias,
):
    micro_count = tokens.shape[0]
    section_index = lax.axis_index("pipe")
    first_section = section_index == 0
    gathered = (
        lax.all_gather(modulation_weight[0], "dp", axis=1, tiled=True),
        lax.all_gather(joint_weight[0], "dp", axis=0, tiled=True),
        lax.all_gather(output_weight[0], "dp", axis=1, tiled=True),
        lax.all_gather(expand_weight[0], "dp", axis=0, tiled=True),
        lax.all_gather(shrink_weight[0], "dp", axis=1, tiled=True),
    )
    ada_rows = gathered[0]
    biases = (joint_bias[0], output_bias[0], expand_bias[0], shrink_bias[0])
    cond_values = conditions.astype(jnp.float32)
    activated = jax.nn.silu(cond_values).astype(jnp.bfloat16)
    mod_part = jnp.einsum("mlr,rf->mlf", activated, ada_rows, preferred_element_type=jnp.float32)
    modulation = lax.psum(mod_part, "tensor") + modulation_bias[0]
    inputs_seq = jnp.swapaxes(tokens, 1, 2)
    cot_seq = jnp.swapaxes(cotangent, 1, 2)
    received = jnp.zeros_like(inputs_seq[0])
    output_ticks = []
    kept_ticks = []
    for step_index in range(micro_count + 1):
        own_in = inputs_seq[min(step_index, micro_count - 1)].astype(jnp.float32)
        layer_input = jnp.where(first_section, own_in, received.astype(jnp.float32))
        position = jnp.clip(step_index - section_index, 0, micro_count - 1)
        mod_now = lax.dynamic_index_in_dim(modulation, position, 0, keepdims=False)
        layer_out, kept_values = layer_forward(layer_input, mod_now, gathered, biases)
        rounded = layer_out.astype(jnp.bfloat16)
        output_ticks.append(rounded)
        kept_ticks.append(kept_values)
        if step_index < micro_count:
            received = section_pass(rounded)
    kept_stack = tuple(
        (
            jnp.stack([kept_one[member_index] for kept_one in kept_ticks])
            for member_index in range(len(kept_ticks[0]))
        )
    )
    received = jnp.zeros_like(inputs_seq[0])
    input_ticks = []
    mod_ticks = []
    pair_ticks = []
    bias_total = None
    for step_index in range(micro_count + 1):
        micro_index = step_index - 1 + section_index
        valid = (micro_index >= 0) & (micro_index < micro_count)
        incoming = jnp.where(
            first_section,
            received.astype(jnp.float32),
            cot_seq[min(step_index, micro_count - 1)].astype(jnp.float32),
        )
        grad_out = jnp.where(valid, incoming, 0.0)
        position = jnp.clip(micro_index, 0, micro_count - 1)
        saved_values = select_index(
            kept_stack, jnp.clip(micro_index + section_index, 0, micro_count)
        )
        mod_now = lax.dynamic_index_in_dim(modulation, position, 0, keepdims=False)
        input_grad, mod_grad, row_pairs, bias_grads = layer_backward(
            grad_out, saved_values, mod_now, gathered
        )
        rounded_grad = input_grad.astype(jnp.bfloat16)
        input_ticks.append(rounded_grad)
        if step_index < micro_count:
            received = section_pass(rounded_grad)
        mod_ticks.append(mod_grad)
        pair_ticks.append(row_pairs)
        if bias_total is None:
            bias_total = tuple(bias_grads)
        else:
            bias_total = tuple(
                (earlier + latest for earlier, latest in zip(bias_total, bias_grads))
            )
    mod_all = jnp.stack(
        [
            jnp.where(first_section, mod_ticks[micro_slot + 1], mod_ticks[micro_slot])
            for micro_slot in range(micro_count)
        ]
    )
    ada_grad, ada_bias_grad, cond_all = modulation_back(mod_all, cond_values, ada_rows)
    pairs_all = tuple(
        (
            jnp.concatenate([pair_one[member_index] for pair_one in pair_ticks], axis=0)
            for member_index in range(8)
        )
    )
    local_weights = weight_products(pairs_all)
    weight_shards = scatter_grads(
        ada_grad, local_weights[0], local_weights[1], local_weights[2], local_weights[3]
    )
    bias_local = (ada_bias_grad,) + tuple(bias_total)
    bias_sums = lax.psum(
        (bias_local[0], bias_local[1], bias_local[2], bias_local[3], bias_local[4]), "dp"
    )
    layer_outputs = jnp.stack(
        [
            jnp.where(first_section, output_ticks[micro_slot], output_ticks[micro_slot + 1])
            for micro_slot in range(micro_count)
        ]
    )
    input_grads = jnp.stack(
        [
            jnp.where(first_section, input_ticks[micro_slot + 1], input_ticks[micro_slot])
            for micro_slot in range(micro_count)
        ]
    )
    layer_outputs = jnp.swapaxes(layer_outputs, 1, 2)[None]
    input_grads = jnp.swapaxes(input_grads, 1, 2)[None]
    return (
        layer_outputs,
        input_grads,
        cond_all[None],
        weight_shards[0][None],
        bias_sums[0][None],
        weight_shards[1][None],
        bias_sums[1][None],
        weight_shards[2][None],
        bias_sums[2][None],
        weight_shards[3][None],
        bias_sums[3][None],
        weight_shards[4][None],
        bias_sums[4][None],
    )


def solution(mesh):
    in_specs = (
        P(None, "dp", "tensor", None),
        P(None, "dp", "tensor"),
        P(None, "dp", "tensor", None),
        P("pipe", "tensor", "dp"),
        P("pipe", None),
        P("pipe", "dp", None, "tensor"),
        P("pipe", None, "tensor"),
        P("pipe", "tensor", "dp"),
        P("pipe", None),
        P("pipe", "dp", "tensor"),
        P("pipe", "tensor"),
        P("pipe", "tensor", "dp"),
        P("pipe", None),
    )
    out_specs = (
        P("pipe", None, "dp", "tensor", None),
        P("pipe", None, "dp", "tensor", None),
        P("pipe", None, "dp", "tensor"),
        P("pipe", "tensor", "dp"),
        P("pipe", None),
        P("pipe", "dp", None, "tensor"),
        P("pipe", None, "tensor"),
        P("pipe", "tensor", "dp"),
        P("pipe", None),
        P("pipe", "dp", "tensor"),
        P("pipe", "tensor"),
        P("pipe", "tensor", "dp"),
        P("pipe", None),
    )
    return jax.shard_map(
        on_device, mesh=mesh, in_specs=in_specs, out_specs=out_specs, check_vma=False
    )
```

profile of v0, /device:TPU:0, one launch (start us, length us, event | category | flops | bytes accessed | tf_op | source)
XLA Modules:
  0.0 805.9 jit_solution(1670656197859299710)
XLA Ops:
  11.2 28.3 %all-gather.2 = bf16[1,192,768]{1,0,2:T(2,128)(2,1)S(1)} all-gather(bf16[1,192,192]{1,0,2:T(2,128)(2,1)S(1)} %copy.85), channel_id=4, replica_groups=mesh['pipe'=2,'dp'=4,'tensor'=4] {'dp'}, dimensions={2}, use_global_device_ids=true | all-gather | bytes 368640 | tf_op jit(solution)/shard_map/all_gather | solution.py:330
  40.0 44.8 %all-gather.1 = bf16[1,768,3,192]{3,2,0,1:T(4,128)(2,1)} all-gather(bf16[1,192,3,192]{3,2,0,1:T(4,128)(2,1)S(1)} %copy.82), channel_id=3, replica_groups=mesh['pipe'=2,'dp'=4,'tensor'=4] {'dp'}, dimensions={1}, use_global_device_ids=true | all-gather | bytes 1105920 | tf_op jit(solution)/shard_map/all_gather | solution.py:329
  90.4 16.7 %psum.49 = f32[2,1,4608]{2,0,1:T(2,128)S(1)} all-reduce(f32[2,1,4608]{2,0,1:T(2,128)S(1)} %convolution_bitcast_fusion), channel_id=1, replica_groups=mesh['pipe'=2,'dp'=4,'tensor'=4] {'tensor'}, use_global_device_ids=true, to_apply=%region_0.1 | all-reduce | flops 9216 | bytes 73728 | tf_op jit(solution)/shard_map/psum | solution.py:339
  121.0 22.7 %reduce-scatter.22.cloned.1.call-done = bf16[64,768]{1,0:T(8,128)(2,1)} async-done(((bf16[256,768]{1,0:T(8,128)(2,1)}), bf16[64,768]{1,0:T(8,128)(2,1)}) %reduce-scatter.22.cloned.1.call-update) | async-done | bytes 98320 | tf_op jit(solution)/shard_map/reduce_scatter | solution.py:127
  157.1 18.6 %all-gather.13.cloned.1.call-done = bf16[1,768,768]{2,1,0:T(8,128)(2,1)} async-done(((bf16[1,192,768]{2,1,0:T(8,128)(2,1)}), bf16[1,768,768]{2,1,0:T(8,128)(2,1)}) %all-gather.13.cloned.1.call-update) | async-done | bytes 1179664 | tf_op jit(solution)/shard_map/all_gather | solution.py:331
  177.5 29.2 %all-gather.15.cloned.1.call-done = bf16[1,768,768]{1,2,0:T(8,128)(2,1)} async-done(((bf16[1,768,192]{1,2,0:T(8,128)(2,1)}), bf16[1,768,768]{1,2,0:T(8,128)(2,1)}) %all-gather.15.cloned.1.call-update) | async-done | bytes 1179664 | tf_op jit(solution)/shard_map/all_gather | solution.py:332
  209.5 24.1 %reduce-scatter.24.cloned.1.call-done = bf16[64,768]{1,0:T(8,128)(2,1)} async-done(((bf16[256,768]{1,0:T(8,128)(2,1)}), bf16[64,768]{1,0:T(8,128)(2,1)}) %reduce-scatter.24.cloned.1.call-update) | async-done | bytes 98320 | tf_op jit(solution)/shard_map/reduce_scatter | solution.py:148
  250.7 24.5 %reduce-scatter.26.cloned.1.call-done = bf16[64,768]{1,0:T(8,128)(2,1)} async-done(((bf16[256,768]{1,0:T(8,128)(2,1)}), bf16[64,768]{1,0:T(8,128)(2,1)}) %reduce-scatter.26.cloned.1.call-update) | async-done | bytes 98320 | tf_op jit(solution)/shard_map/reduce_scatter | solution.py:127
  301.7 12.3 %reduce-scatter.28.cloned.1.call-done = bf16[64,768]{1,0:T(8,128)(2,1)} async-done(((bf16[256,768]{1,0:T(8,128)(2,1)}), bf16[64,768]{1,0:T(8,128)(2,1)}) %reduce-scatter.28.cloned.1.call-update) | async-done | bytes 98320 | tf_op jit(solution)/shard_map/reduce_scatter | solution.py:148
  336.6 19.3 %reduce-scatter.30.cloned.1.call-done = bf16[64,768]{1,0:T(8,128)(2,1)} async-done(((bf16[256,768]{1,0:T(8,128)(2,1)}), bf16[64,768]{1,0:T(8,128)(2,1)}) %reduce-scatter.30.cloned.1.call-update) | async-done | bytes 98320 | tf_op jit(solution)/shard_map/reduce_scatter | solution.py:127
  357.3 9.9 %all_gather.61 = bf16[256,1,768]{2,0,1:T(8,128)(2,1)S(1)} all-gather(bf16[64,1,768]{2,0,1:T(8,128)(2,1)S(1)} %add_convert_fusion.7), channel_id=1, replica_groups=mesh['pipe'=2,'dp'=4,'tensor'=4] {'tensor'}, dimensions={0}, use_global_device_ids=true | all-gather | bytes 491520 | tf_op jit(solution)/shard_map/all_gather | solution.py:141
  378.5 19.5 %reduce-scatter.34.cloned.1.call-done = bf16[64,768]{1,0:T(8,128)(2,1)} async-done(((bf16[256,768]{1,0:T(8,128)(2,1)}), bf16[64,768]{1,0:T(8,128)(2,1)}) %reduce-scatter.34.cloned.1.call-update) | async-done | bytes 98320 | tf_op jit(solution)/shard_map/reduce_scatter | solution.py:217
  403.3 9.8 %all-gather.6 = bf16[256,768]{1,0:T(8,128)(2,1)S(1)} all-gather(bf16[64,768]{1,0:T(8,128)(2,1)S(1)} %multiply_convert_fusion.7), channel_id=8, replica_groups=mesh['pipe'=2,'dp'=4,'tensor'=4] {'tensor'}, dimensions={0}, use_global_device_ids=true | all-gather | bytes 491520 | tf_op jit(solution)/shard_map/all_gather | solution.py:233
  419.4 23.0 %reduce-scatter.36.cloned.1.call-done = bf16[64,768]{1,0:T(8,128)(2,1)} async-done(((bf16[256,768]{1,0:T(8,128)(2,1)}), bf16[64,768]{1,0:T(8,128)(2,1)}) %reduce-scatter.36.cloned.1.call-update) | async-done | bytes 98320 | tf_op jit(solution)/shard_map/reduce_scatter | solution.py:270
  466.1 21.6 %reduce-scatter.38.cloned.1.call-done = bf16[64,768]{1,0:T(8,128)(2,1)} async-done(((bf16[256,768]{1,0:T(8,128)(2,1)}), bf16[64,768]{1,0:T(8,128)(2,1)}) %reduce-scatter.38.cloned.1.call-update) | async-done | bytes 98320 | tf_op jit(solution)/shard_map/reduce_scatter | solution.py:217
  492.9 10.5 %all_gather.65 = bf16[256,1,768]{2,0,1:T(8,128)(2,1)S(1)} all-gather(bf16[64,1,768]{2,0,1:T(8,128)(2,1)S(1)} %get-tuple-element.142), channel_id=1, replica_groups=mesh['pipe'=2,'dp'=4,'tensor'=4] {'tensor'}, dimensions={0}, use_global_device_ids=true | all-gather | bytes 491520 | tf_op jit(solution)/shard_map/all_gather | solution.py:233
  517.2 26.1 %reduce-scatter.40.cloned.1.call-done = bf16[64,768]{1,0:T(8,128)(2,1)} async-done(((bf16[256,768]{1,0:T(8,128)(2,1)}), bf16[64,768]{1,0:T(8,128)(2,1)}) %reduce-scatter.40.cloned.1.call-update) | async-done | bytes 98320 | tf_op jit(solution)/shard_map/reduce_scatter | solution.py:270
  567.3 22.3 %reduce-scatter.42.cloned.1.call-done = bf16[64,768]{1,0:T(8,128)(2,1)} async-done(((bf16[256,768]{1,0:T(8,128)(2,1)}), bf16[64,768]{1,0:T(8,128)(2,1)}) %reduce-scatter.42.cloned.1.call-update) | async-done | bytes 98320 | tf_op jit(solution)/shard_map/reduce_scatter | solution.py:217
  594.8 9.8 %all_gather.67 = bf16[256,1,768]{2,0,1:T(8,128)(2,1)S(1)} all-gather(bf16[64,1,768]{2,0,1:T(8,128)(2,1)S(1)} %multiply_convert_fusion.3), channel_id=1, replica_groups=mesh['pipe'=2,'dp'=4,'tensor'=4] {'tensor'}, dimensions={0}, use_global_device_ids=true | all-gather | bytes 491520 | tf_op jit(solution)/shard_map/all_gather | solution.py:233
  636.3 16.0 %psum.50 = bf16[2,1,4608]{2,0,1:T(2,128)(2,1)S(1)} all-reduce(f32[2,1,4608]{2,0,1:T(2,128)S(1)} %pad_maximum_fusion.15), channel_id=1, replica_groups=mesh['pipe'=2,'dp'=4,'tensor'=4] {'tensor'}, use_global_device_ids=true, to_apply=%region_76.77 | all-reduce | flops 9216 | bytes 55296 | tf_op jit(solution)/shard_map/psum | solution.py:83
  662.5 21.1 %all-reduce = (f32[1,4608]{1,0:T(1,128)}, f32[1,2,192]{2,1,0:T(2,128)}, f32[1,768]{1,0:T(1,128)}, f32[1,768]{1,0:T(1,128)}, f32[1,768]{1,0:T(1,128)}) all-reduce(f32[1,4608]{1,0:T(1,128)S(1)} %broadcast_in_dim.80, f32[1,2,192]{2,1,0:T(2,128)S(1)} %add_bitcast_fusion.3, ...), channel_id=1, replica_groups=mesh['pipe'=2,'dp'=4,'tensor'=4] {'dp'}, use_global_device_ids=true, to_apply=%region_79.80 | all-reduce | flops 7296 | bytes 58368 | tf_op jit(solution)/shard_map/psum | solution.py:414
  688.5 28.4 %reduce-scatter.50.cloned.1.call-done = bf16[768,192]{0,1:T(8,128)(2,1)} async-done(((bf16[768,768]{0,1:T(8,128)(2,1)}), bf16[768,192]{0,1:T(8,128)(2,1)}) %reduce-scatter.50.cloned.1.call-update) | async-done | bytes 294928 | tf_op jit(solution)/shard_map/reduce_scatter | solution.py:61
  718.7 28.5 %reduce-scatter.46.cloned.1.call-done = bf16[192,3,192]{2,0,1:T(8,128)(2,1)} async-done(((bf16[768,3,192]{2,0,1:T(8,128)(2,1)}), bf16[192,3,192]{2,0,1:T(8,128)(2,1)}) %reduce-scatter.46.cloned.1.call-update) | async-done | bytes 221200 | tf_op jit(solution)/shard_map/reduce_scatter | solution.py:52
  749.1 47.2 %reduce-scatter.52.cloned.1.call-done = bf16[1152,192]{1,0:T(8,128)(2,1)} async-done(((bf16[4608,192]{1,0:T(8,128)(2,1)}), bf16[1152,192]{1,0:T(8,128)(2,1)}) %reduce-scatter.52.cloned.1.call-update) | async-done | bytes 442384
  (710 shorter events, 254.2 us)
Async XLA Ops:
  7.2 81.4 %all-gather.11.cloned.1.call-start = ((), (), s32[]{:S(2)}) async-start(), calls=%async_computation.32 | async-start | bytes 2211840 | tf_op jit(solution)/shard_map/all_gather | solution.py:328
  7.9 135.8 %reduce-scatter.22.cloned.1.call-start = ((), (), s32[]{:S(2)}) async-start(), calls=%async_computation.17 | async-start | bytes 491520 | tf_op jit(solution)/shard_map/reduce_scatter | solution.py:127
  119.5 56.2 %all-gather.13.cloned.1.call-start = ((), (), s32[]{:S(2)}) async-start(), calls=%async_computation.33 | async-start | bytes 1474560 | tf_op jit(solution)/shard_map/all_gather | solution.py:331
  120.3 86.5 %all-gather.15.cloned.1.call-start = ((), (), s32[]{:S(2)}) async-start(), calls=%async_computation.34 | async-start | bytes 1474560 | tf_op jit(solution)/shard_map/all_gather | solution.py:332
  120.8 112.7 %reduce-scatter.24.cloned.1.call-start = ((), (), s32[]{:S(2)}) async-start(), calls=%async_computation.18 | async-start | bytes 491520 | tf_op jit(solution)/shard_map/reduce_scatter | solution.py:148
  209.4 65.8 %reduce-scatter.26.cloned.1.call-start = ((), (), s32[]{:S(2)}) async-start(), calls=%async_computation.19 | async-start | bytes 491520 | tf_op jit(solution)/shard_map/reduce_scatter | solution.py:127
  235.3 1.3 collective-permute-start
  250.7 63.3 %reduce-scatter.28.cloned.1.call-start = ((), (), s32[]{:S(2)}) async-start(), calls=%async_computation.20 | async-start | bytes 491520 | tf_op jit(solution)/shard_map/reduce_scatter | solution.py:148
  289.3 66.5 %reduce-scatter.30.cloned.1.call-start = ((), (), s32[]{:S(2)}) async-start(), calls=%async_computation.21 | async-start | bytes 491520 | tf_op jit(solution)/shard_map/reduce_scatter | solution.py:127
  315.6 1.3 collective-permute-start.1
  331.3 66.8 %reduce-scatter.34.cloned.1.call-start = ((), (), s32[]{:S(2)}) async-start(), calls=%async_computation.23 | async-start | bytes 491520 | tf_op jit(solution)/shard_map/reduce_scatter | solution.py:217
  373.6 68.8 %reduce-scatter.36.cloned.1.call-start = ((), (), s32[]{:S(2)}) async-start(), calls=%async_computation.24 | async-start | bytes 491520 | tf_op jit(solution)/shard_map/reduce_scatter | solution.py:270
  417.9 69.9 %reduce-scatter.38.cloned.1.call-start = ((), (), s32[]{:S(2)}) async-start(), calls=%async_computation.25 | async-start | bytes 491520 | tf_op jit(solution)/shard_map/reduce_scatter | solution.py:217
  447.0 1.4 collective-permute-start.2
  463.2 52.3 %reduce-scatter.32.cloned.1.call-start = ((), (), s32[]{:S(2)}) async-start(), calls=%async_computation.22 | async-start | bytes 491520 | tf_op jit(solution)/shard_map/reduce_scatter | solution.py:148
  466.1 77.2 %reduce-scatter.40.cloned.1.call-start = ((), (), s32[]{:S(2)}) async-start(), calls=%async_computation.26 | async-start | bytes 491520 | tf_op jit(solution)/shard_map/reduce_scatter | solution.py:270
  508.2 81.4 %reduce-scatter.42.cloned.1.call-start = ((), (), s32[]{:S(2)}) async-start(), calls=%async_computation.27 | async-start | bytes 491520 | tf_op jit(solution)/shard_map/reduce_scatter | solution.py:217
  548.6 1.3 collective-permute-start.3
  565.0 68.3 %reduce-scatter.44.cloned.1.call-start = ((), (), s32[]{:S(2)}) async-start(), calls=%async_computation.28 | async-start | bytes 491520 | tf_op jit(solution)/shard_map/reduce_scatter | solution.py:270
  608.7 49.9 %reduce-scatter.54.cloned.1.call-start = ((), (), s32[]{:S(2)}) async-start(), calls=%async_computation.36 | async-start | bytes 491520
  612.5 74.3 %reduce-scatter.48.cloned.1.call-start = ((), (), s32[]{:S(2)}) async-start(), calls=%async_computation.30 | async-start | bytes 1474560 | tf_op jit(solution)/shard_map/reduce_scatter | solution.py:58
  617.9 99.0 %reduce-scatter.50.cloned.1.call-start = ((), (), s32[]{:S(2)}) async-start(), calls=%async_computation.31 | async-start | bytes 1474560 | tf_op jit(solution)/shard_map/reduce_scatter | solution.py:61
  625.3 122.0 %reduce-scatter.46.cloned.1.call-start = ((), (), s32[]{:S(2)}) async-start(), calls=%async_computation.29 | async-start | bytes 1474560 | tf_op jit(solution)/shard_map/reduce_scatter | solution.py:52
  631.1 165.2 %reduce-scatter.52.cloned.1.call-start = ((), (), s32[]{:S(2)}) async-start(), calls=%async_computation.35 | async-start | bytes 2949120
  (204 other events, 2008.8 us)
Sparse Core Ops, SparseCore 0:
  9.6 66.1 all-gather.10
  119.6 24.0 reduce-scatter.21
  145.3 30.4 all-gather.12
  177.2 29.5 all-gather.14
  210.0 23.5 reduce-scatter.23
  250.8 24.4 reduce-scatter.25
  289.5 24.4 reduce-scatter.27
  331.4 24.4 reduce-scatter.29
  373.7 24.3 reduce-scatter.33
  418.0 24.3 reduce-scatter.35
  463.3 24.4 reduce-scatter.37
  491.0 24.4 reduce-scatter.31
  518.8 24.4 reduce-scatter.39
  565.2 24.4 reduce-scatter.41
  608.8 24.4 reduce-scatter.43
  635.5 20.5 reduce-scatter.53
  658.4 28.3 reduce-scatter.47
  689.0 27.8 reduce-scatter.49
  719.3 27.8 reduce-scatter.45
  749.5 46.7 reduce-scatter.51
where the time goes:
time: 817 us; the launch traced here: 806 us
  waiting for transfers between devices  384 us (47%)
  blocking collectives  242 us (30%)
  other arithmetic  75.9 us (9%)
  matrix products  49.8 us (6%)
  local copies, waits for them, and re-layouts  35.9 us (4%)
  between operations  17.4 us (2%)
    reduce_scatter x3, waiting for transfers between devices, layer_forward(): lax.psum_scatter(jnp.dot(piece_rows, final_output_weight, preferred_eleme...  66.6 us
    reduce_scatter x3, waiting for transfers between devices, layer_backward(): lax.psum_scatter(jnp.einsum('rf,df->rd', piece_rows, widen_weight, prefer...  63.4 us
    reduce_scatter x3, waiting for transfers between devices, layer_backward(): lax.psum_scatter(jnp.einsum('rce,dce->rd', piece_rows, combined_weight, p...  51.3 us
    unnamed x22, waiting for transfers between devices  49.4 us
    all_gather x1, blocking collectives, on_device(): lax.all_gather(joint_weight[0], 'dp', axis=0, tiled=True)  44.8 us
    reduce_scatter x3, waiting for transfers between devices, layer_forward(): lax.psum_scatter(jnp.dot(piece_rows, narrow_weight, preferred_element_typ...  42.3 us
    all_gather x3, blocking collectives, layer_backward(): lax.all_gather(attended_grad, 'tensor', axis=0, tiled=True)  30.1 us
    all_gather x1, waiting for transfers between devices, on_device(): lax.all_gather(shrink_weight[0], 'dp', axis=1, tiled=True)  29.2 us
  transfers between devices with their start and end apart: 24, of which 22 were waited for; matrix products, arithmetic and copies ran while one was open for 10% of the time, Pallas kernels for 0%

commit v1 on v0

v1 whole, which is shorter than its diff:
```python
import jax
import jax.numpy as jnp
from jax import lax
from jax.sharding import PartitionSpec as P

HEAD = 64
EPS = 1e-06
F32 = jnp.float32
BF16 = jnp.bfloat16
LINE_LIMIT = 8


def swap(value, axis, mask):
    pairs = [(source, source ^ mask) for source in range(lax.axis_size(axis))]
    return lax.ppermute(value, axis, pairs)


def exchange(parts, axis):
    return [parts[0]] + [swap(parts[k], axis, k) for k in range(1, len(parts))]


def gather(value, axis):
    return exchange([value] * lax.axis_size(axis), axis)


def tree_sum(parts):
    parts = list(parts)
    while len(parts) > 1:
        parts = [parts[k] + parts[k + 1] for k in range(0, len(parts), 2)]
    return parts[0]


def gather_rows(value):
    return jnp.concatenate(gather(value, "tensor"), axis=0)


def scatter_rows(partial, own):
    blocks = partial.reshape(-1, own, partial.shape[-1])
    received = exchange([blocks[k] for k in range(blocks.shape[0])], "tensor")
    return tree_sum([block.astype(F32) for block in received])


def flip_blocks(values, index, count):
    lead = values.shape[:-1]
    blocks = values.reshape(lead + (count, values.shape[-1] // count))
    bit = 1
    while bit < count:
        paired = blocks.reshape(lead + (count // (2 * bit), 2, bit, blocks.shape[-1]))
        flipped = paired[..., ::-1, :, :].reshape(blocks.shape)
        blocks = jnp.where((index & bit) != 0, flipped, blocks)
        bit *= 2
    return blocks.reshape(values.shape)


def dot(left, right):
    return jnp.dot(left, right, preferred_element_type=F32)


def dot_t(left, right):
    return lax.dot_general(left, right, (((1,), (1,)), ((), ())), preferred_element_type=F32)


def t_dot(left, right):
    return lax.dot_general(left, right, (((0,), (0,)), ((), ())), preferred_element_type=F32)


def normalize(values):
    centred = values - jnp.mean(values, axis=-1, keepdims=True)
    rstd = lax.rsqrt(jnp.mean(centred * centred, axis=-1, keepdims=True) + EPS)
    return centred * rstd, rstd


def normalize_back(grad, normed, rstd):
    return rstd * (
        grad
        - jnp.mean(grad, axis=-1, keepdims=True)
        - normed * jnp.mean(grad * normed, axis=-1, keepdims=True)
    )


def tanh_gelu(values):
    return jax.nn.gelu(values, approximate=True)


def layer_forward(h, parts, weights, biases):
    w_joint, w_out, w_expand, w_shrink = weights
    joint_bias, out_bias, expand_bias, shrink_bias = biases
    shift_attn, scale_attn, gate_attn, shift_mlp, scale_mlp, gate_mlp = parts
    own = h.shape[0]
    width = w_out.shape[0]
    normed, _ = normalize(h)
    attn_rows = gather_rows((normed * (1.0 + scale_attn) + shift_attn).astype(BF16))
    joint = dot(attn_rows, w_joint)
    heads = (attn_rows.shape[0], width // HEAD, HEAD)
    query = (joint[:, :width] + joint_bias[0]).astype(BF16).reshape(heads)
    key = joint[:, width : 2 * width].astype(BF16).reshape(heads)
    value = (joint[:, 2 * width :] + joint_bias[1]).astype(BF16).reshape(heads)
    scores = jnp.einsum("qhe,khe->hqk", query, key, preferred_element_type=F32) * HEAD**-0.5
    powers = jnp.exp(scores - jnp.max(scores, axis=-1, keepdims=True))
    probs = powers / jnp.sum(powers, axis=-1, keepdims=True)
    mixed = jnp.einsum("hqk,khe->qhe", probs.astype(BF16), value, preferred_element_type=F32)
    mixed = mixed.astype(BF16).reshape(attn_rows.shape[0], width)
    attended = scatter_rows(dot(mixed, w_out).astype(BF16), own) + out_bias
    middle = h + gate_attn * attended
    normed, _ = normalize(middle)
    mlp_rows = gather_rows((normed * (1.0 + scale_mlp) + shift_mlp).astype(BF16))
    pre = dot(mlp_rows, w_expand) + expand_bias
    hidden = tanh_gelu(pre).astype(BF16)
    shrunk = scatter_rows(dot(hidden, w_shrink).astype(BF16), own) + shrink_bias
    kept = (h, attn_rows, query, key, value, probs, mixed, attended, middle, mlp_rows, pre, hidden, shrunk)
    return middle + gate_mlp * shrunk, kept


def layer_backward(g_y, kept, parts, weights):
    w_joint, w_out, w_expand, w_shrink = weights
    h, attn_rows, query, key, value, probs, mixed, attended, middle, mlp_rows, pre, hidden, shrunk = kept
    shift_attn, scale_attn, gate_attn, shift_mlp, scale_mlp, gate_mlp = parts
    own = h.shape[0]
    rows = attn_rows.shape[0]
    width = w_out.shape[0]
    g_gate_mlp = jnp.sum(g_y * shrunk, axis=0)
    g_shrunk = (gate_mlp * g_y).astype(BF16)
    shrink_bias_grad = jnp.sum(g_shrunk.astype(F32), axis=0)
    shrunk_rows = gather_rows(g_shrunk)
    _, gelu_back = jax.vjp(tanh_gelu, pre)
    g_pre = gelu_back(dot_t(shrunk_rows, w_shrink))[0].astype(BF16)
    expand_bias_grad = jnp.sum(g_pre.astype(F32), axis=0)
    g_mlp_in = scatter_rows(dot_t(g_pre, w_expand).astype(BF16), own)
    w_shrink_grad = t_dot(hidden, shrunk_rows)
    w_expand_grad = t_dot(mlp_rows, g_pre)
    normed, rstd = normalize(middle)
    g_shift_mlp = jnp.sum(g_mlp_in, axis=0)
    g_scale_mlp = jnp.sum(g_mlp_in * normed, axis=0)
    g_middle = g_y + normalize_back(g_mlp_in * (1.0 + scale_mlp), normed, rstd)
    g_gate_attn = jnp.sum(g_middle * attended, axis=0)
    g_attended = (gate_attn * g_middle).astype(BF16)
    out_bias_grad = jnp.sum(g_attended.astype(F32), axis=0)
    attended_rows = gather_rows(g_attended)
    g_mixed = dot_t(attended_rows, w_out).astype(BF16)
    g_heads = g_mixed.reshape(query.shape)
    g_probs = jnp.einsum("qhe,khe->hqk", g_heads, value, preferred_element_type=F32)
    row_dot = jnp.sum(probs * g_probs, axis=-1, keepdims=True)
    g_scores = (probs * (g_probs - row_dot)).astype(BF16)
    g_value = jnp.einsum("hqk,qhe->khe", probs.astype(BF16), g_heads, preferred_element_type=F32)
    g_query = jnp.einsum("hqk,khe->qhe", g_scores, key, preferred_element_type=F32) * HEAD**-0.5
    g_key = jnp.einsum("hqk,qhe->khe", g_scores, query, preferred_element_type=F32) * HEAD**-0.5
    g_joint = jnp.concatenate(
        [part.astype(BF16).reshape(rows, width) for part in (g_query, g_key, g_value)], axis=1
    )
    g_attn_in = scatter_rows(dot_t(g_joint, w_joint).astype(BF16), own)
    joint_sum = jnp.sum(g_joint.astype(F32), axis=0)
    joint_bias_grad = jnp.concatenate([joint_sum[:width], joint_sum[2 * width :]])
    w_out_grad = t_dot(mixed, attended_rows)
    w_joint_grad = t_dot(attn_rows, g_joint)
    normed, rstd = normalize(h)
    g_shift_attn = jnp.sum(g_attn_in, axis=0)
    g_scale_attn = jnp.sum(g_attn_in * normed, axis=0)
    g_h = g_middle + normalize_back(g_attn_in * (1.0 + scale_attn), normed, rstd)
    part_grads = (g_shift_attn, g_scale_attn, g_gate_attn, g_shift_mlp, g_scale_mlp, g_gate_mlp)
    weight_grads = (w_joint_grad, w_out_grad, w_expand_grad, w_shrink_grad)
    bias_grads = (joint_bias_grad, out_bias_grad, expand_bias_grad, shrink_bias_grad)
    return g_h, part_grads, weight_grads, bias_grads


def on_device(
    tokens,
    conditions,
    cotangent,
    modulation_weight,
    modulation_bias,
    joint_weight,
    joint_bias,
    output_weight,
    output_bias,
    expand_weight,
    expand_bias,
    shrink_weight,
    shrink_bias,
):
    core = lax.axis_index("pipe")
    first = core == 0
    line = lax.axis_index("dp")
    line_size = lax.axis_size("dp")
    direct = line_size <= LINE_LIMIT
    micro, _, own, model = tokens.shape
    head_width = output_weight.shape[1]
    hidden_width = expand_weight.shape[2]
    half_hidden = hidden_width // 2
    chunk = model // line_size
    half_chunk = head_width // 2
    ordinal = lambda values: flip_blocks(values, line, line_size) if direct else values

    def mine(pair):
        return jnp.where(first, pair[0], pair[1])

    def other(pair):
        return jnp.where(first, pair[1], pair[0])

    def both_layers(value):
        received = swap(value, "pipe", 1)
        return jnp.where(first, value, received), jnp.where(first, received, value)

    def halves_of_layers(halves):
        keep, give = mine(halves), other(halves)
        received = swap(give, "pipe", 1)
        return jnp.where(first, keep, received), jnp.where(first, received, keep)

    def along_line(value):
        if direct:
            return jnp.stack(gather(value, "dp"))
        return lax.all_gather(value, "dp", axis=0)

    def sum_along_line(blocks):
        blocks = blocks.astype(BF16)
        if direct:
            received = exchange([blocks[k] for k in range(line_size)], "dp")
            return tree_sum([block.astype(F32) for block in received])
        return lax.psum_scatter(blocks, "dp", scatter_dimension=0, tiled=False).astype(F32)

    activated = jax.nn.silu(conditions[:, 0].astype(F32)).astype(BF16)
    activated_all = (
        jnp.stack(gather(activated, "dp")) if direct else lax.all_gather(activated, "dp", axis=0)
    )
    own_rows = modulation_weight[0]
    flat_activated = activated_all.reshape(line_size * micro, -1)
    mod_partial = dot(flat_activated, own_rows)
    mod_sum = tree_sum(gather(mod_partial, "tensor"))
    mod_sum = mod_sum.reshape(line_size, micro, -1)
    mod_columns = mod_sum.shape[-1]
    if direct:
        pieces = jnp.stack(exchange([mod_sum[k] for k in range(line_size)], "dp"), axis=1)
        pieces = pieces.reshape(micro, -1)
        mod_layer = flip_blocks(pieces, line, line_size)
    else:
        mod_layer = lax.all_to_all(mod_sum, "dp", split_axis=0, concat_axis=0)
        mod_layer = jnp.swapaxes(mod_layer, 0, 1).reshape(micro, -1)
    mod_layer = mod_layer + modulation_bias[0]
    mod_received = swap(other(mod_layer), "pipe", 1)
    mod_own = mine(mod_layer)
    mod_layers = (jnp.where(first, mod_own, mod_received), jnp.where(first, mod_received, mod_own))
    parts = [
        [ordinal(part) for part in mod.reshape(6, model)] for mod in mod_layers
    ]

    attn_pack = jnp.concatenate(
        [joint_weight[0].reshape(chunk, -1), output_weight[0].reshape(chunk, -1)], axis=1
    )
    halves_attn = halves_of_layers(
        (attn_pack[: chunk // 2], attn_pack[chunk // 2 :])
    )
    halves_expand = halves_of_layers(
        (expand_weight[0][:, :half_hidden], expand_weight[0][:, half_hidden:])
    )
    halves_shrink = halves_of_layers(
        (shrink_weight[0][:half_hidden], shrink_weight[0][half_hidden:])
    )
    bias_pack = jnp.concatenate(
        [joint_bias[0].reshape(-1), output_bias[0], expand_bias[0], shrink_bias[0]]
    )
    bias_layers = both_layers(bias_pack)

    def order_halves(own_half, other_half, axis):
        return jnp.where(
            first,
            jnp.concatenate([own_half, other_half], axis=axis),
            jnp.concatenate([other_half, own_half], axis=axis),
        )

    def roll_hidden(values):
        return jnp.where(
            first, values, jnp.concatenate([values[half_hidden:], values[:half_hidden]])
        )

    joint_cols = 3 * head_width

    def attn_weights(half):
        lined = along_line(half)
        whole = order_halves(lined, swap(lined, "pipe", 1), 1)
        w_joint = whole[:, :, :joint_cols].reshape(model, joint_cols)
        w_out = whole[:, :, joint_cols:].reshape(line_size, head_width, chunk)
        w_out = jnp.swapaxes(w_out, 0, 1).reshape(head_width, model)
        return w_joint, w_out

    def expand_whole(half):
        lined = along_line(half)
        return jnp.concatenate([lined, swap(lined, "pipe", 1)], axis=2).reshape(model, hidden_width)

    def shrink_whole(half):
        lined = along_line(half)
        both = jnp.stack([lined, swap(lined, "pipe", 1)])
        return jnp.transpose(both, (0, 2, 1, 3)).reshape(hidden_width, model)

    def after(value, earlier):
        return lax.optimization_barrier((value, earlier))

    weights = []
    previous = None
    for layer in range(2):
        half_attn, half_expand, half_shrink = halves_attn[layer], halves_expand[layer], halves_shrink[layer]
        if previous is not None:
            half_attn, _ = after(half_attn, previous)
        w_joint, w_out = attn_weights(half_attn)
        half_expand, w_joint = after(half_expand, w_joint)
        w_expand = expand_whole(half_expand)
        half_shrink, w_expand = after(half_shrink, w_expand)
        w_shrink = shrink_whole(half_shrink)
        previous = w_shrink
        weights.append((w_joint, w_out, w_expand, w_shrink))
    biases = []
    for packed in bias_layers:
        split = 2 * head_width
        biases.append(
            (
                packed[:split].reshape(2, head_width),
                ordinal(packed[split : split + model]),
                roll_hidden(packed[split + model : split + model + hidden_width]),
                ordinal(packed[split + model + hidden_width :]),
            )
        )

    h = ordinal(mine(tokens[:, 0])).astype(F32)
    g_y = ordinal(mine(cotangent[:, 0])).astype(F32)
    y, kept_first = layer_forward(h, parts[0], weights[0], biases[0])
    passed = y.astype(BF16)
    y, kept_second = layer_forward(passed.astype(F32), parts[1], weights[1], biases[1])
    outputs = (passed, y.astype(BF16))

    def reduced(weight_grads):
        w_joint_grad, w_out_grad, w_expand_grad, w_shrink_grad = weight_grads
        blocks = jnp.swapaxes(w_out_grad.reshape(head_width, line_size, chunk), 0, 1)
        attn = jnp.concatenate(
            [
                w_joint_grad.reshape(line_size, chunk, joint_cols),
                blocks.reshape(line_size, chunk, head_width),
            ],
            axis=2,
        )
        attn_halves = (attn[:, : chunk // 2], attn[:, chunk // 2 :])
        attn_own = mine(attn_halves) + swap(other(attn_halves).astype(BF16), "pipe", 1).astype(F32)
        expand = w_expand_grad.reshape(line_size, chunk, hidden_width)
        expand_own = expand[:, :, :half_hidden] + swap(
            expand[:, :, half_hidden:].astype(BF16), "pipe", 1
        ).astype(F32)
        shrink = jnp.swapaxes(w_shrink_grad.reshape(hidden_width, line_size, chunk), 0, 1)
        shrink_own = shrink[:, :half_hidden] + swap(
            shrink[:, half_hidden:].astype(BF16), "pipe", 1
        ).astype(F32)
        return sum_along_line(attn_own), sum_along_line(expand_own), sum_along_line(shrink_own)

    g_h, part_grads_second, weight_grads, bias_grads_second = layer_backward(
        g_y, kept_second, parts[1], weights[1]
    )
    reduced_second = reduced(weight_grads)
    g_passed = g_h.astype(BF16)
    g_h, part_grads_first, weight_grads, bias_grads_first = layer_backward(
        g_passed.astype(F32), kept_first, parts[0], weights[0]
    )
    reduced_first = reduced(weight_grads)
    grads_in = (g_h.astype(BF16), g_passed)

    def own_layer(pair):
        received = swap(other(pair), "pipe", 1)
        return mine(pair), received

    attn_grad = order_halves(*own_layer((reduced_first[0], reduced_second[0])), 0)
    expand_grad = order_halves(*own_layer((reduced_first[1], reduced_second[1])), 1)
    shrink_grad = order_halves(*own_layer((reduced_first[2], reduced_second[2])), 0)
    joint_grad = attn_grad[:, :joint_cols].reshape(joint_weight[0].shape)
    output_grad = attn_grad[:, joint_cols:].reshape(output_weight[0].shape)

    def own_layer_of_micros(pair):
        mine_now, received = own_layer(pair)
        return jnp.stack([jnp.where(first, mine_now, received), jnp.where(first, received, mine_now)])

    layer_outputs = own_layer_of_micros(tuple(ordinal(value) for value in outputs))
    input_grads = own_layer_of_micros(tuple(ordinal(value) for value in grads_in))

    part_packs = tuple(
        jnp.concatenate([ordinal(part) for part in grads])
        for grads in (part_grads_first, part_grads_second)
    )
    mod_grad_layers = jnp.stack(part_packs)
    mod_grad_sum = tree_sum(gather(mod_grad_layers, "tensor")).astype(BF16)
    mod_grad = own_layer_of_micros((mod_grad_sum[0], mod_grad_sum[1]))
    mod_grad_all = (
        jnp.stack(gather(mod_grad, "dp")) if direct else lax.all_gather(mod_grad, "dp", axis=0)
    ).reshape(line_size * micro, -1)
    by_line = mod_grad_all.reshape(line_size, micro, -1).astype(F32)
    ada_bias_grad = tree_sum([jnp.sum(by_line[k], axis=0) for k in range(line_size)])
    mod_grad_own = lax.dynamic_slice_in_dim(mod_grad_all, line * mod_columns, mod_columns, 1)
    ada_grad = t_dot(flat_activated, mod_grad_own)
    act_partial = dot_t(mod_grad_own, own_rows).reshape(line_size, micro, -1)
    if direct:
        act_grad = tree_sum(
            exchange([act_partial[k] for k in range(line_size)], "dp")
        )
    else:
        act_grad = lax.psum_scatter(act_partial, "dp", scatter_dimension=0, tiled=False)
    _, silu_back = jax.vjp(jax.nn.silu, conditions[:, 0].astype(F32))
    cond_grad = silu_back(act_grad)[0]

    def pack_biases(grads):
        joint_bias_grad, out_bias_grad, expand_bias_grad, shrink_bias_grad = grads
        return (
            jnp.concatenate([joint_bias_grad, roll_hidden(expand_bias_grad)]),
            jnp.concatenate([ordinal(out_bias_grad), ordinal(shrink_bias_grad)]),
        )

    packs_first, packs_second = pack_biases(bias_grads_first), pack_biases(bias_grads_second)
    token_sums = jnp.stack([packs_first[1], packs_second[1]])
    token_sums = tree_sum(gather(token_sums, "tensor"))
    bias_first = jnp.concatenate([packs_first[0], token_sums[0]])
    bias_second = jnp.concatenate([packs_second[0], token_sums[1]])
    bias_own = tree_sum(own_layer((bias_first, bias_second)))
    bias_sum = (
        tree_sum(gather(bias_own, "dp")) if direct else lax.psum(bias_own, "dp")
    )
    split = 2 * head_width
    joint_bias_grad = bias_sum[:split].reshape(2, head_width)
    expand_bias_grad = bias_sum[split : split + hidden_width]
    out_bias_grad = bias_sum[split + hidden_width : split + hidden_width + model]
    shrink_bias_grad = bias_sum[split + hidden_width + model :]
    return (
        layer_outputs[None, :, None],
        input_grads[None, :, None],
        cond_grad[None, :, None],
        ada_grad[None],
        ada_bias_grad[None],
        joint_grad[None],
        joint_bias_grad[None],
        output_grad[None],
        out_bias_grad[None],
        expand_grad[None],
        expand_bias_grad[None],
        shrink_grad[None],
        shrink_bias_grad[None],
    )


def solution(mesh):
    in_specs = (
        P(None, "dp", "tensor", None),
        P(None, "dp", "tensor"),
        P(None, "dp", "tensor", None),
        P("pipe", "tensor", "dp"),
        P("pipe", None),
        P("pipe", "dp", None, "tensor"),
        P("pipe", None, "tensor"),
        P("pipe", "tensor", "dp"),
        P("pipe", None),
        P("pipe", "dp", "tensor"),
        P("pipe", "tensor"),
        P("pipe", "tensor", "dp"),
        P("pipe", None),
    )
    out_specs = (
        P("pipe", None, "dp", "tensor", None),
        P("pipe", None, "dp", "tensor", None),
        P("pipe", None, "dp", "tensor"),
        P("pipe", "tensor", "dp"),
        P("pipe", None),
        P("pipe", "dp", None, "tensor"),
        P("pipe", None, "tensor"),
        P("pipe", "tensor", "dp"),
        P("pipe", None),
        P("pipe", "dp", "tensor"),
        P("pipe", "tensor"),
        P("pipe", "tensor", "dp"),
        P("pipe", None),
    )
    return jax.shard_map(
        on_device, mesh=mesh, in_specs=in_specs, out_specs=out_specs, check_vma=False
    )
```

time: 817 us -> 486 us (0.59)
  waiting for transfers between devices: 384 us -> 123 us
  blocking collectives: 242 us -> 0 us
  starting transfers between devices: 0.9 us -> 139 us
  local copies, waits for them, and re-layouts: 35.9 us -> 94.8 us
  between operations: 17.4 us -> 4.57 us
  matrix products: 49.8 us -> 41.2 us
    reduce_scatter x15 -> x0, waiting for transfers between devices: 283 us -> none  [the longest x3 66.6 us: layer_forward(): lax.psum_scatter(jnp.dot(piece_rows, final_output_weight, preferred_eleme...]
    all_gather x14 -> x0, blocking collectives: 189 us -> none  [the longest x1 44.8 us: on_device(): lax.all_gather(joint_weight[0], 'dp', axis=0, tiled=True)]
    ppermute x4 -> x132, starting transfers between devices: 0.08 us -> 139 us  [swap(): return lax.ppermute(value, axis, pairs)]
    ppermute x4 -> x132, waiting for transfers between devices: 3.75 us -> 123 us  [swap(): return lax.ppermute(value, axis, pairs)]
    psum x3 -> x0, blocking collectives: 53.8 us -> none  [the longest x1 21.1 us: on_device(): lax.psum((bias_local[0], bias_local[1], bias_local[2], bias_local[3], bia...]
    unnamed x22 -> x0, waiting for transfers between devices: 49.4 us -> none
    all_gather x3 -> x0, waiting for transfers between devices: 47.8 us -> none  [the longest x1 29.2 us: on_device(): lax.all_gather(shrink_weight[0], 'dp', axis=1, tiled=True)]
    reshape x0 -> x113, local copies, waits for them, and re-layouts: none -> 30.1 us  [the longest x74 24.5 us: flip_blocks(): flipped = paired[..., ::-1, :, :].reshape(blocks.shape)]
  transfers between devices with their start and end apart: 24 -> 132, of which waited for: 22 -> 43; matrix products, arithmetic and copies ran while one was open for 10% -> 40% of each run, Pallas kernels for 0% -> 0%
where the time goes in v1:
time: 486 us; the launch traced here: 477 us
  starting transfers between devices  139 us (29%)
  waiting for transfers between devices  123 us (25%)
  local copies, waits for them, and re-layouts  94.8 us (20%)
  other arithmetic  74.5 us (15%)
  matrix products  41.2 us (8%)
    ppermute x132, starting transfers between devices, swap(): return lax.ppermute(value, axis, pairs)  139 us
    ppermute x132, waiting for transfers between devices, swap(): return lax.ppermute(value, axis, pairs)  123 us
    reshape x74, local copies, waits for them, and re-layouts, flip_blocks(): flipped = paired[..., ::-1, :, :].reshape(blocks.shape)  24.5 us
    unnamed x18, other arithmetic  16.5 us
    rev x76, local copies, waits for them, and re-layouts, flip_blocks(): flipped = paired[..., ::-1, :, :].reshape(blocks.shape)  13.5 us
    dot_general x9, matrix products, t_dot(): lax.dot_general(left, right, (((0,), (0,)), ((), ())), preferred_element_...  11.9 us
    dot_general x9, matrix products, dot_t(): lax.dot_general(left, right, (((1,), (1,)), ((), ())), preferred_element_...  11 us
  transfers between devices with their start and end apart: 132, of which 43 were waited for; matrix products, arithmetic and copies ran while one was open for 40% of the time, Pallas kernels for 0%

profile of v1, /device:TPU:0, one launch (start us, length us, event | category | flops | bytes accessed | tf_op | source)
XLA Modules:
  0.0 477.1 jit_solution(4721677011475850770)
XLA Ops:
  1.4 5.1 %collective-permute-start.2 = (bf16[2,192]{1,0:T(2,128)(2,1)S(1)}, bf16[2,192]{1,0:T(2,128)(2,1)S(1)}, u32[]{:S(2)}, u32[]{:S(2)}) collective-permute-start(bf16[2,192]{1,0:T(2,128)(2,1)S(1)} %fusion.114), channel_id=1, source_target_pairs={{0,12},{4,8},{8,4},{12,0},{1,13},{5,9},{9,5},{13,1},{2,14},{6,10},... | collective-permute-start | bytes 2312 | tf_op jit(solution)/shard_map/ppermute | solution.py:15
  27.5 3.7 collective-permute-start.8
  49.4 3.6 collective-permute-done.17
  54.5 5.8 %collective-permute-done.16 = bf16[96,768]{1,0:T(8,128)(2,1)S(1)} collective-permute-done((bf16[96,768]{1,0:T(8,128)(2,1)S(1)}, bf16[96,768]{1,0:T(8,128)(2,1)S(1)}, u32[]{:S(2)}, u32[]{:S(2)}) %collective-permute-start.16) | collective-permute-done | bytes 147488 | tf_op jit(solution)/shard_map/ppermute | solution.py:15
  66.9 2.7 collective-permute-start.29
  77.7 3.8 collective-permute-done.28
  83.3 2.9 collective-permute-done.21
  91.5 4.2 collective-permute-done.33
  95.6 6.0 %collective-permute-done.32 = bf16[384,192]{0,1:T(8,128)(2,1)S(1)} collective-permute-done((bf16[384,192]{0,1:T(8,128)(2,1)S(1)}, bf16[384,192]{0,1:T(8,128)(2,1)S(1)}, u32[]{:S(2)}, u32[]{:S(2)}) %collective-permute-start.32) | collective-permute-done | bytes 147488 | tf_op jit(solution)/shard_map/ppermute | solution.py:15
  121.5 2.8 collective-permute-start.41
  124.5 4.0 collective-permute-done.43
  128.5 4.4 collective-permute-done.42
  162.7 4.2 collective-permute-done.57
  166.9 5.4 %collective-permute-done.56 = bf16[384,192]{0,1:T(8,128)(2,1)S(1)} collective-permute-done((bf16[384,192]{0,1:T(8,128)(2,1)S(1)}, bf16[384,192]{0,1:T(8,128)(2,1)S(1)}, u32[]{:S(2)}, u32[]{:S(2)}) %collective-permute-start.56) | collective-permute-done | bytes 147488 | tf_op jit(solution)/shard_map/ppermute | solution.py:15
  381.3 3.6 collective-permute-done.94
  387.0 2.9 collective-permute-start.95
  402.9 3.7 collective-permute-start.125
  406.6 9.3 %collective-permute-done.129 = bf16[384,192]{0,1:T(8,128)(2,1)S(1)} collective-permute-done((bf16[384,192]{0,1:T(8,128)(2,1)S(1)}, bf16[384,192]{0,1:T(8,128)(2,1)S(1)}, u32[]{:S(2)}, u32[]{:S(2)}) %collective-permute-start.129) | collective-permute-done | bytes 147488 | tf_op jit(solution)/shard_map/ppermute | solution.py:15
  419.5 9.1 %collective-permute-done.125 = bf16[384,192]{0,1:T(8,128)(2,1)S(1)} collective-permute-done((bf16[384,192]{0,1:T(8,128)(2,1)S(1)}, bf16[384,192]{0,1:T(8,128)(2,1)S(1)}, u32[]{:S(2)}, u32[]{:S(2)}) %collective-permute-start.125) | collective-permute-done | bytes 147488 | tf_op jit(solution)/shard_map/ppermute | solution.py:15
  436.1 4.2 collective-permute-done.103
  440.3 3.3 collective-permute-done.115
  445.7 13.0 %collective-permute-done.116 = bf16[192,384]{1,0:T(8,128)(2,1)S(1)} collective-permute-done((bf16[192,384]{1,0:T(8,128)(2,1)S(1)}, bf16[192,384]{1,0:T(8,128)(2,1)S(1)}, u32[]{:S(2)}, u32[]{:S(2)}) %collective-permute-start.116) | collective-permute-done | bytes 147488 | tf_op jit(solution)/shard_map/ppermute | solution.py:15
  459.9 6.7 %collective-permute-done.104 = bf16[96,768]{1,0:T(8,128)(2,1)S(1)} collective-permute-done((bf16[96,768]{1,0:T(8,128)(2,1)S(1)}, bf16[96,768]{1,0:T(8,128)(2,1)S(1)}, u32[]{:S(2)}, u32[]{:S(2)}) %collective-permute-start.104) | collective-permute-done | bytes 147488 | tf_op jit(solution)/shard_map/ppermute | solution.py:15
  466.6 5.5 %collective-permute-done.100 = bf16[96,768]{1,0:T(8,128)(2,1)S(1)} collective-permute-done((bf16[96,768]{1,0:T(8,128)(2,1)S(1)}, bf16[96,768]{1,0:T(8,128)(2,1)S(1)}, u32[]{:S(2)}, u32[]{:S(2)}) %collective-permute-start.100) | collective-permute-done | bytes 147488 | tf_op jit(solution)/shard_map/ppermute | solution.py:15
  (1168 shorter events, 352.5 us)
Async XLA Ops:
  1.4 18.6 %collective-permute-start.2 = (bf16[2,192]{1,0:T(2,128)(2,1)S(1)}, bf16[2,192]{1,0:T(2,128)(2,1)S(1)}, u32[]{:S(2)}, u32[]{:S(2)}) collective-permute-start(bf16[2,192]{1,0:T(2,128)(2,1)S(1)} %fusion.114), channel_id=1, source_target_pairs={{0,12},{4,8},{8,4},{12,0},{1,13},{5,9},{9,5},{13,1},{2,14},{6,10},... | collective-permute-start | bytes 2312 | tf_op jit(solution)/shard_map/ppermute | solution.py:15
  11.2 71.4 %collective-permute-start.26 = (bf16[384,192]{0,1:T(8,128)(2,1)S(1)}, bf16[384,192]{0,1:T(8,128)(2,1)S(1)}, u32[]{:S(2)}, u32[]{:S(2)}) collective-permute-start(bf16[384,192]{0,1:T(8,128)(2,1)S(1)} %select_bitcast_fusion.2), channel_id=1, source_target_pairs={{0,16},{16,0},{1,17},{17,1},{2,18},{18,2},{3,19},{19,3},{4,20},{20... | collective-permute-start | bytes 442376 | tf_op jit(solution)/shard_map/ppermute | solution.py:15
  20.1 43.2 %collective-permute-start.13 = (bf16[192,384]{1,0:T(8,128)(2,1)S(1)}, bf16[192,384]{1,0:T(8,128)(2,1)S(1)}, u32[]{:S(2)}, u32[]{:S(2)}) collective-permute-start(bf16[192,384]{1,0:T(8,128)(2,1)S(1)} %broadcast_select_fusion.19), channel_id=1, source_target_pairs={{0,16},{16,0},{1,17},{17,1},{2,18},{18,2},{3,19},{19,3},{4,20},{20... | collective-permute-start | bytes 442376 | tf_op jit(solution)/shard_map/ppermute | solution.py:15
  53.0 16.6 %collective-permute-start.12 = (bf16[64,768]{1,0:T(8,128)(2,1)S(1)}, bf16[64,768]{1,0:T(8,128)(2,1)S(1)}, u32[]{:S(2)}, u32[]{:S(2)}) collective-permute-start(bf16[64,768]{1,0:T(8,128)(2,1)S(1)} %get-tuple-element.164), channel_id=1, source_target_pairs={{0,3},{1,2},{2,1},{3,0},{4,7},{5,6},{6,5},{7,4},{8,11},{9,10},{10,... | collective-permute-start | bytes 294920 | tf_op jit(solution)/shard_map/ppermute | solution.py:15
  216.1 84.2 %collective-permute-start.127 = (bf16[4,384,192]{1,2,0:T(8,128)(2,1)}, bf16[4,384,192]{1,2,0:T(8,128)(2,1)}, u32[]{:S(2)}, u32[]{:S(2)}) collective-permute-start(bf16[4,384,192]{1,2,0:T(8,128)(2,1)} %slice.1240), channel_id=1, source_target_pairs={{0,16},{16,0},{1,17},{17,1},{2,18},{18,2},{3,19},{19,3},{4,20},{20... | collective-permute-start | bytes 1769480 | tf_op jit(solution)/shard_map/ppermute | solution.py:15
  217.6 86.3 %collective-permute-start.118 = (bf16[4,192,384]{2,1,0:T(8,128)(2,1)}, bf16[4,192,384]{2,1,0:T(8,128)(2,1)}, u32[]{:S(2)}, u32[]{:S(2)}) collective-permute-start(bf16[4,192,384]{2,1,0:T(8,128)(2,1)} %slice.1242), channel_id=1, source_target_pairs={{0,16},{16,0},{1,17},{17,1},{2,18},{18,2},{3,19},{19,3},{4,20},{20... | collective-permute-start | bytes 1769480 | tf_op jit(solution)/shard_map/ppermute | solution.py:15
  248.1 26.7 %collective-permute-start.77 = (bf16[64,768]{1,0:T(8,128)(2,1)}, bf16[64,768]{1,0:T(8,128)(2,1)}, u32[]{:S(2)}, u32[]{:S(2)}) collective-permute-start(bf16[64,768]{1,0:T(8,128)(2,1)} %get-tuple-element.139), channel_id=1, source_target_pairs={{0,3},{1,2},{2,1},{3,0},{4,7},{5,6},{6,5},{7,4},{8,11},{9,10},{10,... | collective-permute-start | bytes 294920 | tf_op jit(solution)/shard_map/ppermute | solution.py:15
  249.5 25.3 %collective-permute-start.76 = (bf16[64,768]{1,0:T(8,128)(2,1)}, bf16[64,768]{1,0:T(8,128)(2,1)}, u32[]{:S(2)}, u32[]{:S(2)}) collective-permute-start(bf16[64,768]{1,0:T(8,128)(2,1)} %get-tuple-element.139), channel_id=1, source_target_pairs={{0,2},{1,3},{2,0},{3,1},{4,6},{5,7},{6,4},{7,5},{8,10},{9,11},{10,... | collective-permute-start | bytes 294920 | tf_op jit(solution)/shard_map/ppermute | solution.py:15
  250.7 24.1 %collective-permute-start.75 = (bf16[64,768]{1,0:T(8,128)(2,1)}, bf16[64,768]{1,0:T(8,128)(2,1)}, u32[]{:S(2)}, u32[]{:S(2)}) collective-permute-start(bf16[64,768]{1,0:T(8,128)(2,1)} %get-tuple-element.139), channel_id=1, source_target_pairs={{0,1},{1,0},{2,3},{3,2},{4,5},{5,4},{6,7},{7,6},{8,9},{9,8},{10,11... | collective-permute-start | bytes 294920 | tf_op jit(solution)/shard_map/ppermute | solution.py:15
  297.4 97.2 %collective-permute-start.102 = (bf16[4,96,768]{2,1,0:T(8,128)(2,1)}, bf16[4,96,768]{2,1,0:T(8,128)(2,1)}, u32[]{:S(2)}, u32[]{:S(2)}) collective-permute-start(bf16[4,96,768]{2,1,0:T(8,128)(2,1)} %select_convert_fusion), channel_id=1, source_target_pairs={{0,16},{16,0},{1,17},{17,1},{2,18},{18,2},{3,19},{19,3},{4,20},{20... | collective-permute-start | bytes 1769480 | tf_op jit(solution)/shard_map/ppermute | solution.py:15
  297.4 100.5 %collective-permute-start.123 = (bf16[4,384,192]{1,2,0:T(8,128)(2,1)}, bf16[4,384,192]{1,2,0:T(8,128)(2,1)}, u32[]{:S(2)}, u32[]{:S(2)}) collective-permute-start(bf16[4,384,192]{1,2,0:T(8,128)(2,1)} %slice.1241), channel_id=1, source_target_pairs={{0,16},{16,0},{1,17},{17,1},{2,18},{18,2},{3,19},{19,3},{4,20},{20... | collective-permute-start | bytes 1769480 | tf_op jit(solution)/shard_map/ppermute | solution.py:15
  396.3 19.6 %collective-permute-start.129 = (bf16[384,192]{0,1:T(8,128)(2,1)S(1)}, bf16[384,192]{0,1:T(8,128)(2,1)S(1)}, u32[]{:S(2)}, u32[]{:S(2)}) collective-permute-start(bf16[384,192]{0,1:T(8,128)(2,1)S(1)} %copy-done.101), channel_id=1, source_target_pairs={{0,8},{4,12},{8,0},{12,4},{1,9},{5,13},{9,1},{13,5},{2,10},{6,14},... | collective-permute-start | bytes 442376 | tf_op jit(solution)/shard_map/ppermute | solution.py:15
  397.9 31.8 %collective-permute-start.98 = (bf16[4,96,768]{2,1,0:T(8,128)(2,1)S(1)}, bf16[4,96,768]{2,1,0:T(8,128)(2,1)S(1)}, u32[]{:S(2)}, u32[]{:S(2)}) collective-permute-start(bf16[4,96,768]{2,1,0:T(8,128)(2,1)S(1)} %copy-done.47), channel_id=1, source_target_pairs={{0,16},{16,0},{1,17},{17,1},{2,18},{18,2},{3,19},{19,3},{4,20},{20... | collective-permute-start | bytes 1769480 | tf_op jit(solution)/shard_map/ppermute | solution.py:15
  399.7 16.3 %collective-permute-start.124 = (bf16[384,192]{0,1:T(8,128)(2,1)S(1)}, bf16[384,192]{0,1:T(8,128)(2,1)S(1)}, u32[]{:S(2)}, u32[]{:S(2)}) collective-permute-start(bf16[384,192]{0,1:T(8,128)(2,1)S(1)} %get-tuple-element.180), channel_id=1, source_target_pairs={{0,4},{4,0},{8,12},{12,8},{1,5},{5,1},{9,13},{13,9},{2,6},{6,2},{1... | collective-permute-start | bytes 442376 | tf_op jit(solution)/shard_map/ppermute | solution.py:15
  401.3 15.8 %collective-permute-start.126 = (bf16[384,192]{0,1:T(8,128)(2,1)S(1)}, bf16[384,192]{0,1:T(8,128)(2,1)S(1)}, u32[]{:S(2)}, u32[]{:S(2)}) collective-permute-start(bf16[384,192]{0,1:T(8,128)(2,1)S(1)} %get-tuple-element.181), channel_id=1, source_target_pairs={{0,12},{4,8},{8,4},{12,0},{1,13},{5,9},{9,5},{13,1},{2,14},{6,10},... | collective-permute-start | bytes 442376 | tf_op jit(solution)/shard_map/ppermute | solution.py:15
  402.9 25.7 %collective-permute-start.125 = (bf16[384,192]{0,1:T(8,128)(2,1)S(1)}, bf16[384,192]{0,1:T(8,128)(2,1)S(1)}, u32[]{:S(2)}, u32[]{:S(2)}) collective-permute-start(bf16[384,192]{0,1:T(8,128)(2,1)S(1)} %get-tuple-element.182), channel_id=1, source_target_pairs={{0,8},{4,12},{8,0},{12,4},{1,9},{5,13},{9,1},{13,5},{2,10},{6,14},... | collective-permute-start | bytes 442376 | tf_op jit(solution)/shard_map/ppermute | solution.py:15
  416.0 16.1 %collective-permute-start.119 = (bf16[192,384]{1,0:T(8,128)(2,1)S(1)}, bf16[192,384]{1,0:T(8,128)(2,1)S(1)}, u32[]{:S(2)}, u32[]{:S(2)}) collective-permute-start(bf16[192,384]{1,0:T(8,128)(2,1)S(1)} %copy-done.100), channel_id=1, source_target_pairs={{0,4},{4,0},{8,12},{12,8},{1,5},{5,1},{9,13},{13,9},{2,6},{6,2},{1... | collective-permute-start | bytes 442376 | tf_op jit(solution)/shard_map/ppermute | solution.py:15
  416.0 17.3 %collective-permute-start.121 = (bf16[192,384]{1,0:T(8,128)(2,1)S(1)}, bf16[192,384]{1,0:T(8,128)(2,1)S(1)}, u32[]{:S(2)}, u32[]{:S(2)}) collective-permute-start(bf16[192,384]{1,0:T(8,128)(2,1)S(1)} %copy-done.99), channel_id=1, source_target_pairs={{0,12},{4,8},{8,4},{12,0},{1,13},{5,9},{9,5},{13,1},{2,14},{6,10},... | collective-permute-start | bytes 442376 | tf_op jit(solution)/shard_map/ppermute | solution.py:15
  417.1 18.1 %collective-permute-start.120 = (bf16[192,384]{1,0:T(8,128)(2,1)S(1)}, bf16[192,384]{1,0:T(8,128)(2,1)S(1)}, u32[]{:S(2)}, u32[]{:S(2)}) collective-permute-start(bf16[192,384]{1,0:T(8,128)(2,1)S(1)} %copy-done.98), channel_id=1, source_target_pairs={{0,8},{4,12},{8,0},{12,4},{1,9},{5,13},{9,1},{13,5},{2,10},{6,14},... | collective-permute-start | bytes 442376 | tf_op jit(solution)/shard_map/ppermute | solution.py:15
  433.3 25.4 %collective-permute-start.116 = (bf16[192,384]{1,0:T(8,128)(2,1)S(1)}, bf16[192,384]{1,0:T(8,128)(2,1)S(1)}, u32[]{:S(2)}, u32[]{:S(2)}) collective-permute-start(bf16[192,384]{1,0:T(8,128)(2,1)S(1)} %get-tuple-element.188), channel_id=1, source_target_pairs={{0,8},{4,12},{8,0},{12,4},{1,9},{5,13},{9,1},{13,5},{2,10},{6,14},... | collective-permute-start | bytes 442376 | tf_op jit(solution)/shard_map/ppermute | solution.py:15
  435.2 24.6 %collective-permute-start.105 = (bf16[96,768]{1,0:T(8,128)(2,1)S(1)}, bf16[96,768]{1,0:T(8,128)(2,1)S(1)}, u32[]{:S(2)}, u32[]{:S(2)}) collective-permute-start(bf16[96,768]{1,0:T(8,128)(2,1)S(1)} %get-tuple-element.190), channel_id=1, source_target_pairs={{0,12},{4,8},{8,4},{12,0},{1,13},{5,9},{9,5},{13,1},{2,14},{6,10},... | collective-permute-start | bytes 442376 | tf_op jit(solution)/shard_map/ppermute | solution.py:15
  440.3 26.3 %collective-permute-start.104 = (bf16[96,768]{1,0:T(8,128)(2,1)S(1)}, bf16[96,768]{1,0:T(8,128)(2,1)S(1)}, u32[]{:S(2)}, u32[]{:S(2)}) collective-permute-start(bf16[96,768]{1,0:T(8,128)(2,1)S(1)} %get-tuple-element.191), channel_id=1, source_target_pairs={{0,8},{4,12},{8,0},{12,4},{1,9},{5,13},{9,1},{13,5},{2,10},{6,14},... | collective-permute-start | bytes 442376 | tf_op jit(solution)/shard_map/ppermute | solution.py:15
  443.6 23.0 %collective-permute-start.99 = (bf16[96,768]{1,0:T(8,128)(2,1)S(1)}, bf16[96,768]{1,0:T(8,128)(2,1)S(1)}, u32[]{:S(2)}, u32[]{:S(2)}) collective-permute-start(bf16[96,768]{1,0:T(8,128)(2,1)S(1)} %get-tuple-element.192), channel_id=1, source_target_pairs={{0,4},{4,0},{8,12},{12,8},{1,5},{5,1},{9,13},{13,9},{2,6},{6,2},{1... | collective-permute-start | bytes 442376 | tf_op jit(solution)/shard_map/ppermute | solution.py:15
  443.6 23.0 %collective-permute-start.101 = (bf16[96,768]{1,0:T(8,128)(2,1)S(1)}, bf16[96,768]{1,0:T(8,128)(2,1)S(1)}, u32[]{:S(2)}, u32[]{:S(2)}) collective-permute-start(bf16[96,768]{1,0:T(8,128)(2,1)S(1)} %get-tuple-element.193), channel_id=1, source_target_pairs={{0,12},{4,8},{8,4},{12,0},{1,13},{5,9},{9,5},{13,1},{2,14},{6,10},... | collective-permute-start | bytes 442376 | tf_op jit(solution)/shard_map/ppermute | solution.py:15
  (291 other events, 2312.9 us)

commit v2 on v1

v2 whole, which is shorter than its diff:
```python
import functools

import jax
import jax.numpy as jnp
from jax import lax
from jax.experimental import pallas as pl
from jax.experimental.pallas import tpu as pltpu
from jax.sharding import PartitionSpec as P

HEAD = 64
EPS = 1e-06
F32 = jnp.float32
BF16 = jnp.bfloat16
LINE = 4
VMEM_BYTES = 24 * 1024 * 1024
GELU_A = 0.7978845608028654
GELU_B = 0.044715


def swap(value, axis, mask):
    pairs = [(source, source ^ mask) for source in range(lax.axis_size(axis))]
    return lax.ppermute(value, axis, pairs)


def exchange(parts, axis):
    return [parts[0]] + [swap(parts[k], axis, k) for k in range(1, len(parts))]


def gather(value, axis):
    return exchange([value] * lax.axis_size(axis), axis)


def tree_sum(parts):
    parts = list(parts)
    while len(parts) > 1:
        parts = [parts[k] + parts[k + 1] for k in range(0, len(parts), 2)]
    return parts[0]


def shape(dims, dtype):
    return jax.ShapeDtypeStruct(dims, dtype)


def run(name, body, outs, args, place=None):
    specs = [pl.BlockSpec(memory_space=pltpu.VMEM) for _ in args]
    if place is not None:
        specs = [pl.BlockSpec(memory_space=pltpu.SMEM)] + specs
        args = [place] + list(args)
    return pl.pallas_call(
        body,
        out_shape=outs,
        in_specs=specs,
        out_specs=[pl.BlockSpec(memory_space=pltpu.VMEM) for _ in outs],
        compiler_params=pltpu.CompilerParams(vmem_limit_bytes=VMEM_BYTES),
        name=name,
    )(*args)


def dot(left, right):
    return jnp.dot(left, right, preferred_element_type=F32)


def dot_t(left, right):
    return lax.dot_general(left, right, (((1,), (1,)), ((), ())), preferred_element_type=F32)


def t_dot(left, right):
    return lax.dot_general(left, right, (((0,), (0,)), ((), ())), preferred_element_type=F32)


def normalize(values):
    centred = values - jnp.mean(values, axis=-1, keepdims=True)
    rstd = lax.rsqrt(jnp.mean(centred * centred, axis=-1, keepdims=True) + EPS)
    return centred * rstd, rstd


def normalize_back(grad, normed, rstd):
    return rstd * (
        grad
        - jnp.mean(grad, axis=-1, keepdims=True)
        - normed * jnp.mean(grad * normed, axis=-1, keepdims=True)
    )


def total(refs):
    return tree_sum([ref[...].astype(F32) for ref in refs])


def column_sum(values):
    return jnp.sum(values, axis=0, keepdims=True)


def part(mod_ref, index):
    width = mod_ref.shape[1] // 6
    return mod_ref[:, index * width : (index + 1) * width]


def gelu(pre):
    return 0.5 * pre * (1.0 + jnp.tanh(GELU_A * (pre + GELU_B * (pre * pre * pre))))


def gelu_slope(pre):
    square = pre * pre
    bent = jnp.tanh(GELU_A * (pre + GELU_B * (square * pre)))
    return 0.5 * (1.0 + bent) + 0.5 * pre * (1.0 - bent * bent) * (
        GELU_A * (1.0 + 3.0 * GELU_B * square)
    )


def put_rows(ref, refs):
    own = refs[0].shape[0]
    for k, source in enumerate(refs):
        ref[k * own : (k + 1) * own] = source[...]
    return ref[...]


def put_blocks(refs, values):
    own = refs[0].shape[0]
    for k, ref in enumerate(refs):
        ref[...] = values[k * own : (k + 1) * own].astype(ref.dtype)


def enter_body(place, tokens, cotangent, mod0, mod1, h_out, attn_in, g_y_out, g_shrunk):
    core = place[0]
    h = tokens[core].astype(F32)
    h_out[...] = h
    normed, _ = normalize(h)
    attn_in[...] = (normed * (1.0 + part(mod0, 1)) + part(mod0, 0)).astype(BF16)
    g_y = cotangent[core].astype(F32)
    g_y_out[...] = g_y
    g_shrunk[...] = (part(mod1, 5) * g_y).astype(BF16)


def pick_attn(place, own, received):
    first = place[0] == 0
    width = own.shape[1] // 2
    mine, other = own[...], received[...]
    front = jnp.where(first, mine, other)
    back = jnp.where(first, other, mine)
    return front, back[:, :width], back[:, width:]


def attn_body(count, place, *refs):
    chunks = refs[:count]
    w_own, w_received, bias = refs[count : count + 3]
    rows_out, qkv_out, probs_out, mixed_out = refs[count + 3 : count + 7]
    partial = refs[count + 7 :]
    rows = put_rows(rows_out, chunks)
    w_front, w_value, w_out = pick_attn(place, w_own, w_received)
    width = w_value.shape[1]
    front = (dot(rows, w_front) + bias[:, : 2 * width]).astype(BF16)
    value = (dot(rows, w_value) + bias[:, 2 * width :]).astype(BF16)
    qkv_out[:, : 2 * width] = front
    qkv_out[:, 2 * width :] = value
    mixed = []
    for head in range(width // HEAD):
        at = head * HEAD
        query = front[:, at : at + HEAD]
        key = front[:, width + at : width + at + HEAD]
        scores = dot_t(query, key) * HEAD**-0.5
        powers = jnp.exp(scores - jnp.max(scores, axis=-1, keepdims=True))
        probs = powers / jnp.sum(powers, axis=-1, keepdims=True)
        probs_out[head] = probs
        mixed.append(dot(probs.astype(BF16), value[:, at : at + HEAD]))
    mixed = jnp.concatenate(mixed, axis=1).astype(BF16)
    mixed_out[...] = mixed
    put_blocks(partial, dot_t(mixed, w_out))


def middle_body(count, *refs):
    parts, (bias, h, mod, attended_out, middle_out, mlp_in) = refs[:count], refs[count:]
    attended = total(parts) + bias[...]
    attended_out[...] = attended
    middle = h[...] + part(mod, 2) * attended
    middle_out[...] = middle
    normed, _ = normalize(middle)
    mlp_in[...] = (normed * (1.0 + part(mod, 4)) + part(mod, 3)).astype(BF16)


def mlp_body(count, *refs):
    chunks = refs[:count]
    w_own, w_received, bias, rows_out, pre_out, hidden_out = refs[count : count + 6]
    partial = refs[count + 6 :]
    rows = put_rows(rows_out, chunks)
    half = w_own.shape[1] // 2
    shrunk = None
    for index, weight in enumerate((w_own, w_received)):
        at = index * half
        pre = dot(rows, weight[:, :half]) + bias[:, at : at + half]
        pre_out[:, at : at + half] = pre
        hidden = gelu(pre).astype(BF16)
        hidden_out[:, at : at + half] = hidden
        term = dot_t(hidden, weight[:, half:])
        shrunk = term if shrunk is None else shrunk + term
    put_blocks(partial, shrunk)


def mlp_both_body(count, *refs):
    chunks, g_chunks = refs[:count], refs[count : 2 * count]
    w_own, w_received, bias, rows_out, g_rows_out, hidden_out, g_pre_out, bias_grad = refs[
        2 * count : 2 * count + 8
    ]
    partial = refs[2 * count + 8 : 3 * count + 8]
    g_partial = refs[3 * count + 8 :]
    rows = put_rows(rows_out, chunks)
    g_rows = put_rows(g_rows_out, g_chunks)
    half = w_own.shape[1] // 2
    shrunk, g_in = None, None
    for index, weight in enumerate((w_own, w_received)):
        at = index * half
        pre = dot(rows, weight[:, :half]) + bias[:, at : at + half]
        hidden = gelu(pre).astype(BF16)
        hidden_out[:, at : at + half] = hidden
        g_pre = (dot(g_rows, weight[:, half:]) * gelu_slope(pre)).astype(BF16)
        g_pre_out[:, at : at + half] = g_pre
        bias_grad[:, at : at + half] = column_sum(g_pre.astype(F32))
        term = dot_t(hidden, weight[:, half:])
        g_term = dot_t(g_pre, weight[:, :half])
        shrunk = term if shrunk is None else shrunk + term
        g_in = g_term if g_in is None else g_in + g_term
    put_blocks(g_partial, g_in)
    put_blocks(partial, shrunk)


def mlp_back_body(count, *refs):
    g_chunks = refs[:count]
    w_own, w_received, pre_ref, g_rows_out, g_pre_out, bias_grad = refs[count : count + 6]
    g_partial = refs[count + 6 :]
    g_rows = put_rows(g_rows_out, g_chunks)
    half = w_own.shape[1] // 2
    g_in = None
    for index, weight in enumerate((w_own, w_received)):
        at = index * half
        pre = pre_ref[:, at : at + half]
        g_pre = (dot(g_rows, weight[:, half:]) * gelu_slope(pre)).astype(BF16)
        g_pre_out[:, at : at + half] = g_pre
        bias_grad[:, at : at + half] = column_sum(g_pre.astype(F32))
        g_term = dot_t(g_pre, weight[:, :half])
        g_in = g_term if g_in is None else g_in + g_term
    put_blocks(g_partial, g_in)


def between_body(count, *refs):
    parts = refs[:count]
    bias, middle, mod0, mod1, shrunk_out, passed_out, h_out, attn_in = refs[count:]
    shrunk = total(parts) + bias[...]
    shrunk_out[...] = shrunk
    passed = (middle[...] + part(mod0, 5) * shrunk).astype(BF16)
    passed_out[...] = passed
    h = passed.astype(F32)
    h_out[...] = h
    normed, _ = normalize(h)
    attn_in[...] = (normed * (1.0 + part(mod1, 1)) + part(mod1, 0)).astype(BF16)


def leave_body(count, *refs):
    parts = refs[:count]
    bias, middle, mod, g_y_ref, g_shrunk, y_out, g_gate, bias_grad = refs[count:]
    shrunk = total(parts) + bias[...]
    y_out[...] = (middle[...] + part(mod, 5) * shrunk).astype(BF16)
    g_gate[...] = column_sum(g_y_ref[...] * shrunk)
    bias_grad[...] = column_sum(g_shrunk[...].astype(F32))


def middle_back_body(count, *refs):
    parts = refs[:count]
    middle, mod, g_y, attended, g_middle_out, g_attended_out, g_shift, g_scale, g_gate, bias_grad = refs[
        count:
    ]
    g_in = total(parts)
    normed, rstd = normalize(middle[...])
    g_shift[...] = column_sum(g_in)
    g_scale[...] = column_sum(g_in * normed)
    g_middle = g_y[...] + normalize_back(g_in * (1.0 + part(mod, 4)), normed, rstd)
    g_middle_out[...] = g_middle
    g_gate[...] = column_sum(g_middle * attended[...])
    g_attended = (part(mod, 2) * g_middle).astype(BF16)
    g_attended_out[...] = g_attended
    bias_grad[...] = column_sum(g_attended.astype(F32))


def attn_back_body(count, place, *refs):
    g_chunks = refs[:count]
    w_own, w_received, qkv, probs_ref = refs[count : count + 4]
    g_rows_out, g_joint_out, bias_grad = refs[count + 4 : count + 7]
    g_partial = refs[count + 7 :]
    g_rows = put_rows(g_rows_out, g_chunks)
    w_front, w_value, w_out = pick_attn(place, w_own, w_received)
    width = w_value.shape[1]
    g_mixed = dot(g_rows, w_out).astype(BF16)
    g_query, g_key, g_value = [], [], []
    for head in range(width // HEAD):
        at = head * HEAD
        query = qkv[:, at : at + HEAD]
        key = qkv[:, width + at : width + at + HEAD]
        value = qkv[:, 2 * width + at : 2 * width + at + HEAD]
        probs = probs_ref[head]
        g_head = g_mixed[:, at : at + HEAD]
        g_probs = dot_t(g_head, value)
        row_dot = jnp.sum(probs * g_probs, axis=-1, keepdims=True)
        g_scores = (probs * (g_probs - row_dot)).astype(BF16)
        g_value.append(t_dot(probs.astype(BF16), g_head))
        g_query.append(dot(g_scores, key) * HEAD**-0.5)
        g_key.append(t_dot(g_scores, query) * HEAD**-0.5)
    g_front = jnp.concatenate(g_query + g_key, axis=1).astype(BF16)
    g_value = jnp.concatenate(g_value, axis=1).astype(BF16)
    g_joint_out[:, : 2 * width] = g_front
    g_joint_out[:, 2 * width :] = g_value
    bias_grad[:, :width] = column_sum(g_front[:, :width].astype(F32))
    bias_grad[:, width:] = column_sum(g_value.astype(F32))
    put_blocks(g_partial, dot_t(g_front, w_front) + dot_t(g_value, w_value))


def input_grad(parts, h, mod, g_middle, g_shift, g_scale):
    g_in = total(parts)
    normed, rstd = normalize(h[...])
    g_shift[...] = column_sum(g_in)
    g_scale[...] = column_sum(g_in * normed)
    return (g_middle[...] + normalize_back(g_in * (1.0 + part(mod, 1)), normed, rstd)).astype(BF16)


def between_back_body(count, *refs):
    parts = refs[:count]
    h, mod1, mod0, g_middle, shrunk, g_h_out, g_y_out, g_shrunk_out = refs[count : count + 8]
    g_shift, g_scale, g_gate, bias_grad = refs[count + 8 :]
    g_h = input_grad(parts, h, mod1, g_middle, g_shift, g_scale)
    g_h_out[...] = g_h
    g_y = g_h.astype(F32)
    g_y_out[...] = g_y
    g_gate[...] = column_sum(g_y * shrunk[...])
    g_shrunk = (part(mod0, 5) * g_y).astype(BF16)
    g_shrunk_out[...] = g_shrunk
    bias_grad[...] = column_sum(g_shrunk.astype(F32))


def finish_back_body(count, *refs):
    parts = refs[:count]
    h, mod, g_middle, g_h_out, g_shift, g_scale = refs[count:]
    g_h_out[...] = input_grad(parts, h, mod, g_middle, g_shift, g_scale)


def mlp_weights_body(rows, g_pre, g_rows, hidden, keep, give):
    half = keep.shape[1] // 2
    keep[:, :half] = t_dot(rows[...], g_pre[:, :half])
    keep[:, half:] = t_dot(g_rows[...], hidden[:, :half])
    give[:, :half] = t_dot(rows[...], g_pre[:, half:]).astype(BF16)
    give[:, half:] = t_dot(g_rows[...], hidden[:, half:]).astype(BF16)


def attn_weights_body(place, rows, g_joint, g_rows, mixed, keep, give):
    width = mixed.shape[1]
    first = place[0] == 0
    front = t_dot(rows[...], g_joint[:, : 2 * width])
    back = jnp.concatenate(
        [t_dot(rows[...], g_joint[:, 2 * width :]), t_dot(g_rows[...], mixed[...])], axis=1
    )
    keep[...] = jnp.where(first, front, back)
    give[...] = jnp.where(first, back, front).astype(BF16)


def line_blocks(place, k, rows):
    return pl.ds(pl.multiple_of((place[1] ^ k) * rows, 16), rows)


def stack_body(place, *refs):
    out = refs[-1]
    for k, ref in enumerate(refs[:-1]):
        out[line_blocks(place, k, ref.shape[0])] = ref[...]


def line_parts_body(place, keep, received, near, far, own):
    rows = own.shape[0]

    def block(k):
        at = line_blocks(place, k, rows)
        return keep[at] + received[at].astype(F32)

    near[0] = block(1).astype(BF16)
    near[1] = block(3).astype(BF16)
    far[...] = block(2)
    own[...] = block(0)


def mod_first_body(a0, a1, a2, a3, weight, out):
    rows = jnp.concatenate([a0[...], a1[...], a2[...], a3[...]], axis=0)
    out[...] = dot(rows, weight[...])


def mod_sum_body(count, *refs):
    values = total(refs[:count])
    outs = refs[count:]
    micro = outs[0].shape[0]
    for k, out in enumerate(outs):
        out[...] = values[k * micro : (k + 1) * micro]


def mod_join_body(place, p0, p1, p2, p3, bias, mine, other, scratch):
    for k, ref in enumerate((p0, p1, p2, p3)):
        scratch[place[1] ^ k] = ref[...]
    values = jnp.concatenate([scratch[j] for j in range(LINE)], axis=1) + bias[...]
    first = place[0] == 0
    mine[...] = jnp.where(first, values[0:1], values[1:2])
    other[...] = jnp.where(first, values[1:2], values[0:1])


def pack_body(*refs):
    out, pieces = refs[-1], refs[:-1]
    count = len(pieces) // 2
    for row in range(2):
        at = 0
        for ref in pieces[row * count : (row + 1) * count]:
            out[row : row + 1, at : at + ref.shape[1]] = ref[...]
            at += ref.shape[1]


def grads_sum_body(count, place, *refs):
    parts = refs[:count]
    joint0, expand0, joint1, expand1, keep, give = refs[count:]
    first = place[0] == 0
    values = total(parts)
    hidden = expand0.shape[1]
    mod_width = values.shape[1] // 8 * 6
    rounded = values[:, :mod_width].astype(BF16).astype(F32)
    sums = values[:, mod_width:]
    half = hidden // 2

    def natural(ref):
        now = ref[...]
        return jnp.where(first, now, jnp.concatenate([now[:, half:], now[:, :half]], axis=1))

    rows = []
    for row, (joint, expand) in enumerate(((joint0, expand0), (joint1, expand1))):
        rows.append(
            jnp.concatenate(
                [rounded[row : row + 1], joint[...], natural(expand), sums[row : row + 1]], axis=1
            )
        )
    keep[...] = jnp.where(first, rows[0], rows[1])
    give[...] = jnp.where(first, rows[1], rows[0])


def grads_join_body(place, keep, received, out):
    mods = out.shape[1] - keep.shape[1]
    first = place[0] == 0
    own, other = keep[...], received[...]
    out[:, :mods] = jnp.where(first, own, other)[:, :mods]
    out[:, mods : 2 * mods] = jnp.where(first, other, own)[:, :mods]
    out[:, 2 * mods :] = own[:, mods:] + other[:, mods:]


def mod_back_body(place, g0, g1, g2, g3, a0, a1, a2, a3, weight, w_grad, b_grad, bias, c0, c1, c2, c3):
    columns = weight.shape[1]
    mods = columns * LINE
    grads = (g0, g1, g2, g3)
    at = pl.multiple_of(place[1] * columns, 128)
    rows = []
    for ref in grads:
        rows.append(ref[:, pl.ds(at, columns)])
        rows.append(ref[:, pl.ds(pl.multiple_of(at + mods, 128), columns)])
    picked = jnp.concatenate(rows, axis=0).astype(BF16)
    activated = jnp.concatenate([a0[...], a1[...], a2[...], a3[...]], axis=0)
    w_grad[...] = t_dot(activated, picked)
    act = dot_t(picked, weight[...])
    for k, out in enumerate((c0, c1, c2, c3)):
        out[...] = act[2 * k : 2 * k + 2]
    b_grad[...] = tree_sum([ref[:, :mods] + ref[:, mods : 2 * mods] for ref in grads])
    bias[...] = tree_sum([ref[:, 2 * mods :] for ref in grads])


def on_device(
    tokens,
    conditions,
    cotangent,
    modulation_weight,
    modulation_bias,
    joint_weight,
    joint_bias,
    output_weight,
    output_bias,
    expand_weight,
    expand_bias,
    shrink_weight,
    shrink_bias,
):
    core = lax.axis_index("pipe")
    first = core == 0
    line = lax.axis_index("dp")
    place = jnp.stack([core, line]).astype(jnp.int32)
    line_size = lax.axis_size("dp")
    count = lax.axis_size("tensor")
    direct = line_size == LINE
    micro, _, own, model = tokens.shape
    width = output_weight.shape[1]
    hidden = expand_weight.shape[2]
    chunk = model // line_size
    rows = own * count
    columns = modulation_weight.shape[2]
    mods = 6 * model
    bias_width = 2 * width + hidden + 2 * model
    own_rows = modulation_weight[0]

    def mine(pair):
        return jnp.where(first, pair[0], pair[1])

    def other(pair):
        return jnp.where(first, pair[1], pair[0])

    def both_layers(kept, received):
        return jnp.where(first, kept, received), jnp.where(first, received, kept)

    def after(value, earlier):
        return lax.optimization_barrier((value, earlier))[0]

    attn_pack = jnp.concatenate(
        [joint_weight[0].reshape(chunk, 3 * width), output_weight[0].T], axis=1
    )
    shrink_t = shrink_weight[0].T
    expand = expand_weight[0]

    def column_half(index):
        return jnp.concatenate(
            [
                attn_pack[:, index * 2 * width : (index + 1) * 2 * width],
                expand[:, index * (hidden // 2) : (index + 1) * (hidden // 2)],
                shrink_t[:, index * (hidden // 2) : (index + 1) * (hidden // 2)],
            ],
            axis=1,
        )

    halves = (column_half(0), column_half(1))
    halves_of_layers = both_layers(mine(halves), swap(other(halves), "pipe", 1))
    split = 2 * width

    bias_pack = jnp.concatenate(
        [
            joint_bias[0].reshape(-1),
            expand_bias[0],
            output_bias[0],
            shrink_bias[0],
        ]
    )[None]
    bias_layers = both_layers(bias_pack, swap(bias_pack, "pipe", 1))
    biases = []
    for packed in bias_layers:
        at = 2 * width
        joint = jnp.concatenate(
            [packed[:, :width], jnp.zeros((1, width), F32), packed[:, width:at]], axis=1
        )
        grown = packed[:, at : at + hidden]
        rolled = jnp.concatenate([grown[:, hidden // 2 :], grown[:, : hidden // 2]], axis=1)
        grown = jnp.where(first, grown, rolled)
        at += hidden
        biases.append((joint, packed[:, at : at + model], grown, packed[:, at + model :]))

    def along_line(value, earlier):
        if earlier is not None:
            value = after(value, earlier)
        if direct:
            near = swap(value, "dp", 1)
            far = swap(value, "dp", 2)
            farther = swap(far, "dp", 1)
            lined = run(
                "stack_line",
                stack_body,
                [shape((model, value.shape[1]), BF16)],
                [value, near, far, farther],
                place,
            )[0]
            mark = far
        else:
            lined = lax.all_gather(value, "dp", axis=0, tiled=True)
            mark = lined
        return (lined, swap(lined, "pipe", 1)), mark

    weights = []
    mark = None
    for layer in range(2):
        attn, mark = along_line(halves_of_layers[layer][:, :split], mark)
        mlp, mark = along_line(halves_of_layers[layer][:, split:], mark)
        weights.append((attn, mlp))

    activated = jax.nn.silu(conditions[:, 0].astype(F32)).astype(BF16)
    if direct:
        activated_all = gather(activated, "dp")
        mod_partial = run(
            "mod_first",
            mod_first_body,
            [shape((micro * LINE, columns), F32)],
            activated_all + [own_rows],
        )[0]
        pieces = run(
            "mod_sum",
            functools.partial(mod_sum_body, count),
            [shape((micro, columns), F32)] * LINE,
            gather(mod_partial, "tensor"),
        )
        mod_mine, mod_other = pl.pallas_call(
            mod_join_body,
            out_shape=[shape((1, mods), F32)] * 2,
            in_specs=[pl.BlockSpec(memory_space=pltpu.SMEM)]
            + [pl.BlockSpec(memory_space=pltpu.VMEM)] * 5,
            out_specs=[pl.BlockSpec(memory_space=pltpu.VMEM)] * 2,
            scratch_shapes=[pltpu.VMEM((LINE, micro, columns), F32)],
            name="mod_join",
        )(place, *exchange(pieces, "dp"), modulation_bias)
    else:
        activated_all = lax.all_gather(activated, "dp", axis=0).reshape(line_size * micro, -1)
        mod_partial = dot(activated_all, own_rows)
        mod_sum = tree_sum(gather(mod_partial, "tensor")).reshape(line_size, micro, -1)
        mod_layer = lax.all_to_all(mod_sum, "dp", split_axis=0, concat_axis=0)
        mod_layer = jnp.swapaxes(mod_layer, 0, 1).reshape(micro, -1) + modulation_bias
        mod_mine, mod_other = mine(mod_layer)[None], other(mod_layer)[None]
    mod0, mod1 = both_layers(mod_mine, swap(mod_other, "pipe", 1))

    own_f32 = shape((own, model), F32)
    own_bf16 = shape((own, model), BF16)
    blocks = [own_bf16] * count
    vector = shape((1, model), F32)
    h0, attn_in, g_y1, g_shrunk1 = run(
        "enter",
        enter_body,
        [own_f32, own_bf16, own_f32, own_bf16],
        [tokens[:, 0], cotangent[:, 0], mod0, mod1],
        place,
    )

    def attention(attn_in, weight, bias):
        outs = run(
            "attention",
            functools.partial(attn_body, count),
            [
                shape((rows, model), BF16),
                shape((rows, 3 * width), BF16),
                shape((width // HEAD, rows, rows), F32),
                shape((rows, width), BF16),
            ]
            + blocks,
            gather(attn_in, "tensor") + [weight[0], weight[1], bias],
            place,
        )
        return outs[:4], exchange(outs[4:], "tensor")

    def middle_of(parts, bias, h, mod):
        return run(
            "middle",
            functools.partial(middle_body, count),
            [own_f32, own_f32, own_bf16],
            parts + [bias, h, mod],
        )

    kept_attn0, parts = attention(attn_in, weights[0][0], biases[0][0])
    attended0, middle0, mlp_in = middle_of(parts, biases[0][1], h0, mod0)
    outs = run(
        "feed_forward",
        functools.partial(mlp_body, count),
        [shape((rows, model), BF16), shape((rows, hidden), F32), shape((rows, hidden), BF16)] + blocks,
        gather(mlp_in, "tensor") + [weights[0][1][0], weights[0][1][1], biases[0][2]],
    )
    mlp_rows0, pre0, hidden0 = outs[:3]
    shrunk0, passed, h1, attn_in = run(
        "between",
        functools.partial(between_body, count),
        [own_f32, own_bf16, own_f32, own_bf16],
        exchange(outs[3:], "tensor") + [biases[0][3], middle0, mod0, mod1],
    )

    g_shrunk_rows = gather(g_shrunk1, "tensor")
    kept_attn1, parts = attention(attn_in, weights[1][0], biases[1][0])
    attended1, middle1, mlp_in = middle_of(parts, biases[1][1], h1, mod1)
    outs = run(
        "feed_forward_both",
        functools.partial(mlp_both_body, count),
        [
            shape((rows, model), BF16),
            shape((rows, model), BF16),
            shape((rows, hidden), BF16),
            shape((rows, hidden), BF16),
            shape((1, hidden), F32),
        ]
        + blocks
        + blocks,
        gather(mlp_in, "tensor")
        + g_shrunk_rows
        + [weights[1][1][0], weights[1][1][1], biases[1][2]],
    )
    mlp_rows1, g_rows1, hidden1, g_pre1, expand_grad1 = outs[:5]
    y_parts, g_parts = outs[5 : 5 + count], outs[5 + count :]

    def middle_back(parts, middle, mod, g_y, attended):
        return run(
            "middle_back",
            functools.partial(middle_back_body, count),
            [own_f32, own_bf16] + [vector] * 4,
            parts + [middle, mod, g_y, attended],
        )

    def attention_back(g_attended, weight, kept):
        outs = run(
            "attention_back",
            functools.partial(attn_back_body, count),
            [
                shape((rows, model), BF16),
                shape((rows, 3 * width), BF16),
                shape((1, 2 * width), F32),
            ]
            + blocks,
            gather(g_attended, "tensor") + [weight[0], weight[1], kept[1], kept[2]],
            place,
        )
        return outs[:3], exchange(outs[3:], "tensor")

    def reduce_line(keep, give):
        received = swap(give, "pipe", 1)
        if not direct:
            whole = (keep + received.astype(F32)).astype(BF16)
            return lax.psum_scatter(whole, "dp", scatter_dimension=0, tiled=True).astype(F32)
        wide = keep.shape[1]
        near, far, own_part = run(
            "line_parts",
            line_parts_body,
            [
                shape((2, chunk, wide), BF16),
                shape((chunk, wide), F32),
                shape((chunk, wide), F32),
            ],
            [keep, received],
            place,
        )
        near = swap(near, "dp", 1)
        far = swap((far + near[1].astype(F32)).astype(BF16), "dp", 2)
        return own_part + near[0].astype(F32) + far.astype(F32)

    def mlp_weight_grads(mlp_rows, g_pre, g_rows, hidden_rows):
        keep, give = run(
            "mlp_weight_grads",
            mlp_weights_body,
            [shape((model, hidden), F32), shape((model, hidden), BF16)],
            [mlp_rows, g_pre, g_rows, hidden_rows],
        )
        return reduce_line(keep, give)

    def attn_weight_grads(attn_rows, g_joint, g_rows, mixed):
        keep, give = run(
            "attn_weight_grads",
            attn_weights_body,
            [shape((model, 2 * width), F32), shape((model, 2 * width), BF16)],
            [attn_rows, g_joint, g_rows, mixed],
            place,
        )
        return reduce_line(keep, give)

    g_middle1, g_attended, g_shift_mlp1, g_scale_mlp1, g_gate_attn1, out_grad1 = middle_back(
        exchange(g_parts, "tensor"), middle1, mod1, g_y1, attended1
    )
    mlp_grad1 = mlp_weight_grads(mlp_rows1, g_pre1, g_rows1, hidden1)
    y1, g_gate_mlp1, shrink_grad1 = run(
        "leave",
        functools.partial(leave_body, count),
        [own_bf16, vector, vector],
        exchange(y_parts, "tensor") + [biases[1][3], middle1, mod1, g_y1, g_shrunk1],
    )
    (g_rows, g_joint, joint_grad1), parts = attention_back(g_attended, weights[1][0], kept_attn1)
    g_passed, g_y0, g_shrunk0, g_shift_attn1, g_scale_attn1, g_gate_mlp0, shrink_grad0 = run(
        "between_back",
        functools.partial(between_back_body, count),
        [own_bf16, own_f32, own_bf16] + [vector] * 4,
        parts + [h1, mod1, mod0, g_middle1, shrunk0],
    )
    attn_grad1 = attn_weight_grads(kept_attn1[0], g_joint, g_rows, kept_attn1[3])

    outs = run(
        "feed_forward_back",
        functools.partial(mlp_back_body, count),
        [shape((rows, model), BF16), shape((rows, hidden), BF16), shape((1, hidden), F32)] + blocks,
        gather(g_shrunk0, "tensor") + [weights[0][1][0], weights[0][1][1], pre0],
    )
    g_rows0, g_pre0, expand_grad0 = outs[:3]
    g_middle0, g_attended, g_shift_mlp0, g_scale_mlp0, g_gate_attn0, out_grad0 = middle_back(
        exchange(outs[3:], "tensor"), middle0, mod0, g_y0, attended0
    )
    mlp_grad0 = mlp_weight_grads(mlp_rows0, g_pre0, g_rows0, hidden0)
    (g_rows, g_joint, joint_grad0), parts = attention_back(g_attended, weights[0][0], kept_attn0)
    g_h0, g_shift_attn0, g_scale_attn0 = run(
        "finish_back",
        functools.partial(finish_back_body, count),
        [own_bf16, vector, vector],
        parts + [h0, mod0, g_middle0],
    )
    attn_grad0 = attn_weight_grads(kept_attn0[0], g_joint, g_rows, kept_attn0[3])

    def own_layer_of_micros(pair):
        return jnp.stack(both_layers(mine(pair), swap(other(pair), "pipe", 1)))

    layer_outputs = own_layer_of_micros((passed, y1))
    input_grads = own_layer_of_micros((g_h0, g_passed))

    def own_columns(pair):
        return both_layers(mine(pair), swap(other(pair), "pipe", 1))

    mlp_halves = own_columns((mlp_grad0, mlp_grad1))
    half = hidden // 2
    expand_w_grad = jnp.concatenate([part[:, :half] for part in mlp_halves], axis=1)
    shrink_w_grad = jnp.concatenate([part[:, half:] for part in mlp_halves], axis=1).T
    front, back = own_columns((attn_grad0, attn_grad1))
    joint_w_grad = jnp.concatenate([front, back[:, :width]], axis=1).reshape(chunk, 3, width)
    output_w_grad = back[:, width:].T

    packed = run(
        "pack_grads",
        pack_body,
        [shape((2, mods + 2 * model), F32)],
        [
            g_shift_attn0,
            g_scale_attn0,
            g_gate_attn0,
            g_shift_mlp0,
            g_scale_mlp0,
            g_gate_mlp0,
            out_grad0,
            shrink_grad0,
            g_shift_attn1,
            g_scale_attn1,
            g_gate_attn1,
            g_shift_mlp1,
            g_scale_mlp1,
            g_gate_mlp1,
            out_grad1,
            shrink_grad1,
        ],
    )[0]
    keep, give = run(
        "grads_sum",
        functools.partial(grads_sum_body, count),
        [shape((1, mods + bias_width), F32)] * 2,
        gather(packed, "tensor") + [joint_grad0, expand_grad0, joint_grad1, expand_grad1],
        place,
    )
    joined = run(
        "grads_join",
        grads_join_body,
        [shape((1, 2 * mods + bias_width), F32)],
        [keep, swap(give, "pipe", 1)],
        place,
    )[0]
    if direct:
        outs = run(
            "mod_back",
            mod_back_body,
            [shape(own_rows.shape, F32), shape((1, mods), F32), shape((1, bias_width), F32)]
            + [shape((micro, own_rows.shape[0]), F32)] * LINE,
            gather(joined, "dp") + activated_all + [own_rows],
            place,
        )
        ada_grad, ada_bias_grad, bias_sum = outs[:3]
        act_grad = tree_sum(exchange(outs[3:], "dp"))
    else:
        joined_all = lax.all_gather(joined, "dp", axis=0, tiled=True)
        mod_grads = joined_all[:, : 2 * mods].reshape(line_size * micro, mods)
        bias_sum = jnp.sum(joined_all[:, 2 * mods :], axis=0, keepdims=True)
        ada_bias_grad = jnp.sum(mod_grads, axis=0, keepdims=True)
        picked = lax.dynamic_slice_in_dim(mod_grads, line * columns, columns, 1).astype(BF16)
        ada_grad = t_dot(activated_all, picked)
        act_partial = dot_t(picked, own_rows).reshape(line_size, micro, -1)
        act_grad = lax.psum_scatter(act_partial, "dp", scatter_dimension=0, tiled=False)
    _, silu_back = jax.vjp(jax.nn.silu, conditions[:, 0].astype(F32))
    cond_grad = silu_back(act_grad)[0]
    at = 2 * width
    return (
        layer_outputs[None, :, None],
        input_grads[None, :, None],
        cond_grad[None, :, None],
        ada_grad[None],
        ada_bias_grad,
        joint_w_grad[None],
        bias_sum[:, :at].reshape(1, 2, width),
        output_w_grad[None],
        bias_sum[:, at + hidden : at + hidden + model],
        expand_w_grad[None],
        bias_sum[:, at : at + hidden],
        shrink_w_grad[None],
        bias_sum[:, at + hidden + model :],
    )


def solution(mesh):
    in_specs = (
        P(None, "dp", "tensor", None),
        P(None, "dp", "tensor"),
        P(None, "dp", "tensor", None),
        P("pipe", "tensor", "dp"),
        P("pipe", None),
        P("pipe", "dp", None, "tensor"),
        P("pipe", None, "tensor"),
        P("pipe", "tensor", "dp"),
        P("pipe", None),
        P("pipe", "dp", "tensor"),
        P("pipe", "tensor"),
        P("pipe", "tensor", "dp"),
        P("pipe", None),
    )
    out_specs = (
        P("pipe", None, "dp", "tensor", None),
        P("pipe", None, "dp", "tensor", None),
        P("pipe", None, "dp", "tensor"),
        P("pipe", "tensor", "dp"),
        P("pipe", None),
        P("pipe", "dp", None, "tensor"),
        P("pipe", None, "tensor"),
        P("pipe", "tensor", "dp"),
        P("pipe", None),
        P("pipe", "dp", "tensor"),
        P("pipe", "tensor"),
        P("pipe", "tensor", "dp"),
        P("pipe", None),
    )
    return jax.shard_map(
        on_device, mesh=mesh, in_specs=in_specs, out_specs=out_specs, check_vma=False
    )
```

time: 486 us -> 336 us (0.69); the launches traced: 477 us -> 335 us
  local copies, waits for them, and re-layouts: 94.8 us -> 10.3 us
  other arithmetic: 74.5 us -> 14.8 us
  waiting for transfers between devices: 123 us -> 169 us
  matrix products: 41.2 us -> 0 us
  Pallas kernels: 0 us -> 35.2 us
  starting transfers between devices: 139 us -> 105 us
    ppermute x132 -> x102, waiting for transfers between devices: 123 us -> 169 us  [swap(): return lax.ppermute(value, axis, pairs)]
    dot_general x37 -> x0, matrix products: 38.6 us -> none  [the longest x9 11.9 us: t_dot(): lax.dot_general(left, right, (((0,), (0,)), ((), ())), preferred_element_...]
    pallas_call x0 -> x35, Pallas kernels: none -> 35.2 us  [the longest x34 33.8 us: run(): pl.pallas_call(body, out_shape=outs, in_specs=specs, out_specs=[pl.BlockS...]
    ppermute x132 -> x102, starting transfers between devices: 139 us -> 105 us  [swap(): return lax.ppermute(value, axis, pairs)]
    reshape x113 -> x1, local copies, waits for them, and re-layouts: 30.1 us -> 0.66 us  [on_device(): bias_sum[:, :at].reshape(1, 2, width)]
    unnamed x18 -> x5, other arithmetic: 16.5 us -> 1.65 us
    reduce_sum x21 -> x0, other arithmetic: 13.6 us -> none  [the longest x2 3.58 us: layer_backward(): out_bias_grad = jnp.sum(g_attended.astype(F32), axis=0)]
    rev x76 -> x0, local copies, waits for them, and re-layouts: 13.5 us -> none  [flip_blocks(): flipped = paired[..., ::-1, :, :].reshape(blocks.shape)]
  transfers between devices with their start and end apart: 132 -> 102, of which waited for: 43 -> 60; matrix products, arithmetic and copies ran while one was open for 40% -> 5% of each run, Pallas kernels for 0% -> 8%
where the time goes in v2:
time: 336 us; the launch traced here: 335 us
  waiting for transfers between devices  169 us (50%)
  starting transfers between devices  105 us (31%)
  Pallas kernels  35.2 us (10%)
  other arithmetic  14.8 us (4%)
  local copies, waits for them, and re-layouts  10.3 us (3%)
    ppermute x102, waiting for transfers between devices, swap(): return lax.ppermute(value, axis, pairs)  169 us
    ppermute x102, starting transfers between devices, swap(): return lax.ppermute(value, axis, pairs)  105 us
    pallas_call x34, Pallas kernels, run(): pl.pallas_call(body, out_shape=outs, in_specs=specs, out_specs=[pl.BlockS...  33.8 us
    unnamed x71, local copies, waits for them, and re-layouts  7.41 us
  transfers between devices with their start and end apart: 102, of which 60 were waited for; matrix products, arithmetic and copies ran while one was open for 5% of the time, Pallas kernels for 8%

profile of v2, /device:TPU:0, one launch (start us, length us, event | category | flops | bytes accessed | tf_op | source)
XLA Modules:
  0.0 335.5 jit_solution(8946508774068270394)
XLA Ops:
  5.7 4.0 %collective-permute-start.15 = (bf16[192,384]{1,0:T(8,128)(2,1)S(1)}, bf16[192,384]{1,0:T(8,128)(2,1)S(1)}, u32[]{:S(2)}, u32[]{:S(2)}) collective-permute-start(bf16[192,384]{1,0:T(8,128)(2,1)S(1)} %slice.177.refs_0_), channel_id=1, source_target_pairs={{0,8},{4,12},{8,0},{12,4},{1,9},{5,13},{9,1},{13,5},{2,10},{6,14},... | collective-permute-start | bytes 442376 | tf_op jit(solution)/shard_map/ppermute | solution.py:22
  9.7 7.3 %collective-permute-done.15.refs_2_ = bf16[192,384]{1,0:T(8,128)(2,1)S(1)} collective-permute-done((bf16[192,384]{1,0:T(8,128)(2,1)S(1)}, bf16[192,384]{1,0:T(8,128)(2,1)S(1)}, u32[]{:S(2)}, u32[]{:S(2)}) %collective-permute-start.15) | collective-permute-done | bytes 147488 | tf_op jit(solution)/shard_map/ppermute | solution.py:22
  17.0 3.6 %collective-permute-start.2 = (bf16[2,192]{1,0:T(2,128)(2,1)S(1)}, bf16[2,192]{1,0:T(2,128)(2,1)S(1)}, u32[]{:S(2)}, u32[]{:S(2)}) collective-permute-start(bf16[2,192]{1,0:T(2,128)(2,1)S(1)} %fusion.16.a0), channel_id=1, source_target_pairs={{0,12},{4,8},{8,4},{12,0},{1,13},{5,9},{9,5},{13,1},{2,14},{6,10},... | collective-permute-start | bytes 2312 | tf_op jit(solution)/shard_map/ppermute | solution.py:22
  22.7 5.2 %collective-permute-done.2.a3 = bf16[2,192]{1,0:T(2,128)(2,1)S(1)} collective-permute-done((bf16[2,192]{1,0:T(2,128)(2,1)S(1)}, bf16[2,192]{1,0:T(2,128)(2,1)S(1)}, u32[]{:S(2)}, u32[]{:S(2)}) %collective-permute-start.2) | collective-permute-done | bytes 800 | tf_op jit(solution)/shard_map/ppermute | solution.py:22
  27.9 5.0 %collective-permute-done.1.a2 = bf16[2,192]{1,0:T(2,128)(2,1)S(1)} collective-permute-done((bf16[2,192]{1,0:T(2,128)(2,1)S(1)}, bf16[2,192]{1,0:T(2,128)(2,1)S(1)}, u32[]{:S(2)}, u32[]{:S(2)}) %collective-permute-start.1) | collective-permute-done | bytes 800 | tf_op jit(solution)/shard_map/ppermute | solution.py:22
  42.1 2.6 collective-permute-start.8
  58.0 8.6 %collective-permute-done.16.refs_3_ = bf16[192,384]{1,0:T(8,128)(2,1)S(1)} collective-permute-done((bf16[192,384]{1,0:T(8,128)(2,1)S(1)}, bf16[192,384]{1,0:T(8,128)(2,1)S(1)}, u32[]{:S(2)}, u32[]{:S(2)}) %collective-permute-start.16) | collective-permute-done | bytes 147488 | tf_op jit(solution)/shard_map/ppermute | solution.py:22
  74.8 10.7 %collective-permute-done.49.refs_2_ = bf16[192,768]{1,0:T(8,128)(2,1)S(1)} collective-permute-done((bf16[192,768]{1,0:T(8,128)(2,1)S(1)}, bf16[192,768]{1,0:T(8,128)(2,1)S(1)}, u32[]{:S(2)}, u32[]{:S(2)}) %collective-permute-start.49) | collective-permute-done | bytes 294944 | tf_op jit(solution)/shard_map/ppermute | solution.py:22
  87.2 3.1 collective-permute-done.10.refs_1_
  97.3 2.4 collective-permute-done.35.refs_1_
  105.0 5.1 %collective-permute-done.20.refs_2_ = bf16[64,768]{1,0:T(8,128)(2,1)S(1)} collective-permute-done((bf16[64,768]{1,0:T(8,128)(2,1)S(1)}, bf16[64,768]{1,0:T(8,128)(2,1)S(1)}, u32[]{:S(2)}, u32[]{:S(2)}) %collective-permute-start.20) | collective-permute-done | bytes 98336 | tf_op jit(solution)/shard_map/ppermute | solution.py:22
  112.5 3.5 %collective-permute-done.24.refs_3_ = bf16[64,768]{1,0:T(8,128)(2,1)S(1)} collective-permute-done((bf16[64,768]{1,0:T(8,128)(2,1)S(1)}, bf16[64,768]{1,0:T(8,128)(2,1)S(1)}, u32[]{:S(2)}, u32[]{:S(2)}) %collective-permute-start.24) | collective-permute-done | bytes 98336 | tf_op jit(solution)/shard_map/ppermute | solution.py:22
  117.0 3.6 %collective-permute-done.22.refs_1_ = bf16[64,768]{1,0:T(8,128)(2,1)S(1)} collective-permute-done((bf16[64,768]{1,0:T(8,128)(2,1)S(1)}, bf16[64,768]{1,0:T(8,128)(2,1)S(1)}, u32[]{:S(2)}, u32[]{:S(2)}) %collective-permute-start.22) | collective-permute-done | bytes 98336 | tf_op jit(solution)/shard_map/ppermute | solution.py:22
  146.8 5.2 %collective-permute-done.40.refs_2_ = bf16[64,768]{1,0:T(8,128)(2,1)S(1)} collective-permute-done((bf16[64,768]{1,0:T(8,128)(2,1)S(1)}, bf16[64,768]{1,0:T(8,128)(2,1)S(1)}, u32[]{:S(2)}, u32[]{:S(2)}) %collective-permute-start.40) | collective-permute-done | bytes 98336 | tf_op jit(solution)/shard_map/ppermute | solution.py:22
  157.3 2.8 collective-permute-done.44.refs_3_
  214.3 2.4 attention_back.3
  239.7 3.4 %collective-permute-start.84 = (f32[1,11904]{1,0:T(1,128)S(1)}, f32[1,11904]{1,0:T(1,128)S(1)}, u32[]{:S(2)}, u32[]{:S(2)}) collective-permute-start(f32[1,11904]{1,0:T(1,128)S(1)} %grads_join.1.g0), channel_id=1, source_target_pairs={{0,12},{4,8},{8,4},{12,0},{1,13},{5,9},{9,5},{13,1},{2,14},{6,10},... | collective-permute-start | bytes 142856 | tf_op jit(solution)/shard_map/ppermute | solution.py:22
  246.6 3.0 collective-permute-done.83.g2
  268.8 11.7 %collective-permute-done.99 = bf16[2,192,768]{2,1,0:T(8,128)(2,1)} collective-permute-done((bf16[2,192,768]{2,1,0:T(8,128)(2,1)}, bf16[2,192,768]{2,1,0:T(8,128)(2,1)}, u32[]{:S(2)}, u32[]{:S(2)}) %collective-permute-start.99) | collective-permute-done | bytes 589856 | tf_op jit(solution)/shard_map/ppermute | solution.py:22
  281.6 10.9 %collective-permute-done.96 = bf16[2,192,768]{2,1,0:T(8,128)(2,1)S(1)} collective-permute-done((bf16[2,192,768]{2,1,0:T(8,128)(2,1)S(1)}, bf16[2,192,768]{2,1,0:T(8,128)(2,1)S(1)}, u32[]{:S(2)}, u32[]{:S(2)}) %collective-permute-start.96) | collective-permute-done | bytes 589856 | tf_op jit(solution)/shard_map/ppermute | solution.py:22
  292.9 2.6 collective-permute-start.100
  296.6 17.2 %collective-permute-done.90 = bf16[192,384]{1,0:T(8,128)(2,1)S(1)} collective-permute-done((bf16[192,384]{1,0:T(8,128)(2,1)S(1)}, bf16[192,384]{1,0:T(8,128)(2,1)S(1)}, u32[]{:S(2)}, u32[]{:S(2)}) %collective-permute-start.90) | collective-permute-done | bytes 147488 | tf_op jit(solution)/shard_map/ppermute | solution.py:22
  314.9 5.1 %collective-permute-done.100 = bf16[192,768]{1,0:T(8,128)(2,1)S(1)} collective-permute-done((bf16[192,768]{1,0:T(8,128)(2,1)S(1)}, bf16[192,768]{1,0:T(8,128)(2,1)S(1)}, u32[]{:S(2)}, u32[]{:S(2)}) %collective-permute-start.100) | collective-permute-done | bytes 294944 | tf_op jit(solution)/shard_map/ppermute | solution.py:22
  320.1 5.4 %collective-permute-done.97 = bf16[192,768]{1,0:T(8,128)(2,1)S(1)} collective-permute-done((bf16[192,768]{1,0:T(8,128)(2,1)S(1)}, bf16[192,768]{1,0:T(8,128)(2,1)S(1)}, u32[]{:S(2)}, u32[]{:S(2)}) %collective-permute-start.97) | collective-permute-done | bytes 294944 | tf_op jit(solution)/shard_map/ppermute | solution.py:22
  (337 shorter events, 199.3 us)
Async XLA Ops:
  17.0 33.4 %collective-permute-start.26 = (bf16[192,768]{1,0:T(8,128)(2,1)S(1)}, bf16[192,768]{1,0:T(8,128)(2,1)S(1)}, u32[]{:S(2)}, u32[]{:S(2)}) collective-permute-start(bf16[192,768]{1,0:T(8,128)(2,1)S(1)} %slice.181.refs_0_), channel_id=1, source_target_pairs={{0,8},{4,12},{8,0},{12,4},{1,9},{5,13},{9,1},{13,5},{2,10},{6,14},... | collective-permute-start | bytes 884744 | tf_op jit(solution)/shard_map/ppermute | solution.py:22
  49.7 23.0 %collective-permute-start.18 = (f32[1,2688]{1,0:T(1,128)S(1)}, f32[1,2688]{1,0:T(1,128)S(1)}, u32[]{:S(2)}, u32[]{:S(2)}) collective-permute-start(f32[1,2688]{1,0:T(1,128)S(1)} %broadcast_in_dim.24), channel_id=1, source_target_pairs={{0,16},{16,0},{1,17},{17,1},{2,18},{18,2},{3,19},{19,3},{4,20},{20... | collective-permute-start | bytes 32264 | tf_op jit(solution)/shard_map/ppermute | solution.py:22
  50.4 18.4 %collective-permute-start.25 = (bf16[192,768]{1,0:T(8,128)(2,1)S(1)}, bf16[192,768]{1,0:T(8,128)(2,1)S(1)}, u32[]{:S(2)}, u32[]{:S(2)}) collective-permute-start(bf16[192,768]{1,0:T(8,128)(2,1)S(1)} %slice.181.refs_0_), channel_id=1, source_target_pairs={{0,4},{4,0},{8,12},{12,8},{1,5},{5,1},{9,13},{13,9},{2,6},{6,2},{1... | collective-permute-start | bytes 884744 | tf_op jit(solution)/shard_map/ppermute | solution.py:22
  50.5 16.2 %collective-permute-start.16 = (bf16[192,384]{1,0:T(8,128)(2,1)S(1)}, bf16[192,384]{1,0:T(8,128)(2,1)S(1)}, u32[]{:S(2)}, u32[]{:S(2)}) collective-permute-start(bf16[192,384]{1,0:T(8,128)(2,1)S(1)} %collective-permute-done.15.refs_2_), channel_id=1, source_target_pairs={{0,4},{4,0},{8,12},{12,8},{1,5},{5,1},{9,13},{13,9},{2,6},{6,2},{1... | collective-permute-start | bytes 442376 | tf_op jit(solution)/shard_map/ppermute | solution.py:22
  52.5 16.3 %collective-permute-start.36 = (bf16[192,384]{1,0:T(8,128)(2,1)S(1)}, bf16[192,384]{1,0:T(8,128)(2,1)S(1)}, u32[]{:S(2)}, u32[]{:S(2)}) collective-permute-start(bf16[192,384]{1,0:T(8,128)(2,1)S(1)} %slice.186.refs_0_), channel_id=1, source_target_pairs={{0,8},{4,12},{8,0},{12,4},{1,9},{5,13},{9,1},{13,5},{2,10},{6,14},... | collective-permute-start | bytes 442376 | tf_op jit(solution)/shard_map/ppermute | solution.py:22
  53.8 18.2 %collective-permute-start.27 = (bf16[192,768]{1,0:T(8,128)(2,1)S(1)}, bf16[192,768]{1,0:T(8,128)(2,1)S(1)}, u32[]{:S(2)}, u32[]{:S(2)}) collective-permute-start(bf16[192,768]{1,0:T(8,128)(2,1)S(1)} %collective-permute-done.26.refs_2_), channel_id=1, source_target_pairs={{0,4},{4,0},{8,12},{12,8},{1,5},{5,1},{9,13},{13,9},{2,6},{6,2},{1... | collective-permute-start | bytes 884744 | tf_op jit(solution)/shard_map/ppermute | solution.py:22
  68.7 23.6 %collective-permute-start.17 = (bf16[768,384]{1,0:T(8,128)(2,1)S(1)}, bf16[768,384]{1,0:T(8,128)(2,1)S(1)}, u32[]{:S(2)}, u32[]{:S(2)}) collective-permute-start(bf16[768,384]{1,0:T(8,128)(2,1)S(1)} %stack_line.4.refs_4_), channel_id=1, source_target_pairs={{0,16},{16,0},{1,17},{17,1},{2,18},{18,2},{3,19},{19,3},{4,20},{20... | collective-permute-start | bytes 1769480 | tf_op jit(solution)/shard_map/ppermute | solution.py:22
  68.8 16.7 %collective-permute-start.49 = (bf16[192,768]{1,0:T(8,128)(2,1)S(1)}, bf16[192,768]{1,0:T(8,128)(2,1)S(1)}, u32[]{:S(2)}, u32[]{:S(2)}) collective-permute-start(bf16[192,768]{1,0:T(8,128)(2,1)S(1)} %slice.190.refs_0_), channel_id=1, source_target_pairs={{0,8},{4,12},{8,0},{12,4},{1,9},{5,13},{9,1},{13,5},{2,10},{6,14},... | collective-permute-start | bytes 884744 | tf_op jit(solution)/shard_map/ppermute | solution.py:22
  72.6 48.0 %collective-permute-start.28 = (bf16[768,768]{1,0:T(8,128)(2,1)S(1)}, bf16[768,768]{1,0:T(8,128)(2,1)S(1)}, u32[]{:S(2)}, u32[]{:S(2)}) collective-permute-start(bf16[768,768]{1,0:T(8,128)(2,1)S(1)} %stack_line.5.refs_4_), channel_id=1, source_target_pairs={{0,16},{16,0},{1,17},{17,1},{2,18},{18,2},{3,19},{19,3},{4,20},{20... | collective-permute-start | bytes 3538952 | tf_op jit(solution)/shard_map/ppermute | solution.py:22
  74.3 20.1 %collective-permute-start.48 = (bf16[192,768]{1,0:T(8,128)(2,1)S(1)}, bf16[192,768]{1,0:T(8,128)(2,1)S(1)}, u32[]{:S(2)}, u32[]{:S(2)}) collective-permute-start(bf16[192,768]{1,0:T(8,128)(2,1)S(1)} %slice.190.refs_0_), channel_id=1, source_target_pairs={{0,4},{4,0},{8,12},{12,8},{1,5},{5,1},{9,13},{13,9},{2,6},{6,2},{1... | collective-permute-start | bytes 884744 | tf_op jit(solution)/shard_map/ppermute | solution.py:22
  97.2 64.2 %collective-permute-start.51 = (bf16[768,768]{1,0:T(8,128)(2,1)S(1)}, bf16[768,768]{1,0:T(8,128)(2,1)S(1)}, u32[]{:S(2)}, u32[]{:S(2)}) collective-permute-start(bf16[768,768]{1,0:T(8,128)(2,1)S(1)} %stack_line.7.refs_8_), channel_id=1, source_target_pairs={{0,16},{16,0},{1,17},{17,1},{2,18},{18,2},{3,19},{19,3},{4,20},{20... | collective-permute-start | bytes 3538952 | tf_op jit(solution)/shard_map/ppermute | solution.py:22
  102.7 30.6 %collective-permute-start.38 = (bf16[768,384]{1,0:T(8,128)(2,1)S(1)}, bf16[768,384]{1,0:T(8,128)(2,1)S(1)}, u32[]{:S(2)}, u32[]{:S(2)}) collective-permute-start(bf16[768,384]{1,0:T(8,128)(2,1)S(1)} %stack_line.6.refs_4_), channel_id=1, source_target_pairs={{0,16},{16,0},{1,17},{17,1},{2,18},{18,2},{3,19},{19,3},{4,20},{20... | collective-permute-start | bytes 1769480 | tf_op jit(solution)/shard_map/ppermute | solution.py:22
  227.3 28.1 %collective-permute-start.98 = (bf16[768,768]{1,0:T(8,128)(2,1)S(1)}, bf16[768,768]{1,0:T(8,128)(2,1)S(1)}, u32[]{:S(2)}, u32[]{:S(2)}) collective-permute-start(bf16[768,768]{1,0:T(8,128)(2,1)S(1)} %get-tuple-element.277), channel_id=1, source_target_pairs={{0,16},{16,0},{1,17},{17,1},{2,18},{18,2},{3,19},{19,3},{4,20},{20... | collective-permute-start | bytes 3538952 | tf_op jit(solution)/shard_map/ppermute | solution.py:22
  231.2 29.3 %collective-permute-start.95 = (bf16[768,768]{1,0:T(8,128)(2,1)}, bf16[768,768]{1,0:T(8,128)(2,1)}, u32[]{:S(2)}, u32[]{:S(2)}) collective-permute-start(bf16[768,768]{1,0:T(8,128)(2,1)} %get-tuple-element.268), channel_id=1, source_target_pairs={{0,16},{16,0},{1,17},{17,1},{2,18},{18,2},{3,19},{19,3},{4,20},{20... | collective-permute-start | bytes 3538952 | tf_op jit(solution)/shard_map/ppermute | solution.py:22
  235.3 17.2 %collective-permute-start.88 = (bf16[768,384]{1,0:T(8,128)(2,1)S(1)}, bf16[768,384]{1,0:T(8,128)(2,1)S(1)}, u32[]{:S(2)}, u32[]{:S(2)}) collective-permute-start(bf16[768,384]{1,0:T(8,128)(2,1)S(1)} %get-tuple-element.249), channel_id=1, source_target_pairs={{0,16},{16,0},{1,17},{17,1},{2,18},{18,2},{3,19},{19,3},{4,20},{20... | collective-permute-start | bytes 1769480 | tf_op jit(solution)/shard_map/ppermute | solution.py:22
  257.7 22.7 %collective-permute-start.99 = (bf16[2,192,768]{2,1,0:T(8,128)(2,1)}, bf16[2,192,768]{2,1,0:T(8,128)(2,1)}, u32[]{:S(2)}, u32[]{:S(2)}) collective-permute-start(bf16[2,192,768]{2,1,0:T(8,128)(2,1)} %get-tuple-element.279), channel_id=1, source_target_pairs={{0,4},{4,0},{8,12},{12,8},{1,5},{5,1},{9,13},{13,9},{2,6},{6,2},{1... | collective-permute-start | bytes 1769480 | tf_op jit(solution)/shard_map/ppermute | solution.py:22
  258.9 34.0 %collective-permute-start.85 = (f32[2,192]{1,0:T(2,128)}, f32[2,192]{1,0:T(2,128)S(1)}, u32[]{:S(2)}, u32[]{:S(2)}) collective-permute-start(f32[2,192]{1,0:T(2,128)} %get-tuple-element.239), channel_id=1, source_target_pairs={{0,4},{4,0},{8,12},{12,8},{1,5},{5,1},{9,13},{13,9},{2,6},{6,2},{1... | collective-permute-start | bytes 4616 | tf_op jit(solution)/shard_map/ppermute | solution.py:22
  260.5 35.1 %collective-permute-start.86 = (f32[2,192]{1,0:T(2,128)}, f32[2,192]{1,0:T(2,128)S(1)}, u32[]{:S(2)}, u32[]{:S(2)}) collective-permute-start(f32[2,192]{1,0:T(2,128)} %get-tuple-element.240), channel_id=1, source_target_pairs={{0,8},{4,12},{8,0},{12,4},{1,9},{5,13},{9,1},{13,5},{2,10},{6,14},... | collective-permute-start | bytes 4616 | tf_op jit(solution)/shard_map/ppermute | solution.py:22
  264.1 28.3 %collective-permute-start.96 = (bf16[2,192,768]{2,1,0:T(8,128)(2,1)S(1)}, bf16[2,192,768]{2,1,0:T(8,128)(2,1)S(1)}, u32[]{:S(2)}, u32[]{:S(2)}) collective-permute-start(bf16[2,192,768]{2,1,0:T(8,128)(2,1)S(1)} %get-tuple-element.270), channel_id=1, source_target_pairs={{0,4},{4,0},{8,12},{12,8},{1,5},{5,1},{9,13},{13,9},{2,6},{6,2},{1... | collective-permute-start | bytes 1769480 | tf_op jit(solution)/shard_map/ppermute | solution.py:22
  266.2 29.7 %collective-permute-start.87 = (f32[2,192]{1,0:T(2,128)S(1)}, f32[2,192]{1,0:T(2,128)S(1)}, u32[]{:S(2)}, u32[]{:S(2)}) collective-permute-start(f32[2,192]{1,0:T(2,128)S(1)} %copy-done.21), channel_id=1, source_target_pairs={{0,12},{4,8},{8,4},{12,0},{1,13},{5,9},{9,5},{13,1},{2,14},{6,10},... | collective-permute-start | bytes 4616 | tf_op jit(solution)/shard_map/ppermute | solution.py:22
  280.4 16.1 %collective-permute-start.93 = (bf16[192,384]{1,0:T(8,128)(2,1)S(1)}, bf16[192,384]{1,0:T(8,128)(2,1)S(1)}, u32[]{:S(2)}, u32[]{:S(2)}) collective-permute-start(bf16[192,384]{1,0:T(8,128)(2,1)S(1)} %fusion.6), channel_id=1, source_target_pairs={{0,8},{4,12},{8,0},{12,4},{1,9},{5,13},{9,1},{13,5},{2,10},{6,14},... | collective-permute-start | bytes 442376 | tf_op jit(solution)/shard_map/ppermute | solution.py:22
  292.5 21.3 %collective-permute-start.90 = (bf16[192,384]{1,0:T(8,128)(2,1)S(1)}, bf16[192,384]{1,0:T(8,128)(2,1)S(1)}, u32[]{:S(2)}, u32[]{:S(2)}) collective-permute-start(bf16[192,384]{1,0:T(8,128)(2,1)S(1)} %fusion.8), channel_id=1, source_target_pairs={{0,8},{4,12},{8,0},{12,4},{1,9},{5,13},{9,1},{13,5},{2,10},{6,14},... | collective-permute-start | bytes 442376 | tf_op jit(solution)/shard_map/ppermute | solution.py:22
  292.9 27.1 %collective-permute-start.100 = (bf16[192,768]{1,0:T(8,128)(2,1)S(1)}, bf16[192,768]{1,0:T(8,128)(2,1)S(1)}, u32[]{:S(2)}, u32[]{:S(2)}) collective-permute-start(bf16[192,768]{1,0:T(8,128)(2,1)S(1)} %fusion), channel_id=1, source_target_pairs={{0,8},{4,12},{8,0},{12,4},{1,9},{5,13},{9,1},{13,5},{2,10},{6,14},... | collective-permute-start | bytes 884744 | tf_op jit(solution)/shard_map/ppermute | solution.py:22
  295.5 30.0 %collective-permute-start.97 = (bf16[192,768]{1,0:T(8,128)(2,1)S(1)}, bf16[192,768]{1,0:T(8,128)(2,1)S(1)}, u32[]{:S(2)}, u32[]{:S(2)}) collective-permute-start(bf16[192,768]{1,0:T(8,128)(2,1)S(1)} %fusion.2), channel_id=1, source_target_pairs={{0,8},{4,12},{8,0},{12,4},{1,9},{5,13},{9,1},{13,5},{2,10},{6,14},... | collective-permute-start | bytes 884744 | tf_op jit(solution)/shard_map/ppermute | solution.py:22
  (111 other events, 1022.1 us)

commit v3 on v2

--- a/solution.py
+++ b/solution.py
@@ -35,6 +35,10 @@
     while len(parts) > 1:
         parts = [parts[k] + parts[k + 1] for k in range(0, len(parts), 2)]
     return parts[0]
+
+
+def trade(rows, axis):
+    return lax.all_to_all(rows, axis, 0, 0, tiled=True)
 
 
 def shape(dims, dtype):
@@ -107,17 +111,15 @@
     )
 
 
-def put_rows(ref, refs):
-    own = refs[0].shape[0]
-    for k, source in enumerate(refs):
-        ref[k * own : (k + 1) * own] = source[...]
-    return ref[...]
-
-
-def put_blocks(refs, values):
-    own = refs[0].shape[0]
-    for k, ref in enumerate(refs):
-        ref[...] = values[k * own : (k + 1) * own].astype(ref.dtype)
+def block_sum(ref, own):
+    count = ref.shape[0] // own
+    return tree_sum([ref[k * own : (k + 1) * own].astype(F32) for k in range(count)])
+
+
+def copies(ref, values):
+    own = values.shape[0]
+    for k in range(ref.shape[0] // own):
+        ref[k * own : (k + 1) * own] = values
 
 
 def enter_body(place, tokens, cotangent, mod0, mod1, h_out, attn_in, g_y_out, g_shrunk):
@@ -125,10 +127,10 @@
     h = tokens[core].astype(F32)
     h_out[...] = h
     normed, _ = normalize(h)
-    attn_in[...] = (normed * (1.0 + part(mod0, 1)) + part(mod0, 0)).astype(BF16)
+    copies(attn_in, (normed * (1.0 + part(mod0, 1)) + part(mod0, 0)).astype(BF16))
     g_y = cotangent[core].astype(F32)
     g_y_out[...] = g_y
-    g_shrunk[...] = (part(mod1, 5) * g_y).astype(BF16)
+    copies(g_shrunk, (part(mod1, 5) * g_y).astype(BF16))
 
 
 def pick_attn(place, own, received):
@@ -140,12 +142,8 @@
     return front, back[:, :width], back[:, width:]
 
 
-def attn_body(count, place, *refs):
-    chunks = refs[:count]
-    w_own, w_received, bias = refs[count : count + 3]
-    rows_out, qkv_out, probs_out, mixed_out = refs[count + 3 : count + 7]
-    partial = refs[count + 7 :]
-    rows = put_rows(rows_out, chunks)
+def attn_body(place, rows_ref, w_own, w_received, bias, qkv_out, probs_out, mixed_out, partial):
+    rows = rows_ref[...]
     w_front, w_value, w_out = pick_attn(place, w_own, w_received)
     width = w_value.shape[1]
     front = (dot(rows, w_front) + bias[:, : 2 * width]).astype(BF16)
@@ -164,24 +162,20 @@
         mixed.append(dot(probs.astype(BF16), value[:, at : at + HEAD]))
     mixed = jnp.concatenate(mixed, axis=1).astype(BF16)
     mixed_out[...] = mixed
-    put_blocks(partial, dot_t(mixed, w_out))
-
-
-def middle_body(count, *refs):
-    parts, (bias, h, mod, attended_out, middle_out, mlp_in) = refs[:count], refs[count:]
-    attended = total(parts) + bias[...]
+    partial[...] = dot_t(mixed, w_out).astype(BF16)
+
+
+def middle_body(parts, bias, h, mod, attended_out, middle_out, mlp_in):
+    attended = block_sum(parts, h.shape[0]) + bias[...]
     attended_out[...] = attended
     middle = h[...] + part(mod, 2) * attended
     middle_out[...] = middle
     normed, _ = normalize(middle)
-    mlp_in[...] = (normed * (1.0 + part(mod, 4)) + part(mod, 3)).astype(BF16)
-
-
-def mlp_body(count, *refs):
-    chunks = refs[:count]
-    w_own, w_received, bias, rows_out, pre_out, hidden_out = refs[count : count + 6]
-    partial = refs[count + 6 :]
-    rows = put_rows(rows_out, chunks)
+    copies(mlp_in, (normed * (1.0 + part(mod, 4)) + part(mod, 3)).astype(BF16))
+
+
+def mlp_body(rows_ref, w_own, w_received, bias, pre_out, hidden_out, partial):
+    rows = rows_ref[...]
     half = w_own.shape[1] // 2
     shrunk = None
     for index, weight in enumerate((w_own, w_received)):
@@ -192,18 +186,14 @@
         hidden_out[:, at : at + half] = hidden
         term = dot_t(hidden, weight[:, half:])
         shrunk = term if shrunk is None else shrunk + term
-    put_blocks(partial, shrunk)
-
-
-def mlp_both_body(count, *refs):
-    chunks, g_chunks = refs[:count], refs[count : 2 * count]
-    w_own, w_received, bias, rows_out, g_rows_out, hidden_out, g_pre_out, bias_grad = refs[
-        2 * count : 2 * count + 8
-    ]
-    partial = refs[2 * count + 8 : 3 * count + 8]
-    g_partial = refs[3 * count + 8 :]
-    rows = put_rows(rows_out, chunks)
-    g_rows = put_rows(g_rows_out, g_chunks)
+    partial[...] = shrunk.astype(BF16)
+
+
+def mlp_both_body(
+    rows_ref, g_rows_ref, w_own, w_received, bias, hidden_out, g_pre_out, bias_grad, partial, g_partial
+):
+    rows = rows_ref[...]
+    g_rows = g_rows_ref[...]
     half = w_own.shape[1] // 2
     shrunk, g_in = None, None
     for index, weight in enumerate((w_own, w_received)):
@@ -218,15 +208,12 @@
         g_term = dot_t(g_pre, weight[:, :half])
         shrunk = term if shrunk is None else shrunk + term
         g_in = g_term if g_in is None else g_in + g_term
-    put_blocks(g_partial, g_in)
-    put_blocks(partial, shrunk)
-
-
-def mlp_back_body(count, *refs):
-    g_chunks = refs[:count]
-    w_own, w_received, pre_ref, g_rows_out, g_pre_out, bias_grad = refs[count : count + 6]
-    g_partial = refs[count + 6 :]
-    g_rows = put_rows(g_rows_out, g_chunks)
+    g_partial[...] = g_in.astype(BF16)
+    partial[...] = shrunk.astype(BF16)
+
+
+def mlp_back_body(g_rows_ref, w_own, w_received, pre_ref, g_pre_out, bias_grad, g_partial):
+    g_rows = g_rows_ref[...]
     half = w_own.shape[1] // 2
     g_in = None
     for index, weight in enumerate((w_own, w_received)):
@@ -237,37 +224,41 @@
         bias_grad[:, at : at + half] = column_sum(g_pre.astype(F32))
         g_term = dot_t(g_pre, weight[:, :half])
         g_in = g_term if g_in is None else g_in + g_term
-    put_blocks(g_partial, g_in)
-
-
-def between_body(count, *refs):
-    parts = refs[:count]
-    bias, middle, mod0, mod1, shrunk_out, passed_out, h_out, attn_in = refs[count:]
-    shrunk = total(parts) + bias[...]
+    g_partial[...] = g_in.astype(BF16)
+
+
+def between_body(parts, bias, middle, mod0, mod1, shrunk_out, passed_out, h_out, attn_in):
+    shrunk = block_sum(parts, middle.shape[0]) + bias[...]
     shrunk_out[...] = shrunk
     passed = (middle[...] + part(mod0, 5) * shrunk).astype(BF16)
     passed_out[...] = passed
     h = passed.astype(F32)
     h_out[...] = h
     normed, _ = normalize(h)
-    attn_in[...] = (normed * (1.0 + part(mod1, 1)) + part(mod1, 0)).astype(BF16)
-
-
-def leave_body(count, *refs):
-    parts = refs[:count]
-    bias, middle, mod, g_y_ref, g_shrunk, y_out, g_gate, bias_grad = refs[count:]
-    shrunk = total(parts) + bias[...]
+    copies(attn_in, (normed * (1.0 + part(mod1, 1)) + part(mod1, 0)).astype(BF16))
+
+
+def leave_body(parts, bias, middle, mod, g_y_ref, y_out, g_gate, bias_grad):
+    shrunk = block_sum(parts, middle.shape[0]) + bias[...]
     y_out[...] = (middle[...] + part(mod, 5) * shrunk).astype(BF16)
     g_gate[...] = column_sum(g_y_ref[...] * shrunk)
-    bias_grad[...] = column_sum(g_shrunk[...].astype(F32))
-
-
-def middle_back_body(count, *refs):
-    parts = refs[:count]
-    middle, mod, g_y, attended, g_middle_out, g_attended_out, g_shift, g_scale, g_gate, bias_grad = refs[
-        count:
-    ]
-    g_in = total(parts)
+    bias_grad[...] = column_sum((part(mod, 5) * g_y_ref[...]).astype(BF16).astype(F32))
+
+
+def middle_back_body(
+    parts,
+    middle,
+    mod,
+    g_y,
+    attended,
+    g_middle_out,
+    g_attended_out,
+    g_shift,
+    g_scale,
+    g_gate,
+    bias_grad,
+):
+    g_in = block_sum(parts, middle.shape[0])
     normed, rstd = normalize(middle[...])
     g_shift[...] = column_sum(g_in)
     g_scale[...] = column_sum(g_in * normed)
@@ -275,16 +266,14 @@
     g_middle_out[...] = g_middle
     g_gate[...] = column_sum(g_middle * attended[...])
     g_attended = (part(mod, 2) * g_middle).astype(BF16)
-    g_attended_out[...] = g_attended
+    copies(g_attended_out, g_attended)
     bias_grad[...] = column_sum(g_attended.astype(F32))
 
 
-def attn_back_body(count, place, *refs):
-    g_chunks = refs[:count]
-    w_own, w_received, qkv, probs_ref = refs[count : count + 4]
-    g_rows_out, g_joint_out, bias_grad = refs[count + 4 : count + 7]
-    g_partial = refs[count + 7 :]
-    g_rows = put_rows(g_rows_out, g_chunks)
+def attn_back_body(
+    place, g_rows_ref, w_own, w_received, qkv, probs_ref, g_joint_out, bias_grad, g_partial
+):
+    g_rows = g_rows_ref[...]
     w_front, w_value, w_out = pick_attn(place, w_own, w_received)
     width = w_value.shape[1]
     g_mixed = dot(g_rows, w_out).astype(BF16)
@@ -308,34 +297,43 @@
     g_joint_out[:, 2 * width :] = g_value
     bias_grad[:, :width] = column_sum(g_front[:, :width].astype(F32))
     bias_grad[:, width:] = column_sum(g_value.astype(F32))
-    put_blocks(g_partial, dot_t(g_front, w_front) + dot_t(g_value, w_value))
+    g_partial[...] = (dot_t(g_front, w_front) + dot_t(g_value, w_value)).astype(BF16)
 
 
 def input_grad(parts, h, mod, g_middle, g_shift, g_scale):
-    g_in = total(parts)
+    g_in = block_sum(parts, h.shape[0])
     normed, rstd = normalize(h[...])
     g_shift[...] = column_sum(g_in)
     g_scale[...] = column_sum(g_in * normed)
     return (g_middle[...] + normalize_back(g_in * (1.0 + part(mod, 1)), normed, rstd)).astype(BF16)
 
 
-def between_back_body(count, *refs):
-    parts = refs[:count]
-    h, mod1, mod0, g_middle, shrunk, g_h_out, g_y_out, g_shrunk_out = refs[count : count + 8]
-    g_shift, g_scale, g_gate, bias_grad = refs[count + 8 :]
+def between_back_body(
+    parts,
+    h,
+    mod1,
+    mod0,
+    g_middle,
+    shrunk,
+    g_h_out,
+    g_y_out,
+    g_shrunk_out,
+    g_shift,
+    g_scale,
+    g_gate,
+    bias_grad,
+):
     g_h = input_grad(parts, h, mod1, g_middle, g_shift, g_scale)
     g_h_out[...] = g_h
     g_y = g_h.astype(F32)
     g_y_out[...] = g_y
     g_gate[...] = column_sum(g_y * shrunk[...])
     g_shrunk = (part(mod0, 5) * g_y).astype(BF16)
-    g_shrunk_out[...] = g_shrunk
+    copies(g_shrunk_out, g_shrunk)
     bias_grad[...] = column_sum(g_shrunk.astype(F32))
 
 
-def finish_back_body(count, *refs):
-    parts = refs[:count]
-    h, mod, g_middle, g_h_out, g_shift, g_scale = refs[count:]
+def finish_back_body(parts, h, mod, g_middle, g_h_out, g_shift, g_scale):
     g_h_out[...] = input_grad(parts, h, mod, g_middle, g_shift, g_scale)
 
 
@@ -511,6 +509,9 @@
     def after(value, earlier):
         return lax.optimization_barrier((value, earlier))[0]
 
+    def tie(*values):
+        return lax.optimization_barrier(values)
+
     attn_pack = jnp.concatenate(
         [joint_weight[0].reshape(chunk, 3 * width), output_weight[0].T], axis=1
     )
@@ -552,13 +553,19 @@
         at += hidden
         biases.append((joint, packed[:, at : at + model], grown, packed[:, at + model :]))
 
-    def along_line(value, earlier):
+    activated = jax.nn.silu(conditions[:, 0].astype(F32)).astype(BF16)
+    if direct:
+        activated_all = gather(activated, "dp")
+    else:
+        activated_all = lax.all_gather(activated, "dp", axis=0).reshape(line_size * micro, -1)
+
+    def along_line(value, earlier, at_once=False):
         if earlier is not None:
             value = after(value, earlier)
         if direct:
             near = swap(value, "dp", 1)
             far = swap(value, "dp", 2)
-            farther = swap(far, "dp", 1)
+            farther = swap(value, "dp", 3) if at_once else swap(far, "dp", 1)
             lined = run(
                 "stack_line",
                 stack_body,
@@ -566,22 +573,20 @@
                 [value, near, far, farther],
                 place,
             )[0]
-            mark = far
+            mark = (near, far, farther) if at_once else far
         else:
             lined = lax.all_gather(value, "dp", axis=0, tiled=True)
             mark = lined
         return (lined, swap(lined, "pipe", 1)), mark
 
     weights = []
-    mark = None
+    mark = activated_all
     for layer in range(2):
-        attn, mark = along_line(halves_of_layers[layer][:, :split], mark)
+        attn, mark = along_line(halves_of_layers[layer][:, :split], mark, layer == 0)
         mlp, mark = along_line(halves_of_layers[layer][:, split:], mark)
         weights.append((attn, mlp))
 
-    activated = jax.nn.silu(conditions[:, 0].astype(F32)).astype(BF16)
     if direct:
-        activated_all = gather(activated, "dp")
         mod_partial = run(
             "mod_first",
             mod_first_body,
@@ -604,7 +609,6 @@
             name="mod_join",
         )(place, *exchange(pieces, "dp"), modulation_bias)
     else:
-        activated_all = lax.all_gather(activated, "dp", axis=0).reshape(line_size * micro, -1)
         mod_partial = dot(activated_all, own_rows)
         mod_sum = tree_sum(gather(mod_partial, "tensor")).reshape(line_size, micro, -1)
         mod_layer = lax.all_to_all(mod_sum, "dp", split_axis=0, concat_axis=0)
@@ -614,179 +618,192 @@
 
     own_f32 = shape((own, model), F32)
     own_bf16 = shape((own, model), BF16)
-    blocks = [own_bf16] * count
+    wide_bf16 = shape((rows, model), BF16)
+    hidden_bf16 = shape((rows, hidden), BF16)
     vector = shape((1, model), F32)
+    hidden_vector = shape((1, hidden), F32)
     h0, attn_in, g_y1, g_shrunk1 = run(
         "enter",
         enter_body,
-        [own_f32, own_bf16, own_f32, own_bf16],
+        [own_f32, wide_bf16, own_f32, wide_bf16],
         [tokens[:, 0], cotangent[:, 0], mod0, mod1],
         place,
     )
 
-    def attention(attn_in, weight, bias):
-        outs = run(
+    def attention(attn_rows, weight, bias):
+        qkv, probs, mixed, partial = run(
             "attention",
-            functools.partial(attn_body, count),
+            attn_body,
             [
-                shape((rows, model), BF16),
                 shape((rows, 3 * width), BF16),
                 shape((width // HEAD, rows, rows), F32),
                 shape((rows, width), BF16),
-            ]
-            + blocks,
-            gather(attn_in, "tensor") + [weight[0], weight[1], bias],
+                wide_bf16,
+            ],
+            [attn_rows, weight[0], weight[1], bias],
             place,
         )
-        return outs[:4], exchange(outs[4:], "tensor")
+        return (attn_rows, qkv, probs, mixed), trade(partial, "tensor")
 
     def middle_of(parts, bias, h, mod):
         return run(
-            "middle",
-            functools.partial(middle_body, count),
-            [own_f32, own_f32, own_bf16],
-            parts + [bias, h, mod],
-        )
-
-    kept_attn0, parts = attention(attn_in, weights[0][0], biases[0][0])
+            "middle", middle_body, [own_f32, own_f32, wide_bf16], [parts, bias, h, mod]
+        )
+
+    kept_attn0, parts = attention(trade(attn_in, "tensor"), weights[0][0], biases[0][0])
     attended0, middle0, mlp_in = middle_of(parts, biases[0][1], h0, mod0)
-    outs = run(
+    mlp_rows0 = trade(mlp_in, "tensor")
+    pre0, hidden0, partial = run(
         "feed_forward",
-        functools.partial(mlp_body, count),
-        [shape((rows, model), BF16), shape((rows, hidden), F32), shape((rows, hidden), BF16)] + blocks,
-        gather(mlp_in, "tensor") + [weights[0][1][0], weights[0][1][1], biases[0][2]],
-    )
-    mlp_rows0, pre0, hidden0 = outs[:3]
+        mlp_body,
+        [shape((rows, hidden), F32), hidden_bf16, wide_bf16],
+        [mlp_rows0, weights[0][1][0], weights[0][1][1], biases[0][2]],
+    )
     shrunk0, passed, h1, attn_in = run(
         "between",
-        functools.partial(between_body, count),
-        [own_f32, own_bf16, own_f32, own_bf16],
-        exchange(outs[3:], "tensor") + [biases[0][3], middle0, mod0, mod1],
-    )
-
-    g_shrunk_rows = gather(g_shrunk1, "tensor")
-    kept_attn1, parts = attention(attn_in, weights[1][0], biases[1][0])
+        between_body,
+        [own_f32, own_bf16, own_f32, wide_bf16],
+        [trade(partial, "tensor"), biases[0][3], middle0, mod0, mod1],
+    )
+
+    g_rows1 = trade(g_shrunk1, "tensor")
+    kept_attn1, parts = attention(trade(attn_in, "tensor"), weights[1][0], biases[1][0])
     attended1, middle1, mlp_in = middle_of(parts, biases[1][1], h1, mod1)
-    outs = run(
+    mlp_rows1 = trade(mlp_in, "tensor")
+    hidden1, g_pre1, expand_grad1, y_partial, g_partial = run(
         "feed_forward_both",
-        functools.partial(mlp_both_body, count),
-        [
-            shape((rows, model), BF16),
-            shape((rows, model), BF16),
-            shape((rows, hidden), BF16),
-            shape((rows, hidden), BF16),
-            shape((1, hidden), F32),
-        ]
-        + blocks
-        + blocks,
-        gather(mlp_in, "tensor")
-        + g_shrunk_rows
-        + [weights[1][1][0], weights[1][1][1], biases[1][2]],
-    )
-    mlp_rows1, g_rows1, hidden1, g_pre1, expand_grad1 = outs[:5]
-    y_parts, g_parts = outs[5 : 5 + count], outs[5 + count :]
+        mlp_both_body,
+        [hidden_bf16, hidden_bf16, hidden_vector, wide_bf16, wide_bf16],
+        [mlp_rows1, g_rows1, weights[1][1][0], weights[1][1][1], biases[1][2]],
+    )
 
     def middle_back(parts, middle, mod, g_y, attended):
         return run(
             "middle_back",
-            functools.partial(middle_back_body, count),
-            [own_f32, own_bf16] + [vector] * 4,
-            parts + [middle, mod, g_y, attended],
-        )
-
-    def attention_back(g_attended, weight, kept):
-        outs = run(
+            middle_back_body,
+            [own_f32, wide_bf16] + [vector] * 4,
+            [parts, middle, mod, g_y, attended],
+        )
+
+    def attention_back(g_rows, weight, kept):
+        return run(
             "attention_back",
-            functools.partial(attn_back_body, count),
-            [
-                shape((rows, model), BF16),
-                shape((rows, 3 * width), BF16),
-                shape((1, 2 * width), F32),
-            ]
-            + blocks,
-            gather(g_attended, "tensor") + [weight[0], weight[1], kept[1], kept[2]],
+            attn_back_body,
+            [shape((rows, 3 * width), BF16), shape((1, 2 * width), F32), wide_bf16],
+            [g_rows, weight[0], weight[1], kept[1], kept[2]],
             place,
         )
-        return outs[:3], exchange(outs[3:], "tensor")
-
-    def reduce_line(keep, give):
-        received = swap(give, "pipe", 1)
-        if not direct:
-            whole = (keep + received.astype(F32)).astype(BF16)
-            return lax.psum_scatter(whole, "dp", scatter_dimension=0, tiled=True).astype(F32)
-        wide = keep.shape[1]
-        near, far, own_part = run(
-            "line_parts",
-            line_parts_body,
-            [
-                shape((2, chunk, wide), BF16),
-                shape((chunk, wide), F32),
-                shape((chunk, wide), F32),
-            ],
-            [keep, received],
-            place,
-        )
-        near = swap(near, "dp", 1)
-        far = swap((far + near[1].astype(F32)).astype(BF16), "dp", 2)
-        return own_part + near[0].astype(F32) + far.astype(F32)
 
     def mlp_weight_grads(mlp_rows, g_pre, g_rows, hidden_rows):
-        keep, give = run(
+        return run(
             "mlp_weight_grads",
             mlp_weights_body,
             [shape((model, hidden), F32), shape((model, hidden), BF16)],
             [mlp_rows, g_pre, g_rows, hidden_rows],
         )
-        return reduce_line(keep, give)
-
-    def attn_weight_grads(attn_rows, g_joint, g_rows, mixed):
-        keep, give = run(
+
+    def attn_weight_grads(kept, g_joint, g_rows):
+        return run(
             "attn_weight_grads",
             attn_weights_body,
             [shape((model, 2 * width), F32), shape((model, 2 * width), BF16)],
-            [attn_rows, g_joint, g_rows, mixed],
+            [kept[0], g_joint, g_rows, kept[3]],
             place,
         )
-        return reduce_line(keep, give)
-
+
+    def line_parts(keep, received):
+        if not direct:
+            return None, (keep + received.astype(F32)).astype(BF16), None
+        wide = keep.shape[1]
+        return run(
+            "line_parts",
+            line_parts_body,
+            [shape((2, chunk, wide), BF16), shape((chunk, wide), F32), shape((chunk, wide), F32)],
+            [keep, received],
+            place,
+        )
+
+    def line_near(parts):
+        return swap(parts[0], "dp", 1) if direct else parts[1]
+
+    def line_far(parts, near):
+        if not direct:
+            return near
+        return swap((parts[1] + near[1].astype(F32)).astype(BF16), "dp", 2)
+
+    def line_total(parts, near, far):
+        if not direct:
+            return lax.psum_scatter(far, "dp", scatter_dimension=0, tiled=True).astype(F32)
+        return parts[2] + near[0].astype(F32) + far.astype(F32)
+
+    y_parts = trade(y_partial, "tensor")
+    g_parts = trade(g_partial, "tensor")
+    keep_m1, give_m1 = mlp_weight_grads(mlp_rows1, g_pre1, g_rows1, hidden1)
+    g_parts, give_m1 = tie(g_parts, give_m1)
     g_middle1, g_attended, g_shift_mlp1, g_scale_mlp1, g_gate_attn1, out_grad1 = middle_back(
-        exchange(g_parts, "tensor"), middle1, mod1, g_y1, attended1
-    )
-    mlp_grad1 = mlp_weight_grads(mlp_rows1, g_pre1, g_rows1, hidden1)
+        g_parts, middle1, mod1, g_y1, attended1
+    )
+    g_rows = trade(g_attended, "tensor")
+    got_m1 = swap(give_m1, "pipe", 1)
+    g_rows, got_m1 = tie(g_rows, got_m1)
+    g_joint, joint_grad1, partial = attention_back(g_rows, weights[1][0], kept_attn1)
+    parts = trade(partial, "tensor")
+    parts_m1 = line_parts(keep_m1, got_m1)
+    keep_a1, give_a1 = attn_weight_grads(kept_attn1, g_joint, g_rows)
+    parts, parts_m1, give_a1 = tie(parts, parts_m1, give_a1)
+    g_passed, g_y0, g_shrunk0, g_shift_attn1, g_scale_attn1, g_gate_mlp0, shrink_grad0 = run(
+        "between_back",
+        between_back_body,
+        [own_bf16, own_f32, wide_bf16] + [vector] * 4,
+        [parts, h1, mod1, mod0, g_middle1, shrunk0],
+    )
+    g_rows0 = trade(g_shrunk0, "tensor")
+    near_m1 = line_near(parts_m1)
+    got_a1 = swap(give_a1, "pipe", 1)
+    g_rows0, got_a1 = tie(g_rows0, got_a1)
+
+    g_pre0, expand_grad0, partial = run(
+        "feed_forward_back",
+        mlp_back_body,
+        [hidden_bf16, hidden_vector, wide_bf16],
+        [g_rows0, weights[0][1][0], weights[0][1][1], pre0],
+    )
+    parts = trade(partial, "tensor")
+    parts_a1 = line_parts(keep_a1, got_a1)
+    keep_m0, give_m0 = mlp_weight_grads(mlp_rows0, g_pre0, g_rows0, hidden0)
+    parts, near_m1, parts_a1, give_m0 = tie(parts, near_m1, parts_a1, give_m0)
+    g_middle0, g_attended, g_shift_mlp0, g_scale_mlp0, g_gate_attn0, out_grad0 = middle_back(
+        parts, middle0, mod0, g_y0, attended0
+    )
+    g_rows = trade(g_attended, "tensor")
+    far_m1 = line_far(parts_m1, near_m1)
+    near_a1 = line_near(parts_a1)
+    got_m0 = swap(give_m0, "pipe", 1)
+    g_rows, got_m0 = tie(g_rows, got_m0)
     y1, g_gate_mlp1, shrink_grad1 = run(
         "leave",
-        functools.partial(leave_body, count),
+        leave_body,
         [own_bf16, vector, vector],
-        exchange(y_parts, "tensor") + [biases[1][3], middle1, mod1, g_y1, g_shrunk1],
-    )
-    (g_rows, g_joint, joint_grad1), parts = attention_back(g_attended, weights[1][0], kept_attn1)
-    g_passed, g_y0, g_shrunk0, g_shift_attn1, g_scale_attn1, g_gate_mlp0, shrink_grad0 = run(
-        "between_back",
-        functools.partial(between_back_body, count),
-        [own_bf16, own_f32, own_bf16] + [vector] * 4,
-        parts + [h1, mod1, mod0, g_middle1, shrunk0],
-    )
-    attn_grad1 = attn_weight_grads(kept_attn1[0], g_joint, g_rows, kept_attn1[3])
-
-    outs = run(
-        "feed_forward_back",
-        functools.partial(mlp_back_body, count),
-        [shape((rows, model), BF16), shape((rows, hidden), BF16), shape((1, hidden), F32)] + blocks,
-        gather(g_shrunk0, "tensor") + [weights[0][1][0], weights[0][1][1], pre0],
-    )
-    g_rows0, g_pre0, expand_grad0 = outs[:3]
-    g_middle0, g_attended, g_shift_mlp0, g_scale_mlp0, g_gate_attn0, out_grad0 = middle_back(
-        exchange(outs[3:], "tensor"), middle0, mod0, g_y0, attended0
-    )
-    mlp_grad0 = mlp_weight_grads(mlp_rows0, g_pre0, g_rows0, hidden0)
-    (g_rows, g_joint, joint_grad0), parts = attention_back(g_attended, weights[0][0], kept_attn0)
+        [y_parts, biases[1][3], middle1, mod1, g_y1],
+    )
+    g_joint, joint_grad0, partial = attention_back(g_rows, weights[0][0], kept_attn0)
+    parts = trade(partial, "tensor")
+    parts_m0 = line_parts(keep_m0, got_m0)
+    keep_a0, give_a0 = attn_weight_grads(kept_attn0, g_joint, g_rows)
+    parts, far_m1, near_a1, parts_m0, give_a0 = tie(parts, far_m1, near_a1, parts_m0, give_a0)
     g_h0, g_shift_attn0, g_scale_attn0 = run(
-        "finish_back",
-        functools.partial(finish_back_body, count),
-        [own_bf16, vector, vector],
-        parts + [h0, mod0, g_middle0],
-    )
-    attn_grad0 = attn_weight_grads(kept_attn0[0], g_joint, g_rows, kept_attn0[3])
+        "finish_back", finish_back_body, [own_bf16, vector, vector], [parts, h0, mod0, g_middle0]
+    )
+    near_m0 = line_near(parts_m0)
+    far_a1 = line_far(parts_a1, near_a1)
+    parts_a0 = line_parts(keep_a0, swap(give_a0, "pipe", 1))
+    near_a0 = line_near(parts_a0)
+    far_m0 = line_far(parts_m0, near_m0)
+    far_a0 = line_far(parts_a0, near_a0)
+    mlp_grad1 = line_total(parts_m1, near_m1, far_m1)
+    attn_grad1 = line_total(parts_a1, near_a1, far_a1)
+    mlp_grad0 = line_total(parts_m0, near_m0, far_m0)
+    attn_grad0 = line_total(parts_a0, near_a0, far_a0)
 
     def own_layer_of_micros(pair):
         return jnp.stack(both_layers(mine(pair), swap(other(pair), "pipe", 1)))

time: 336 us -> 364 us (1.083)
  waiting for transfers between devices: 169 us -> 89.3 us
  local copies, waits for them, and re-layouts: 10.3 us -> 71.9 us
  blocking collectives: 0 us -> 35.2 us
  Pallas kernels: 35.2 us -> 41.4 us
  other arithmetic: 14.8 us -> 19.3 us
    ppermute x102 -> x54, waiting for transfers between devices: 169 us -> 65.4 us  [swap(): return lax.ppermute(value, axis, pairs)]
    unnamed x71 -> x285, local copies, waits for them, and re-layouts: 7.41 us -> 66.5 us
    ppermute x102 -> x54, starting transfers between devices: 105 us -> 52.8 us  [swap(): return lax.ppermute(value, axis, pairs)]
    all_to_all x0 -> x13, starting transfers between devices: none -> 49.4 us  [trade(): return lax.all_to_all(rows, axis, 0, 0, tiled=True)]
    all_to_all x0 -> x3, blocking collectives: none -> 35.2 us  [trade(): return lax.all_to_all(rows, axis, 0, 0, tiled=True)]
    all_to_all x0 -> x13, waiting for transfers between devices: none -> 23.9 us  [trade(): return lax.all_to_all(rows, axis, 0, 0, tiled=True)]
    pallas_call x34, Pallas kernels: 33.8 us -> 39.9 us  [run(): pl.pallas_call(body, out_shape=outs, in_specs=specs, out_specs=[pl.BlockS...]
  transfers between devices with their start and end apart: 102 -> 67, of which waited for: 60 -> 30; matrix products, arithmetic and copies ran while one was open for 5% -> 6% of each run, Pallas kernels for 8% -> 10%
where the time goes in v3:
time: 364 us; the launch traced here: 361 us
  starting transfers between devices  102 us (28%)
  waiting for transfers between devices  89.3 us (25%)
  local copies, waits for them, and re-layouts  71.9 us (20%)
  Pallas kernels  41.4 us (11%)
  blocking collectives  35.2 us (10%)
  other arithmetic  19.3 us (5%)
    unnamed x285, local copies, waits for them, and re-layouts  66.5 us
    ppermute x54, waiting for transfers between devices, swap(): return lax.ppermute(value, axis, pairs)  65.4 us
    ppermute x54, starting transfers between devices, swap(): return lax.ppermute(value, axis, pairs)  52.8 us
    all_to_all x13, starting transfers between devices, trade(): return lax.all_to_all(rows, axis, 0, 0, tiled=True)  49.4 us
    pallas_call x34, Pallas kernels, run(): pl.pallas_call(body, out_shape=outs, in_specs=specs, out_specs=[pl.BlockS...  39.9 us
    all_to_all x3, blocking collectives, trade(): return lax.all_to_all(rows, axis, 0, 0, tiled=True)  35.2 us
    all_to_all x13, waiting for transfers between devices, trade(): return lax.all_to_all(rows, axis, 0, 0, tiled=True)  23.9 us
  transfers between devices with their start and end apart: 67, of which 30 were waited for; matrix products, arithmetic and copies ran while one was open for 6% of the time, Pallas kernels for 10%

profile of v3, /device:TPU:0, one launch (start us, length us, event | category | flops | bytes accessed | tf_op | source)
XLA Modules:
  0.0 361.3 jit_solution(4061841063820671625)
XLA Ops:
  3.9 5.0 %collective-permute-start.2 = (bf16[2,192]{1,0:T(2,128)(2,1)S(1)}, bf16[2,192]{1,0:T(2,128)(2,1)S(1)}, u32[]{:S(2)}, u32[]{:S(2)}) collective-permute-start(bf16[2,192]{1,0:T(2,128)(2,1)S(1)} %fusion.16.a0), channel_id=1, source_target_pairs={{0,12},{4,8},{8,4},{12,0},{1,13},{5,9},{9,5},{13,1},{2,14},{6,10},... | collective-permute-start | bytes 2312 | tf_op jit(solution)/shard_map/ppermute | solution.py:22
  17.9 4.2 %collective-permute-done.13.refs_3_ = bf16[192,384]{1,0:T(8,128)(2,1)S(1)} collective-permute-done((bf16[192,384]{1,0:T(8,128)(2,1)S(1)}, bf16[192,384]{1,0:T(8,128)(2,1)S(1)}, u32[]{:S(2)}, u32[]{:S(2)}) %collective-permute-start.13) | collective-permute-done | bytes 147488 | tf_op jit(solution)/shard_map/ppermute | solution.py:22
  22.1 5.6 %collective-permute-done.12.refs_2_ = bf16[192,384]{1,0:T(8,128)(2,1)S(1)} collective-permute-done((bf16[192,384]{1,0:T(8,128)(2,1)S(1)}, bf16[192,384]{1,0:T(8,128)(2,1)S(1)}, u32[]{:S(2)}, u32[]{:S(2)}) %collective-permute-start.12) | collective-permute-done | bytes 147488 | tf_op jit(solution)/shard_map/ppermute | solution.py:22
  49.5 6.3 %collective-permute-done.16.refs_1_ = bf16[192,768]{1,0:T(8,128)(2,1)S(1)} collective-permute-done((bf16[192,768]{1,0:T(8,128)(2,1)S(1)}, bf16[192,768]{1,0:T(8,128)(2,1)S(1)}, u32[]{:S(2)}, u32[]{:S(2)}) %collective-permute-start.16) | collective-permute-done | bytes 294944 | tf_op jit(solution)/shard_map/ppermute | solution.py:22
  55.9 5.9 %collective-permute-done.18.refs_3_ = bf16[192,768]{1,0:T(8,128)(2,1)S(1)} collective-permute-done((bf16[192,768]{1,0:T(8,128)(2,1)S(1)}, bf16[192,768]{1,0:T(8,128)(2,1)S(1)}, u32[]{:S(2)}, u32[]{:S(2)}) %collective-permute-start.18) | collective-permute-done | bytes 294944 | tf_op jit(solution)/shard_map/ppermute | solution.py:22
  69.8 7.4 %all-to-all-done = bf16[4,64,768]{2,1,0:T(8,128)(2,1)S(1)} async-done(((bf16[4,64,768]{2,1,0:T(8,128)(2,1)}), bf16[4,64,768]{2,1,0:T(8,128)(2,1)S(1)}, u32[]{:S(2)}, u32[]{:S(2)}) %all-to-all-start) | async-done | bytes 393248 | tf_op jit(solution)/shard_map/all_to_all | solution.py:41
  82.5 4.1 %all-to-all-start.1 = ((bf16[4,64,768]{2,1,0:T(8,128)(2,1)}), bf16[4,64,768]{2,1,0:T(8,128)(2,1)}, u32[]{:S(2)}, u32[]{:S(2)}) async-start(bf16[4,64,768]{2,1,0:T(8,128)(2,1)} %bitcast.165), calls=%async_computation.1 | async-start | bytes 786432 | tf_op jit(solution)/shard_map/all_to_all | solution.py:41
  110.6 3.6 all-to-all-start.3
  123.1 4.1 %all-to-all-start.4 = ((bf16[4,64,768]{2,1,0:T(8,128)(2,1)}), bf16[4,64,768]{2,1,0:T(8,128)(2,1)}, u32[]{:S(2)}, u32[]{:S(2)}) async-start(bf16[4,64,768]{2,1,0:T(8,128)(2,1)} %bitcast.22), calls=%async_computation.4 | async-start | bytes 786432 | tf_op jit(solution)/shard_map/all_to_all | solution.py:41
  128.6 5.5 %collective-permute-done.26.refs_3_ = bf16[192,768]{1,0:T(8,128)(2,1)} collective-permute-done((bf16[192,768]{1,0:T(8,128)(2,1)}, bf16[192,768]{1,0:T(8,128)(2,1)}, u32[]{:S(2)}, u32[]{:S(2)}) %collective-permute-start.26) | collective-permute-done | bytes 294944 | tf_op jit(solution)/shard_map/ppermute | solution.py:22
  140.0 11.5 %all_to_all.183 = bf16[4,64,768]{2,1,0:T(8,128)(2,1)} all-to-all(bf16[4,64,768]{2,1,0:T(8,128)(2,1)S(1)} %bitcast.173), channel_id=1, replica_groups=mesh['pipe'=2,'dp'=4,'tensor'=4] {'tensor'}, dimensions={0} | all-to-all | bytes 786432 | tf_op jit(solution)/shard_map/all_to_all | solution.py:41
  151.5 4.1 %all-to-all-start.7 = ((bf16[4,64,768]{2,1,0:T(8,128)(2,1)}), bf16[4,64,768]{2,1,0:T(8,128)(2,1)}, u32[]{:S(2)}, u32[]{:S(2)}) async-start(bf16[4,64,768]{2,1,0:T(8,128)(2,1)} %bitcast.159), calls=%async_computation.7 | async-start | bytes 786432 | tf_op jit(solution)/shard_map/all_to_all | solution.py:41
  161.7 4.1 %all-to-all-start.6 = ((bf16[4,64,768]{2,1,0:T(8,128)(2,1)}), bf16[4,64,768]{2,1,0:T(8,128)(2,1)}, u32[]{:S(2)}, u32[]{:S(2)}) async-start(bf16[4,64,768]{2,1,0:T(8,128)(2,1)} %bitcast.170), calls=%async_computation.6 | async-start | bytes 786432 | tf_op jit(solution)/shard_map/all_to_all | solution.py:41
  165.9 5.9 %all-to-all-done.6 = bf16[4,64,768]{2,1,0:T(8,128)(2,1)} async-done(((bf16[4,64,768]{2,1,0:T(8,128)(2,1)}), bf16[4,64,768]{2,1,0:T(8,128)(2,1)}, u32[]{:S(2)}, u32[]{:S(2)}) %all-to-all-start.6) | async-done | bytes 393248 | tf_op jit(solution)/shard_map/all_to_all | solution.py:41
  178.9 3.8 %all-to-all-start.9 = ((bf16[4,64,768]{2,1,0:T(8,128)(2,1)}), bf16[4,64,768]{2,1,0:T(8,128)(2,1)S(1)}, u32[]{:S(2)}, u32[]{:S(2)}) async-start(bf16[4,64,768]{2,1,0:T(8,128)(2,1)} %bitcast.171), calls=%async_computation.9 | async-start | bytes 786432 | tf_op jit(solution)/shard_map/all_to_all | solution.py:41
  189.8 11.7 %all_to_all.184 = bf16[4,64,768]{2,1,0:T(8,128)(2,1)S(1)} all-to-all(bf16[4,64,768]{2,1,0:T(8,128)(2,1)S(1)} %bitcast.172), channel_id=1, replica_groups=mesh['pipe'=2,'dp'=4,'tensor'=4] {'tensor'}, dimensions={0} | all-to-all | bytes 786432 | tf_op jit(solution)/shard_map/all_to_all | solution.py:41
  225.4 4.2 %all-to-all-start.12 = ((bf16[4,64,768]{2,1,0:T(8,128)(2,1)}), bf16[4,64,768]{2,1,0:T(8,128)(2,1)S(1)}, u32[]{:S(2)}, u32[]{:S(2)}) async-start(bf16[4,64,768]{2,1,0:T(8,128)(2,1)} %bitcast.169), calls=%async_computation.12 | async-start | bytes 786432 | tf_op jit(solution)/shard_map/all_to_all | solution.py:41
  231.3 5.4 %all-to-all-done.12 = bf16[4,64,768]{2,1,0:T(8,128)(2,1)S(1)} async-done(((bf16[4,64,768]{2,1,0:T(8,128)(2,1)}), bf16[4,64,768]{2,1,0:T(8,128)(2,1)S(1)}, u32[]{:S(2)}, u32[]{:S(2)}) %all-to-all-start.12) | async-done | bytes 393248 | tf_op jit(solution)/shard_map/all_to_all | solution.py:41
  240.7 3.6 all-to-all-start.13
  251.9 11.9 %all_to_all.185 = bf16[4,64,768]{2,1,0:T(8,128)(2,1)S(1)} all-to-all(bf16[4,64,768]{2,1,0:T(8,128)(2,1)} %bitcast.160), channel_id=1, replica_groups=mesh['pipe'=2,'dp'=4,'tensor'=4] {'tensor'}, dimensions={0} | all-to-all | bytes 786432 | tf_op jit(solution)/shard_map/all_to_all | solution.py:41
  267.3 3.6 all-to-all-start.14
  282.8 3.8 %all-to-all-start.15 = ((bf16[4,64,768]{2,1,0:T(8,128)(2,1)}), bf16[4,64,768]{2,1,0:T(8,128)(2,1)S(1)}, u32[]{:S(2)}, u32[]{:S(2)}) async-start(bf16[4,64,768]{2,1,0:T(8,128)(2,1)} %bitcast.161), calls=%async_computation.15 | async-start | bytes 786432 | tf_op jit(solution)/shard_map/all_to_all | solution.py:41
  310.5 8.6 %collective-permute-done.42.g3 = f32[1,11904]{1,0:T(1,128)S(1)} collective-permute-done((f32[1,11904]{1,0:T(1,128)S(1)}, f32[1,11904]{1,0:T(1,128)S(1)}, u32[]{:S(2)}, u32[]{:S(2)}) %collective-permute-start.42) | collective-permute-done | bytes 47648 | tf_op jit(solution)/shard_map/ppermute | solution.py:22
  334.7 16.2 %collective-permute-done.48 = bf16[192,384]{1,0:T(8,128)(2,1)S(1)} collective-permute-done((bf16[192,384]{1,0:T(8,128)(2,1)S(1)}, bf16[192,384]{1,0:T(8,128)(2,1)S(1)}, u32[]{:S(2)}, u32[]{:S(2)}) %collective-permute-start.48) | collective-permute-done | bytes 147488 | tf_op jit(solution)/shard_map/ppermute | solution.py:22
  (484 shorter events, 209.0 us)
Async XLA Ops:
  27.7 18.6 %collective-permute-start.17 = (bf16[192,768]{1,0:T(8,128)(2,1)S(1)}, bf16[192,768]{1,0:T(8,128)(2,1)S(1)}, u32[]{:S(2)}, u32[]{:S(2)}) collective-permute-start(bf16[192,768]{1,0:T(8,128)(2,1)S(1)} %slice.181.refs_0_), channel_id=1, source_target_pairs={{0,8},{4,12},{8,0},{12,4},{1,9},{5,13},{9,1},{13,5},{2,10},{6,14},... | collective-permute-start | bytes 884744 | tf_op jit(solution)/shard_map/ppermute | solution.py:22
  31.6 16.5 %collective-permute-start.15 = (f32[1,2688]{1,0:T(1,128)S(1)}, f32[1,2688]{1,0:T(1,128)S(1)}, u32[]{:S(2)}, u32[]{:S(2)}) collective-permute-start(f32[1,2688]{1,0:T(1,128)S(1)} %broadcast_in_dim.24), channel_id=1, source_target_pairs={{0,16},{16,0},{1,17},{17,1},{2,18},{18,2},{3,19},{19,3},{4,20},{20... | collective-permute-start | bytes 32264 | tf_op jit(solution)/shard_map/ppermute | solution.py:22
  46.1 16.5 %collective-permute-start.9 = (f32[1,4608]{1,0:T(1,128)}, f32[1,4608]{1,0:T(1,128)S(1)}, u32[]{:S(2)}, u32[]{:S(2)}) collective-permute-start(f32[1,4608]{1,0:T(1,128)} %get-tuple-element.147), channel_id=1, source_target_pairs={{0,16},{16,0},{1,17},{17,1},{2,18},{18,2},{3,19},{19,3},{4,20},{20... | collective-permute-start | bytes 55304 | tf_op jit(solution)/shard_map/ppermute | solution.py:22
  46.3 15.5 %collective-permute-start.18 = (bf16[192,768]{1,0:T(8,128)(2,1)S(1)}, bf16[192,768]{1,0:T(8,128)(2,1)S(1)}, u32[]{:S(2)}, u32[]{:S(2)}) collective-permute-start(bf16[192,768]{1,0:T(8,128)(2,1)S(1)} %collective-permute-done.17.refs_2_), channel_id=1, source_target_pairs={{0,4},{4,0},{8,12},{12,8},{1,5},{5,1},{9,13},{13,9},{2,6},{6,2},{1... | collective-permute-start | bytes 884744 | tf_op jit(solution)/shard_map/ppermute | solution.py:22
  49.5 27.8 %collective-permute-start.14 = (bf16[768,384]{1,0:T(8,128)(2,1)S(1)}, bf16[768,384]{1,0:T(8,128)(2,1)}, u32[]{:S(2)}, u32[]{:S(2)}) collective-permute-start(bf16[768,384]{1,0:T(8,128)(2,1)S(1)} %stack_line.4.w_own), channel_id=1, source_target_pairs={{0,16},{16,0},{1,17},{17,1},{2,18},{18,2},{3,19},{19,3},{4,20},{20... | collective-permute-start | bytes 1769480 | tf_op jit(solution)/shard_map/ppermute | solution.py:22
  62.4 44.6 %collective-permute-start.19 = (bf16[768,768]{1,0:T(8,128)(2,1)S(1)}, bf16[768,768]{1,0:T(8,128)(2,1)S(1)}, u32[]{:S(2)}, u32[]{:S(2)}) collective-permute-start(bf16[768,768]{1,0:T(8,128)(2,1)S(1)} %stack_line.5.w_own), channel_id=1, source_target_pairs={{0,16},{16,0},{1,17},{17,1},{2,18},{18,2},{3,19},{19,3},{4,20},{20... | collective-permute-start | bytes 3538952 | tf_op jit(solution)/shard_map/ppermute | solution.py:22
  88.2 14.7 %collective-permute-start.21 = (bf16[192,384]{1,0:T(8,128)(2,1)S(1)}, bf16[192,384]{1,0:T(8,128)(2,1)}, u32[]{:S(2)}, u32[]{:S(2)}) collective-permute-start(bf16[192,384]{1,0:T(8,128)(2,1)S(1)} %slice.186.refs_0_), channel_id=1, source_target_pairs={{0,8},{4,12},{8,0},{12,4},{1,9},{5,13},{9,1},{13,5},{2,10},{6,14},... | collective-permute-start | bytes 442376 | tf_op jit(solution)/shard_map/ppermute | solution.py:22
  102.9 16.9 %collective-permute-start.25 = (bf16[192,768]{1,0:T(8,128)(2,1)}, bf16[192,768]{1,0:T(8,128)(2,1)}, u32[]{:S(2)}, u32[]{:S(2)}) collective-permute-start(bf16[192,768]{1,0:T(8,128)(2,1)} %slice.190.refs_0_), channel_id=1, source_target_pairs={{0,8},{4,12},{8,0},{12,4},{1,9},{5,13},{9,1},{13,5},{2,10},{6,14},... | collective-permute-start | bytes 884744 | tf_op jit(solution)/shard_map/ppermute | solution.py:22
  117.2 19.1 %collective-permute-start.23 = (bf16[768,384]{1,0:T(8,128)(2,1)S(1)}, bf16[768,384]{1,0:T(8,128)(2,1)}, u32[]{:S(2)}, u32[]{:S(2)}) collective-permute-start(bf16[768,384]{1,0:T(8,128)(2,1)S(1)} %stack_line.6.w_own), channel_id=1, source_target_pairs={{0,16},{16,0},{1,17},{17,1},{2,18},{18,2},{3,19},{19,3},{4,20},{20... | collective-permute-start | bytes 1769480 | tf_op jit(solution)/shard_map/ppermute | solution.py:22
  119.8 14.2 %collective-permute-start.26 = (bf16[192,768]{1,0:T(8,128)(2,1)}, bf16[192,768]{1,0:T(8,128)(2,1)}, u32[]{:S(2)}, u32[]{:S(2)}) collective-permute-start(bf16[192,768]{1,0:T(8,128)(2,1)} %collective-permute-done.25.refs_2_), channel_id=1, source_target_pairs={{0,4},{4,0},{8,12},{12,8},{1,5},{5,1},{9,13},{13,9},{2,6},{6,2},{1... | collective-permute-start | bytes 884744 | tf_op jit(solution)/shard_map/ppermute | solution.py:22
  123.1 13.2 %all-to-all-start.4 = ((bf16[4,64,768]{2,1,0:T(8,128)(2,1)}), bf16[4,64,768]{2,1,0:T(8,128)(2,1)}, u32[]{:S(2)}, u32[]{:S(2)}) async-start(bf16[4,64,768]{2,1,0:T(8,128)(2,1)} %bitcast.22), calls=%async_computation.4 | async-start | bytes 786432 | tf_op jit(solution)/shard_map/all_to_all | solution.py:41
  136.2 29.6 %collective-permute-start.27 = (bf16[768,768]{1,0:T(8,128)(2,1)S(1)}, bf16[768,768]{1,0:T(8,128)(2,1)}, u32[]{:S(2)}, u32[]{:S(2)}) collective-permute-start(bf16[768,768]{1,0:T(8,128)(2,1)S(1)} %stack_line.7.w_own), channel_id=1, source_target_pairs={{0,16},{16,0},{1,17},{17,1},{2,18},{18,2},{3,19},{19,3},{4,20},{20... | collective-permute-start | bytes 3538952 | tf_op jit(solution)/shard_map/ppermute | solution.py:22
  220.7 16.1 %collective-permute-start.30 = (bf16[768,384]{1,0:T(8,128)(2,1)}, bf16[768,384]{1,0:T(8,128)(2,1)}, u32[]{:S(2)}, u32[]{:S(2)}) collective-permute-start(bf16[768,384]{1,0:T(8,128)(2,1)} %copy-done.124), channel_id=1, source_target_pairs={{0,16},{16,0},{1,17},{17,1},{2,18},{18,2},{3,19},{19,3},{4,20},{20... | collective-permute-start | bytes 1769480 | tf_op jit(solution)/shard_map/ppermute | solution.py:22
  229.6 22.2 %collective-permute-start.31 = (bf16[2,192,768]{2,1,0:T(8,128)(2,1)}, bf16[2,192,768]{2,1,0:T(8,128)(2,1)}, u32[]{:S(2)}, u32[]{:S(2)}) collective-permute-start(bf16[2,192,768]{2,1,0:T(8,128)(2,1)} %copy-done.123), channel_id=1, source_target_pairs={{0,4},{4,0},{8,12},{12,8},{1,5},{5,1},{9,13},{13,9},{2,6},{6,2},{1... | collective-permute-start | bytes 1769480 | tf_op jit(solution)/shard_map/ppermute | solution.py:22
  251.8 25.0 %collective-permute-start.32 = (bf16[768,768]{1,0:T(8,128)(2,1)}, bf16[768,768]{1,0:T(8,128)(2,1)S(1)}, u32[]{:S(2)}, u32[]{:S(2)}) collective-permute-start(bf16[768,768]{1,0:T(8,128)(2,1)} %copy-done.119), channel_id=1, source_target_pairs={{0,16},{16,0},{1,17},{17,1},{2,18},{18,2},{3,19},{19,3},{4,20},{20... | collective-permute-start | bytes 3538952 | tf_op jit(solution)/shard_map/ppermute | solution.py:22
  272.5 14.1 %collective-permute-start.28 = (bf16[64,768]{1,0:T(8,128)(2,1)}, bf16[64,768]{1,0:T(8,128)(2,1)}, u32[]{:S(2)}, u32[]{:S(2)}) collective-permute-start(bf16[64,768]{1,0:T(8,128)(2,1)} %broadcast_select_fusion.14), channel_id=1, source_target_pairs={{0,16},{16,0},{1,17},{17,1},{2,18},{18,2},{3,19},{19,3},{4,20},{20... | collective-permute-start | bytes 294920 | tf_op jit(solution)/shard_map/ppermute | solution.py:22
  272.5 21.8 %collective-permute-start.34 = (bf16[2,192,384]{2,1,0:T(8,128)(2,1)}, bf16[2,192,384]{2,1,0:T(8,128)(2,1)}, u32[]{:S(2)}, u32[]{:S(2)}) collective-permute-start(bf16[2,192,384]{2,1,0:T(8,128)(2,1)} %copy-done.125), channel_id=1, source_target_pairs={{0,4},{4,0},{8,12},{12,8},{1,5},{5,1},{9,13},{13,9},{2,6},{6,2},{1... | collective-permute-start | bytes 884744 | tf_op jit(solution)/shard_map/ppermute | solution.py:22
  276.2 18.2 %collective-permute-start.33 = (bf16[192,768]{1,0:T(8,128)(2,1)}, bf16[192,768]{1,0:T(8,128)(2,1)}, u32[]{:S(2)}, u32[]{:S(2)}) collective-permute-start(bf16[192,768]{1,0:T(8,128)(2,1)} %fusion.3), channel_id=1, source_target_pairs={{0,8},{4,12},{8,0},{12,4},{1,9},{5,13},{9,1},{13,5},{2,10},{6,14},... | collective-permute-start | bytes 884744 | tf_op jit(solution)/shard_map/ppermute | solution.py:22
  298.5 23.0 %collective-permute-start.46 = (bf16[768,384]{1,0:T(8,128)(2,1)S(1)}, bf16[768,384]{1,0:T(8,128)(2,1)S(1)}, u32[]{:S(2)}, u32[]{:S(2)}) collective-permute-start(bf16[768,384]{1,0:T(8,128)(2,1)S(1)} %copy-done.122), channel_id=1, source_target_pairs={{0,16},{16,0},{1,17},{17,1},{2,18},{18,2},{3,19},{19,3},{4,20},{20... | collective-permute-start | bytes 1769480 | tf_op jit(solution)/shard_map/ppermute | solution.py:22
  299.8 28.7 %collective-permute-start.51 = (bf16[2,192,768]{2,1,0:T(8,128)(2,1)}, bf16[2,192,768]{2,1,0:T(8,128)(2,1)}, u32[]{:S(2)}, u32[]{:S(2)}) collective-permute-start(bf16[2,192,768]{2,1,0:T(8,128)(2,1)} %get-tuple-element.267), channel_id=1, source_target_pairs={{0,4},{4,0},{8,12},{12,8},{1,5},{5,1},{9,13},{13,9},{2,6},{6,2},{1... | collective-permute-start | bytes 1769480 | tf_op jit(solution)/shard_map/ppermute | solution.py:22
  305.3 13.7 %collective-permute-start.42 = (f32[1,11904]{1,0:T(1,128)S(1)}, f32[1,11904]{1,0:T(1,128)S(1)}, u32[]{:S(2)}, u32[]{:S(2)}) collective-permute-start(f32[1,11904]{1,0:T(1,128)S(1)} %grads_join.1.g0), channel_id=1, source_target_pairs={{0,12},{4,8},{8,4},{12,0},{1,13},{5,9},{9,5},{13,1},{2,14},{6,10},... | collective-permute-start | bytes 142856 | tf_op jit(solution)/shard_map/ppermute | solution.py:22
  319.1 15.6 %collective-permute-start.49 = (bf16[192,384]{1,0:T(8,128)(2,1)}, bf16[192,384]{1,0:T(8,128)(2,1)S(1)}, u32[]{:S(2)}, u32[]{:S(2)}) collective-permute-start(bf16[192,384]{1,0:T(8,128)(2,1)} %fusion.6), channel_id=1, source_target_pairs={{0,8},{4,12},{8,0},{12,4},{1,9},{5,13},{9,1},{13,5},{2,10},{6,14},... | collective-permute-start | bytes 442376 | tf_op jit(solution)/shard_map/ppermute | solution.py:22
  331.0 21.0 %collective-permute-start.52 = (bf16[192,768]{1,0:T(8,128)(2,1)S(1)}, bf16[192,768]{1,0:T(8,128)(2,1)S(1)}, u32[]{:S(2)}, u32[]{:S(2)}) collective-permute-start(bf16[192,768]{1,0:T(8,128)(2,1)S(1)} %fusion.1), channel_id=1, source_target_pairs={{0,8},{4,12},{8,0},{12,4},{1,9},{5,13},{9,1},{13,5},{2,10},{6,14},... | collective-permute-start | bytes 884744 | tf_op jit(solution)/shard_map/ppermute | solution.py:22
  333.5 17.4 %collective-permute-start.48 = (bf16[192,384]{1,0:T(8,128)(2,1)S(1)}, bf16[192,384]{1,0:T(8,128)(2,1)S(1)}, u32[]{:S(2)}, u32[]{:S(2)}) collective-permute-start(bf16[192,384]{1,0:T(8,128)(2,1)S(1)} %fusion.8), channel_id=1, source_target_pairs={{0,8},{4,12},{8,0},{12,4},{1,9},{5,13},{9,1},{13,5},{2,10},{6,14},... | collective-permute-start | bytes 442376 | tf_op jit(solution)/shard_map/ppermute | solution.py:22
  (183 other events, 1357.5 us)

commit v4 on v2

--- a/solution.py
+++ b/solution.py
@@ -23,7 +23,8 @@
 
 
 def exchange(parts, axis):
-    return [parts[0]] + [swap(parts[k], axis, k) for k in range(1, len(parts))]
+    received = {k: swap(parts[k], axis, k) for k in range(len(parts) - 1, 0, -1)}
+    return [parts[0]] + [received[k] for k in range(1, len(parts))]
 
 
 def gather(value, axis):
@@ -379,6 +380,33 @@
     near[1] = block(3).astype(BF16)
     far[...] = block(2)
     own[...] = block(0)
+
+
+def line_total_body(place, own0, near0, far0, own1, near1, far1, mine, give):
+    first = place[0] == 0
+    total0 = own0[...] + near0[0].astype(F32) + far0[...].astype(F32)
+    total1 = own1[...] + near1[0].astype(F32) + far1[...].astype(F32)
+    mine[...] = jnp.where(first, total0, total1)
+    give[...] = jnp.where(first, total1, total0)
+
+
+def final_mlp_body(place, mine, received, expand_out, shrink_out):
+    first = place[0] == 0
+    half = mine.shape[1] // 2
+    own, other = mine[...], received[...]
+    for index, values in enumerate((jnp.where(first, own, other), jnp.where(first, other, own))):
+        expand_out[:, index * half : (index + 1) * half] = values[:, :half]
+        shrink_out[index * half : (index + 1) * half] = values[:, half:].T
+
+
+def final_attn_body(place, mine, received, joint_out, out_out):
+    first = place[0] == 0
+    width = mine.shape[1] // 2
+    own, other = mine[...], received[...]
+    front, back = jnp.where(first, own, other), jnp.where(first, other, own)
+    joint_out[:, : 2 * width] = front
+    joint_out[:, 2 * width :] = back[:, :width]
+    out_out[...] = back[:, width:].T
 
 
 def mod_first_body(a0, a1, a2, a3, weight, out):
@@ -511,6 +539,9 @@
     def after(value, earlier):
         return lax.optimization_barrier((value, earlier))[0]
 
+    def tie(*values):
+        return lax.optimization_barrier(values)
+
     attn_pack = jnp.concatenate(
         [joint_weight[0].reshape(chunk, 3 * width), output_weight[0].T], axis=1
     )
@@ -552,36 +583,31 @@
         at += hidden
         biases.append((joint, packed[:, at : at + model], grown, packed[:, at + model :]))
 
-    def along_line(value, earlier):
-        if earlier is not None:
-            value = after(value, earlier)
+    activated = jax.nn.silu(conditions[:, 0].astype(F32)).astype(BF16)
+    if direct:
+        activated_all = gather(activated, "dp")
+    else:
+        activated_all = lax.all_gather(activated, "dp", axis=0).reshape(line_size * micro, -1)
+
+    def along_line(value):
         if direct:
-            near = swap(value, "dp", 1)
-            far = swap(value, "dp", 2)
-            farther = swap(far, "dp", 1)
             lined = run(
                 "stack_line",
                 stack_body,
                 [shape((model, value.shape[1]), BF16)],
-                [value, near, far, farther],
+                gather(value, "dp"),
                 place,
             )[0]
-            mark = far
         else:
             lined = lax.all_gather(value, "dp", axis=0, tiled=True)
-            mark = lined
-        return (lined, swap(lined, "pipe", 1)), mark
-
-    weights = []
-    mark = None
-    for layer in range(2):
-        attn, mark = along_line(halves_of_layers[layer][:, :split], mark)
-        mlp, mark = along_line(halves_of_layers[layer][:, split:], mark)
-        weights.append((attn, mlp))
-
-    activated = jax.nn.silu(conditions[:, 0].astype(F32)).astype(BF16)
+        return lined, swap(lined, "pipe", 1)
+
+    def half_of(layer, mlp):
+        return halves_of_layers[layer][:, split:] if mlp else halves_of_layers[layer][:, :split]
+
+    w_attn0 = along_line(after(half_of(0, False), activated_all))
+
     if direct:
-        activated_all = gather(activated, "dp")
         mod_partial = run(
             "mod_first",
             mod_first_body,
@@ -604,7 +630,6 @@
             name="mod_join",
         )(place, *exchange(pieces, "dp"), modulation_bias)
     else:
-        activated_all = lax.all_gather(activated, "dp", axis=0).reshape(line_size * micro, -1)
         mod_partial = dot(activated_all, own_rows)
         mod_sum = tree_sum(gather(mod_partial, "tensor")).reshape(line_size, micro, -1)
         mod_layer = lax.all_to_all(mod_sum, "dp", split_axis=0, concat_axis=0)
@@ -612,10 +637,14 @@
         mod_mine, mod_other = mine(mod_layer)[None], other(mod_layer)[None]
     mod0, mod1 = both_layers(mod_mine, swap(mod_other, "pipe", 1))
 
+    w_mlp0 = along_line(after(half_of(0, True), (mod0, w_attn0[0])))
     own_f32 = shape((own, model), F32)
     own_bf16 = shape((own, model), BF16)
     blocks = [own_bf16] * count
+    wide_bf16 = shape((rows, model), BF16)
+    hidden_bf16 = shape((rows, hidden), BF16)
     vector = shape((1, model), F32)
+    hidden_vector = shape((1, hidden), F32)
     h0, attn_in, g_y1, g_shrunk1 = run(
         "enter",
         enter_body,
@@ -624,186 +653,223 @@
         place,
     )
 
-    def attention(attn_in, weight, bias):
-        outs = run(
+    def kernel(name, body, outs, args, where=None):
+        return run(name, functools.partial(body, count), outs, args, where)
+
+    def attention(attn_rows, weight, bias):
+        outs = kernel(
             "attention",
-            functools.partial(attn_body, count),
+            attn_body,
             [
-                shape((rows, model), BF16),
+                wide_bf16,
                 shape((rows, 3 * width), BF16),
                 shape((width // HEAD, rows, rows), F32),
                 shape((rows, width), BF16),
             ]
             + blocks,
-            gather(attn_in, "tensor") + [weight[0], weight[1], bias],
+            attn_rows + [weight[0], weight[1], bias],
             place,
         )
         return outs[:4], exchange(outs[4:], "tensor")
 
     def middle_of(parts, bias, h, mod):
-        return run(
-            "middle",
-            functools.partial(middle_body, count),
-            [own_f32, own_f32, own_bf16],
-            parts + [bias, h, mod],
-        )
-
-    kept_attn0, parts = attention(attn_in, weights[0][0], biases[0][0])
+        return kernel(
+            "middle", middle_body, [own_f32, own_f32, own_bf16], parts + [bias, h, mod]
+        )
+
+    kept_attn0, parts = attention(gather(attn_in, "tensor"), w_attn0, biases[0][0])
     attended0, middle0, mlp_in = middle_of(parts, biases[0][1], h0, mod0)
-    outs = run(
+    mlp_rows0, half = tie(gather(mlp_in, "tensor"), half_of(1, False))
+    w_attn1 = along_line(half)
+    outs = kernel(
         "feed_forward",
-        functools.partial(mlp_body, count),
-        [shape((rows, model), BF16), shape((rows, hidden), F32), shape((rows, hidden), BF16)] + blocks,
-        gather(mlp_in, "tensor") + [weights[0][1][0], weights[0][1][1], biases[0][2]],
+        mlp_body,
+        [wide_bf16, shape((rows, hidden), F32), hidden_bf16] + blocks,
+        mlp_rows0 + [w_mlp0[0], w_mlp0[1], biases[0][2]],
     )
     mlp_rows0, pre0, hidden0 = outs[:3]
-    shrunk0, passed, h1, attn_in = run(
+    parts, half = tie(exchange(outs[3:], "tensor"), half_of(1, True))
+    w_mlp1 = along_line(half)
+    shrunk0, passed, h1, attn_in = kernel(
         "between",
-        functools.partial(between_body, count),
+        between_body,
         [own_f32, own_bf16, own_f32, own_bf16],
-        exchange(outs[3:], "tensor") + [biases[0][3], middle0, mod0, mod1],
-    )
-
-    g_shrunk_rows = gather(g_shrunk1, "tensor")
-    kept_attn1, parts = attention(attn_in, weights[1][0], biases[1][0])
+        parts + [biases[0][3], middle0, mod0, mod1],
+    )
+
+    g_rows1 = gather(g_shrunk1, "tensor")
+    kept_attn1, parts = attention(gather(attn_in, "tensor"), w_attn1, biases[1][0])
     attended1, middle1, mlp_in = middle_of(parts, biases[1][1], h1, mod1)
-    outs = run(
+    outs = kernel(
         "feed_forward_both",
-        functools.partial(mlp_both_body, count),
-        [
-            shape((rows, model), BF16),
-            shape((rows, model), BF16),
-            shape((rows, hidden), BF16),
-            shape((rows, hidden), BF16),
-            shape((1, hidden), F32),
-        ]
-        + blocks
-        + blocks,
-        gather(mlp_in, "tensor")
-        + g_shrunk_rows
-        + [weights[1][1][0], weights[1][1][1], biases[1][2]],
+        mlp_both_body,
+        [wide_bf16, wide_bf16, hidden_bf16, hidden_bf16, hidden_vector] + blocks + blocks,
+        gather(mlp_in, "tensor") + g_rows1 + [w_mlp1[0], w_mlp1[1], biases[1][2]],
     )
     mlp_rows1, g_rows1, hidden1, g_pre1, expand_grad1 = outs[:5]
-    y_parts, g_parts = outs[5 : 5 + count], outs[5 + count :]
+    y_partial, g_partial = outs[5 : 5 + count], outs[5 + count :]
 
     def middle_back(parts, middle, mod, g_y, attended):
-        return run(
+        return kernel(
             "middle_back",
-            functools.partial(middle_back_body, count),
+            middle_back_body,
             [own_f32, own_bf16] + [vector] * 4,
             parts + [middle, mod, g_y, attended],
         )
 
-    def attention_back(g_attended, weight, kept):
-        outs = run(
+    def attention_back(g_rows, weight, kept):
+        outs = kernel(
             "attention_back",
-            functools.partial(attn_back_body, count),
-            [
-                shape((rows, model), BF16),
-                shape((rows, 3 * width), BF16),
-                shape((1, 2 * width), F32),
-            ]
-            + blocks,
-            gather(g_attended, "tensor") + [weight[0], weight[1], kept[1], kept[2]],
+            attn_back_body,
+            [wide_bf16, shape((rows, 3 * width), BF16), shape((1, 2 * width), F32)] + blocks,
+            g_rows + [weight[0], weight[1], kept[1], kept[2]],
             place,
         )
         return outs[:3], exchange(outs[3:], "tensor")
 
-    def reduce_line(keep, give):
+    def line_parts(grads):
+        keep, give = grads
         received = swap(give, "pipe", 1)
         if not direct:
-            whole = (keep + received.astype(F32)).astype(BF16)
-            return lax.psum_scatter(whole, "dp", scatter_dimension=0, tiled=True).astype(F32)
+            return None, (keep + received.astype(F32)).astype(BF16), None
         wide = keep.shape[1]
-        near, far, own_part = run(
+        return run(
             "line_parts",
             line_parts_body,
-            [
-                shape((2, chunk, wide), BF16),
-                shape((chunk, wide), F32),
-                shape((chunk, wide), F32),
-            ],
+            [shape((2, chunk, wide), BF16), shape((chunk, wide), F32), shape((chunk, wide), F32)],
             [keep, received],
             place,
         )
-        near = swap(near, "dp", 1)
-        far = swap((far + near[1].astype(F32)).astype(BF16), "dp", 2)
-        return own_part + near[0].astype(F32) + far.astype(F32)
 
     def mlp_weight_grads(mlp_rows, g_pre, g_rows, hidden_rows):
-        keep, give = run(
-            "mlp_weight_grads",
-            mlp_weights_body,
-            [shape((model, hidden), F32), shape((model, hidden), BF16)],
-            [mlp_rows, g_pre, g_rows, hidden_rows],
-        )
-        return reduce_line(keep, give)
-
-    def attn_weight_grads(attn_rows, g_joint, g_rows, mixed):
-        keep, give = run(
-            "attn_weight_grads",
-            attn_weights_body,
-            [shape((model, 2 * width), F32), shape((model, 2 * width), BF16)],
-            [attn_rows, g_joint, g_rows, mixed],
-            place,
-        )
-        return reduce_line(keep, give)
-
+        return line_parts(
+            run(
+                "mlp_weight_grads",
+                mlp_weights_body,
+                [shape((model, hidden), F32), shape((model, hidden), BF16)],
+                [mlp_rows, g_pre, g_rows, hidden_rows],
+            )
+        )
+
+    def attn_weight_grads(kept, g_joint, g_rows):
+        return line_parts(
+            run(
+                "attn_weight_grads",
+                attn_weights_body,
+                [shape((model, 2 * width), F32), shape((model, 2 * width), BF16)],
+                [kept[0], g_joint, g_rows, kept[3]],
+                place,
+            )
+        )
+
+    def line_near(parts):
+        return swap(parts[0], "dp", 1) if direct else parts[1]
+
+    def line_far(parts, near):
+        if not direct:
+            return near
+        return swap((parts[1] + near[1].astype(F32)).astype(BF16), "dp", 2)
+
+    def line_total(first_layer, second_layer):
+        if not direct:
+            sums = [
+                lax.psum_scatter(far, "dp", scatter_dimension=0, tiled=True).astype(F32)
+                for _, _, far in (first_layer, second_layer)
+            ]
+            return mine(sums), swap(other(sums), "pipe", 1)
+        args = [x for parts, near, far in (first_layer, second_layer) for x in (parts[2], near, far)]
+        kept, given = run(
+            "line_total", line_total_body, [shape(args[0].shape, F32)] * 2, args, place
+        )
+        return kept, swap(given, "pipe", 1)
+
+    g_parts, y_partial, parts_m1 = tie(
+        exchange(g_partial, "tensor"),
+        y_partial,
+        mlp_weight_grads(mlp_rows1, g_pre1, g_rows1, hidden1),
+    )
     g_middle1, g_attended, g_shift_mlp1, g_scale_mlp1, g_gate_attn1, out_grad1 = middle_back(
-        exchange(g_parts, "tensor"), middle1, mod1, g_y1, attended1
-    )
-    mlp_grad1 = mlp_weight_grads(mlp_rows1, g_pre1, g_rows1, hidden1)
-    y1, g_gate_mlp1, shrink_grad1 = run(
-        "leave",
-        functools.partial(leave_body, count),
-        [own_bf16, vector, vector],
-        exchange(y_parts, "tensor") + [biases[1][3], middle1, mod1, g_y1, g_shrunk1],
-    )
-    (g_rows, g_joint, joint_grad1), parts = attention_back(g_attended, weights[1][0], kept_attn1)
-    g_passed, g_y0, g_shrunk0, g_shift_attn1, g_scale_attn1, g_gate_mlp0, shrink_grad0 = run(
+        g_parts, middle1, mod1, g_y1, attended1
+    )
+    near_m1 = line_near(parts_m1)
+    y_parts = exchange(y_partial, "tensor")
+    (g_rows, g_joint, joint_grad1), parts = attention_back(
+        gather(g_attended, "tensor"), w_attn1, kept_attn1
+    )
+    parts, near_m1, parts_a1 = tie(
+        parts, near_m1, attn_weight_grads(kept_attn1, g_joint, g_rows)
+    )
+    g_passed, g_y0, g_shrunk0, g_shift_attn1, g_scale_attn1, g_gate_mlp0, shrink_grad0 = kernel(
         "between_back",
-        functools.partial(between_back_body, count),
+        between_back_body,
         [own_bf16, own_f32, own_bf16] + [vector] * 4,
         parts + [h1, mod1, mod0, g_middle1, shrunk0],
     )
-    attn_grad1 = attn_weight_grads(kept_attn1[0], g_joint, g_rows, kept_attn1[3])
-
-    outs = run(
+    far_m1 = line_far(parts_m1, near_m1)
+    near_a1 = line_near(parts_a1)
+
+    outs = kernel(
         "feed_forward_back",
-        functools.partial(mlp_back_body, count),
-        [shape((rows, model), BF16), shape((rows, hidden), BF16), shape((1, hidden), F32)] + blocks,
-        gather(g_shrunk0, "tensor") + [weights[0][1][0], weights[0][1][1], pre0],
+        mlp_back_body,
+        [wide_bf16, hidden_bf16, hidden_vector] + blocks,
+        gather(g_shrunk0, "tensor") + [w_mlp0[0], w_mlp0[1], pre0],
     )
     g_rows0, g_pre0, expand_grad0 = outs[:3]
+    parts, far_m1, near_a1, parts_m0 = tie(
+        exchange(outs[3:], "tensor"),
+        far_m1,
+        near_a1,
+        mlp_weight_grads(mlp_rows0, g_pre0, g_rows0, hidden0),
+    )
     g_middle0, g_attended, g_shift_mlp0, g_scale_mlp0, g_gate_attn0, out_grad0 = middle_back(
-        exchange(outs[3:], "tensor"), middle0, mod0, g_y0, attended0
-    )
-    mlp_grad0 = mlp_weight_grads(mlp_rows0, g_pre0, g_rows0, hidden0)
-    (g_rows, g_joint, joint_grad0), parts = attention_back(g_attended, weights[0][0], kept_attn0)
-    g_h0, g_shift_attn0, g_scale_attn0 = run(
+        parts, middle0, mod0, g_y0, attended0
+    )
+    near_m0 = line_near(parts_m0)
+    far_a1 = line_far(parts_a1, near_a1)
+    y1, g_gate_mlp1, shrink_grad1 = kernel(
+        "leave",
+        leave_body,
+        [own_bf16, vector, vector],
+        y_parts + [biases[1][3], middle1, mod1, g_y1, g_shrunk1],
+    )
+    (g_rows, g_joint, joint_grad0), parts = attention_back(
+        gather(g_attended, "tensor"), w_attn0, kept_attn0
+    )
+    parts, far_a1, near_m0, parts_a0 = tie(
+        parts, far_a1, near_m0, attn_weight_grads(kept_attn0, g_joint, g_rows)
+    )
+    g_h0, g_shift_attn0, g_scale_attn0 = kernel(
         "finish_back",
-        functools.partial(finish_back_body, count),
+        finish_back_body,
         [own_bf16, vector, vector],
         parts + [h0, mod0, g_middle0],
     )
-    attn_grad0 = attn_weight_grads(kept_attn0[0], g_joint, g_rows, kept_attn0[3])
+    far_m0 = line_far(parts_m0, near_m0)
+    near_a0 = line_near(parts_a0)
+    far_a0 = line_far(parts_a0, near_a0)
+    mlp_halves = line_total((parts_m0, near_m0, far_m0), (parts_m1, near_m1, far_m1))
+    attn_halves = line_total((parts_a0, near_a0, far_a0), (parts_a1, near_a1, far_a1))
+    expand_w_grad, shrink_w_grad = run(
+        "final_mlp",
+        final_mlp_body,
+        [shape((chunk, hidden), F32), shape((hidden, chunk), F32)],
+        mlp_halves,
+        place,
+    )
+    joint_w_grad, output_w_grad = run(
+        "final_attn",
+        final_attn_body,
+        [shape((chunk, 3 * width), F32), shape((width, chunk), F32)],
+        attn_halves,
+        place,
+    )
+    joint_w_grad = joint_w_grad.reshape(chunk, 3, width)
 
     def own_layer_of_micros(pair):
         return jnp.stack(both_layers(mine(pair), swap(other(pair), "pipe", 1)))
 
     layer_outputs = own_layer_of_micros((passed, y1))
     input_grads = own_layer_of_micros((g_h0, g_passed))
-
-    def own_columns(pair):
-        return both_layers(mine(pair), swap(other(pair), "pipe", 1))
-
-    mlp_halves = own_columns((mlp_grad0, mlp_grad1))
-    half = hidden // 2
-    expand_w_grad = jnp.concatenate([part[:, :half] for part in mlp_halves], axis=1)
-    shrink_w_grad = jnp.concatenate([part[:, half:] for part in mlp_halves], axis=1).T
-    front, back = own_columns((attn_grad0, attn_grad1))
-    joint_w_grad = jnp.concatenate([front, back[:, :width]], axis=1).reshape(chunk, 3, width)
-    output_w_grad = back[:, width:].T
 
     packed = run(
         "pack_grads",

time: 336 us -> 329 us (0.979)
  other arithmetic: 14.8 us -> 2.86 us
  starting transfers between devices: 105 us -> 109 us
    ppermute x102, starting transfers between devices: 105 us -> 109 us  [swap(): return lax.ppermute(value, axis, pairs)]
    unnamed x71 -> x37, local copies, waits for them, and re-layouts: 7.41 us -> 6.15 us
    pallas_call x34 -> x38, Pallas kernels: 33.8 us -> 34.5 us  [run(): pl.pallas_call(body, out_shape=outs, in_specs=specs, out_specs=[pl.BlockS...]
  transfers between devices with their start and end apart: 102 -> 102, of which waited for: 60 -> 59; matrix products, arithmetic and copies ran while one was open for 5% -> 2% of each run, Pallas kernels for 8% -> 5%
where the time goes in v4:
time: 329 us
  waiting for transfers between devices  171 us (52%)
  starting transfers between devices  109 us (33%)
  Pallas kernels  36 us (11%)
  local copies, waits for them, and re-layouts  8.23 us (3%)
    ppermute x102, waiting for transfers between devices, swap(): return lax.ppermute(value, axis, pairs)  171 us
    ppermute x102, starting transfers between devices, swap(): return lax.ppermute(value, axis, pairs)  109 us
    pallas_call x38, Pallas kernels, run(): pl.pallas_call(body, out_shape=outs, in_specs=specs, out_specs=[pl.BlockS...  34.5 us
  transfers between devices with their start and end apart: 102, of which 59 were waited for; matrix products, arithmetic and copies ran while one was open for 2% of the time, Pallas kernels for 5%

profile of v4, /device:TPU:0, one launch (start us, length us, event | category | flops | bytes accessed | tf_op | source)
XLA Modules:
  0.0 328.9 jit_solution(10676764437288475345)
XLA Ops:
  3.9 5.0 %collective-permute-start.2 = (bf16[2,192]{1,0:T(2,128)(2,1)S(1)}, bf16[2,192]{1,0:T(2,128)(2,1)S(1)}, u32[]{:S(2)}, u32[]{:S(2)}) collective-permute-start(bf16[2,192]{1,0:T(2,128)(2,1)S(1)} %fusion.12.a0), channel_id=1, source_target_pairs={{0,12},{4,8},{8,4},{12,0},{1,13},{5,9},{9,5},{13,1},{2,14},{6,10},... | collective-permute-start | bytes 2312 | tf_op jit(solution)/shard_map/ppermute | solution.py:22
  10.5 2.9 collective-permute-done.1.a2
  35.7 4.1 %collective-permute-done.16.refs_3_ = bf16[192,384]{1,0:T(8,128)(2,1)S(1)} collective-permute-done((bf16[192,384]{1,0:T(8,128)(2,1)S(1)}, bf16[192,384]{1,0:T(8,128)(2,1)S(1)}, u32[]{:S(2)}, u32[]{:S(2)}) %collective-permute-start.16) | collective-permute-done | bytes 147488 | tf_op jit(solution)/shard_map/ppermute | solution.py:22
  39.8 6.8 %collective-permute-done.15.refs_2_ = bf16[192,384]{1,0:T(8,128)(2,1)S(1)} collective-permute-done((bf16[192,384]{1,0:T(8,128)(2,1)S(1)}, bf16[192,384]{1,0:T(8,128)(2,1)S(1)}, u32[]{:S(2)}, u32[]{:S(2)}) %collective-permute-start.15) | collective-permute-done | bytes 147488 | tf_op jit(solution)/shard_map/ppermute | solution.py:22
  48.7 3.0 collective-permute-start.25
  52.5 6.5 %collective-permute-done.27.refs_3_ = bf16[192,768]{1,0:T(8,128)(2,1)S(1)} collective-permute-done((bf16[192,768]{1,0:T(8,128)(2,1)S(1)}, bf16[192,768]{1,0:T(8,128)(2,1)S(1)}, u32[]{:S(2)}, u32[]{:S(2)}) %collective-permute-start.27) | collective-permute-done | bytes 294944 | tf_op jit(solution)/shard_map/ppermute | solution.py:22
  59.1 14.8 %collective-permute-done.26.refs_2_ = bf16[192,768]{1,0:T(8,128)(2,1)S(1)} collective-permute-done((bf16[192,768]{1,0:T(8,128)(2,1)S(1)}, bf16[192,768]{1,0:T(8,128)(2,1)S(1)}, u32[]{:S(2)}, u32[]{:S(2)}) %collective-permute-start.26) | collective-permute-done | bytes 294944 | tf_op jit(solution)/shard_map/ppermute | solution.py:22
  79.1 3.0 collective-permute-done.12.refs_3_
  111.4 2.9 collective-permute-start.48
  114.3 7.4 %collective-permute-done.50.refs_3_ = bf16[192,768]{1,0:T(8,128)(2,1)S(1)} collective-permute-done((bf16[192,768]{1,0:T(8,128)(2,1)S(1)}, bf16[192,768]{1,0:T(8,128)(2,1)S(1)}, u32[]{:S(2)}, u32[]{:S(2)}) %collective-permute-start.50) | collective-permute-done | bytes 294944 | tf_op jit(solution)/shard_map/ppermute | solution.py:22
  121.6 10.8 %collective-permute-done.49.refs_2_ = bf16[192,768]{1,0:T(8,128)(2,1)S(1)} collective-permute-done((bf16[192,768]{1,0:T(8,128)(2,1)S(1)}, bf16[192,768]{1,0:T(8,128)(2,1)S(1)}, u32[]{:S(2)}, u32[]{:S(2)}) %collective-permute-start.49) | collective-permute-done | bytes 294944 | tf_op jit(solution)/shard_map/ppermute | solution.py:22
  135.0 2.6 collective-permute-start.35
  137.6 4.2 %collective-permute-done.37.refs_3_ = bf16[192,384]{1,0:T(8,128)(2,1)S(1)} collective-permute-done((bf16[192,384]{1,0:T(8,128)(2,1)S(1)}, bf16[192,384]{1,0:T(8,128)(2,1)S(1)}, u32[]{:S(2)}, u32[]{:S(2)}) %collective-permute-start.37) | collective-permute-done | bytes 147488 | tf_op jit(solution)/shard_map/ppermute | solution.py:22
  141.8 5.8 %collective-permute-done.36.refs_2_ = bf16[192,384]{1,0:T(8,128)(2,1)S(1)} collective-permute-done((bf16[192,384]{1,0:T(8,128)(2,1)S(1)}, bf16[192,384]{1,0:T(8,128)(2,1)S(1)}, u32[]{:S(2)}, u32[]{:S(2)}) %collective-permute-start.36) | collective-permute-done | bytes 147488 | tf_op jit(solution)/shard_map/ppermute | solution.py:22
  152.1 3.0 collective-permute-done.34.refs_3_
  165.2 6.0 %collective-permute-done.40.refs_2_ = bf16[64,768]{1,0:T(8,128)(2,1)S(1)} collective-permute-done((bf16[64,768]{1,0:T(8,128)(2,1)S(1)}, bf16[64,768]{1,0:T(8,128)(2,1)S(1)}, u32[]{:S(2)}, u32[]{:S(2)}) %collective-permute-start.40) | collective-permute-done | bytes 98336 | tf_op jit(solution)/shard_map/ppermute | solution.py:22
  210.4 8.0 %collective-permute-done.66.near1 = bf16[2,192,768]{2,1,0:T(8,128)(2,1)S(1)} collective-permute-done((bf16[2,192,768]{2,1,0:T(8,128)(2,1)S(1)}, bf16[2,192,768]{2,1,0:T(8,128)(2,1)S(1)}, u32[]{:S(2)}, u32[]{:S(2)}) %collective-permute-start.66) | collective-permute-done | bytes 589856 | tf_op jit(solution)/shard_map/ppermute | solution.py:22
  222.3 3.0 collective-permute-done.70.refs_3_
  233.1 2.7 collective-permute-done.71.refs_1_
  249.7 2.8 collective-permute-done.79.refs_3_
  264.4 9.3 %collective-permute-done.83.far1 = bf16[192,384]{1,0:T(8,128)(2,1)S(1)} collective-permute-done((bf16[192,384]{1,0:T(8,128)(2,1)S(1)}, bf16[192,384]{1,0:T(8,128)(2,1)S(1)}, u32[]{:S(2)}, u32[]{:S(2)}) %collective-permute-start.83) | collective-permute-done | bytes 147488 | tf_op jit(solution)/shard_map/ppermute | solution.py:22
  290.9 7.1 %collective-permute-done.93.g3 = f32[1,11904]{1,0:T(1,128)S(1)} collective-permute-done((f32[1,11904]{1,0:T(1,128)S(1)}, f32[1,11904]{1,0:T(1,128)S(1)}, u32[]{:S(2)}, u32[]{:S(2)}) %collective-permute-start.93) | collective-permute-done | bytes 47648 | tf_op jit(solution)/shard_map/ppermute | solution.py:22
  298.0 6.7 %collective-permute-done.92.g2 = f32[1,11904]{1,0:T(1,128)S(1)} collective-permute-done((f32[1,11904]{1,0:T(1,128)S(1)}, f32[1,11904]{1,0:T(1,128)S(1)}, u32[]{:S(2)}, u32[]{:S(2)}) %collective-permute-start.92) | collective-permute-done | bytes 47648 | tf_op jit(solution)/shard_map/ppermute | solution.py:22
  312.5 8.7 %collective-permute-done.98.far0 = bf16[192,384]{1,0:T(8,128)(2,1)S(1)} collective-permute-done((bf16[192,384]{1,0:T(8,128)(2,1)S(1)}, bf16[192,384]{1,0:T(8,128)(2,1)S(1)}, u32[]{:S(2)}, u32[]{:S(2)}) %collective-permute-start.98) | collective-permute-done | bytes 147488 | tf_op jit(solution)/shard_map/ppermute | solution.py:22
  (297 shorter events, 190.4 us)
Async XLA Ops:
  3.4 27.4 %collective-permute-start.13 = (bf16[192,1152]{1,0:T(8,128)(2,1)S(1)}, bf16[192,1152]{1,0:T(8,128)(2,1)S(1)}, u32[]{:S(2)}, u32[]{:S(2)}) collective-permute-start(bf16[192,1152]{1,0:T(8,128)(2,1)S(1)} %broadcast_select_fusion.2), channel_id=1, source_target_pairs={{0,16},{16,0},{1,17},{17,1},{2,18},{18,2},{3,19},{19,3},{4,20},{20... | collective-permute-start | bytes 1327112 | tf_op jit(solution)/shard_map/ppermute | solution.py:22
  48.6 25.3 %collective-permute-start.26 = (bf16[192,768]{1,0:T(8,128)(2,1)S(1)}, bf16[192,768]{1,0:T(8,128)(2,1)S(1)}, u32[]{:S(2)}, u32[]{:S(2)}) collective-permute-start(bf16[192,768]{1,0:T(8,128)(2,1)S(1)} %slice.142.refs_0_), channel_id=1, source_target_pairs={{0,8},{4,12},{8,0},{12,4},{1,9},{5,13},{9,1},{13,5},{2,10},{6,14},... | collective-permute-start | bytes 884744 | tf_op jit(solution)/shard_map/ppermute | solution.py:22
  48.7 25.3 %collective-permute-start.25 = (bf16[192,768]{1,0:T(8,128)(2,1)S(1)}, bf16[192,768]{1,0:T(8,128)(2,1)S(1)}, u32[]{:S(2)}, u32[]{:S(2)}) collective-permute-start(bf16[192,768]{1,0:T(8,128)(2,1)S(1)} %slice.142.refs_0_), channel_id=1, source_target_pairs={{0,4},{4,0},{8,12},{12,8},{1,5},{5,1},{9,13},{13,9},{2,6},{6,2},{1... | collective-permute-start | bytes 884744 | tf_op jit(solution)/shard_map/ppermute | solution.py:22
  51.9 22.8 %collective-permute-start.18 = (f32[1,2688]{1,0:T(1,128)S(1)}, f32[1,2688]{1,0:T(1,128)S(1)}, u32[]{:S(2)}, u32[]{:S(2)}) collective-permute-start(f32[1,2688]{1,0:T(1,128)S(1)} %broadcast_in_dim.24), channel_id=1, source_target_pairs={{0,16},{16,0},{1,17},{17,1},{2,18},{18,2},{3,19},{19,3},{4,20},{20... | collective-permute-start | bytes 32264 | tf_op jit(solution)/shard_map/ppermute | solution.py:22
  52.0 31.9 %collective-permute-start.17 = (bf16[768,384]{1,0:T(8,128)(2,1)S(1)}, bf16[768,384]{1,0:T(8,128)(2,1)S(1)}, u32[]{:S(2)}, u32[]{:S(2)}) collective-permute-start(bf16[768,384]{1,0:T(8,128)(2,1)S(1)} %stack_line.4.refs_4_), channel_id=1, source_target_pairs={{0,16},{16,0},{1,17},{17,1},{2,18},{18,2},{3,19},{19,3},{4,20},{20... | collective-permute-start | bytes 1769480 | tf_op jit(solution)/shard_map/ppermute | solution.py:22
  74.5 26.6 %collective-permute-start.28 = (bf16[768,768]{1,0:T(8,128)(2,1)S(1)}, bf16[768,768]{1,0:T(8,128)(2,1)S(1)}, u32[]{:S(2)}, u32[]{:S(2)}) collective-permute-start(bf16[768,768]{1,0:T(8,128)(2,1)S(1)} %stack_line.5.refs_4_), channel_id=1, source_target_pairs={{0,16},{16,0},{1,17},{17,1},{2,18},{18,2},{3,19},{19,3},{4,20},{20... | collective-permute-start | bytes 3538952 | tf_op jit(solution)/shard_map/ppermute | solution.py:22
  111.3 21.1 %collective-permute-start.49 = (bf16[192,768]{1,0:T(8,128)(2,1)S(1)}, bf16[192,768]{1,0:T(8,128)(2,1)S(1)}, u32[]{:S(2)}, u32[]{:S(2)}) collective-permute-start(bf16[192,768]{1,0:T(8,128)(2,1)S(1)} %slice.146.refs_0_), channel_id=1, source_target_pairs={{0,8},{4,12},{8,0},{12,4},{1,9},{5,13},{9,1},{13,5},{2,10},{6,14},... | collective-permute-start | bytes 884744 | tf_op jit(solution)/shard_map/ppermute | solution.py:22
  111.4 21.1 %collective-permute-start.48 = (bf16[192,768]{1,0:T(8,128)(2,1)S(1)}, bf16[192,768]{1,0:T(8,128)(2,1)S(1)}, u32[]{:S(2)}, u32[]{:S(2)}) collective-permute-start(bf16[192,768]{1,0:T(8,128)(2,1)S(1)} %slice.146.refs_0_), channel_id=1, source_target_pairs={{0,4},{4,0},{8,12},{12,8},{1,5},{5,1},{9,13},{13,9},{2,6},{6,2},{1... | collective-permute-start | bytes 884744 | tf_op jit(solution)/shard_map/ppermute | solution.py:22
  133.1 46.8 %collective-permute-start.51 = (bf16[768,768]{1,0:T(8,128)(2,1)S(1)}, bf16[768,768]{1,0:T(8,128)(2,1)S(1)}, u32[]{:S(2)}, u32[]{:S(2)}) collective-permute-start(bf16[768,768]{1,0:T(8,128)(2,1)S(1)} %stack_line.7.refs_8_), channel_id=1, source_target_pairs={{0,16},{16,0},{1,17},{17,1},{2,18},{18,2},{3,19},{19,3},{4,20},{20... | collective-permute-start | bytes 3538952 | tf_op jit(solution)/shard_map/ppermute | solution.py:22
  159.4 14.2 %collective-permute-start.47 = (bf16[64,768]{1,0:T(8,128)(2,1)S(1)}, bf16[64,768]{1,0:T(8,128)(2,1)S(1)}, u32[]{:S(2)}, u32[]{:S(2)}) collective-permute-start(bf16[64,768]{1,0:T(8,128)(2,1)S(1)} %get-tuple-element.238.refs_4_.refs_8_), channel_id=1, source_target_pairs={{0,3},{1,2},{2,1},{3,0},{4,7},{5,6},{6,5},{7,4},{8,11},{9,10},{10,... | collective-permute-start | bytes 294920 | tf_op jit(solution)/shard_map/ppermute | solution.py:22
  202.7 15.7 %collective-permute-start.66 = (bf16[2,192,768]{2,1,0:T(8,128)(2,1)S(1)}, bf16[2,192,768]{2,1,0:T(8,128)(2,1)S(1)}, u32[]{:S(2)}, u32[]{:S(2)}) collective-permute-start(bf16[2,192,768]{2,1,0:T(8,128)(2,1)S(1)} %get-tuple-element.276), channel_id=1, source_target_pairs={{0,4},{4,0},{8,12},{12,8},{1,5},{5,1},{9,13},{13,9},{2,6},{6,2},{1... | collective-permute-start | bytes 1769480 | tf_op jit(solution)/shard_map/ppermute | solution.py:22
  228.6 14.7 %collective-permute-start.75 = (bf16[2,192,384]{2,1,0:T(8,128)(2,1)S(1)}, bf16[2,192,384]{2,1,0:T(8,128)(2,1)S(1)}, u32[]{:S(2)}, u32[]{:S(2)}) collective-permute-start(bf16[2,192,384]{2,1,0:T(8,128)(2,1)S(1)} %get-tuple-element.300), channel_id=1, source_target_pairs={{0,4},{4,0},{8,12},{12,8},{1,5},{5,1},{9,13},{13,9},{2,6},{6,2},{1... | collective-permute-start | bytes 884744 | tf_op jit(solution)/shard_map/ppermute | solution.py:22
  229.2 16.4 %collective-permute-start.74 = (bf16[192,768]{1,0:T(8,128)(2,1)S(1)}, bf16[192,768]{1,0:T(8,128)(2,1)S(1)}, u32[]{:S(2)}, u32[]{:S(2)}) collective-permute-start(bf16[192,768]{1,0:T(8,128)(2,1)S(1)} %fusion.1), channel_id=1, source_target_pairs={{0,8},{4,12},{8,0},{12,4},{1,9},{5,13},{9,1},{13,5},{2,10},{6,14},... | collective-permute-start | bytes 884744 | tf_op jit(solution)/shard_map/ppermute | solution.py:22
  257.4 18.5 %collective-permute-start.84 = (bf16[2,192,768]{2,1,0:T(8,128)(2,1)S(1)}, bf16[2,192,768]{2,1,0:T(8,128)(2,1)S(1)}, u32[]{:S(2)}, u32[]{:S(2)}) collective-permute-start(bf16[2,192,768]{2,1,0:T(8,128)(2,1)S(1)} %get-tuple-element.325), channel_id=1, source_target_pairs={{0,4},{4,0},{8,12},{12,8},{1,5},{5,1},{9,13},{13,9},{2,6},{6,2},{1... | collective-permute-start | bytes 1769480 | tf_op jit(solution)/shard_map/ppermute | solution.py:22
  257.5 16.2 %collective-permute-start.83 = (bf16[192,384]{1,0:T(8,128)(2,1)S(1)}, bf16[192,384]{1,0:T(8,128)(2,1)S(1)}, u32[]{:S(2)}, u32[]{:S(2)}) collective-permute-start(bf16[192,384]{1,0:T(8,128)(2,1)S(1)} %fusion.5), channel_id=1, source_target_pairs={{0,8},{4,12},{8,0},{12,4},{1,9},{5,13},{9,1},{13,5},{2,10},{6,14},... | collective-permute-start | bytes 442376 | tf_op jit(solution)/shard_map/ppermute | solution.py:22
  259.5 14.2 %collective-permute-start.80 = (bf16[64,768]{1,0:T(8,128)(2,1)S(1)}, bf16[64,768]{1,0:T(8,128)(2,1)S(1)}, u32[]{:S(2)}, u32[]{:S(2)}) collective-permute-start(bf16[64,768]{1,0:T(8,128)(2,1)S(1)} %get-tuple-element.320), channel_id=1, source_target_pairs={{0,1},{1,0},{2,3},{3,2},{4,5},{5,4},{6,7},{7,6},{8,9},{9,8},{10,11... | collective-permute-start | bytes 294920 | tf_op jit(solution)/shard_map/ppermute | solution.py:22
  280.0 31.8 %collective-permute-start.97 = (bf16[2,192,384]{2,1,0:T(8,128)(2,1)S(1)}, bf16[2,192,384]{2,1,0:T(8,128)(2,1)S(1)}, u32[]{:S(2)}, u32[]{:S(2)}) collective-permute-start(bf16[2,192,384]{2,1,0:T(8,128)(2,1)S(1)} %get-tuple-element.371), channel_id=1, source_target_pairs={{0,4},{4,0},{8,12},{12,8},{1,5},{5,1},{9,13},{13,9},{2,6},{6,2},{1... | collective-permute-start | bytes 884744 | tf_op jit(solution)/shard_map/ppermute | solution.py:22
  283.8 27.0 %collective-permute-start.100 = (bf16[192,768]{1,0:T(8,128)(2,1)S(1)}, bf16[192,768]{1,0:T(8,128)(2,1)S(1)}, u32[]{:S(2)}, u32[]{:S(2)}) collective-permute-start(bf16[192,768]{1,0:T(8,128)(2,1)S(1)} %fusion), channel_id=1, source_target_pairs={{0,8},{4,12},{8,0},{12,4},{1,9},{5,13},{9,1},{13,5},{2,10},{6,14},... | collective-permute-start | bytes 884744 | tf_op jit(solution)/shard_map/ppermute | solution.py:22
  287.4 17.3 %collective-permute-start.92 = (f32[1,11904]{1,0:T(1,128)S(1)}, f32[1,11904]{1,0:T(1,128)S(1)}, u32[]{:S(2)}, u32[]{:S(2)}) collective-permute-start(f32[1,11904]{1,0:T(1,128)S(1)} %grads_join.1.g0), channel_id=1, source_target_pairs={{0,8},{4,12},{8,0},{12,4},{1,9},{5,13},{9,1},{13,5},{2,10},{6,14},... | collective-permute-start | bytes 142856 | tf_op jit(solution)/shard_map/ppermute | solution.py:22
  288.2 16.5 %collective-permute-start.91 = (f32[1,11904]{1,0:T(1,128)S(1)}, f32[1,11904]{1,0:T(1,128)S(1)}, u32[]{:S(2)}, u32[]{:S(2)}) collective-permute-start(f32[1,11904]{1,0:T(1,128)S(1)} %grads_join.1.g0), channel_id=1, source_target_pairs={{0,4},{4,0},{8,12},{12,8},{1,5},{5,1},{9,13},{13,9},{2,6},{6,2},{1... | collective-permute-start | bytes 142856 | tf_op jit(solution)/shard_map/ppermute | solution.py:22
  306.5 16.2 %collective-permute-start.94 = (f32[2,192]{1,0:T(2,128)S(1)}, f32[2,192]{1,0:T(2,128)S(1)}, u32[]{:S(2)}, u32[]{:S(2)}) collective-permute-start(f32[2,192]{1,0:T(2,128)S(1)} %get-tuple-element.365), channel_id=1, source_target_pairs={{0,4},{4,0},{8,12},{12,8},{1,5},{5,1},{9,13},{13,9},{2,6},{6,2},{1... | collective-permute-start | bytes 4616 | tf_op jit(solution)/shard_map/ppermute | solution.py:22
  306.5 16.2 %collective-permute-start.95 = (f32[2,192]{1,0:T(2,128)S(1)}, f32[2,192]{1,0:T(2,128)S(1)}, u32[]{:S(2)}, u32[]{:S(2)}) collective-permute-start(f32[2,192]{1,0:T(2,128)S(1)} %get-tuple-element.366), channel_id=1, source_target_pairs={{0,8},{4,12},{8,0},{12,4},{1,9},{5,13},{9,1},{13,5},{2,10},{6,14},... | collective-permute-start | bytes 4616 | tf_op jit(solution)/shard_map/ppermute | solution.py:22
  308.7 14.0 %collective-permute-start.96 = (f32[2,192]{1,0:T(2,128)S(1)}, f32[2,192]{1,0:T(2,128)S(1)}, u32[]{:S(2)}, u32[]{:S(2)}) collective-permute-start(f32[2,192]{1,0:T(2,128)S(1)} %get-tuple-element.367), channel_id=1, source_target_pairs={{0,12},{4,8},{8,4},{12,0},{1,13},{5,9},{9,5},{13,1},{2,14},{6,10},... | collective-permute-start | bytes 4616 | tf_op jit(solution)/shard_map/ppermute | solution.py:22
  311.7 14.5 %collective-permute-start.101 = (f32[192,768]{1,0:T(8,128)S(1)}, f32[192,768]{1,0:T(8,128)S(1)}, u32[]{:S(2)}, u32[]{:S(2)}) collective-permute-start(f32[192,768]{1,0:T(8,128)S(1)} %get-tuple-element.386), channel_id=1, source_target_pairs={{0,16},{16,0},{1,17},{17,1},{2,18},{18,2},{3,19},{19,3},{4,20},{20... | collective-permute-start | bytes 1769480 | tf_op jit(solution)/shard_map/ppermute | solution.py:22
  (94 other events, 690.5 us)

commit v5 on v4

--- a/solution.py
+++ b/solution.py
@@ -363,37 +363,33 @@
     return pl.ds(pl.multiple_of((place[1] ^ k) * rows, 16), rows)
 
 
-def stack_body(place, *refs):
-    out = refs[-1]
-    for k, ref in enumerate(refs[:-1]):
-        out[line_blocks(place, k, ref.shape[0])] = ref[...]
-
-
-def line_parts_body(place, keep, received, near, far, own):
-    rows = own.shape[0]
-
-    def block(k):
-        at = line_blocks(place, k, rows)
-        return keep[at] + received[at].astype(F32)
-
-    near[0] = block(1).astype(BF16)
-    near[1] = block(3).astype(BF16)
-    far[...] = block(2)
-    own[...] = block(0)
-
-
-def line_total_body(place, own0, near0, far0, own1, near1, far1, mine, give):
-    first = place[0] == 0
-    total0 = own0[...] + near0[0].astype(F32) + far0[...].astype(F32)
-    total1 = own1[...] + near1[0].astype(F32) + far1[...].astype(F32)
-    mine[...] = jnp.where(first, total0, total1)
-    give[...] = jnp.where(first, total1, total0)
+def stack_body(place, pair, other_pair, out):
+    rows = pair.shape[1]
+    for k, block in enumerate((pair[0], other_pair[0], pair[1], other_pair[1])):
+        out[line_blocks(place, k, rows)] = block
+
+
+def line_parts_body(place, keep, received, *outs):
+    rows, wide = outs[2].shape
+
+    for piece in range(len(outs) // 3):
+        near, far, own = outs[3 * piece : 3 * piece + 3]
+        columns = slice(piece * wide, (piece + 1) * wide)
+
+        def block(k):
+            at = line_blocks(place, k, rows)
+            return keep[at, columns] + received[at, columns].astype(F32)
+
+        near[0] = block(1).astype(BF16)
+        near[1] = block(3).astype(BF16)
+        far[...] = block(2)
+        own[...] = block(0)
 
 
 def final_mlp_body(place, mine, received, expand_out, shrink_out):
     first = place[0] == 0
     half = mine.shape[1] // 2
-    own, other = mine[...], received[...]
+    own, other = mine[...].astype(F32), received[...].astype(F32)
     for index, values in enumerate((jnp.where(first, own, other), jnp.where(first, other, own))):
         expand_out[:, index * half : (index + 1) * half] = values[:, :half]
         shrink_out[index * half : (index + 1) * half] = values[:, half:].T
@@ -402,7 +398,7 @@
 def final_attn_body(place, mine, received, joint_out, out_out):
     first = place[0] == 0
     width = mine.shape[1] // 2
-    own, other = mine[...], received[...]
+    own, other = mine[...].astype(F32), received[...].astype(F32)
     front, back = jnp.where(first, own, other), jnp.where(first, other, own)
     joint_out[:, : 2 * width] = front
     joint_out[:, 2 * width :] = back[:, :width]
@@ -590,22 +586,30 @@
         activated_all = lax.all_gather(activated, "dp", axis=0).reshape(line_size * micro, -1)
 
     def along_line(value):
-        if direct:
-            lined = run(
-                "stack_line",
-                stack_body,
-                [shape((model, value.shape[1]), BF16)],
-                gather(value, "dp"),
-                place,
-            )[0]
-        else:
-            lined = lax.all_gather(value, "dp", axis=0, tiled=True)
+        return lax.all_gather(value, "dp", axis=0, tiled=True)
+
+    def line_first(value):
+        return jnp.stack([value, swap(value, "dp", 2)]) if direct else value
+
+    def line_second(pair):
+        if not direct:
+            return along_line(pair)
+        return run(
+            "stack_line",
+            stack_body,
+            [shape((model, pair.shape[2]), BF16)],
+            [pair, swap(pair, "dp", 1)],
+            place,
+        )[0]
+
+    def both_cores(lined, ready):
+        lined = after(lined, ready)
         return lined, swap(lined, "pipe", 1)
 
     def half_of(layer, mlp):
         return halves_of_layers[layer][:, split:] if mlp else halves_of_layers[layer][:, :split]
 
-    w_attn0 = along_line(after(half_of(0, False), activated_all))
+    lined_a0 = along_line(half_of(0, False))
 
     if direct:
         mod_partial = run(
@@ -614,11 +618,14 @@
             [shape((micro * LINE, columns), F32)],
             activated_all + [own_rows],
         )[0]
+        mod_partials, lined_a0 = tie(gather(mod_partial, "tensor"), lined_a0)
+        w_attn0 = both_cores(lined_a0, mod_partials)
+        lined_m0 = along_line(after(half_of(0, True), lined_a0))
         pieces = run(
             "mod_sum",
             functools.partial(mod_sum_body, count),
             [shape((micro, columns), F32)] * LINE,
-            gather(mod_partial, "tensor"),
+            mod_partials,
         )
         mod_mine, mod_other = pl.pallas_call(
             mod_join_body,
@@ -631,13 +638,16 @@
         )(place, *exchange(pieces, "dp"), modulation_bias)
     else:
         mod_partial = dot(activated_all, own_rows)
-        mod_sum = tree_sum(gather(mod_partial, "tensor")).reshape(line_size, micro, -1)
+        mod_partials = gather(mod_partial, "tensor")
+        w_attn0 = both_cores(lined_a0, mod_partials)
+        lined_m0 = along_line(after(half_of(0, True), lined_a0))
+        mod_sum = tree_sum(mod_partials).reshape(line_size, micro, -1)
         mod_layer = lax.all_to_all(mod_sum, "dp", split_axis=0, concat_axis=0)
         mod_layer = jnp.swapaxes(mod_layer, 0, 1).reshape(micro, -1) + modulation_bias
         mod_mine, mod_other = mine(mod_layer)[None], other(mod_layer)[None]
     mod0, mod1 = both_layers(mod_mine, swap(mod_other, "pipe", 1))
 
-    w_mlp0 = along_line(after(half_of(0, True), (mod0, w_attn0[0])))
+    pair_a1 = line_first(after(half_of(1, False), mod0))
     own_f32 = shape((own, model), F32)
     own_bf16 = shape((own, model), BF16)
     blocks = [own_bf16] * count
@@ -677,10 +687,14 @@
             "middle", middle_body, [own_f32, own_f32, own_bf16], parts + [bias, h, mod]
         )
 
-    kept_attn0, parts = attention(gather(attn_in, "tensor"), w_attn0, biases[0][0])
+    attn_rows, pair_a1 = tie(gather(attn_in, "tensor"), pair_a1)
+    lined_a1 = line_second(pair_a1)
+    kept_attn0, parts = attention(attn_rows, w_attn0, biases[0][0])
+    w_mlp0 = both_cores(lined_m0, parts)
+    lined_m1 = along_line(after(half_of(1, True), w_mlp0[0]))
     attended0, middle0, mlp_in = middle_of(parts, biases[0][1], h0, mod0)
-    mlp_rows0, half = tie(gather(mlp_in, "tensor"), half_of(1, False))
-    w_attn1 = along_line(half)
+    mlp_rows0 = gather(mlp_in, "tensor")
+    w_attn1 = both_cores(lined_a1, mlp_rows0)
     outs = kernel(
         "feed_forward",
         mlp_body,
@@ -688,17 +702,16 @@
         mlp_rows0 + [w_mlp0[0], w_mlp0[1], biases[0][2]],
     )
     mlp_rows0, pre0, hidden0 = outs[:3]
-    parts, half = tie(exchange(outs[3:], "tensor"), half_of(1, True))
-    w_mlp1 = along_line(half)
     shrunk0, passed, h1, attn_in = kernel(
         "between",
         between_body,
         [own_f32, own_bf16, own_f32, own_bf16],
-        parts + [biases[0][3], middle0, mod0, mod1],
+        exchange(outs[3:], "tensor") + [biases[0][3], middle0, mod0, mod1],
     )
 
     g_rows1 = gather(g_shrunk1, "tensor")
     kept_attn1, parts = attention(gather(attn_in, "tensor"), w_attn1, biases[1][0])
+    w_mlp1 = both_cores(lined_m1, parts)
     attended1, middle1, mlp_in = middle_of(parts, biases[1][1], h1, mod1)
     outs = kernel(
         "feed_forward_both",
@@ -727,144 +740,141 @@
         )
         return outs[:3], exchange(outs[3:], "tensor")
 
-    def line_parts(grads):
+    def chip_sum(grads):
         keep, give = grads
-        received = swap(give, "pipe", 1)
+        return (keep + swap(give, "pipe", 1).astype(F32)).astype(BF16)
+
+    def line_sum(whole):
+        return lax.psum_scatter(whole, "dp", scatter_dimension=0, tiled=True)
+
+    def line_parts(grads, pieces):
+        keep, give = grads
+        wide = keep.shape[1] // pieces
         if not direct:
-            return None, (keep + received.astype(F32)).astype(BF16), None
-        wide = keep.shape[1]
-        return run(
+            whole = chip_sum(grads)
+            return [[whole[:, k * wide : (k + 1) * wide]] for k in range(pieces)]
+        outs = run(
             "line_parts",
             line_parts_body,
-            [shape((2, chunk, wide), BF16), shape((chunk, wide), F32), shape((chunk, wide), F32)],
-            [keep, received],
+            [shape((2, chunk, wide), BF16), shape((chunk, wide), F32), shape((chunk, wide), F32)]
+            * pieces,
+            [keep, swap(give, "pipe", 1)],
             place,
         )
-
-    def mlp_weight_grads(mlp_rows, g_pre, g_rows, hidden_rows):
-        return line_parts(
-            run(
-                "mlp_weight_grads",
-                mlp_weights_body,
-                [shape((model, hidden), F32), shape((model, hidden), BF16)],
-                [mlp_rows, g_pre, g_rows, hidden_rows],
-            )
-        )
-
-    def attn_weight_grads(kept, g_joint, g_rows):
-        return line_parts(
-            run(
-                "attn_weight_grads",
-                attn_weights_body,
-                [shape((model, 2 * width), F32), shape((model, 2 * width), BF16)],
-                [kept[0], g_joint, g_rows, kept[3]],
-                place,
-            )
-        )
+        return [outs[3 * k : 3 * k + 3] for k in range(pieces)]
 
     def line_near(parts):
-        return swap(parts[0], "dp", 1) if direct else parts[1]
+        return swap(parts[0], "dp", 1) if direct else parts[0]
 
     def line_far(parts, near):
         if not direct:
-            return near
+            return line_sum(near)
         return swap((parts[1] + near[1].astype(F32)).astype(BF16), "dp", 2)
 
-    def line_total(first_layer, second_layer):
+    def line_total(parts, near, far):
         if not direct:
-            sums = [
-                lax.psum_scatter(far, "dp", scatter_dimension=0, tiled=True).astype(F32)
-                for _, _, far in (first_layer, second_layer)
-            ]
-            return mine(sums), swap(other(sums), "pipe", 1)
-        args = [x for parts, near, far in (first_layer, second_layer) for x in (parts[2], near, far)]
-        kept, given = run(
-            "line_total", line_total_body, [shape(args[0].shape, F32)] * 2, args, place
-        )
-        return kept, swap(given, "pipe", 1)
-
-    g_parts, y_partial, parts_m1 = tie(
+            return far
+        return (parts[2] + near[0].astype(F32) + far.astype(F32)).astype(BF16)
+
+    def own_halves(pair):
+        return mine(pair), swap(other(pair), "pipe", 1)
+
+    def mlp_weight_grads(mlp_rows, g_pre, g_rows, hidden_rows):
+        return run(
+            "mlp_weight_grads",
+            mlp_weights_body,
+            [shape((model, hidden), F32), shape((model, hidden), BF16)],
+            [mlp_rows, g_pre, g_rows, hidden_rows],
+        )
+
+    def attn_weight_grads(kept, g_joint, g_rows):
+        return run(
+            "attn_weight_grads",
+            attn_weights_body,
+            [shape((model, 2 * width), F32), shape((model, 2 * width), BF16)],
+            [kept[0], g_joint, g_rows, kept[3]],
+            place,
+        )
+
+    g_parts, y_partial, (parts_e1, parts_s1) = tie(
         exchange(g_partial, "tensor"),
         y_partial,
-        mlp_weight_grads(mlp_rows1, g_pre1, g_rows1, hidden1),
-    )
+        line_parts(mlp_weight_grads(mlp_rows1, g_pre1, g_rows1, hidden1), 2),
+    )
+    near_e1 = line_near(parts_e1)
     g_middle1, g_attended, g_shift_mlp1, g_scale_mlp1, g_gate_attn1, out_grad1 = middle_back(
         g_parts, middle1, mod1, g_y1, attended1
     )
-    near_m1 = line_near(parts_m1)
     y_parts = exchange(y_partial, "tensor")
-    (g_rows, g_joint, joint_grad1), parts = attention_back(
-        gather(g_attended, "tensor"), w_attn1, kept_attn1
-    )
-    parts, near_m1, parts_a1 = tie(
-        parts, near_m1, attn_weight_grads(kept_attn1, g_joint, g_rows)
-    )
+    g_rows, near_e1, parts_e1, parts_s1 = tie(
+        gather(g_attended, "tensor"), near_e1, parts_e1, parts_s1
+    )
+    far_e1 = line_far(parts_e1, near_e1)
+    near_s1 = line_near(parts_s1)
+    (g_rows, g_joint, joint_grad1), parts = attention_back(g_rows, w_attn1, kept_attn1)
+    parts, (parts_a1,), far_e1, near_s1, parts_s1 = tie(
+        parts,
+        line_parts(attn_weight_grads(kept_attn1, g_joint, g_rows), 1),
+        far_e1,
+        near_s1,
+        parts_s1,
+    )
+    near_a1 = line_near(parts_a1)
+    far_s1 = line_far(parts_s1, near_s1)
     g_passed, g_y0, g_shrunk0, g_shift_attn1, g_scale_attn1, g_gate_mlp0, shrink_grad0 = kernel(
         "between_back",
         between_back_body,
         [own_bf16, own_f32, own_bf16] + [vector] * 4,
         parts + [h1, mod1, mod0, g_middle1, shrunk0],
     )
-    far_m1 = line_far(parts_m1, near_m1)
-    near_a1 = line_near(parts_a1)
-
+
+    g_rows0, near_a1, far_s1, parts_a1 = tie(
+        gather(g_shrunk0, "tensor"), near_a1, far_s1, parts_a1
+    )
+    far_a1 = line_far(parts_a1, near_a1)
     outs = kernel(
         "feed_forward_back",
         mlp_back_body,
         [wide_bf16, hidden_bf16, hidden_vector] + blocks,
-        gather(g_shrunk0, "tensor") + [w_mlp0[0], w_mlp0[1], pre0],
+        g_rows0 + [w_mlp0[0], w_mlp0[1], pre0],
     )
     g_rows0, g_pre0, expand_grad0 = outs[:3]
-    parts, far_m1, near_a1, parts_m0 = tie(
+    parts, (parts_e0, parts_s0), far_a1 = tie(
         exchange(outs[3:], "tensor"),
-        far_m1,
-        near_a1,
-        mlp_weight_grads(mlp_rows0, g_pre0, g_rows0, hidden0),
-    )
+        line_parts(mlp_weight_grads(mlp_rows0, g_pre0, g_rows0, hidden0), 2),
+        far_a1,
+    )
+    near_e0 = line_near(parts_e0)
     g_middle0, g_attended, g_shift_mlp0, g_scale_mlp0, g_gate_attn0, out_grad0 = middle_back(
         parts, middle0, mod0, g_y0, attended0
     )
-    near_m0 = line_near(parts_m0)
-    far_a1 = line_far(parts_a1, near_a1)
     y1, g_gate_mlp1, shrink_grad1 = kernel(
         "leave",
         leave_body,
         [own_bf16, vector, vector],
         y_parts + [biases[1][3], middle1, mod1, g_y1, g_shrunk1],
     )
-    (g_rows, g_joint, joint_grad0), parts = attention_back(
-        gather(g_attended, "tensor"), w_attn0, kept_attn0
-    )
-    parts, far_a1, near_m0, parts_a0 = tie(
-        parts, far_a1, near_m0, attn_weight_grads(kept_attn0, g_joint, g_rows)
-    )
+    g_rows, near_e0, parts_e0, parts_s0 = tie(
+        gather(g_attended, "tensor"), near_e0, parts_e0, parts_s0
+    )
+    far_e0 = line_far(parts_e0, near_e0)
+    near_s0 = line_near(parts_s0)
+    (g_rows, g_joint, joint_grad0), parts = attention_back(g_rows, w_attn0, kept_attn0)
+    parts, (parts_a0,), far_e0, near_s0, parts_s0 = tie(
+        parts,
+        line_parts(attn_weight_grads(kept_attn0, g_joint, g_rows), 1),
+        far_e0,
+        near_s0,
+        parts_s0,
+    )
+    near_a0 = line_near(parts_a0)
+    far_s0 = line_far(parts_s0, near_s0)
     g_h0, g_shift_attn0, g_scale_attn0 = kernel(
         "finish_back",
         finish_back_body,
         [own_bf16, vector, vector],
         parts + [h0, mod0, g_middle0],
     )
-    far_m0 = line_far(parts_m0, near_m0)
-    near_a0 = line_near(parts_a0)
-    far_a0 = line_far(parts_a0, near_a0)
-    mlp_halves = line_total((parts_m0, near_m0, far_m0), (parts_m1, near_m1, far_m1))
-    attn_halves = line_total((parts_a0, near_a0, far_a0), (parts_a1, near_a1, far_a1))
-    expand_w_grad, shrink_w_grad = run(
-        "final_mlp",
-        final_mlp_body,
-        [shape((chunk, hidden), F32), shape((hidden, chunk), F32)],
-        mlp_halves,
-        place,
-    )
-    joint_w_grad, output_w_grad = run(
-        "final_attn",
-        final_attn_body,
-        [shape((chunk, 3 * width), F32), shape((width, chunk), F32)],
-        attn_halves,
-        place,
-    )
-    joint_w_grad = joint_w_grad.reshape(chunk, 3, width)
-
     def own_layer_of_micros(pair):
         return jnp.stack(both_layers(mine(pair), swap(other(pair), "pipe", 1)))
 
@@ -894,11 +904,15 @@
             shrink_grad1,
         ],
     )[0]
+    packed_all, near_a0, far_s0, parts_a0 = tie(
+        gather(packed, "tensor"), near_a0, far_s0, parts_a0
+    )
+    far_a0 = line_far(parts_a0, near_a0)
     keep, give = run(
         "grads_sum",
         functools.partial(grads_sum_body, count),
         [shape((1, mods + bias_width), F32)] * 2,
-        gather(packed, "tensor") + [joint_grad0, expand_grad0, joint_grad1, expand_grad1],
+        packed_all + [joint_grad0, expand_grad0, joint_grad1, expand_grad1],
         place,
     )
     joined = run(
@@ -908,19 +922,45 @@
         [keep, swap(give, "pipe", 1)],
         place,
     )[0]
+    joined_all = gather(joined, "dp") if direct else lax.all_gather(joined, "dp", axis=0, tiled=True)
+    joined_all, far_a0 = tie(joined_all, far_a0)
+    mlp_grad0, mlp_grad1 = (
+        jnp.concatenate([line_total(*first_piece), line_total(*second_piece)], axis=1)
+        for first_piece, second_piece in (
+            ((parts_e0, near_e0, far_e0), (parts_s0, near_s0, far_s0)),
+            ((parts_e1, near_e1, far_e1), (parts_s1, near_s1, far_s1)),
+        )
+    )
+    attn_grad0 = line_total(parts_a0, near_a0, far_a0)
+    attn_grad1 = line_total(parts_a1, near_a1, far_a1)
+    expand_w_grad, shrink_w_grad = run(
+        "final_mlp",
+        final_mlp_body,
+        [shape((chunk, hidden), F32), shape((hidden, chunk), F32)],
+        own_halves((mlp_grad0, mlp_grad1)),
+        place,
+    )
+    joint_w_grad, output_w_grad = run(
+        "final_attn",
+        final_attn_body,
+        [shape((chunk, 3 * width), F32), shape((width, chunk), F32)],
+        own_halves((attn_grad0, attn_grad1)),
+        place,
+    )
+    joint_w_grad = joint_w_grad.reshape(chunk, 3, width)
+
     if direct:
         outs = run(
             "mod_back",
             mod_back_body,
             [shape(own_rows.shape, F32), shape((1, mods), F32), shape((1, bias_width), F32)]
             + [shape((micro, own_rows.shape[0]), F32)] * LINE,
-            gather(joined, "dp") + activated_all + [own_rows],
+            joined_all + activated_all + [own_rows],
             place,
         )
         ada_grad, ada_bias_grad, bias_sum = outs[:3]
         act_grad = tree_sum(exchange(outs[3:], "dp"))
     else:
-        joined_all = lax.all_gather(joined, "dp", axis=0, tiled=True)
         mod_grads = joined_all[:, : 2 * mods].reshape(line_size * micro, mods)
         bias_sum = jnp.sum(joined_all[:, 2 * mods :], axis=0, keepdims=True)
         ada_bias_grad = jnp.sum(mod_grads, axis=0, keepdims=True)

time: 329 us -> 312 us (0.948)
  waiting for transfers between devices: 171 us -> 106 us
  local copies, waits for them, and re-layouts: 8.23 us -> 36.7 us
  blocking collectives: 0 us -> 16.5 us
  between operations: 1.38 us -> 15.5 us
  starting transfers between devices: 109 us -> 98.8 us
    ppermute x102 -> x96, waiting for transfers between devices: 171 us -> 106 us  [swap(): return lax.ppermute(value, axis, pairs)]
    unnamed x37 -> x195, local copies, waits for them, and re-layouts: 6.15 us -> 32.6 us
    all_gather x0 -> x1, blocking collectives: none -> 16.5 us  [along_line(): return lax.all_gather(value, 'dp', axis=0, tiled=True)]
    ppermute x102 -> x96, starting transfers between devices: 109 us -> 98.5 us  [swap(): return lax.ppermute(value, axis, pairs)]
    pallas_call x38 -> x33, Pallas kernels: 34.5 us -> 31.6 us  [run(): pl.pallas_call(body, out_shape=outs, in_specs=specs, out_specs=[pl.BlockS...]
  transfers between devices with their start and end apart: 102 -> 98, of which waited for: 59 -> 48; matrix products, arithmetic and copies ran while one was open for 2% -> 3% of each run, Pallas kernels for 5% -> 6%
where the time goes in v5:
time: 312 us; the launch traced here: 311 us
  waiting for transfers between devices  106 us (34%)
  starting transfers between devices  98.8 us (32%)
  local copies, waits for them, and re-layouts  36.7 us (12%)
  Pallas kernels  33 us (11%)
  blocking collectives  16.5 us (5%)
  between operations  15.5 us (5%)
  other arithmetic  4.83 us (2%)
    ppermute x96, waiting for transfers between devices, swap(): return lax.ppermute(value, axis, pairs)  106 us
    ppermute x96, starting transfers between devices, swap(): return lax.ppermute(value, axis, pairs)  98.5 us
    unnamed x195, local copies, waits for them, and re-layouts  32.6 us
    pallas_call x33, Pallas kernels, run(): pl.pallas_call(body, out_shape=outs, in_specs=specs, out_specs=[pl.BlockS...  31.6 us
    all_gather x1, blocking collectives, along_line(): return lax.all_gather(value, 'dp', axis=0, tiled=True)  16.5 us
  transfers between devices with their start and end apart: 98, of which 48 were waited for; matrix products, arithmetic and copies ran while one was open for 3% of the time, Pallas kernels for 6%

profile of v5, /device:TPU:0, one launch (start us, length us, event | category | flops | bytes accessed | tf_op | source)
XLA Modules:
  0.0 311.4 jit_solution(2929896950866633419)
XLA Ops:
  10.5 5.0 %collective-permute-start.2 = (bf16[2,192]{1,0:T(2,128)(2,1)S(1)}, bf16[2,192]{1,0:T(2,128)(2,1)S(1)}, u32[]{:S(2)}, u32[]{:S(2)}) collective-permute-start(bf16[2,192]{1,0:T(2,128)(2,1)S(1)} %fusion.26.a0), channel_id=1, source_target_pairs={{0,12},{4,8},{8,4},{12,0},{1,13},{5,9},{9,5},{13,1},{2,14},{6,10},... | collective-permute-start | bytes 2312 | tf_op jit(solution)/shard_map/ppermute | solution.py:22
  17.0 2.9 collective-permute-done.1.a2
  20.1 2.5 collective-permute-start.5
  24.0 16.5 %all_gather.9.refs_4_ = bf16[768,384]{1,0:T(8,128)(2,1)S(1)} all-gather(bf16[192,384]{1,0:T(8,128)(2,1)S(1)} %slice.169), channel_id=1, replica_groups=mesh['pipe'=2,'dp'=4,'tensor'=4] {'dp'}, dimensions={0}, use_global_device_ids=true | all-gather | bytes 737280 | tf_op jit(solution)/shard_map/all_gather | solution.py:589
  53.5 2.5 collective-permute-start.13
  57.1 13.8 %collective-permute-done.14 = bf16[192,384]{1,0:T(8,128)(2,1)S(1)} collective-permute-done((bf16[192,384]{1,0:T(8,128)(2,1)S(1)}, bf16[192,384]{1,0:T(8,128)(2,1)S(1)}, u32[]{:S(2)}, u32[]{:S(2)}) %collective-permute-start.14) | collective-permute-done | bytes 147488 | tf_op jit(solution)/shard_map/ppermute | solution.py:22
  71.0 2.8 attention.2
  94.4 5.1 %collective-permute-done.30.other_pair = bf16[2,192,384]{2,1,0:T(8,128)(2,1)S(1)} collective-permute-done((bf16[2,192,384]{2,1,0:T(8,128)(2,1)S(1)}, bf16[2,192,384]{2,1,0:T(8,128)(2,1)S(1)}, u32[]{:S(2)}, u32[]{:S(2)}) %collective-permute-start.30) | collective-permute-done | bytes 294944 | tf_op jit(solution)/shard_map/ppermute | solution.py:22
  104.0 2.6 collective-permute-start.25
  119.1 2.8 collective-permute-done.29.refs_3_
  165.6 3.1 %collective-permute-done.43.refs_2_ = bf16[64,768]{1,0:T(8,128)(2,1)S(1)} collective-permute-done((bf16[64,768]{1,0:T(8,128)(2,1)S(1)}, bf16[64,768]{1,0:T(8,128)(2,1)S(1)}, u32[]{:S(2)}, u32[]{:S(2)}) %collective-permute-start.43) | collective-permute-done | bytes 98336 | tf_op jit(solution)/shard_map/ppermute | solution.py:22
  172.6 2.9 collective-permute-done.52.refs_3_
  176.8 2.7 attention_back.2
  187.2 3.1 collective-permute-done.55.refs_2_
  199.6 3.0 collective-permute-done.62.refs_3_
  223.4 4.6 %collective-permute-done.69 = bf16[192,384]{1,0:T(8,128)(2,1)S(1)} collective-permute-done((bf16[192,384]{1,0:T(8,128)(2,1)S(1)}, bf16[192,384]{1,0:T(8,128)(2,1)S(1)}, u32[]{:S(2)}, u32[]{:S(2)}) %collective-permute-start.69) | collective-permute-done | bytes 147488 | tf_op jit(solution)/shard_map/ppermute | solution.py:22
  248.3 6.2 %collective-permute-done.78 = bf16[192,384]{1,0:T(8,128)(2,1)S(1)} collective-permute-done((bf16[192,384]{1,0:T(8,128)(2,1)S(1)}, bf16[192,384]{1,0:T(8,128)(2,1)S(1)}, u32[]{:S(2)}, u32[]{:S(2)}) %collective-permute-start.78) | collective-permute-done | bytes 147488 | tf_op jit(solution)/shard_map/ppermute | solution.py:22
  259.3 2.7 collective-permute-start.85
  263.3 6.5 %collective-permute-done.85 = bf16[192,384]{1,0:T(8,128)(2,1)S(1)} collective-permute-done((bf16[192,384]{1,0:T(8,128)(2,1)S(1)}, bf16[192,384]{1,0:T(8,128)(2,1)S(1)}, u32[]{:S(2)}, u32[]{:S(2)}) %collective-permute-start.85) | collective-permute-done | bytes 147488 | tf_op jit(solution)/shard_map/ppermute | solution.py:22
  269.8 3.1 collective-permute-done.84
  281.1 2.5 collective-permute-done.89.g3
  283.5 4.5 %collective-permute-done.88.g2 = f32[1,11904]{1,0:T(1,128)S(1)} collective-permute-done((f32[1,11904]{1,0:T(1,128)S(1)}, f32[1,11904]{1,0:T(1,128)S(1)}, u32[]{:S(2)}, u32[]{:S(2)}) %collective-permute-start.88) | collective-permute-done | bytes 47648 | tf_op jit(solution)/shard_map/ppermute | solution.py:22
  290.8 2.5 collective-permute-start.92
  295.9 2.8 collective-permute-done.93
  (455 shorter events, 189.5 us)
Async XLA Ops:
  7.2 79.1 %all-gather.3.cloned.1.call-start = ((), (), s32[]{:S(2)}) async-start(), calls=%async_computation | async-start | bytes 1474560 | tf_op jit(solution)/shard_map/all_gather | solution.py:589
  10.0 13.7 %collective-permute-start.6 = (bf16[192,1152]{1,0:T(8,128)(2,1)S(1)}, bf16[192,1152]{1,0:T(8,128)(2,1)S(1)}, u32[]{:S(2)}, u32[]{:S(2)}) collective-permute-start(bf16[192,1152]{1,0:T(8,128)(2,1)S(1)} %broadcast_select_fusion.2), channel_id=1, source_target_pairs={{0,16},{16,0},{1,17},{17,1},{2,18},{18,2},{3,19},{19,3},{4,20},{20... | collective-permute-start | bytes 1327112 | tf_op jit(solution)/shard_map/ppermute | solution.py:22
  16.3 34.0 %collective-permute-start.16 = (f32[1,2688]{1,0:T(1,128)S(1)}, f32[1,2688]{1,0:T(1,128)S(1)}, u32[]{:S(2)}, u32[]{:S(2)}) collective-permute-start(f32[1,2688]{1,0:T(1,128)S(1)} %broadcast_in_dim.24), channel_id=1, source_target_pairs={{0,16},{16,0},{1,17},{17,1},{2,18},{18,2},{3,19},{19,3},{4,20},{20... | collective-permute-start | bytes 32264 | tf_op jit(solution)/shard_map/ppermute | solution.py:22
  20.1 20.4 %collective-permute-start.5 = (f32[8,1152]{1,0:T(8,128)S(1)}, f32[8,1152]{1,0:T(8,128)S(1)}, u32[]{:S(2)}, u32[]{:S(2)}) collective-permute-start(f32[8,1152]{1,0:T(8,128)S(1)} %mod_first.1.refs_0_), channel_id=1, source_target_pairs={{0,3},{1,2},{2,1},{3,0},{4,7},{5,6},{6,5},{7,4},{8,11},{9,10},{10,... | collective-permute-start | bytes 110600 | tf_op jit(solution)/shard_map/ppermute | solution.py:22
  22.6 17.9 %collective-permute-start.4 = (f32[8,1152]{1,0:T(8,128)S(1)}, f32[8,1152]{1,0:T(8,128)S(1)}, u32[]{:S(2)}, u32[]{:S(2)}) collective-permute-start(f32[8,1152]{1,0:T(8,128)S(1)} %mod_first.1.refs_0_), channel_id=1, source_target_pairs={{0,2},{1,3},{2,0},{3,1},{4,6},{5,7},{6,4},{7,5},{8,10},{9,11},{10,... | collective-permute-start | bytes 110600 | tf_op jit(solution)/shard_map/ppermute | solution.py:22
  23.1 17.4 %collective-permute-start.3 = (f32[8,1152]{1,0:T(8,128)S(1)}, f32[8,1152]{1,0:T(8,128)S(1)}, u32[]{:S(2)}, u32[]{:S(2)}) collective-permute-start(f32[8,1152]{1,0:T(8,128)S(1)} %mod_first.1.refs_0_), channel_id=1, source_target_pairs={{0,1},{1,0},{2,3},{3,2},{4,5},{5,4},{6,7},{7,6},{8,9},{9,8},{10,11... | collective-permute-start | bytes 110600 | tf_op jit(solution)/shard_map/ppermute | solution.py:22
  46.5 91.4 %all-gather.5.cloned.1.call-start = ((), (), s32[]{:S(2)}) async-start(), calls=%async_computation.1 | async-start | bytes 1474560 | tf_op jit(solution)/shard_map/all_gather | solution.py:589
  50.4 20.6 %collective-permute-start.15 = (bf16[768,384]{1,0:T(8,128)(2,1)S(1)}, bf16[768,384]{1,0:T(8,128)(2,1)S(1)}, u32[]{:S(2)}, u32[]{:S(2)}) collective-permute-start(bf16[768,384]{1,0:T(8,128)(2,1)S(1)} %all_gather.9.refs_4_), channel_id=1, source_target_pairs={{0,16},{16,0},{1,17},{17,1},{2,18},{18,2},{3,19},{19,3},{4,20},{20... | collective-permute-start | bytes 1769480 | tf_op jit(solution)/shard_map/ppermute | solution.py:22
  52.5 18.4 %collective-permute-start.14 = (bf16[192,384]{1,0:T(8,128)(2,1)S(1)}, bf16[192,384]{1,0:T(8,128)(2,1)S(1)}, u32[]{:S(2)}, u32[]{:S(2)}) collective-permute-start(bf16[192,384]{1,0:T(8,128)(2,1)S(1)} %slice.170), channel_id=1, source_target_pairs={{0,8},{4,12},{8,0},{12,4},{1,9},{5,13},{9,1},{13,5},{2,10},{6,14},... | collective-permute-start | bytes 442376 | tf_op jit(solution)/shard_map/ppermute | solution.py:22
  53.5 17.4 %collective-permute-start.13 = (bf16[64,768]{1,0:T(8,128)(2,1)S(1)}, bf16[64,768]{1,0:T(8,128)(2,1)S(1)}, u32[]{:S(2)}, u32[]{:S(2)}) collective-permute-start(bf16[64,768]{1,0:T(8,128)(2,1)S(1)} %get-tuple-element.271.refs_0_), channel_id=1, source_target_pairs={{0,3},{1,2},{2,1},{3,0},{4,7},{5,6},{6,5},{7,4},{8,11},{9,10},{10,... | collective-permute-start | bytes 294920 | tf_op jit(solution)/shard_map/ppermute | solution.py:22
  56.0 14.9 %collective-permute-start.12 = (bf16[64,768]{1,0:T(8,128)(2,1)S(1)}, bf16[64,768]{1,0:T(8,128)(2,1)S(1)}, u32[]{:S(2)}, u32[]{:S(2)}) collective-permute-start(bf16[64,768]{1,0:T(8,128)(2,1)S(1)} %get-tuple-element.271.refs_0_), channel_id=1, source_target_pairs={{0,2},{1,3},{2,0},{3,1},{4,6},{5,7},{6,4},{7,5},{8,10},{9,11},{10,... | collective-permute-start | bytes 294920 | tf_op jit(solution)/shard_map/ppermute | solution.py:22
  56.5 14.4 %collective-permute-start.11 = (bf16[64,768]{1,0:T(8,128)(2,1)S(1)}, bf16[64,768]{1,0:T(8,128)(2,1)S(1)}, u32[]{:S(2)}, u32[]{:S(2)}) collective-permute-start(bf16[64,768]{1,0:T(8,128)(2,1)S(1)} %get-tuple-element.271.refs_0_), channel_id=1, source_target_pairs={{0,1},{1,0},{2,3},{3,2},{4,5},{5,4},{6,7},{7,6},{8,9},{9,8},{10,11... | collective-permute-start | bytes 294920 | tf_op jit(solution)/shard_map/ppermute | solution.py:22
  86.3 14.8 %collective-permute-start.23 = (bf16[768,768]{1,0:T(8,128)(2,1)}, bf16[768,768]{1,0:T(8,128)(2,1)S(1)}, u32[]{:S(2)}, u32[]{:S(2)}) collective-permute-start(bf16[768,768]{1,0:T(8,128)(2,1)} %all-gather.3.cloned.1.call-done.refs_4_), channel_id=1, source_target_pairs={{0,16},{16,0},{1,17},{17,1},{2,18},{18,2},{3,19},{19,3},{4,20},{20... | collective-permute-start | bytes 3538952 | tf_op jit(solution)/shard_map/ppermute | solution.py:22
  87.0 12.5 %collective-permute-start.30 = (bf16[2,192,384]{2,1,0:T(8,128)(2,1)S(1)}, bf16[2,192,384]{2,1,0:T(8,128)(2,1)S(1)}, u32[]{:S(2)}, u32[]{:S(2)}) collective-permute-start(bf16[2,192,384]{2,1,0:T(8,128)(2,1)S(1)} %pad_maximum_fusion.2.pair), channel_id=1, source_target_pairs={{0,4},{4,0},{8,12},{12,8},{1,5},{5,1},{9,13},{13,9},{2,6},{6,2},{1... | collective-permute-start | bytes 884744 | tf_op jit(solution)/shard_map/ppermute | solution.py:22
  101.1 18.0 %collective-permute-start.31 = (bf16[768,384]{1,0:T(8,128)(2,1)S(1)}, bf16[768,384]{1,0:T(8,128)(2,1)S(1)}, u32[]{:S(2)}, u32[]{:S(2)}) collective-permute-start(bf16[768,384]{1,0:T(8,128)(2,1)S(1)} %stack_line.1.refs_4_), channel_id=1, source_target_pairs={{0,16},{16,0},{1,17},{17,1},{2,18},{18,2},{3,19},{19,3},{4,20},{20... | collective-permute-start | bytes 1769480 | tf_op jit(solution)/shard_map/ppermute | solution.py:22
  137.9 17.2 %collective-permute-start.41 = (bf16[768,768]{1,0:T(8,128)(2,1)}, bf16[768,768]{1,0:T(8,128)(2,1)S(1)}, u32[]{:S(2)}, u32[]{:S(2)}) collective-permute-start(bf16[768,768]{1,0:T(8,128)(2,1)} %all-gather.5.cloned.1.call-done.refs_8_), channel_id=1, source_target_pairs={{0,16},{16,0},{1,17},{17,1},{2,18},{18,2},{3,19},{19,3},{4,20},{20... | collective-permute-start | bytes 3538952 | tf_op jit(solution)/shard_map/ppermute | solution.py:22
  137.9 11.9 %collective-permute-start.40 = (bf16[64,768]{1,0:T(8,128)(2,1)}, bf16[64,768]{1,0:T(8,128)(2,1)S(1)}, u32[]{:S(2)}, u32[]{:S(2)}) collective-permute-start(bf16[64,768]{1,0:T(8,128)(2,1)} %copy-done.32), channel_id=1, source_target_pairs={{0,3},{1,2},{2,1},{3,0},{4,7},{5,6},{6,5},{7,4},{8,11},{9,10},{10,... | collective-permute-start | bytes 294920 | tf_op jit(solution)/shard_map/ppermute | solution.py:22
  180.8 12.6 %collective-permute-start.59 = (bf16[2,192,384]{2,1,0:T(8,128)(2,1)S(1)}, bf16[2,192,384]{2,1,0:T(8,128)(2,1)S(1)}, u32[]{:S(2)}, u32[]{:S(2)}) collective-permute-start(bf16[2,192,384]{2,1,0:T(8,128)(2,1)S(1)} %get-tuple-element.363), channel_id=1, source_target_pairs={{0,4},{4,0},{8,12},{12,8},{1,5},{5,1},{9,13},{13,9},{2,6},{6,2},{1... | collective-permute-start | bytes 884744 | tf_op jit(solution)/shard_map/ppermute | solution.py:22
  193.4 11.7 %collective-permute-start.63 = (bf16[2,192,384]{2,1,0:T(8,128)(2,1)S(1)}, bf16[2,192,384]{2,1,0:T(8,128)(2,1)S(1)}, u32[]{:S(2)}, u32[]{:S(2)}) collective-permute-start(bf16[2,192,384]{2,1,0:T(8,128)(2,1)S(1)} %get-tuple-element.373), channel_id=1, source_target_pairs={{0,4},{4,0},{8,12},{12,8},{1,5},{5,1},{9,13},{13,9},{2,6},{6,2},{1... | collective-permute-start | bytes 884744 | tf_op jit(solution)/shard_map/ppermute | solution.py:22
  207.5 13.4 %collective-permute-start.68 = (bf16[768,768]{1,0:T(8,128)(2,1)S(1)}, bf16[768,768]{1,0:T(8,128)(2,1)S(1)}, u32[]{:S(2)}, u32[]{:S(2)}) collective-permute-start(bf16[768,768]{1,0:T(8,128)(2,1)S(1)} %get-tuple-element.392), channel_id=1, source_target_pairs={{0,16},{16,0},{1,17},{17,1},{2,18},{18,2},{3,19},{19,3},{4,20},{20... | collective-permute-start | bytes 3538952 | tf_op jit(solution)/shard_map/ppermute | solution.py:22
  243.4 11.8 %collective-permute-start.79 = (bf16[2,192,384]{2,1,0:T(8,128)(2,1)S(1)}, bf16[2,192,384]{2,1,0:T(8,128)(2,1)S(1)}, u32[]{:S(2)}, u32[]{:S(2)}) collective-permute-start(bf16[2,192,384]{2,1,0:T(8,128)(2,1)S(1)} %get-tuple-element.435), channel_id=1, source_target_pairs={{0,4},{4,0},{8,12},{12,8},{1,5},{5,1},{9,13},{13,9},{2,6},{6,2},{1... | collective-permute-start | bytes 884744 | tf_op jit(solution)/shard_map/ppermute | solution.py:22
  273.6 14.5 %collective-permute-start.90 = (bf16[192,384]{1,0:T(8,128)(2,1)S(1)}, bf16[192,384]{1,0:T(8,128)(2,1)S(1)}, u32[]{:S(2)}, u32[]{:S(2)}) collective-permute-start(bf16[192,384]{1,0:T(8,128)(2,1)S(1)} %fusion.14), channel_id=1, source_target_pairs={{0,8},{4,12},{8,0},{12,4},{1,9},{5,13},{9,1},{13,5},{2,10},{6,14},... | collective-permute-start | bytes 442376 | tf_op jit(solution)/shard_map/ppermute | solution.py:22
  281.0 21.0 %collective-permute-start.95 = (bf16[192,768]{1,0:T(8,128)(2,1)S(1)}, bf16[192,768]{1,0:T(8,128)(2,1)S(1)}, u32[]{:S(2)}, u32[]{:S(2)}) collective-permute-start(bf16[192,768]{1,0:T(8,128)(2,1)S(1)} %get-tuple-element.536), channel_id=1, source_target_pairs={{0,16},{16,0},{1,17},{17,1},{2,18},{18,2},{3,19},{19,3},{4,20},{20... | collective-permute-start | bytes 884744 | tf_op jit(solution)/shard_map/ppermute | solution.py:22
  288.2 11.0 %collective-permute-start.94 = (bf16[192,384]{1,0:T(8,128)(2,1)S(1)}, bf16[192,384]{1,0:T(8,128)(2,1)S(1)}, u32[]{:S(2)}, u32[]{:S(2)}) collective-permute-start(bf16[192,384]{1,0:T(8,128)(2,1)S(1)} %get-tuple-element.531), channel_id=1, source_target_pairs={{0,16},{16,0},{1,17},{17,1},{2,18},{18,2},{3,19},{19,3},{4,20},{20... | collective-permute-start | bytes 442376 | tf_op jit(solution)/shard_map/ppermute | solution.py:22
  (169 other events, 1203.1 us)
Sparse Core Ops, SparseCore 0:
  46.6 34.8 all-gather.2
  86.5 29.2 all-gather.4

commit v6 on v5

--- a/solution.py
+++ b/solution.py
@@ -363,10 +363,15 @@
     return pl.ds(pl.multiple_of((place[1] ^ k) * rows, 16), rows)
 
 
-def stack_body(place, pair, other_pair, out):
-    rows = pair.shape[1]
-    for k, block in enumerate((pair[0], other_pair[0], pair[1], other_pair[1])):
-        out[line_blocks(place, k, rows)] = block
+def stack_body(place, *refs):
+    out = refs[-1]
+    pieces = len(refs) // 2
+    _, rows, wide = refs[0].shape
+    for piece in range(pieces):
+        pair, other = refs[piece], refs[pieces + piece]
+        columns = slice(piece * wide, (piece + 1) * wide)
+        for k, block in enumerate((pair[0], other[0], pair[1], other[1])):
+            out[line_blocks(place, k, rows), columns] = block
 
 
 def line_parts_body(place, keep, received, *outs):
@@ -585,31 +590,28 @@
     else:
         activated_all = lax.all_gather(activated, "dp", axis=0).reshape(line_size * micro, -1)
 
-    def along_line(value):
-        return lax.all_gather(value, "dp", axis=0, tiled=True)
-
     def line_first(value):
         return jnp.stack([value, swap(value, "dp", 2)]) if direct else value
 
     def line_second(pair):
-        if not direct:
-            return along_line(pair)
-        return run(
-            "stack_line",
-            stack_body,
-            [shape((model, pair.shape[2]), BF16)],
-            [pair, swap(pair, "dp", 1)],
-            place,
-        )[0]
-
-    def both_cores(lined, ready):
-        lined = after(lined, ready)
+        if direct:
+            return swap(pair, "dp", 1)
+        return lax.all_gather(pair, "dp", axis=0, tiled=True)
+
+    def both_cores(pairs, others):
+        if direct:
+            wide = sum(pair.shape[2] for pair in pairs)
+            lined = run(
+                "stack_line", stack_body, [shape((model, wide), BF16)], pairs + others, place
+            )[0]
+        else:
+            lined = jnp.concatenate(others, axis=1)
         return lined, swap(lined, "pipe", 1)
 
-    def half_of(layer, mlp):
-        return halves_of_layers[layer][:, split:] if mlp else halves_of_layers[layer][:, :split]
-
-    lined_a0 = along_line(half_of(0, False))
+    def piece_of(layer, index):
+        return halves_of_layers[layer][:, index * split : (index + 1) * split]
+
+    first_a0 = line_first(piece_of(0, 0))
 
     if direct:
         mod_partial = run(
@@ -618,15 +620,16 @@
             [shape((micro * LINE, columns), F32)],
             activated_all + [own_rows],
         )[0]
-        mod_partials, lined_a0 = tie(gather(mod_partial, "tensor"), lined_a0)
-        w_attn0 = both_cores(lined_a0, mod_partials)
-        lined_m0 = along_line(after(half_of(0, True), lined_a0))
+        mod_partials, first_a0 = tie(gather(mod_partial, "tensor"), first_a0)
+        second_a0 = line_second(first_a0)
+        first_e0 = line_first(after(piece_of(0, 1), first_a0))
         pieces = run(
             "mod_sum",
             functools.partial(mod_sum_body, count),
             [shape((micro, columns), F32)] * LINE,
             mod_partials,
         )
+        pieces, second_a0 = tie(exchange(pieces, "dp"), second_a0)
         mod_mine, mod_other = pl.pallas_call(
             mod_join_body,
             out_shape=[shape((1, mods), F32)] * 2,
@@ -635,19 +638,22 @@
             out_specs=[pl.BlockSpec(memory_space=pltpu.VMEM)] * 2,
             scratch_shapes=[pltpu.VMEM((LINE, micro, columns), F32)],
             name="mod_join",
-        )(place, *exchange(pieces, "dp"), modulation_bias)
+        )(place, *pieces, modulation_bias)
     else:
         mod_partial = dot(activated_all, own_rows)
         mod_partials = gather(mod_partial, "tensor")
-        w_attn0 = both_cores(lined_a0, mod_partials)
-        lined_m0 = along_line(after(half_of(0, True), lined_a0))
+        second_a0 = line_second(first_a0)
+        first_e0 = line_first(piece_of(0, 1))
         mod_sum = tree_sum(mod_partials).reshape(line_size, micro, -1)
         mod_layer = lax.all_to_all(mod_sum, "dp", split_axis=0, concat_axis=0)
         mod_layer = jnp.swapaxes(mod_layer, 0, 1).reshape(micro, -1) + modulation_bias
         mod_mine, mod_other = mine(mod_layer)[None], other(mod_layer)[None]
     mod0, mod1 = both_layers(mod_mine, swap(mod_other, "pipe", 1))
 
-    pair_a1 = line_first(after(half_of(1, False), mod0))
+    w_attn0 = both_cores([first_a0], [second_a0])
+    mod0, mod1, first_e0 = tie(mod0, mod1, first_e0)
+    second_e0 = line_second(first_e0)
+    first_s0 = line_first(after(piece_of(0, 2), first_e0))
     own_f32 = shape((own, model), F32)
     own_bf16 = shape((own, model), BF16)
     blocks = [own_bf16] * count
@@ -687,14 +693,19 @@
             "middle", middle_body, [own_f32, own_f32, own_bf16], parts + [bias, h, mod]
         )
 
-    attn_rows, pair_a1 = tie(gather(attn_in, "tensor"), pair_a1)
-    lined_a1 = line_second(pair_a1)
+    attn_rows, second_e0, first_s0 = tie(gather(attn_in, "tensor"), second_e0, first_s0)
+    second_s0 = line_second(first_s0)
+    first_a1 = line_first(after(piece_of(1, 0), first_s0))
     kept_attn0, parts = attention(attn_rows, w_attn0, biases[0][0])
-    w_mlp0 = both_cores(lined_m0, parts)
-    lined_m1 = along_line(after(half_of(1, True), w_mlp0[0]))
+    parts, second_s0, first_a1 = tie(parts, second_s0, first_a1)
+    w_mlp0 = both_cores([first_e0, first_s0], [second_e0, second_s0])
+    second_a1 = line_second(first_a1)
+    first_e1 = line_first(after(piece_of(1, 1), first_a1))
     attended0, middle0, mlp_in = middle_of(parts, biases[0][1], h0, mod0)
-    mlp_rows0 = gather(mlp_in, "tensor")
-    w_attn1 = both_cores(lined_a1, mlp_rows0)
+    mlp_rows0, second_a1, first_e1 = tie(gather(mlp_in, "tensor"), second_a1, first_e1)
+    w_attn1 = both_cores([first_a1], [second_a1])
+    second_e1 = line_second(first_e1)
+    first_s1 = line_first(after(piece_of(1, 2), first_e1))
     outs = kernel(
         "feed_forward",
         mlp_body,
@@ -702,16 +713,19 @@
         mlp_rows0 + [w_mlp0[0], w_mlp0[1], biases[0][2]],
     )
     mlp_rows0, pre0, hidden0 = outs[:3]
+    parts, second_e1, first_s1 = tie(exchange(outs[3:], "tensor"), second_e1, first_s1)
+    second_s1 = line_second(first_s1)
     shrunk0, passed, h1, attn_in = kernel(
         "between",
         between_body,
         [own_f32, own_bf16, own_f32, own_bf16],
-        exchange(outs[3:], "tensor") + [biases[0][3], middle0, mod0, mod1],
+        parts + [biases[0][3], middle0, mod0, mod1],
     )
 
     g_rows1 = gather(g_shrunk1, "tensor")
-    kept_attn1, parts = attention(gather(attn_in, "tensor"), w_attn1, biases[1][0])
-    w_mlp1 = both_cores(lined_m1, parts)
+    attn_rows, second_s1 = tie(gather(attn_in, "tensor"), second_s1)
+    w_mlp1 = both_cores([first_e1, first_s1], [second_e1, second_s1])
+    kept_attn1, parts = attention(attn_rows, w_attn1, biases[1][0])
     attended1, middle1, mlp_in = middle_of(parts, biases[1][1], h1, mod1)
     outs = kernel(
         "feed_forward_both",
@@ -860,15 +874,7 @@
     far_e0 = line_far(parts_e0, near_e0)
     near_s0 = line_near(parts_s0)
     (g_rows, g_joint, joint_grad0), parts = attention_back(g_rows, w_attn0, kept_attn0)
-    parts, (parts_a0,), far_e0, near_s0, parts_s0 = tie(
-        parts,
-        line_parts(attn_weight_grads(kept_attn0, g_joint, g_rows), 1),
-        far_e0,
-        near_s0,
-        parts_s0,
-    )
-    near_a0 = line_near(parts_a0)
-    far_s0 = line_far(parts_s0, near_s0)
+    (parts_a0,) = line_parts(attn_weight_grads(kept_attn0, g_joint, g_rows), 1)
     g_h0, g_shift_attn0, g_scale_attn0 = kernel(
         "finish_back",
         finish_back_body,
@@ -904,10 +910,11 @@
             shrink_grad1,
         ],
     )[0]
-    packed_all, near_a0, far_s0, parts_a0 = tie(
-        gather(packed, "tensor"), near_a0, far_s0, parts_a0
-    )
-    far_a0 = line_far(parts_a0, near_a0)
+    packed_all, parts_a0, far_e0, near_s0, parts_s0 = tie(
+        gather(packed, "tensor"), parts_a0, far_e0, near_s0, parts_s0
+    )
+    near_a0 = line_near(parts_a0)
+    far_s0 = line_far(parts_s0, near_s0)
     keep, give = run(
         "grads_sum",
         functools.partial(grads_sum_body, count),
@@ -923,7 +930,8 @@
         place,
     )[0]
     joined_all = gather(joined, "dp") if direct else lax.all_gather(joined, "dp", axis=0, tiled=True)
-    joined_all, far_a0 = tie(joined_all, far_a0)
+    joined_all, near_a0, far_s0 = tie(joined_all, near_a0, far_s0)
+    far_a0 = line_far(parts_a0, near_a0)
     mlp_grad0, mlp_grad1 = (
         jnp.concatenate([line_total(*first_piece), line_total(*second_piece)], axis=1)
         for first_piece, second_piece in (

time: 312 us -> 273 us (0.88)
  local copies, waits for them, and re-layouts: 36.7 us -> 7.64 us
  starting transfers between devices: 98.8 us -> 119 us
  blocking collectives: 16.5 us -> 0 us
  between operations: 15.5 us -> 1.48 us
    unnamed x195 -> x37, local copies, waits for them, and re-layouts: 32.6 us -> 5.55 us
    ppermute x96 -> x106, starting transfers between devices: 98.5 us -> 119 us  [swap(): return lax.ppermute(value, axis, pairs)]
    all_gather x1 -> x0, blocking collectives: 16.5 us -> none  [along_line(): return lax.all_gather(value, 'dp', axis=0, tiled=True)]
    pallas_call x33 -> x36, Pallas kernels: 31.6 us -> 33.1 us  [run(): pl.pallas_call(body, out_shape=outs, in_specs=specs, out_specs=[pl.BlockS...]
    ppermute x96 -> x106, waiting for transfers between devices: 106 us -> 107 us  [swap(): return lax.ppermute(value, axis, pairs)]
  transfers between devices with their start and end apart: 98 -> 106, of which waited for: 48 -> 60; matrix products, arithmetic and copies ran while one was open for 3% -> 2% of each run, Pallas kernels for 6% -> 6%
where the time goes in v6:
time: 273 us
  starting transfers between devices  119 us (44%)
  waiting for transfers between devices  107 us (39%)
  Pallas kernels  34.6 us (13%)
  local copies, waits for them, and re-layouts  7.64 us (3%)
  other arithmetic  3.58 us (1%)
    ppermute x106, starting transfers between devices, swap(): return lax.ppermute(value, axis, pairs)  119 us
    ppermute x106, waiting for transfers between devices, swap(): return lax.ppermute(value, axis, pairs)  107 us
    pallas_call x36, Pallas kernels, run(): pl.pallas_call(body, out_shape=outs, in_specs=specs, out_specs=[pl.BlockS...  33.1 us
    unnamed x37, local copies, waits for them, and re-layouts  5.55 us
  transfers between devices with their start and end apart: 106, of which 60 were waited for; matrix products, arithmetic and copies ran while one was open for 2% of the time, Pallas kernels for 6%

profile of v6, /device:TPU:0, one launch (start us, length us, event | category | flops | bytes accessed | tf_op | source)
XLA Modules:
  0.0 272.7 jit_solution(16700525223396294827)
XLA Ops:
  3.9 5.0 %collective-permute-start.2 = (bf16[2,192]{1,0:T(2,128)(2,1)S(1)}, bf16[2,192]{1,0:T(2,128)(2,1)S(1)}, u32[]{:S(2)}, u32[]{:S(2)}) collective-permute-start(bf16[2,192]{1,0:T(2,128)(2,1)S(1)} %fusion.26.a0), channel_id=1, source_target_pairs={{0,12},{4,8},{8,4},{12,0},{1,13},{5,9},{9,5},{13,1},{2,14},{6,10},... | collective-permute-start | bytes 2312 | tf_op jit(solution)/shard_map/ppermute | solution.py:22
  13.6 2.5 collective-permute-start.5
  17.1 2.5 collective-permute-done.7
  27.1 2.8 %collective-permute-done.8.p1 = f32[2,1152]{1,0:T(2,128)S(1)} collective-permute-done((f32[2,1152]{1,0:T(2,128)S(1)}, f32[2,1152]{1,0:T(2,128)S(1)}, u32[]{:S(2)}, u32[]{:S(2)}) %collective-permute-start.8) | collective-permute-done | bytes 9248 | tf_op jit(solution)/shard_map/ppermute | solution.py:22
  29.9 2.4 collective-permute-done.10.p3
  42.2 4.1 %collective-permute-done.18 = bf16[192,384]{1,0:T(8,128)(2,1)S(1)} collective-permute-done((bf16[192,384]{1,0:T(8,128)(2,1)S(1)}, bf16[192,384]{1,0:T(8,128)(2,1)S(1)}, u32[]{:S(2)}, u32[]{:S(2)}) %collective-permute-start.18) | collective-permute-done | bytes 147488 | tf_op jit(solution)/shard_map/ppermute | solution.py:22
  47.9 3.0 %collective-permute-done.14.refs_1_ = bf16[64,768]{1,0:T(8,128)(2,1)S(1)} collective-permute-done((bf16[64,768]{1,0:T(8,128)(2,1)S(1)}, bf16[64,768]{1,0:T(8,128)(2,1)S(1)}, u32[]{:S(2)}, u32[]{:S(2)}) %collective-permute-start.14) | collective-permute-done | bytes 98336 | tf_op jit(solution)/shard_map/ppermute | solution.py:22
  50.9 3.0 %collective-permute-start.24 = (bf16[2,192,384]{2,1,0:T(8,128)(2,1)S(1)}, bf16[2,192,384]{2,1,0:T(8,128)(2,1)S(1)}, u32[]{:S(2)}, u32[]{:S(2)}) collective-permute-start(bf16[2,192,384]{2,1,0:T(8,128)(2,1)S(1)} %pad_maximum_fusion.4.refs_1_), channel_id=1, source_target_pairs={{0,4},{4,0},{8,12},{12,8},{1,5},{5,1},{9,13},{13,9},{2,6},{6,2},{1... | collective-permute-start | bytes 884744 | tf_op jit(solution)/shard_map/ppermute | solution.py:22
  70.8 7.2 %collective-permute-done.30 = bf16[192,384]{1,0:T(8,128)(2,1)S(1)} collective-permute-done((bf16[192,384]{1,0:T(8,128)(2,1)S(1)}, bf16[192,384]{1,0:T(8,128)(2,1)S(1)}, u32[]{:S(2)}, u32[]{:S(2)}) %collective-permute-start.30) | collective-permute-done | bytes 147488 | tf_op jit(solution)/shard_map/ppermute | solution.py:22
  78.6 4.1 %collective-permute-done.26.refs_1_ = bf16[64,768]{1,0:T(8,128)(2,1)S(1)} collective-permute-done((bf16[64,768]{1,0:T(8,128)(2,1)S(1)}, bf16[64,768]{1,0:T(8,128)(2,1)S(1)}, u32[]{:S(2)}, u32[]{:S(2)}) %collective-permute-start.26) | collective-permute-done | bytes 98336 | tf_op jit(solution)/shard_map/ppermute | solution.py:22
  82.7 2.6 collective-permute-start.35
  88.3 2.4 collective-permute-start.34
  90.8 2.6 collective-permute-done.36
  94.1 2.7 collective-permute-start.40
  105.7 2.5 collective-permute-done.41.refs_5_
  117.5 6.4 %collective-permute-done.43.refs_2_ = bf16[64,768]{1,0:T(8,128)(2,1)S(1)} collective-permute-done((bf16[64,768]{1,0:T(8,128)(2,1)S(1)}, bf16[64,768]{1,0:T(8,128)(2,1)S(1)}, u32[]{:S(2)}, u32[]{:S(2)}) %collective-permute-start.43) | collective-permute-done | bytes 98336 | tf_op jit(solution)/shard_map/ppermute | solution.py:22
  147.5 2.6 collective-permute-done.62.refs_3_
  162.4 3.5 %collective-permute-done.65.refs_2_ = bf16[64,768]{1,0:T(8,128)(2,1)S(1)} collective-permute-done((bf16[64,768]{1,0:T(8,128)(2,1)S(1)}, bf16[64,768]{1,0:T(8,128)(2,1)S(1)}, u32[]{:S(2)}, u32[]{:S(2)}) %collective-permute-start.65) | collective-permute-done | bytes 98336 | tf_op jit(solution)/shard_map/ppermute | solution.py:22
  174.8 3.1 %collective-permute-done.72.refs_3_ = bf16[64,768]{1,0:T(8,128)(2,1)S(1)} collective-permute-done((bf16[64,768]{1,0:T(8,128)(2,1)S(1)}, bf16[64,768]{1,0:T(8,128)(2,1)S(1)}, u32[]{:S(2)}, u32[]{:S(2)}) %collective-permute-start.72) | collective-permute-done | bytes 98336 | tf_op jit(solution)/shard_map/ppermute | solution.py:22
  187.6 3.1 %collective-permute-done.57.refs_2_ = bf16[64,768]{1,0:T(8,128)(2,1)S(1)} collective-permute-done((bf16[64,768]{1,0:T(8,128)(2,1)S(1)}, bf16[64,768]{1,0:T(8,128)(2,1)S(1)}, u32[]{:S(2)}, u32[]{:S(2)}) %collective-permute-start.57) | collective-permute-done | bytes 98336 | tf_op jit(solution)/shard_map/ppermute | solution.py:22
  198.8 5.3 %collective-permute-done.79 = bf16[192,384]{1,0:T(8,128)(2,1)S(1)} collective-permute-done((bf16[192,384]{1,0:T(8,128)(2,1)S(1)}, bf16[192,384]{1,0:T(8,128)(2,1)S(1)}, u32[]{:S(2)}, u32[]{:S(2)}) %collective-permute-start.79) | collective-permute-done | bytes 147488 | tf_op jit(solution)/shard_map/ppermute | solution.py:22
  222.7 2.7 collective-permute-start.92
  233.2 3.1 %collective-permute-done.93 = bf16[2,192,384]{2,1,0:T(8,128)(2,1)S(1)} collective-permute-done((bf16[2,192,384]{2,1,0:T(8,128)(2,1)S(1)}, bf16[2,192,384]{2,1,0:T(8,128)(2,1)S(1)}, u32[]{:S(2)}, u32[]{:S(2)}) %collective-permute-start.93) | collective-permute-done | bytes 294944 | tf_op jit(solution)/shard_map/ppermute | solution.py:22
  244.8 7.7 %collective-permute-done.97.g3 = f32[1,11904]{1,0:T(1,128)S(1)} collective-permute-done((f32[1,11904]{1,0:T(1,128)S(1)}, f32[1,11904]{1,0:T(1,128)S(1)}, u32[]{:S(2)}, u32[]{:S(2)}) %collective-permute-start.97) | collective-permute-done | bytes 47648 | tf_op jit(solution)/shard_map/ppermute | solution.py:22
  (316 shorter events, 184.3 us)
Async XLA Ops:
  12.5 14.4 %collective-permute-start.20 = (f32[1,2688]{1,0:T(1,128)S(1)}, f32[1,2688]{1,0:T(1,128)S(1)}, u32[]{:S(2)}, u32[]{:S(2)}) collective-permute-start(f32[1,2688]{1,0:T(1,128)S(1)} %broadcast_in_dim.24), channel_id=1, source_target_pairs={{0,16},{16,0},{1,17},{17,1},{2,18},{18,2},{3,19},{19,3},{4,20},{20... | collective-permute-start | bytes 32264 | tf_op jit(solution)/shard_map/ppermute | solution.py:22
  20.5 11.9 %collective-permute-start.11 = (bf16[2,192,384]{2,1,0:T(8,128)(2,1)S(1)}, bf16[2,192,384]{2,1,0:T(8,128)(2,1)S(1)}, u32[]{:S(2)}, u32[]{:S(2)}) collective-permute-start(bf16[2,192,384]{2,1,0:T(8,128)(2,1)S(1)} %pad_maximum_fusion.2.refs_0_), channel_id=1, source_target_pairs={{0,4},{4,0},{8,12},{12,8},{1,5},{5,1},{9,13},{13,9},{2,6},{6,2},{1... | collective-permute-start | bytes 884744 | tf_op jit(solution)/shard_map/ppermute | solution.py:22
  35.7 18.7 %collective-permute-start.19 = (bf16[768,384]{1,0:T(8,128)(2,1)S(1)}, bf16[768,384]{1,0:T(8,128)(2,1)S(1)}, u32[]{:S(2)}, u32[]{:S(2)}) collective-permute-start(bf16[768,384]{1,0:T(8,128)(2,1)S(1)} %stack_line.4.refs_4_), channel_id=1, source_target_pairs={{0,16},{16,0},{1,17},{17,1},{2,18},{18,2},{3,19},{19,3},{4,20},{20... | collective-permute-start | bytes 1769480 | tf_op jit(solution)/shard_map/ppermute | solution.py:22
  35.9 15.0 %collective-permute-start.17 = (bf16[2,192,384]{2,1,0:T(8,128)(2,1)S(1)}, bf16[2,192,384]{2,1,0:T(8,128)(2,1)S(1)}, u32[]{:S(2)}, u32[]{:S(2)}) collective-permute-start(bf16[2,192,384]{2,1,0:T(8,128)(2,1)S(1)} %pad_maximum_fusion.3.refs_0_), channel_id=1, source_target_pairs={{0,4},{4,0},{8,12},{12,8},{1,5},{5,1},{9,13},{13,9},{2,6},{6,2},{1... | collective-permute-start | bytes 884744 | tf_op jit(solution)/shard_map/ppermute | solution.py:22
  50.9 11.8 %collective-permute-start.24 = (bf16[2,192,384]{2,1,0:T(8,128)(2,1)S(1)}, bf16[2,192,384]{2,1,0:T(8,128)(2,1)S(1)}, u32[]{:S(2)}, u32[]{:S(2)}) collective-permute-start(bf16[2,192,384]{2,1,0:T(8,128)(2,1)S(1)} %pad_maximum_fusion.4.refs_1_), channel_id=1, source_target_pairs={{0,4},{4,0},{8,12},{12,8},{1,5},{5,1},{9,13},{13,9},{2,6},{6,2},{1... | collective-permute-start | bytes 884744 | tf_op jit(solution)/shard_map/ppermute | solution.py:22
  65.9 20.2 %collective-permute-start.31 = (bf16[768,768]{1,0:T(8,128)(2,1)S(1)}, bf16[768,768]{1,0:T(8,128)(2,1)S(1)}, u32[]{:S(2)}, u32[]{:S(2)}) collective-permute-start(bf16[768,768]{1,0:T(8,128)(2,1)S(1)} %stack_line.5.refs_4_), channel_id=1, source_target_pairs={{0,16},{16,0},{1,17},{17,1},{2,18},{18,2},{3,19},{19,3},{4,20},{20... | collective-permute-start | bytes 3538952 | tf_op jit(solution)/shard_map/ppermute | solution.py:22
  65.9 16.7 %collective-permute-start.29 = (bf16[2,192,384]{2,1,0:T(8,128)(2,1)S(1)}, bf16[2,192,384]{2,1,0:T(8,128)(2,1)S(1)}, u32[]{:S(2)}, u32[]{:S(2)}) collective-permute-start(bf16[2,192,384]{2,1,0:T(8,128)(2,1)S(1)} %pad_maximum_fusion.5.refs_0_), channel_id=1, source_target_pairs={{0,4},{4,0},{8,12},{12,8},{1,5},{5,1},{9,13},{13,9},{2,6},{6,2},{1... | collective-permute-start | bytes 884744 | tf_op jit(solution)/shard_map/ppermute | solution.py:22
  68.0 10.0 %collective-permute-start.30 = (bf16[192,384]{1,0:T(8,128)(2,1)S(1)}, bf16[192,384]{1,0:T(8,128)(2,1)S(1)}, u32[]{:S(2)}, u32[]{:S(2)}) collective-permute-start(bf16[192,384]{1,0:T(8,128)(2,1)S(1)} %get-tuple-element.321), channel_id=1, source_target_pairs={{0,8},{4,12},{8,0},{12,4},{1,9},{5,13},{9,1},{13,5},{2,10},{6,14},... | collective-permute-start | bytes 442376 | tf_op jit(solution)/shard_map/ppermute | solution.py:22
  68.5 10.1 %collective-permute-start.28 = (bf16[64,768]{1,0:T(8,128)(2,1)S(1)}, bf16[64,768]{1,0:T(8,128)(2,1)S(1)}, u32[]{:S(2)}, u32[]{:S(2)}) collective-permute-start(bf16[64,768]{1,0:T(8,128)(2,1)S(1)} %get-tuple-element.322.refs_0_), channel_id=1, source_target_pairs={{0,3},{1,2},{2,1},{3,0},{4,7},{5,6},{6,5},{7,4},{8,11},{9,10},{10,... | collective-permute-start | bytes 294920 | tf_op jit(solution)/shard_map/ppermute | solution.py:22
  82.7 11.4 %collective-permute-start.35 = (bf16[2,192,384]{2,1,0:T(8,128)(2,1)S(1)}, bf16[2,192,384]{2,1,0:T(8,128)(2,1)S(1)}, u32[]{:S(2)}, u32[]{:S(2)}) collective-permute-start(bf16[2,192,384]{2,1,0:T(8,128)(2,1)S(1)} %pad_maximum_fusion.6.refs_0_), channel_id=1, source_target_pairs={{0,4},{4,0},{8,12},{12,8},{1,5},{5,1},{9,13},{13,9},{2,6},{6,2},{1... | collective-permute-start | bytes 884744 | tf_op jit(solution)/shard_map/ppermute | solution.py:22
  104.4 28.1 %collective-permute-start.51 = (bf16[768,768]{1,0:T(8,128)(2,1)S(1)}, bf16[768,768]{1,0:T(8,128)(2,1)S(1)}, u32[]{:S(2)}, u32[]{:S(2)}) collective-permute-start(bf16[768,768]{1,0:T(8,128)(2,1)S(1)} %stack_line.7.refs_8_), channel_id=1, source_target_pairs={{0,16},{16,0},{1,17},{17,1},{2,18},{18,2},{3,19},{19,3},{4,20},{20... | collective-permute-start | bytes 3538952 | tf_op jit(solution)/shard_map/ppermute | solution.py:22
  111.8 14.3 %collective-permute-start.50 = (bf16[64,768]{1,0:T(8,128)(2,1)S(1)}, bf16[64,768]{1,0:T(8,128)(2,1)S(1)}, u32[]{:S(2)}, u32[]{:S(2)}) collective-permute-start(bf16[64,768]{1,0:T(8,128)(2,1)S(1)} %get-tuple-element.353.refs_4_.refs_8_), channel_id=1, source_target_pairs={{0,3},{1,2},{2,1},{3,0},{4,7},{5,6},{6,5},{7,4},{8,11},{9,10},{10,... | collective-permute-start | bytes 294920 | tf_op jit(solution)/shard_map/ppermute | solution.py:22
  113.4 14.3 %collective-permute-start.49 = (bf16[64,768]{1,0:T(8,128)(2,1)S(1)}, bf16[64,768]{1,0:T(8,128)(2,1)S(1)}, u32[]{:S(2)}, u32[]{:S(2)}) collective-permute-start(bf16[64,768]{1,0:T(8,128)(2,1)S(1)} %get-tuple-element.353.refs_4_.refs_8_), channel_id=1, source_target_pairs={{0,2},{1,3},{2,0},{3,1},{4,6},{5,7},{6,4},{7,5},{8,10},{9,11},{10,... | collective-permute-start | bytes 294920 | tf_op jit(solution)/shard_map/ppermute | solution.py:22
  113.9 10.0 %collective-permute-start.43 = (bf16[64,768]{1,0:T(8,128)(2,1)S(1)}, bf16[64,768]{1,0:T(8,128)(2,1)S(1)}, u32[]{:S(2)}, u32[]{:S(2)}) collective-permute-start(bf16[64,768]{1,0:T(8,128)(2,1)S(1)} %get-tuple-element.349), channel_id=1, source_target_pairs={{0,2},{1,3},{2,0},{3,1},{4,6},{5,7},{6,4},{7,5},{8,10},{9,11},{10,... | collective-permute-start | bytes 294920 | tf_op jit(solution)/shard_map/ppermute | solution.py:22
  155.3 12.8 %collective-permute-start.69 = (bf16[2,192,384]{2,1,0:T(8,128)(2,1)S(1)}, bf16[2,192,384]{2,1,0:T(8,128)(2,1)S(1)}, u32[]{:S(2)}, u32[]{:S(2)}) collective-permute-start(bf16[2,192,384]{2,1,0:T(8,128)(2,1)S(1)} %get-tuple-element.416), channel_id=1, source_target_pairs={{0,4},{4,0},{8,12},{12,8},{1,5},{5,1},{9,13},{13,9},{2,6},{6,2},{1... | collective-permute-start | bytes 884744 | tf_op jit(solution)/shard_map/ppermute | solution.py:22
  168.1 11.9 %collective-permute-start.73 = (bf16[2,192,384]{2,1,0:T(8,128)(2,1)S(1)}, bf16[2,192,384]{2,1,0:T(8,128)(2,1)S(1)}, u32[]{:S(2)}, u32[]{:S(2)}) collective-permute-start(bf16[2,192,384]{2,1,0:T(8,128)(2,1)S(1)} %get-tuple-element.426), channel_id=1, source_target_pairs={{0,4},{4,0},{8,12},{12,8},{1,5},{5,1},{9,13},{13,9},{2,6},{6,2},{1... | collective-permute-start | bytes 884744 | tf_op jit(solution)/shard_map/ppermute | solution.py:22
  182.4 14.5 %collective-permute-start.78 = (bf16[768,768]{1,0:T(8,128)(2,1)S(1)}, bf16[768,768]{1,0:T(8,128)(2,1)S(1)}, u32[]{:S(2)}, u32[]{:S(2)}) collective-permute-start(bf16[768,768]{1,0:T(8,128)(2,1)S(1)} %get-tuple-element.445), channel_id=1, source_target_pairs={{0,16},{16,0},{1,17},{17,1},{2,18},{18,2},{3,19},{19,3},{4,20},{20... | collective-permute-start | bytes 3538952 | tf_op jit(solution)/shard_map/ppermute | solution.py:22
  222.7 10.5 %collective-permute-start.92 = (bf16[192,384]{1,0:T(8,128)(2,1)S(1)}, bf16[192,384]{1,0:T(8,128)(2,1)S(1)}, u32[]{:S(2)}, u32[]{:S(2)}) collective-permute-start(bf16[192,384]{1,0:T(8,128)(2,1)S(1)} %fusion.16), channel_id=1, source_target_pairs={{0,8},{4,12},{8,0},{12,4},{1,9},{5,13},{9,1},{13,5},{2,10},{6,14},... | collective-permute-start | bytes 442376 | tf_op jit(solution)/shard_map/ppermute | solution.py:22
  225.4 10.8 %collective-permute-start.93 = (bf16[2,192,384]{2,1,0:T(8,128)(2,1)S(1)}, bf16[2,192,384]{2,1,0:T(8,128)(2,1)S(1)}, u32[]{:S(2)}, u32[]{:S(2)}) collective-permute-start(bf16[2,192,384]{2,1,0:T(8,128)(2,1)S(1)} %get-tuple-element.507), channel_id=1, source_target_pairs={{0,4},{4,0},{8,12},{12,8},{1,5},{5,1},{9,13},{13,9},{2,6},{6,2},{1... | collective-permute-start | bytes 884744 | tf_op jit(solution)/shard_map/ppermute | solution.py:22
  236.9 15.7 %collective-permute-start.98 = (bf16[2,192,384]{2,1,0:T(8,128)(2,1)S(1)}, bf16[2,192,384]{2,1,0:T(8,128)(2,1)S(1)}, u32[]{:S(2)}, u32[]{:S(2)}) collective-permute-start(bf16[2,192,384]{2,1,0:T(8,128)(2,1)S(1)} %get-tuple-element.520), channel_id=1, source_target_pairs={{0,4},{4,0},{8,12},{12,8},{1,5},{5,1},{9,13},{13,9},{2,6},{6,2},{1... | collective-permute-start | bytes 884744 | tf_op jit(solution)/shard_map/ppermute | solution.py:22
  238.8 13.8 %collective-permute-start.99 = (bf16[192,384]{1,0:T(8,128)(2,1)S(1)}, bf16[192,384]{1,0:T(8,128)(2,1)S(1)}, u32[]{:S(2)}, u32[]{:S(2)}) collective-permute-start(bf16[192,384]{1,0:T(8,128)(2,1)S(1)} %fusion.15), channel_id=1, source_target_pairs={{0,8},{4,12},{8,0},{12,4},{1,9},{5,13},{9,1},{13,5},{2,10},{6,14},... | collective-permute-start | bytes 442376 | tf_op jit(solution)/shard_map/ppermute | solution.py:22
  240.3 12.2 %collective-permute-start.97 = (f32[1,11904]{1,0:T(1,128)S(1)}, f32[1,11904]{1,0:T(1,128)S(1)}, u32[]{:S(2)}, u32[]{:S(2)}) collective-permute-start(f32[1,11904]{1,0:T(1,128)S(1)} %grads_join.1.g0), channel_id=1, source_target_pairs={{0,12},{4,8},{8,4},{12,0},{1,13},{5,9},{9,5},{13,1},{2,14},{6,10},... | collective-permute-start | bytes 142856 | tf_op jit(solution)/shard_map/ppermute | solution.py:22
  242.1 10.4 %collective-permute-start.96 = (f32[1,11904]{1,0:T(1,128)S(1)}, f32[1,11904]{1,0:T(1,128)S(1)}, u32[]{:S(2)}, u32[]{:S(2)}) collective-permute-start(f32[1,11904]{1,0:T(1,128)S(1)} %grads_join.1.g0), channel_id=1, source_target_pairs={{0,8},{4,12},{8,0},{12,4},{1,9},{5,13},{9,1},{13,5},{2,10},{6,14},... | collective-permute-start | bytes 142856 | tf_op jit(solution)/shard_map/ppermute | solution.py:22
  255.1 10.7 %collective-permute-start.103 = (bf16[192,384]{1,0:T(8,128)(2,1)S(1)}, bf16[192,384]{1,0:T(8,128)(2,1)S(1)}, u32[]{:S(2)}, u32[]{:S(2)}) collective-permute-start(bf16[192,384]{1,0:T(8,128)(2,1)S(1)} %fusion.12), channel_id=1, source_target_pairs={{0,8},{4,12},{8,0},{12,4},{1,9},{5,13},{9,1},{13,5},{2,10},{6,14},... | collective-permute-start | bytes 442376 | tf_op jit(solution)/shard_map/ppermute | solution.py:22
  (98 other events, 580.8 us)

commit v7 on v6

--- a/solution.py
+++ b/solution.py
@@ -130,6 +130,37 @@
     g_y = cotangent[core].astype(F32)
     g_y_out[...] = g_y
     g_shrunk[...] = (part(mod1, 5) * g_y).astype(BF16)
+
+
+def pack_weights_body(place, joint, out, expand, shrink_t, keep, give):
+    first = place[0] == 0
+    width = out.shape[0]
+    half = expand.shape[1] // 2
+    pieces = (
+        (
+            jnp.concatenate([joint[0].astype(F32), joint[1].astype(F32)], axis=1),
+            jnp.concatenate([joint[2].astype(F32), out[...].astype(F32).T], axis=1),
+        ),
+        (expand[:, :half], expand[:, half:]),
+        (shrink_t[:, :half], shrink_t[:, half:]),
+    )
+    at = 0
+    for front, back in pieces:
+        columns = slice(at, at + front.shape[1])
+        keep[:, columns] = jnp.where(first, front, back).astype(BF16)
+        give[:, columns] = jnp.where(first, back, front).astype(BF16)
+        at += front.shape[1]
+
+
+def weight_pieces_body(place, keep, received, *outs):
+    first = place[0] == 0
+    pieces = len(outs) // 2
+    wide = outs[0].shape[1]
+    for piece in range(pieces):
+        own = keep[:, piece * wide : (piece + 1) * wide]
+        other = received[:, piece * wide : (piece + 1) * wide]
+        outs[piece][...] = jnp.where(first, own, other)
+        outs[pieces + piece][...] = jnp.where(first, other, own)
 
 
 def pick_attn(place, own, received):
@@ -391,13 +422,13 @@
         own[...] = block(0)
 
 
-def final_mlp_body(place, mine, received, expand_out, shrink_out):
+def final_mlp_body(place, mine, received, expand_out, shrink_t_out):
     first = place[0] == 0
     half = mine.shape[1] // 2
     own, other = mine[...].astype(F32), received[...].astype(F32)
     for index, values in enumerate((jnp.where(first, own, other), jnp.where(first, other, own))):
         expand_out[:, index * half : (index + 1) * half] = values[:, :half]
-        shrink_out[index * half : (index + 1) * half] = values[:, half:].T
+        shrink_t_out[:, index * half : (index + 1) * half] = values[:, half:]
 
 
 def final_attn_body(place, mine, received, joint_out, out_out):
@@ -405,8 +436,9 @@
     width = mine.shape[1] // 2
     own, other = mine[...].astype(F32), received[...].astype(F32)
     front, back = jnp.where(first, own, other), jnp.where(first, other, own)
-    joint_out[:, : 2 * width] = front
-    joint_out[:, 2 * width :] = back[:, :width]
+    joint_out[0] = front[:, :width]
+    joint_out[1] = front[:, width:]
+    joint_out[2] = back[:, :width]
     out_out[...] = back[:, width:].T
 
 
@@ -540,28 +572,30 @@
     def after(value, earlier):
         return lax.optimization_barrier((value, earlier))[0]
 
-    def tie(*values):
-        return lax.optimization_barrier(values)
-
-    attn_pack = jnp.concatenate(
-        [joint_weight[0].reshape(chunk, 3 * width), output_weight[0].T], axis=1
-    )
-    shrink_t = shrink_weight[0].T
-    expand = expand_weight[0]
-
-    def column_half(index):
-        return jnp.concatenate(
-            [
-                attn_pack[:, index * 2 * width : (index + 1) * 2 * width],
-                expand[:, index * (hidden // 2) : (index + 1) * (hidden // 2)],
-                shrink_t[:, index * (hidden // 2) : (index + 1) * (hidden // 2)],
-            ],
-            axis=1,
-        )
-
-    halves = (column_half(0), column_half(1))
-    halves_of_layers = both_layers(mine(halves), swap(other(halves), "pipe", 1))
+    def tie(main, *rest):
+        return lax.optimization_barrier((lax.optimization_barrier(main),) + rest)
+
     split = 2 * width
+    pieces_shape = shape((chunk, split), BF16)
+    keep, give = run(
+        "pack_weights",
+        pack_weights_body,
+        [shape((chunk, split + 2 * (hidden // 2)), BF16)] * 2,
+        [
+            jnp.transpose(joint_weight[0], (1, 0, 2)),
+            output_weight[0],
+            expand_weight[0],
+            shrink_weight[0].T,
+        ],
+        place,
+    )
+    line_pieces = run(
+        "weight_pieces",
+        weight_pieces_body,
+        [pieces_shape] * 6,
+        [keep, swap(give, "pipe", 1)],
+        place,
+    )
 
     bias_pack = jnp.concatenate(
         [
@@ -609,7 +643,7 @@
         return lined, swap(lined, "pipe", 1)
 
     def piece_of(layer, index):
-        return halves_of_layers[layer][:, index * split : (index + 1) * split]
+        return line_pieces[3 * layer + index]
 
     first_a0 = line_first(piece_of(0, 0))
 
@@ -702,7 +736,10 @@
     second_a1 = line_second(first_a1)
     first_e1 = line_first(after(piece_of(1, 1), first_a1))
     attended0, middle0, mlp_in = middle_of(parts, biases[0][1], h0, mod0)
-    mlp_rows0, second_a1, first_e1 = tie(gather(mlp_in, "tensor"), second_a1, first_e1)
+    g_rows1 = gather(after(g_shrunk1, parts), "tensor")
+    mlp_rows0, second_a1, first_e1, g_rows1 = tie(
+        gather(mlp_in, "tensor"), second_a1, first_e1, g_rows1
+    )
     w_attn1 = both_cores([first_a1], [second_a1])
     second_e1 = line_second(first_e1)
     first_s1 = line_first(after(piece_of(1, 2), first_e1))
@@ -722,8 +759,7 @@
         parts + [biases[0][3], middle0, mod0, mod1],
     )
 
-    g_rows1 = gather(g_shrunk1, "tensor")
-    attn_rows, second_s1 = tie(gather(attn_in, "tensor"), second_s1)
+    (attn_rows, w_attn1), second_s1 = tie((gather(attn_in, "tensor"), w_attn1), second_s1)
     w_mlp1 = both_cores([first_e1, first_s1], [second_e1, second_s1])
     kept_attn1, parts = attention(attn_rows, w_attn1, biases[1][0])
     attended1, middle1, mlp_in = middle_of(parts, biases[1][1], h1, mod1)
@@ -810,10 +846,12 @@
             place,
         )
 
-    g_parts, y_partial, (parts_e1, parts_s1) = tie(
-        exchange(g_partial, "tensor"),
+    (g_parts, (parts_e1, parts_s1)), y_partial = tie(
+        (
+            exchange(g_partial, "tensor"),
+            line_parts(mlp_weight_grads(mlp_rows1, g_pre1, g_rows1, hidden1), 2),
+        ),
         y_partial,
-        line_parts(mlp_weight_grads(mlp_rows1, g_pre1, g_rows1, hidden1), 2),
     )
     near_e1 = line_near(parts_e1)
     g_middle1, g_attended, g_shift_mlp1, g_scale_mlp1, g_gate_attn1, out_grad1 = middle_back(
@@ -826,9 +864,8 @@
     far_e1 = line_far(parts_e1, near_e1)
     near_s1 = line_near(parts_s1)
     (g_rows, g_joint, joint_grad1), parts = attention_back(g_rows, w_attn1, kept_attn1)
-    parts, (parts_a1,), far_e1, near_s1, parts_s1 = tie(
-        parts,
-        line_parts(attn_weight_grads(kept_attn1, g_joint, g_rows), 1),
+    (parts, (parts_a1,)), far_e1, near_s1, parts_s1 = tie(
+        (parts, line_parts(attn_weight_grads(kept_attn1, g_joint, g_rows), 1)),
         far_e1,
         near_s1,
         parts_s1,
@@ -853,10 +890,11 @@
         g_rows0 + [w_mlp0[0], w_mlp0[1], pre0],
     )
     g_rows0, g_pre0, expand_grad0 = outs[:3]
-    parts, (parts_e0, parts_s0), far_a1 = tie(
-        exchange(outs[3:], "tensor"),
-        line_parts(mlp_weight_grads(mlp_rows0, g_pre0, g_rows0, hidden0), 2),
-        far_a1,
+    ((parts, (parts_e0, parts_s0)),) = tie(
+        (
+            exchange(outs[3:], "tensor"),
+            line_parts(mlp_weight_grads(mlp_rows0, g_pre0, g_rows0, hidden0), 2),
+        )
     )
     near_e0 = line_near(parts_e0)
     g_middle0, g_attended, g_shift_mlp0, g_scale_mlp0, g_gate_attn0, out_grad0 = middle_back(
@@ -868,13 +906,20 @@
         [own_bf16, vector, vector],
         y_parts + [biases[1][3], middle1, mod1, g_y1, g_shrunk1],
     )
-    g_rows, near_e0, parts_e0, parts_s0 = tie(
-        gather(g_attended, "tensor"), near_e0, parts_e0, parts_s0
+    g_rows, near_e0, parts_e0, parts_s0, far_a1 = tie(
+        gather(g_attended, "tensor"), near_e0, parts_e0, parts_s0, far_a1
     )
     far_e0 = line_far(parts_e0, near_e0)
     near_s0 = line_near(parts_s0)
     (g_rows, g_joint, joint_grad0), parts = attention_back(g_rows, w_attn0, kept_attn0)
-    (parts_a0,) = line_parts(attn_weight_grads(kept_attn0, g_joint, g_rows), 1)
+    (parts, (parts_a0,)), far_e0, near_s0, parts_s0 = tie(
+        (parts, line_parts(attn_weight_grads(kept_attn0, g_joint, g_rows), 1)),
+        far_e0,
+        near_s0,
+        parts_s0,
+    )
+    near_a0 = line_near(parts_a0)
+    far_s0 = line_far(parts_s0, near_s0)
     g_h0, g_shift_attn0, g_scale_attn0 = kernel(
         "finish_back",
         finish_back_body,
@@ -910,11 +955,8 @@
             shrink_grad1,
         ],
     )[0]
-    packed_all, parts_a0, far_e0, near_s0, parts_s0 = tie(
-        gather(packed, "tensor"), parts_a0, far_e0, near_s0, parts_s0
-    )
-    near_a0 = line_near(parts_a0)
-    far_s0 = line_far(parts_s0, near_s0)
+    packed_all, near_a0, far_s0 = tie(gather(packed, "tensor"), near_a0, far_s0)
+    far_a0 = line_far(parts_a0, near_a0)
     keep, give = run(
         "grads_sum",
         functools.partial(grads_sum_body, count),
@@ -930,8 +972,7 @@
         place,
     )[0]
     joined_all = gather(joined, "dp") if direct else lax.all_gather(joined, "dp", axis=0, tiled=True)
-    joined_all, near_a0, far_s0 = tie(joined_all, near_a0, far_s0)
-    far_a0 = line_far(parts_a0, near_a0)
+    joined_all, far_a0 = tie(joined_all, far_a0)
     mlp_grad0, mlp_grad1 = (
         jnp.concatenate([line_total(*first_piece), line_total(*second_piece)], axis=1)
         for first_piece, second_piece in (
@@ -941,21 +982,20 @@
     )
     attn_grad0 = line_total(parts_a0, near_a0, far_a0)
     attn_grad1 = line_total(parts_a1, near_a1, far_a1)
-    expand_w_grad, shrink_w_grad = run(
+    expand_w_grad, shrink_t_grad = run(
         "final_mlp",
         final_mlp_body,
-        [shape((chunk, hidden), F32), shape((hidden, chunk), F32)],
+        [shape((chunk, hidden), F32)] * 2,
         own_halves((mlp_grad0, mlp_grad1)),
         place,
     )
     joint_w_grad, output_w_grad = run(
         "final_attn",
         final_attn_body,
-        [shape((chunk, 3 * width), F32), shape((width, chunk), F32)],
+        [shape((3, chunk, width), F32), shape((width, chunk), F32)],
         own_halves((attn_grad0, attn_grad1)),
         place,
     )
-    joint_w_grad = joint_w_grad.reshape(chunk, 3, width)
 
     if direct:
         outs = run(
@@ -985,13 +1025,13 @@
         cond_grad[None, :, None],
         ada_grad[None],
         ada_bias_grad,
-        joint_w_grad[None],
+        jnp.transpose(joint_w_grad, (1, 0, 2))[None],
         bias_sum[:, :at].reshape(1, 2, width),
         output_w_grad[None],
         bias_sum[:, at + hidden : at + hidden + model],
         expand_w_grad[None],
         bias_sum[:, at : at + hidden],
-        shrink_w_grad[None],
+        shrink_t_grad.T[None],
         bias_sum[:, at + hidden + model :],
     )
 

time: 273 us -> 281 us (1.029)
  waiting for transfers between devices: 107 us -> 112 us
    ppermute x106, waiting for transfers between devices: 107 us -> 112 us  [swap(): return lax.ppermute(value, axis, pairs)]
    pallas_call x36 -> x38, Pallas kernels: 33.1 us -> 34.8 us  [run(): pl.pallas_call(body, out_shape=outs, in_specs=specs, out_specs=[pl.BlockS...]
  transfers between devices with their start and end apart: 106 -> 106, of which waited for: 60 -> 65; matrix products, arithmetic and copies ran while one was open for 2% -> 2% of each run, Pallas kernels for 6% -> 6%
where the time goes in v7:
time: 281 us
  starting transfers between devices  121 us (43%)
  waiting for transfers between devices  112 us (40%)
  Pallas kernels  36.3 us (13%)
  local copies, waits for them, and re-layouts  7.16 us (3%)
  other arithmetic  3.33 us (1%)
    ppermute x106, starting transfers between devices, swap(): return lax.ppermute(value, axis, pairs)  121 us
    ppermute x106, waiting for transfers between devices, swap(): return lax.ppermute(value, axis, pairs)  112 us
    pallas_call x38, Pallas kernels, run(): pl.pallas_call(body, out_shape=outs, in_specs=specs, out_specs=[pl.BlockS...  34.8 us
    unnamed x37, local copies, waits for them, and re-layouts  5.64 us
  transfers between devices with their start and end apart: 106, of which 65 were waited for; matrix products, arithmetic and copies ran while one was open for 2% of the time, Pallas kernels for 6%

profile of v7, /device:TPU:0, one launch (start us, length us, event | category | flops | bytes accessed | tf_op | source)
XLA Modules:
  0.0 280.8 jit_solution(626253399913084488)
XLA Ops:
  8.0 4.0 %collective-permute-start.7 = (bf16[192,384]{1,0:T(8,128)(2,1)S(1)}, bf16[192,384]{1,0:T(8,128)(2,1)S(1)}, u32[]{:S(2)}, u32[]{:S(2)}) collective-permute-start(bf16[192,384]{1,0:T(8,128)(2,1)S(1)} %get-tuple-element.382), channel_id=1, source_target_pairs={{0,8},{4,12},{8,0},{12,4},{1,9},{5,13},{9,1},{13,5},{2,10},{6,14},... | collective-permute-start | bytes 442376 | tf_op jit(solution)/shard_map/ppermute | solution.py:22
  19.7 2.6 collective-permute-start.5
  27.5 3.4 %collective-permute-start.13 = (bf16[192,384]{1,0:T(8,128)(2,1)S(1)}, bf16[192,384]{1,0:T(8,128)(2,1)S(1)}, u32[]{:S(2)}, u32[]{:S(2)}) collective-permute-start(bf16[192,384]{1,0:T(8,128)(2,1)S(1)} %get-tuple-element.403), channel_id=1, source_target_pairs={{0,8},{4,12},{8,0},{12,4},{1,9},{5,13},{9,1},{13,5},{2,10},{6,14},... | collective-permute-start | bytes 442376 | tf_op jit(solution)/shard_map/ppermute | solution.py:22
  32.4 3.5 %collective-permute-start.10 = (f32[2,1152]{1,0:T(2,128)S(1)}, f32[2,1152]{1,0:T(2,128)S(1)}, u32[]{:S(2)}, u32[]{:S(2)}) collective-permute-start(f32[2,1152]{1,0:T(2,128)S(1)} %get-tuple-element.390), channel_id=1, source_target_pairs={{0,12},{4,8},{8,4},{12,0},{1,13},{5,9},{9,5},{13,1},{2,14},{6,10},... | collective-permute-start | bytes 27656 | tf_op jit(solution)/shard_map/ppermute | solution.py:22
  53.3 4.8 %collective-permute-done.18 = bf16[192,384]{1,0:T(8,128)(2,1)S(1)} collective-permute-done((bf16[192,384]{1,0:T(8,128)(2,1)S(1)}, bf16[192,384]{1,0:T(8,128)(2,1)S(1)}, u32[]{:S(2)}, u32[]{:S(2)}) %collective-permute-start.18) | collective-permute-done | bytes 147488 | tf_op jit(solution)/shard_map/ppermute | solution.py:22
  90.6 2.8 collective-permute-start.38
  98.8 5.5 %collective-permute-done.39 = bf16[192,384]{1,0:T(8,128)(2,1)S(1)} collective-permute-done((bf16[192,384]{1,0:T(8,128)(2,1)S(1)}, bf16[192,384]{1,0:T(8,128)(2,1)S(1)}, u32[]{:S(2)}, u32[]{:S(2)}) %collective-permute-start.39) | collective-permute-done | bytes 147488 | tf_op jit(solution)/shard_map/ppermute | solution.py:22
  106.5 3.3 %collective-permute-done.37.refs_3_ = bf16[64,768]{1,0:T(8,128)(2,1)S(1)} collective-permute-done((bf16[64,768]{1,0:T(8,128)(2,1)S(1)}, bf16[64,768]{1,0:T(8,128)(2,1)S(1)}, u32[]{:S(2)}, u32[]{:S(2)}) %collective-permute-start.37) | collective-permute-done | bytes 98336 | tf_op jit(solution)/shard_map/ppermute | solution.py:22
  113.7 2.9 %collective-permute-done.42.refs_3_ = bf16[64,768]{1,0:T(8,128)(2,1)S(1)} collective-permute-done((bf16[64,768]{1,0:T(8,128)(2,1)S(1)}, bf16[64,768]{1,0:T(8,128)(2,1)S(1)}, u32[]{:S(2)}, u32[]{:S(2)}) %collective-permute-start.42) | collective-permute-done | bytes 98336 | tf_op jit(solution)/shard_map/ppermute | solution.py:22
  132.6 2.9 %collective-permute-done.50.refs_3_ = bf16[64,768]{1,0:T(8,128)(2,1)S(1)} collective-permute-done((bf16[64,768]{1,0:T(8,128)(2,1)S(1)}, bf16[64,768]{1,0:T(8,128)(2,1)S(1)}, u32[]{:S(2)}, u32[]{:S(2)}) %collective-permute-start.50) | collective-permute-done | bytes 98336 | tf_op jit(solution)/shard_map/ppermute | solution.py:22
  157.2 2.4 attention_back.2
  168.1 3.2 %collective-permute-done.65.refs_2_ = bf16[64,768]{1,0:T(8,128)(2,1)S(1)} collective-permute-done((bf16[64,768]{1,0:T(8,128)(2,1)S(1)}, bf16[64,768]{1,0:T(8,128)(2,1)S(1)}, u32[]{:S(2)}, u32[]{:S(2)}) %collective-permute-start.65) | collective-permute-done | bytes 98336 | tf_op jit(solution)/shard_map/ppermute | solution.py:22
  179.9 2.7 collective-permute-done.72.refs_3_
  193.2 2.6 collective-permute-done.57.refs_2_
  213.5 2.4 attention_back.3
  226.5 6.4 %collective-permute-done.88 = bf16[192,384]{1,0:T(8,128)(2,1)S(1)} collective-permute-done((bf16[192,384]{1,0:T(8,128)(2,1)S(1)}, bf16[192,384]{1,0:T(8,128)(2,1)S(1)}, u32[]{:S(2)}, u32[]{:S(2)}) %collective-permute-start.88) | collective-permute-done | bytes 147488 | tf_op jit(solution)/shard_map/ppermute | solution.py:22
  237.6 2.7 collective-permute-start.95
  242.1 6.1 %collective-permute-done.95 = bf16[192,384]{1,0:T(8,128)(2,1)S(1)} collective-permute-done((bf16[192,384]{1,0:T(8,128)(2,1)S(1)}, bf16[192,384]{1,0:T(8,128)(2,1)S(1)}, u32[]{:S(2)}, u32[]{:S(2)}) %collective-permute-start.95) | collective-permute-done | bytes 147488 | tf_op jit(solution)/shard_map/ppermute | solution.py:22
  248.1 3.1 %collective-permute-done.94 = bf16[2,192,384]{2,1,0:T(8,128)(2,1)S(1)} collective-permute-done((bf16[2,192,384]{2,1,0:T(8,128)(2,1)S(1)}, bf16[2,192,384]{2,1,0:T(8,128)(2,1)S(1)}, u32[]{:S(2)}, u32[]{:S(2)}) %collective-permute-start.94) | collective-permute-done | bytes 294944 | tf_op jit(solution)/shard_map/ppermute | solution.py:22
  251.9 2.4 collective-permute-start.100
  256.9 2.5 collective-permute-start.97
  261.9 4.5 %collective-permute-done.98.g2 = f32[1,11904]{1,0:T(1,128)S(1)} collective-permute-done((f32[1,11904]{1,0:T(1,128)S(1)}, f32[1,11904]{1,0:T(1,128)S(1)}, u32[]{:S(2)}, u32[]{:S(2)}) %collective-permute-start.98) | collective-permute-done | bytes 47648 | tf_op jit(solution)/shard_map/ppermute | solution.py:22
  269.0 2.6 collective-permute-start.102
  274.1 2.9 %collective-permute-done.103 = f32[2,192]{1,0:T(2,128)S(1)} collective-permute-done((f32[2,192]{1,0:T(2,128)S(1)}, f32[2,192]{1,0:T(2,128)S(1)}, u32[]{:S(2)}, u32[]{:S(2)}) %collective-permute-start.103) | collective-permute-done | bytes 1568 | tf_op jit(solution)/shard_map/ppermute | solution.py:22
  (310 shorter events, 197.3 us)
Async XLA Ops:
  8.0 18.7 %collective-permute-start.7 = (bf16[192,384]{1,0:T(8,128)(2,1)S(1)}, bf16[192,384]{1,0:T(8,128)(2,1)S(1)}, u32[]{:S(2)}, u32[]{:S(2)}) collective-permute-start(bf16[192,384]{1,0:T(8,128)(2,1)S(1)} %get-tuple-element.382), channel_id=1, source_target_pairs={{0,8},{4,12},{8,0},{12,4},{1,9},{5,13},{9,1},{13,5},{2,10},{6,14},... | collective-permute-start | bytes 442376 | tf_op jit(solution)/shard_map/ppermute | solution.py:22
  26.7 12.9 %collective-permute-start.11 = (bf16[2,192,384]{2,1,0:T(8,128)(2,1)S(1)}, bf16[2,192,384]{2,1,0:T(8,128)(2,1)S(1)}, u32[]{:S(2)}, u32[]{:S(2)}) collective-permute-start(bf16[2,192,384]{2,1,0:T(8,128)(2,1)S(1)} %pad_maximum_fusion.refs_0_), channel_id=1, source_target_pairs={{0,4},{4,0},{8,12},{12,8},{1,5},{5,1},{9,13},{13,9},{2,6},{6,2},{1... | collective-permute-start | bytes 884744 | tf_op jit(solution)/shard_map/ppermute | solution.py:22
  27.5 14.3 %collective-permute-start.13 = (bf16[192,384]{1,0:T(8,128)(2,1)S(1)}, bf16[192,384]{1,0:T(8,128)(2,1)S(1)}, u32[]{:S(2)}, u32[]{:S(2)}) collective-permute-start(bf16[192,384]{1,0:T(8,128)(2,1)S(1)} %get-tuple-element.403), channel_id=1, source_target_pairs={{0,8},{4,12},{8,0},{12,4},{1,9},{5,13},{9,1},{13,5},{2,10},{6,14},... | collective-permute-start | bytes 442376 | tf_op jit(solution)/shard_map/ppermute | solution.py:22
  47.3 15.2 %collective-permute-start.19 = (bf16[768,384]{1,0:T(8,128)(2,1)S(1)}, bf16[768,384]{1,0:T(8,128)(2,1)S(1)}, u32[]{:S(2)}, u32[]{:S(2)}) collective-permute-start(bf16[768,384]{1,0:T(8,128)(2,1)S(1)} %stack_line.4.refs_4_), channel_id=1, source_target_pairs={{0,16},{16,0},{1,17},{17,1},{2,18},{18,2},{3,19},{19,3},{4,20},{20... | collective-permute-start | bytes 1769480 | tf_op jit(solution)/shard_map/ppermute | solution.py:22
  48.2 11.9 %collective-permute-start.17 = (bf16[2,192,384]{2,1,0:T(8,128)(2,1)S(1)}, bf16[2,192,384]{2,1,0:T(8,128)(2,1)S(1)}, u32[]{:S(2)}, u32[]{:S(2)}) collective-permute-start(bf16[2,192,384]{2,1,0:T(8,128)(2,1)S(1)} %pad_maximum_fusion.1.refs_0_), channel_id=1, source_target_pairs={{0,4},{4,0},{8,12},{12,8},{1,5},{5,1},{9,13},{13,9},{2,6},{6,2},{1... | collective-permute-start | bytes 884744 | tf_op jit(solution)/shard_map/ppermute | solution.py:22
  60.1 13.2 %collective-permute-start.24 = (bf16[2,192,384]{2,1,0:T(8,128)(2,1)S(1)}, bf16[2,192,384]{2,1,0:T(8,128)(2,1)S(1)}, u32[]{:S(2)}, u32[]{:S(2)}) collective-permute-start(bf16[2,192,384]{2,1,0:T(8,128)(2,1)S(1)} %pad_maximum_fusion.2.refs_1_), channel_id=1, source_target_pairs={{0,4},{4,0},{8,12},{12,8},{1,5},{5,1},{9,13},{13,9},{2,6},{6,2},{1... | collective-permute-start | bytes 884744 | tf_op jit(solution)/shard_map/ppermute | solution.py:22
  73.9 20.8 %collective-permute-start.34 = (bf16[768,768]{1,0:T(8,128)(2,1)S(1)}, bf16[768,768]{1,0:T(8,128)(2,1)S(1)}, u32[]{:S(2)}, u32[]{:S(2)}) collective-permute-start(bf16[768,768]{1,0:T(8,128)(2,1)S(1)} %stack_line.5.refs_4_), channel_id=1, source_target_pairs={{0,16},{16,0},{1,17},{17,1},{2,18},{18,2},{3,19},{19,3},{4,20},{20... | collective-permute-start | bytes 3538952 | tf_op jit(solution)/shard_map/ppermute | solution.py:22
  74.8 15.8 %collective-permute-start.29 = (bf16[2,192,384]{2,1,0:T(8,128)(2,1)S(1)}, bf16[2,192,384]{2,1,0:T(8,128)(2,1)S(1)}, u32[]{:S(2)}, u32[]{:S(2)}) collective-permute-start(bf16[2,192,384]{2,1,0:T(8,128)(2,1)S(1)} %pad_maximum_fusion.3.refs_0_), channel_id=1, source_target_pairs={{0,4},{4,0},{8,12},{12,8},{1,5},{5,1},{9,13},{13,9},{2,6},{6,2},{1... | collective-permute-start | bytes 884744 | tf_op jit(solution)/shard_map/ppermute | solution.py:22
  90.6 19.2 %collective-permute-start.38 = (bf16[2,192,384]{2,1,0:T(8,128)(2,1)S(1)}, bf16[2,192,384]{2,1,0:T(8,128)(2,1)S(1)}, u32[]{:S(2)}, u32[]{:S(2)}) collective-permute-start(bf16[2,192,384]{2,1,0:T(8,128)(2,1)S(1)} %pad_maximum_fusion.4.refs_0_), channel_id=1, source_target_pairs={{0,4},{4,0},{8,12},{12,8},{1,5},{5,1},{9,13},{13,9},{2,6},{6,2},{1... | collective-permute-start | bytes 884744 | tf_op jit(solution)/shard_map/ppermute | solution.py:22
  94.0 19.7 %collective-permute-start.43 = (bf16[768,384]{1,0:T(8,128)(2,1)S(1)}, bf16[768,384]{1,0:T(8,128)(2,1)S(1)}, u32[]{:S(2)}, u32[]{:S(2)}) collective-permute-start(bf16[768,384]{1,0:T(8,128)(2,1)S(1)} %stack_line.6.refs_4_), channel_id=1, source_target_pairs={{0,16},{16,0},{1,17},{17,1},{2,18},{18,2},{3,19},{19,3},{4,20},{20... | collective-permute-start | bytes 1769480 | tf_op jit(solution)/shard_map/ppermute | solution.py:22
  94.1 10.1 %collective-permute-start.39 = (bf16[192,384]{1,0:T(8,128)(2,1)S(1)}, bf16[192,384]{1,0:T(8,128)(2,1)S(1)}, u32[]{:S(2)}, u32[]{:S(2)}) collective-permute-start(bf16[192,384]{1,0:T(8,128)(2,1)S(1)} %get-tuple-element.461), channel_id=1, source_target_pairs={{0,8},{4,12},{8,0},{12,4},{1,9},{5,13},{9,1},{13,5},{2,10},{6,14},... | collective-permute-start | bytes 442376 | tf_op jit(solution)/shard_map/ppermute | solution.py:22
  95.9 10.6 %collective-permute-start.35 = (bf16[64,768]{1,0:T(8,128)(2,1)S(1)}, bf16[64,768]{1,0:T(8,128)(2,1)S(1)}, u32[]{:S(2)}, u32[]{:S(2)}) collective-permute-start(bf16[64,768]{1,0:T(8,128)(2,1)S(1)} %get-tuple-element.452), channel_id=1, source_target_pairs={{0,1},{1,0},{2,3},{3,2},{4,5},{5,4},{6,7},{7,6},{8,9},{9,8},{10,11... | collective-permute-start | bytes 294920 | tf_op jit(solution)/shard_map/ppermute | solution.py:22
  118.2 18.0 %collective-permute-start.51 = (bf16[768,768]{1,0:T(8,128)(2,1)S(1)}, bf16[768,768]{1,0:T(8,128)(2,1)S(1)}, u32[]{:S(2)}, u32[]{:S(2)}) collective-permute-start(bf16[768,768]{1,0:T(8,128)(2,1)S(1)} %stack_line.7.refs_8_), channel_id=1, source_target_pairs={{0,16},{16,0},{1,17},{17,1},{2,18},{18,2},{3,19},{19,3},{4,20},{20... | collective-permute-start | bytes 3538952 | tf_op jit(solution)/shard_map/ppermute | solution.py:22
  161.0 12.6 %collective-permute-start.69 = (bf16[2,192,384]{2,1,0:T(8,128)(2,1)S(1)}, bf16[2,192,384]{2,1,0:T(8,128)(2,1)S(1)}, u32[]{:S(2)}, u32[]{:S(2)}) collective-permute-start(bf16[2,192,384]{2,1,0:T(8,128)(2,1)S(1)} %get-tuple-element.576), channel_id=1, source_target_pairs={{0,4},{4,0},{8,12},{12,8},{1,5},{5,1},{9,13},{13,9},{2,6},{6,2},{1... | collective-permute-start | bytes 884744 | tf_op jit(solution)/shard_map/ppermute | solution.py:22
  161.5 10.0 %collective-permute-start.68 = (bf16[192,384]{1,0:T(8,128)(2,1)S(1)}, bf16[192,384]{1,0:T(8,128)(2,1)S(1)}, u32[]{:S(2)}, u32[]{:S(2)}) collective-permute-start(bf16[192,384]{1,0:T(8,128)(2,1)S(1)} %fusion.17), channel_id=1, source_target_pairs={{0,8},{4,12},{8,0},{12,4},{1,9},{5,13},{9,1},{13,5},{2,10},{6,14},... | collective-permute-start | bytes 442376 | tf_op jit(solution)/shard_map/ppermute | solution.py:22
  173.6 11.7 %collective-permute-start.73 = (bf16[2,192,384]{2,1,0:T(8,128)(2,1)S(1)}, bf16[2,192,384]{2,1,0:T(8,128)(2,1)S(1)}, u32[]{:S(2)}, u32[]{:S(2)}) collective-permute-start(bf16[2,192,384]{2,1,0:T(8,128)(2,1)S(1)} %get-tuple-element.590), channel_id=1, source_target_pairs={{0,4},{4,0},{8,12},{12,8},{1,5},{5,1},{9,13},{13,9},{2,6},{6,2},{1... | collective-permute-start | bytes 884744 | tf_op jit(solution)/shard_map/ppermute | solution.py:22
  187.7 11.8 %collective-permute-start.78 = (bf16[768,768]{1,0:T(8,128)(2,1)S(1)}, bf16[768,768]{1,0:T(8,128)(2,1)S(1)}, u32[]{:S(2)}, u32[]{:S(2)}) collective-permute-start(bf16[768,768]{1,0:T(8,128)(2,1)S(1)} %get-tuple-element.609), channel_id=1, source_target_pairs={{0,16},{16,0},{1,17},{17,1},{2,18},{18,2},{3,19},{19,3},{4,20},{20... | collective-permute-start | bytes 3538952 | tf_op jit(solution)/shard_map/ppermute | solution.py:22
  203.6 9.9 %collective-permute-start.82 = (bf16[2,192,384]{2,1,0:T(8,128)(2,1)S(1)}, bf16[2,192,384]{2,1,0:T(8,128)(2,1)S(1)}, u32[]{:S(2)}, u32[]{:S(2)}) collective-permute-start(bf16[2,192,384]{2,1,0:T(8,128)(2,1)S(1)} %get-tuple-element.627), channel_id=1, source_target_pairs={{0,4},{4,0},{8,12},{12,8},{1,5},{5,1},{9,13},{13,9},{2,6},{6,2},{1... | collective-permute-start | bytes 884744 | tf_op jit(solution)/shard_map/ppermute | solution.py:22
  221.5 12.1 %collective-permute-start.89 = (bf16[2,192,384]{2,1,0:T(8,128)(2,1)S(1)}, bf16[2,192,384]{2,1,0:T(8,128)(2,1)S(1)}, u32[]{:S(2)}, u32[]{:S(2)}) collective-permute-start(bf16[2,192,384]{2,1,0:T(8,128)(2,1)S(1)} %get-tuple-element.663), channel_id=1, source_target_pairs={{0,4},{4,0},{8,12},{12,8},{1,5},{5,1},{9,13},{13,9},{2,6},{6,2},{1... | collective-permute-start | bytes 884744 | tf_op jit(solution)/shard_map/ppermute | solution.py:22
  237.6 10.5 %collective-permute-start.95 = (bf16[192,384]{1,0:T(8,128)(2,1)S(1)}, bf16[192,384]{1,0:T(8,128)(2,1)S(1)}, u32[]{:S(2)}, u32[]{:S(2)}) collective-permute-start(bf16[192,384]{1,0:T(8,128)(2,1)S(1)} %fusion.13), channel_id=1, source_target_pairs={{0,8},{4,12},{8,0},{12,4},{1,9},{5,13},{9,1},{13,5},{2,10},{6,14},... | collective-permute-start | bytes 442376 | tf_op jit(solution)/shard_map/ppermute | solution.py:22
  240.4 10.8 %collective-permute-start.94 = (bf16[2,192,384]{2,1,0:T(8,128)(2,1)S(1)}, bf16[2,192,384]{2,1,0:T(8,128)(2,1)S(1)}, u32[]{:S(2)}, u32[]{:S(2)}) collective-permute-start(bf16[2,192,384]{2,1,0:T(8,128)(2,1)S(1)} %get-tuple-element.693), channel_id=1, source_target_pairs={{0,4},{4,0},{8,12},{12,8},{1,5},{5,1},{9,13},{13,9},{2,6},{6,2},{1... | collective-permute-start | bytes 884744 | tf_op jit(solution)/shard_map/ppermute | solution.py:22
  251.9 14.5 %collective-permute-start.100 = (bf16[192,384]{1,0:T(8,128)(2,1)S(1)}, bf16[192,384]{1,0:T(8,128)(2,1)S(1)}, u32[]{:S(2)}, u32[]{:S(2)}) collective-permute-start(bf16[192,384]{1,0:T(8,128)(2,1)S(1)} %fusion.12), channel_id=1, source_target_pairs={{0,8},{4,12},{8,0},{12,4},{1,9},{5,13},{9,1},{13,5},{2,10},{6,14},... | collective-permute-start | bytes 442376 | tf_op jit(solution)/shard_map/ppermute | solution.py:22
  259.5 19.6 %collective-permute-start.105 = (bf16[192,768]{1,0:T(8,128)(2,1)S(1)}, bf16[192,768]{1,0:T(8,128)(2,1)S(1)}, u32[]{:S(2)}, u32[]{:S(2)}) collective-permute-start(bf16[192,768]{1,0:T(8,128)(2,1)S(1)} %get-tuple-element.755), channel_id=1, source_target_pairs={{0,16},{16,0},{1,17},{17,1},{2,18},{18,2},{3,19},{19,3},{4,20},{20... | collective-permute-start | bytes 884744 | tf_op jit(solution)/shard_map/ppermute | solution.py:22
  266.5 11.1 %collective-permute-start.104 = (bf16[192,384]{1,0:T(8,128)(2,1)S(1)}, bf16[192,384]{1,0:T(8,128)(2,1)S(1)}, u32[]{:S(2)}, u32[]{:S(2)}) collective-permute-start(bf16[192,384]{1,0:T(8,128)(2,1)S(1)} %get-tuple-element.752), channel_id=1, source_target_pairs={{0,16},{16,0},{1,17},{17,1},{2,18},{18,2},{3,19},{19,3},{4,20},{20... | collective-permute-start | bytes 442376 | tf_op jit(solution)/shard_map/ppermute | solution.py:22
  (100 other events, 746.2 us)

commit v8 on v7

--- a/solution.py
+++ b/solution.py
@@ -130,26 +130,6 @@
     g_y = cotangent[core].astype(F32)
     g_y_out[...] = g_y
     g_shrunk[...] = (part(mod1, 5) * g_y).astype(BF16)
-
-
-def pack_weights_body(place, joint, out, expand, shrink_t, keep, give):
-    first = place[0] == 0
-    width = out.shape[0]
-    half = expand.shape[1] // 2
-    pieces = (
-        (
-            jnp.concatenate([joint[0].astype(F32), joint[1].astype(F32)], axis=1),
-            jnp.concatenate([joint[2].astype(F32), out[...].astype(F32).T], axis=1),
-        ),
-        (expand[:, :half], expand[:, half:]),
-        (shrink_t[:, :half], shrink_t[:, half:]),
-    )
-    at = 0
-    for front, back in pieces:
-        columns = slice(at, at + front.shape[1])
-        keep[:, columns] = jnp.where(first, front, back).astype(BF16)
-        give[:, columns] = jnp.where(first, back, front).astype(BF16)
-        at += front.shape[1]
 
 
 def weight_pieces_body(place, keep, received, *outs):
@@ -573,22 +553,22 @@
         return lax.optimization_barrier((value, earlier))[0]
 
     def tie(main, *rest):
-        return lax.optimization_barrier((lax.optimization_barrier(main),) + rest)
+        return lax.optimization_barrier((main,) + rest)
 
     split = 2 * width
     pieces_shape = shape((chunk, split), BF16)
-    keep, give = run(
-        "pack_weights",
-        pack_weights_body,
-        [shape((chunk, split + 2 * (hidden // 2)), BF16)] * 2,
-        [
-            jnp.transpose(joint_weight[0], (1, 0, 2)),
-            output_weight[0],
-            expand_weight[0],
-            shrink_weight[0].T,
-        ],
-        place,
-    )
+    joint_blocks = jnp.transpose(joint_weight[0], (1, 0, 2))
+    expand, shrink_t = expand_weight[0], shrink_weight[0].T
+    half = hidden // 2
+    halves = (
+        jnp.concatenate(
+            [joint_blocks[0], joint_blocks[1], expand[:, :half], shrink_t[:, :half]], axis=1
+        ),
+        jnp.concatenate(
+            [joint_blocks[2], output_weight[0].T, expand[:, half:], shrink_t[:, half:]], axis=1
+        ),
+    )
+    keep, give = mine(halves), other(halves)
     line_pieces = run(
         "weight_pieces",
         weight_pieces_body,
@@ -625,14 +605,16 @@
         activated_all = lax.all_gather(activated, "dp", axis=0).reshape(line_size * micro, -1)
 
     def line_first(value):
-        return jnp.stack([value, swap(value, "dp", 2)]) if direct else value
+        return (value, swap(value, "dp", 2)) if direct else value
 
     def line_second(pair):
-        if direct:
-            return swap(pair, "dp", 1)
-        return lax.all_gather(pair, "dp", axis=0, tiled=True)
-
-    def both_cores(pairs, others):
+        if not direct:
+            return pair, lax.all_gather(pair, "dp", axis=0, tiled=True)
+        stacked = jnp.stack(pair)
+        return stacked, swap(stacked, "dp", 1)
+
+    def both_cores(*steps):
+        pairs, others = [step[0] for step in steps], [step[1] for step in steps]
         if direct:
             wide = sum(pair.shape[2] for pair in pairs)
             lined = run(
@@ -645,7 +627,7 @@
     def piece_of(layer, index):
         return line_pieces[3 * layer + index]
 
-    first_a0 = line_first(piece_of(0, 0))
+    first_a0 = line_first(after(piece_of(0, 0), activated_all))
 
     if direct:
         mod_partial = run(
@@ -684,7 +666,7 @@
         mod_mine, mod_other = mine(mod_layer)[None], other(mod_layer)[None]
     mod0, mod1 = both_layers(mod_mine, swap(mod_other, "pipe", 1))
 
-    w_attn0 = both_cores([first_a0], [second_a0])
+    w_attn0 = both_cores(second_a0)
     mod0, mod1, first_e0 = tie(mod0, mod1, first_e0)
     second_e0 = line_second(first_e0)
     first_s0 = line_first(after(piece_of(0, 2), first_e0))
@@ -732,7 +714,7 @@
     first_a1 = line_first(after(piece_of(1, 0), first_s0))
     kept_attn0, parts = attention(attn_rows, w_attn0, biases[0][0])
     parts, second_s0, first_a1 = tie(parts, second_s0, first_a1)
-    w_mlp0 = both_cores([first_e0, first_s0], [second_e0, second_s0])
+    w_mlp0 = both_cores(second_e0, second_s0)
     second_a1 = line_second(first_a1)
     first_e1 = line_first(after(piece_of(1, 1), first_a1))
     attended0, middle0, mlp_in = middle_of(parts, biases[0][1], h0, mod0)
@@ -740,7 +722,7 @@
     mlp_rows0, second_a1, first_e1, g_rows1 = tie(
         gather(mlp_in, "tensor"), second_a1, first_e1, g_rows1
     )
-    w_attn1 = both_cores([first_a1], [second_a1])
+    w_attn1 = both_cores(second_a1)
     second_e1 = line_second(first_e1)
     first_s1 = line_first(after(piece_of(1, 2), first_e1))
     outs = kernel(
@@ -750,7 +732,8 @@
         mlp_rows0 + [w_mlp0[0], w_mlp0[1], biases[0][2]],
     )
     mlp_rows0, pre0, hidden0 = outs[:3]
-    parts, second_e1, first_s1 = tie(exchange(outs[3:], "tensor"), second_e1, first_s1)
+    (parts,) = tie(exchange(outs[3:], "tensor"))
+    parts, second_e1, first_s1 = tie(parts, second_e1, first_s1)
     second_s1 = line_second(first_s1)
     shrunk0, passed, h1, attn_in = kernel(
         "between",
@@ -760,7 +743,7 @@
     )
 
     (attn_rows, w_attn1), second_s1 = tie((gather(attn_in, "tensor"), w_attn1), second_s1)
-    w_mlp1 = both_cores([first_e1, first_s1], [second_e1, second_s1])
+    w_mlp1 = both_cores(second_e1, second_s1)
     kept_attn1, parts = attention(attn_rows, w_attn1, biases[1][0])
     attended1, middle1, mlp_in = middle_of(parts, biases[1][1], h1, mod1)
     outs = kernel(
@@ -890,13 +873,11 @@
         g_rows0 + [w_mlp0[0], w_mlp0[1], pre0],
     )
     g_rows0, g_pre0, expand_grad0 = outs[:3]
-    ((parts, (parts_e0, parts_s0)),) = tie(
-        (
-            exchange(outs[3:], "tensor"),
-            line_parts(mlp_weight_grads(mlp_rows0, g_pre0, g_rows0, hidden0), 2),
-        )
-    )
-    near_e0 = line_near(parts_e0)
+    parts, (parts_m0,) = tie(
+        exchange(outs[3:], "tensor"),
+        line_parts(mlp_weight_grads(mlp_rows0, g_pre0, g_rows0, hidden0), 1),
+    )
+    near_m0 = line_near(parts_m0)
     g_middle0, g_attended, g_shift_mlp0, g_scale_mlp0, g_gate_attn0, out_grad0 = middle_back(
         parts, middle0, mod0, g_y0, attended0
     )
@@ -906,20 +887,13 @@
         [own_bf16, vector, vector],
         y_parts + [biases[1][3], middle1, mod1, g_y1, g_shrunk1],
     )
-    g_rows, near_e0, parts_e0, parts_s0, far_a1 = tie(
-        gather(g_attended, "tensor"), near_e0, parts_e0, parts_s0, far_a1
-    )
-    far_e0 = line_far(parts_e0, near_e0)
-    near_s0 = line_near(parts_s0)
+    g_rows, near_m0, far_a1 = tie(gather(g_attended, "tensor"), near_m0, far_a1)
+    far_m0 = line_far(parts_m0, near_m0)
     (g_rows, g_joint, joint_grad0), parts = attention_back(g_rows, w_attn0, kept_attn0)
-    (parts, (parts_a0,)), far_e0, near_s0, parts_s0 = tie(
-        (parts, line_parts(attn_weight_grads(kept_attn0, g_joint, g_rows), 1)),
-        far_e0,
-        near_s0,
-        parts_s0,
+    parts, (parts_a0,) = tie(
+        parts, line_parts(attn_weight_grads(kept_attn0, g_joint, g_rows), 1)
     )
     near_a0 = line_near(parts_a0)
-    far_s0 = line_far(parts_s0, near_s0)
     g_h0, g_shift_attn0, g_scale_attn0 = kernel(
         "finish_back",
         finish_back_body,
@@ -955,7 +929,7 @@
             shrink_grad1,
         ],
     )[0]
-    packed_all, near_a0, far_s0 = tie(gather(packed, "tensor"), near_a0, far_s0)
+    packed_all, near_a0, far_m0 = tie(gather(packed, "tensor"), near_a0, far_m0)
     far_a0 = line_far(parts_a0, near_a0)
     keep, give = run(
         "grads_sum",
@@ -973,12 +947,9 @@
     )[0]
     joined_all = gather(joined, "dp") if direct else lax.all_gather(joined, "dp", axis=0, tiled=True)
     joined_all, far_a0 = tie(joined_all, far_a0)
-    mlp_grad0, mlp_grad1 = (
-        jnp.concatenate([line_total(*first_piece), line_total(*second_piece)], axis=1)
-        for first_piece, second_piece in (
-            ((parts_e0, near_e0, far_e0), (parts_s0, near_s0, far_s0)),
-            ((parts_e1, near_e1, far_e1), (parts_s1, near_s1, far_s1)),
-        )
+    mlp_grad0 = line_total(parts_m0, near_m0, far_m0)
+    mlp_grad1 = jnp.concatenate(
+        [line_total(parts_e1, near_e1, far_e1), line_total(parts_s1, near_s1, far_s1)], axis=1
     )
     attn_grad0 = line_total(parts_a0, near_a0, far_a0)
     attn_grad1 = line_total(parts_a1, near_a1, far_a1)

time: 281 us -> 275 us (0.979)
  starting transfers between devices: 121 us -> 105 us
  waiting for transfers between devices: 112 us -> 123 us
    ppermute x106 -> x104, starting transfers between devices: 121 us -> 105 us  [swap(): return lax.ppermute(value, axis, pairs)]
    ppermute x106 -> x104, waiting for transfers between devices: 112 us -> 123 us  [swap(): return lax.ppermute(value, axis, pairs)]
    unnamed x37 -> x34, local copies, waits for them, and re-layouts: 5.64 us -> 2.87 us
    pallas_call x38 -> x37, Pallas kernels: 34.8 us -> 33.7 us  [run(): pl.pallas_call(body, out_shape=outs, in_specs=specs, out_specs=[pl.BlockS...]
  transfers between devices with their start and end apart: 106 -> 104, of which waited for: 65 -> 64; matrix products, arithmetic and copies ran while one was open for 2% -> 2% of each run, Pallas kernels for 6% -> 6%
where the time goes in v8:
time: 275 us
  waiting for transfers between devices  123 us (45%)
  starting transfers between devices  105 us (38%)
  Pallas kernels  35.1 us (13%)
  local copies, waits for them, and re-layouts  6.88 us (3%)
  other arithmetic  2.9 us (1%)
    ppermute x104, waiting for transfers between devices, swap(): return lax.ppermute(value, axis, pairs)  123 us
    ppermute x104, starting transfers between devices, swap(): return lax.ppermute(value, axis, pairs)  105 us
    pallas_call x37, Pallas kernels, run(): pl.pallas_call(body, out_shape=outs, in_specs=specs, out_specs=[pl.BlockS...  33.7 us
  transfers between devices with their start and end apart: 104, of which 64 were waited for; matrix products, arithmetic and copies ran while one was open for 2% of the time, Pallas kernels for 6%

profile of v8, /device:TPU:0, one launch (start us, length us, event | category | flops | bytes accessed | tf_op | source)
XLA Modules:
  0.0 274.6 jit_solution(1070488678783300672)
XLA Ops:
  4.9 5.0 %collective-permute-start.2 = (bf16[2,192]{1,0:T(2,128)(2,1)S(1)}, bf16[2,192]{1,0:T(2,128)(2,1)S(1)}, u32[]{:S(2)}, u32[]{:S(2)}) collective-permute-start(bf16[2,192]{1,0:T(2,128)(2,1)S(1)} %fusion.21.a0), channel_id=1, source_target_pairs={{0,12},{4,8},{8,4},{12,0},{1,13},{5,9},{9,5},{13,1},{2,14},{6,10},... | collective-permute-start | bytes 2312 | tf_op jit(solution)/shard_map/ppermute | solution.py:22
  11.4 2.9 %collective-permute-done.1.a2 = bf16[2,192]{1,0:T(2,128)(2,1)S(1)} collective-permute-done((bf16[2,192]{1,0:T(2,128)(2,1)S(1)}, bf16[2,192]{1,0:T(2,128)(2,1)S(1)}, u32[]{:S(2)}, u32[]{:S(2)}) %collective-permute-start.1) | collective-permute-done | bytes 800 | tf_op jit(solution)/shard_map/ppermute | solution.py:22
  16.5 2.5 collective-permute-start.5
  28.3 2.6 collective-permute-done.8.p1
  36.4 7.6 %collective-permute-done.13 = bf16[192,384]{1,0:T(8,128)(2,1)S(1)} collective-permute-done((bf16[192,384]{1,0:T(8,128)(2,1)S(1)}, bf16[192,384]{1,0:T(8,128)(2,1)S(1)}, u32[]{:S(2)}, u32[]{:S(2)}) %collective-permute-start.13) | collective-permute-done | bytes 147488 | tf_op jit(solution)/shard_map/ppermute | solution.py:22
  44.9 2.5 collective-permute-start.16
  52.7 4.0 %collective-permute-done.18 = bf16[192,384]{1,0:T(8,128)(2,1)S(1)} collective-permute-done((bf16[192,384]{1,0:T(8,128)(2,1)S(1)}, bf16[192,384]{1,0:T(8,128)(2,1)S(1)}, u32[]{:S(2)}, u32[]{:S(2)}) %collective-permute-start.18) | collective-permute-done | bytes 147488 | tf_op jit(solution)/shard_map/ppermute | solution.py:22
  56.8 4.9 %collective-permute-done.17.refs_2_ = bf16[2,192,384]{2,1,0:T(8,128)(2,1)S(1)} collective-permute-done((bf16[2,192,384]{2,1,0:T(8,128)(2,1)S(1)}, bf16[2,192,384]{2,1,0:T(8,128)(2,1)S(1)}, u32[]{:S(2)}, u32[]{:S(2)}) %collective-permute-start.17) | collective-permute-done | bytes 294944 | tf_op jit(solution)/shard_map/ppermute | solution.py:22
  79.4 2.6 collective-permute-done.33.refs_7_
  85.1 2.5 collective-permute-done.28.refs_3_
  89.6 2.6 collective-permute-done.26.refs_1_
  96.1 2.7 collective-permute-start.39
  100.8 4.9 %collective-permute-done.36.refs_2_ = bf16[64,768]{1,0:T(8,128)(2,1)S(1)} collective-permute-done((bf16[64,768]{1,0:T(8,128)(2,1)S(1)}, bf16[64,768]{1,0:T(8,128)(2,1)S(1)}, u32[]{:S(2)}, u32[]{:S(2)}) %collective-permute-start.36) | collective-permute-done | bytes 98336 | tf_op jit(solution)/shard_map/ppermute | solution.py:22
  110.4 3.1 %collective-permute-done.42.refs_3_ = bf16[64,768]{1,0:T(8,128)(2,1)S(1)} collective-permute-done((bf16[64,768]{1,0:T(8,128)(2,1)S(1)}, bf16[64,768]{1,0:T(8,128)(2,1)S(1)}, u32[]{:S(2)}, u32[]{:S(2)}) %collective-permute-start.42) | collective-permute-done | bytes 98336 | tf_op jit(solution)/shard_map/ppermute | solution.py:22
  129.5 2.7 collective-permute-done.50.refs_3_
  153.3 2.4 attention_back.2
  164.7 2.9 %collective-permute-done.65.refs_2_ = bf16[64,768]{1,0:T(8,128)(2,1)S(1)} collective-permute-done((bf16[64,768]{1,0:T(8,128)(2,1)S(1)}, bf16[64,768]{1,0:T(8,128)(2,1)S(1)}, u32[]{:S(2)}, u32[]{:S(2)}) %collective-permute-start.65) | collective-permute-done | bytes 98336 | tf_op jit(solution)/shard_map/ppermute | solution.py:22
  176.3 2.5 collective-permute-done.72.refs_3_
  203.8 8.7 %collective-permute-done.83 = bf16[192,384]{1,0:T(8,128)(2,1)S(1)} collective-permute-done((bf16[192,384]{1,0:T(8,128)(2,1)S(1)}, bf16[192,384]{1,0:T(8,128)(2,1)S(1)}, u32[]{:S(2)}, u32[]{:S(2)}) %collective-permute-start.83) | collective-permute-done | bytes 147488 | tf_op jit(solution)/shard_map/ppermute | solution.py:22
  223.0 2.9 %collective-permute-done.85.refs_2_ = bf16[64,768]{1,0:T(8,128)(2,1)S(1)} collective-permute-done((bf16[64,768]{1,0:T(8,128)(2,1)S(1)}, bf16[64,768]{1,0:T(8,128)(2,1)S(1)}, u32[]{:S(2)}, u32[]{:S(2)}) %collective-permute-start.85) | collective-permute-done | bytes 98336 | tf_op jit(solution)/shard_map/ppermute | solution.py:22
  226.4 2.7 collective-permute-start.93
  233.4 9.8 %collective-permute-done.93 = bf16[192,768]{1,0:T(8,128)(2,1)S(1)} collective-permute-done((bf16[192,768]{1,0:T(8,128)(2,1)S(1)}, bf16[192,768]{1,0:T(8,128)(2,1)S(1)}, u32[]{:S(2)}, u32[]{:S(2)}) %collective-permute-start.93) | collective-permute-done | bytes 294944 | tf_op jit(solution)/shard_map/ppermute | solution.py:22
  247.8 2.7 collective-permute-start.97
  254.6 6.0 %collective-permute-done.96.g2 = f32[1,11904]{1,0:T(1,128)S(1)} collective-permute-done((f32[1,11904]{1,0:T(1,128)S(1)}, f32[1,11904]{1,0:T(1,128)S(1)}, u32[]{:S(2)}, u32[]{:S(2)}) %collective-permute-start.96) | collective-permute-done | bytes 47648 | tf_op jit(solution)/shard_map/ppermute | solution.py:22
  (305 shorter events, 179.3 us)
Async XLA Ops:
  34.2 14.3 %collective-permute-start.20 = (f32[1,2688]{1,0:T(1,128)S(1)}, f32[1,2688]{1,0:T(1,128)S(1)}, u32[]{:S(2)}, u32[]{:S(2)}) collective-permute-start(f32[1,2688]{1,0:T(1,128)S(1)} %broadcast_in_dim.27), channel_id=1, source_target_pairs={{0,16},{16,0},{1,17},{17,1},{2,18},{18,2},{3,19},{19,3},{4,20},{20... | collective-permute-start | bytes 32264 | tf_op jit(solution)/shard_map/ppermute | solution.py:22
  36.3 27.9 %collective-permute-start.19 = (bf16[768,384]{1,0:T(8,128)(2,1)S(1)}, bf16[768,384]{1,0:T(8,128)(2,1)S(1)}, u32[]{:S(2)}, u32[]{:S(2)}) collective-permute-start(bf16[768,384]{1,0:T(8,128)(2,1)S(1)} %stack_line.4.refs_4_), channel_id=1, source_target_pairs={{0,16},{16,0},{1,17},{17,1},{2,18},{18,2},{3,19},{19,3},{4,20},{20... | collective-permute-start | bytes 1769480 | tf_op jit(solution)/shard_map/ppermute | solution.py:22
  50.6 11.1 %collective-permute-start.17 = (bf16[2,192,384]{2,1,0:T(8,128)(2,1)S(1)}, bf16[2,192,384]{2,1,0:T(8,128)(2,1)S(1)}, u32[]{:S(2)}, u32[]{:S(2)}) collective-permute-start(bf16[2,192,384]{2,1,0:T(8,128)(2,1)S(1)} %pad_maximum_fusion.1.refs_0_), channel_id=1, source_target_pairs={{0,4},{4,0},{8,12},{12,8},{1,5},{5,1},{9,13},{13,9},{2,6},{6,2},{1... | collective-permute-start | bytes 884744 | tf_op jit(solution)/shard_map/ppermute | solution.py:22
  61.7 11.1 %collective-permute-start.24 = (bf16[2,192,384]{2,1,0:T(8,128)(2,1)S(1)}, bf16[2,192,384]{2,1,0:T(8,128)(2,1)S(1)}, u32[]{:S(2)}, u32[]{:S(2)}) collective-permute-start(bf16[2,192,384]{2,1,0:T(8,128)(2,1)S(1)} %pad_maximum_fusion.2.refs_1_), channel_id=1, source_target_pairs={{0,4},{4,0},{8,12},{12,8},{1,5},{5,1},{9,13},{13,9},{2,6},{6,2},{1... | collective-permute-start | bytes 884744 | tf_op jit(solution)/shard_map/ppermute | solution.py:22
  75.3 17.4 %collective-permute-start.34 = (bf16[768,768]{1,0:T(8,128)(2,1)S(1)}, bf16[768,768]{1,0:T(8,128)(2,1)S(1)}, u32[]{:S(2)}, u32[]{:S(2)}) collective-permute-start(bf16[768,768]{1,0:T(8,128)(2,1)S(1)} %stack_line.5.refs_4_), channel_id=1, source_target_pairs={{0,16},{16,0},{1,17},{17,1},{2,18},{18,2},{3,19},{19,3},{4,20},{20... | collective-permute-start | bytes 3538952 | tf_op jit(solution)/shard_map/ppermute | solution.py:22
  77.9 14.8 %collective-permute-start.29 = (bf16[2,192,384]{2,1,0:T(8,128)(2,1)S(1)}, bf16[2,192,384]{2,1,0:T(8,128)(2,1)S(1)}, u32[]{:S(2)}, u32[]{:S(2)}) collective-permute-start(bf16[2,192,384]{2,1,0:T(8,128)(2,1)S(1)} %pad_maximum_fusion.3.refs_0_), channel_id=1, source_target_pairs={{0,4},{4,0},{8,12},{12,8},{1,5},{5,1},{9,13},{13,9},{2,6},{6,2},{1... | collective-permute-start | bytes 884744 | tf_op jit(solution)/shard_map/ppermute | solution.py:22
  92.7 13.8 %collective-permute-start.38 = (bf16[2,192,384]{2,1,0:T(8,128)(2,1)S(1)}, bf16[2,192,384]{2,1,0:T(8,128)(2,1)S(1)}, u32[]{:S(2)}, u32[]{:S(2)}) collective-permute-start(bf16[2,192,384]{2,1,0:T(8,128)(2,1)S(1)} %pad_maximum_fusion.4.refs_0_), channel_id=1, source_target_pairs={{0,4},{4,0},{8,12},{12,8},{1,5},{5,1},{9,13},{13,9},{2,6},{6,2},{1... | collective-permute-start | bytes 884744 | tf_op jit(solution)/shard_map/ppermute | solution.py:22
  96.0 14.4 %collective-permute-start.43 = (bf16[768,384]{1,0:T(8,128)(2,1)S(1)}, bf16[768,384]{1,0:T(8,128)(2,1)S(1)}, u32[]{:S(2)}, u32[]{:S(2)}) collective-permute-start(bf16[768,384]{1,0:T(8,128)(2,1)S(1)} %stack_line.6.refs_4_), channel_id=1, source_target_pairs={{0,16},{16,0},{1,17},{17,1},{2,18},{18,2},{3,19},{19,3},{4,20},{20... | collective-permute-start | bytes 1769480 | tf_op jit(solution)/shard_map/ppermute | solution.py:22
  96.1 10.4 %collective-permute-start.39 = (bf16[192,384]{1,0:T(8,128)(2,1)S(1)}, bf16[192,384]{1,0:T(8,128)(2,1)S(1)}, u32[]{:S(2)}, u32[]{:S(2)}) collective-permute-start(bf16[192,384]{1,0:T(8,128)(2,1)S(1)} %get-tuple-element.384), channel_id=1, source_target_pairs={{0,8},{4,12},{8,0},{12,4},{1,9},{5,13},{9,1},{13,5},{2,10},{6,14},... | collective-permute-start | bytes 442376 | tf_op jit(solution)/shard_map/ppermute | solution.py:22
  115.8 17.7 %collective-permute-start.51 = (bf16[768,768]{1,0:T(8,128)(2,1)S(1)}, bf16[768,768]{1,0:T(8,128)(2,1)S(1)}, u32[]{:S(2)}, u32[]{:S(2)}) collective-permute-start(bf16[768,768]{1,0:T(8,128)(2,1)S(1)} %stack_line.7.refs_8_), channel_id=1, source_target_pairs={{0,16},{16,0},{1,17},{17,1},{2,18},{18,2},{3,19},{19,3},{4,20},{20... | collective-permute-start | bytes 3538952 | tf_op jit(solution)/shard_map/ppermute | solution.py:22
  157.0 12.6 %collective-permute-start.69 = (bf16[2,192,384]{2,1,0:T(8,128)(2,1)S(1)}, bf16[2,192,384]{2,1,0:T(8,128)(2,1)S(1)}, u32[]{:S(2)}, u32[]{:S(2)}) collective-permute-start(bf16[2,192,384]{2,1,0:T(8,128)(2,1)S(1)} %get-tuple-element.466), channel_id=1, source_target_pairs={{0,4},{4,0},{8,12},{12,8},{1,5},{5,1},{9,13},{13,9},{2,6},{6,2},{1... | collective-permute-start | bytes 884744 | tf_op jit(solution)/shard_map/ppermute | solution.py:22
  169.6 11.8 %collective-permute-start.73 = (bf16[2,192,384]{2,1,0:T(8,128)(2,1)S(1)}, bf16[2,192,384]{2,1,0:T(8,128)(2,1)S(1)}, u32[]{:S(2)}, u32[]{:S(2)}) collective-permute-start(bf16[2,192,384]{2,1,0:T(8,128)(2,1)S(1)} %get-tuple-element.476), channel_id=1, source_target_pairs={{0,4},{4,0},{8,12},{12,8},{1,5},{5,1},{9,13},{13,9},{2,6},{6,2},{1... | collective-permute-start | bytes 884744 | tf_op jit(solution)/shard_map/ppermute | solution.py:22
  196.7 16.4 %collective-permute-start.82 = (bf16[2,192,768]{2,1,0:T(8,128)(2,1)S(1)}, bf16[2,192,768]{2,1,0:T(8,128)(2,1)S(1)}, u32[]{:S(2)}, u32[]{:S(2)}) collective-permute-start(bf16[2,192,768]{2,1,0:T(8,128)(2,1)S(1)} %get-tuple-element.506), channel_id=1, source_target_pairs={{0,4},{4,0},{8,12},{12,8},{1,5},{5,1},{9,13},{13,9},{2,6},{6,2},{1... | collective-permute-start | bytes 1769480 | tf_op jit(solution)/shard_map/ppermute | solution.py:22
  198.3 14.2 %collective-permute-start.83 = (bf16[192,384]{1,0:T(8,128)(2,1)S(1)}, bf16[192,384]{1,0:T(8,128)(2,1)S(1)}, u32[]{:S(2)}, u32[]{:S(2)}) collective-permute-start(bf16[192,384]{1,0:T(8,128)(2,1)S(1)} %fusion.12), channel_id=1, source_target_pairs={{0,8},{4,12},{8,0},{12,4},{1,9},{5,13},{9,1},{13,5},{2,10},{6,14},... | collective-permute-start | bytes 442376 | tf_op jit(solution)/shard_map/ppermute | solution.py:22
  200.2 12.2 %collective-permute-start.81 = (bf16[64,768]{1,0:T(8,128)(2,1)S(1)}, bf16[64,768]{1,0:T(8,128)(2,1)S(1)}, u32[]{:S(2)}, u32[]{:S(2)}) collective-permute-start(bf16[64,768]{1,0:T(8,128)(2,1)S(1)} %get-tuple-element.509.refs_0_), channel_id=1, source_target_pairs={{0,3},{1,2},{2,1},{3,0},{4,7},{5,6},{6,5},{7,4},{8,11},{9,10},{10,... | collective-permute-start | bytes 294920 | tf_op jit(solution)/shard_map/ppermute | solution.py:22
  201.1 11.4 %collective-permute-start.80 = (bf16[64,768]{1,0:T(8,128)(2,1)S(1)}, bf16[64,768]{1,0:T(8,128)(2,1)S(1)}, u32[]{:S(2)}, u32[]{:S(2)}) collective-permute-start(bf16[64,768]{1,0:T(8,128)(2,1)S(1)} %get-tuple-element.509.refs_0_), channel_id=1, source_target_pairs={{0,2},{1,3},{2,0},{3,1},{4,6},{5,7},{6,4},{7,5},{8,10},{9,11},{10,... | collective-permute-start | bytes 294920 | tf_op jit(solution)/shard_map/ppermute | solution.py:22
  226.4 16.8 %collective-permute-start.93 = (bf16[192,768]{1,0:T(8,128)(2,1)S(1)}, bf16[192,768]{1,0:T(8,128)(2,1)S(1)}, u32[]{:S(2)}, u32[]{:S(2)}) collective-permute-start(bf16[192,768]{1,0:T(8,128)(2,1)S(1)} %fusion.2), channel_id=1, source_target_pairs={{0,8},{4,12},{8,0},{12,4},{1,9},{5,13},{9,1},{13,5},{2,10},{6,14},... | collective-permute-start | bytes 884744 | tf_op jit(solution)/shard_map/ppermute | solution.py:22
  229.1 14.1 %collective-permute-start.91 = (f32[2,6144]{1,0:T(2,128)S(1)}, f32[2,6144]{1,0:T(2,128)S(1)}, u32[]{:S(2)}, u32[]{:S(2)}) collective-permute-start(f32[2,6144]{1,0:T(2,128)S(1)} %pack_grads.1.refs_0_), channel_id=1, source_target_pairs={{0,3},{1,2},{2,1},{3,0},{4,7},{5,6},{6,5},{7,4},{8,11},{9,10},{10,... | collective-permute-start | bytes 147464 | tf_op jit(solution)/shard_map/ppermute | solution.py:22
  230.7 12.5 %collective-permute-start.90 = (f32[2,6144]{1,0:T(2,128)S(1)}, f32[2,6144]{1,0:T(2,128)S(1)}, u32[]{:S(2)}, u32[]{:S(2)}) collective-permute-start(f32[2,6144]{1,0:T(2,128)S(1)} %pack_grads.1.refs_0_), channel_id=1, source_target_pairs={{0,2},{1,3},{2,0},{3,1},{4,6},{5,7},{6,4},{7,5},{8,10},{9,11},{10,... | collective-permute-start | bytes 147464 | tf_op jit(solution)/shard_map/ppermute | solution.py:22
  231.6 11.7 %collective-permute-start.89 = (f32[2,6144]{1,0:T(2,128)S(1)}, f32[2,6144]{1,0:T(2,128)S(1)}, u32[]{:S(2)}, u32[]{:S(2)}) collective-permute-start(f32[2,6144]{1,0:T(2,128)S(1)} %pack_grads.1.refs_0_), channel_id=1, source_target_pairs={{0,1},{1,0},{2,3},{3,2},{4,5},{5,4},{6,7},{7,6},{8,9},{9,8},{10,11... | collective-permute-start | bytes 147464 | tf_op jit(solution)/shard_map/ppermute | solution.py:22
  232.7 12.7 %collective-permute-start.92 = (bf16[2,192,384]{2,1,0:T(8,128)(2,1)S(1)}, bf16[2,192,384]{2,1,0:T(8,128)(2,1)S(1)}, u32[]{:S(2)}, u32[]{:S(2)}) collective-permute-start(bf16[2,192,384]{2,1,0:T(8,128)(2,1)S(1)} %get-tuple-element.551), channel_id=1, source_target_pairs={{0,4},{4,0},{8,12},{12,8},{1,5},{5,1},{9,13},{13,9},{2,6},{6,2},{1... | collective-permute-start | bytes 884744 | tf_op jit(solution)/shard_map/ppermute | solution.py:22
  246.1 14.5 %collective-permute-start.98 = (bf16[192,384]{1,0:T(8,128)(2,1)S(1)}, bf16[192,384]{1,0:T(8,128)(2,1)S(1)}, u32[]{:S(2)}, u32[]{:S(2)}) collective-permute-start(bf16[192,384]{1,0:T(8,128)(2,1)S(1)} %fusion.11), channel_id=1, source_target_pairs={{0,8},{4,12},{8,0},{12,4},{1,9},{5,13},{9,1},{13,5},{2,10},{6,14},... | collective-permute-start | bytes 442376 | tf_op jit(solution)/shard_map/ppermute | solution.py:22
  252.3 20.6 %collective-permute-start.103 = (bf16[192,768]{1,0:T(8,128)(2,1)S(1)}, bf16[192,768]{1,0:T(8,128)(2,1)S(1)}, u32[]{:S(2)}, u32[]{:S(2)}) collective-permute-start(bf16[192,768]{1,0:T(8,128)(2,1)S(1)} %get-tuple-element.604), channel_id=1, source_target_pairs={{0,16},{16,0},{1,17},{17,1},{2,18},{18,2},{3,19},{19,3},{4,20},{20... | collective-permute-start | bytes 884744 | tf_op jit(solution)/shard_map/ppermute | solution.py:22
  260.7 10.7 %collective-permute-start.102 = (bf16[192,384]{1,0:T(8,128)(2,1)S(1)}, bf16[192,384]{1,0:T(8,128)(2,1)S(1)}, u32[]{:S(2)}, u32[]{:S(2)}) collective-permute-start(bf16[192,384]{1,0:T(8,128)(2,1)S(1)} %get-tuple-element.606), channel_id=1, source_target_pairs={{0,16},{16,0},{1,17},{17,1},{2,18},{18,2},{3,19},{19,3},{4,20},{20... | collective-permute-start | bytes 442376 | tf_op jit(solution)/shard_map/ppermute | solution.py:22
  (96 other events, 691.1 us)

commit v9 on v8

--- a/solution.py
+++ b/solution.py
@@ -484,9 +484,9 @@
     mods = out.shape[1] - keep.shape[1]
     first = place[0] == 0
     own, other = keep[...], received[...]
-    out[:, :mods] = jnp.where(first, own, other)[:, :mods]
-    out[:, mods : 2 * mods] = jnp.where(first, other, own)[:, :mods]
-    out[:, 2 * mods :] = own[:, mods:] + other[:, mods:]
+    out[:, :mods] = jnp.where(first, own, other)[:, :mods].astype(BF16)
+    out[:, mods : 2 * mods] = jnp.where(first, other, own)[:, :mods].astype(BF16)
+    out[:, 2 * mods :] = (own[:, mods:] + other[:, mods:]).astype(BF16)
 
 
 def mod_back_body(place, g0, g1, g2, g3, a0, a1, a2, a3, weight, w_grad, b_grad, bias, c0, c1, c2, c3):
@@ -496,16 +496,18 @@
     at = pl.multiple_of(place[1] * columns, 128)
     rows = []
     for ref in grads:
-        rows.append(ref[:, pl.ds(at, columns)])
-        rows.append(ref[:, pl.ds(pl.multiple_of(at + mods, 128), columns)])
+        rows.append(ref[:, pl.ds(at, columns)].astype(F32))
+        rows.append(ref[:, pl.ds(pl.multiple_of(at + mods, 128), columns)].astype(F32))
     picked = jnp.concatenate(rows, axis=0).astype(BF16)
     activated = jnp.concatenate([a0[...], a1[...], a2[...], a3[...]], axis=0)
     w_grad[...] = t_dot(activated, picked)
     act = dot_t(picked, weight[...])
     for k, out in enumerate((c0, c1, c2, c3)):
         out[...] = act[2 * k : 2 * k + 2]
-    b_grad[...] = tree_sum([ref[:, :mods] + ref[:, mods : 2 * mods] for ref in grads])
-    bias[...] = tree_sum([ref[:, 2 * mods :] for ref in grads])
+    b_grad[...] = tree_sum(
+        [ref[:, :mods].astype(F32) + ref[:, mods : 2 * mods].astype(F32) for ref in grads]
+    )
+    bias[...] = tree_sum([ref[:, 2 * mods :].astype(F32) for ref in grads])
 
 
 def on_device(
@@ -667,9 +669,6 @@
     mod0, mod1 = both_layers(mod_mine, swap(mod_other, "pipe", 1))
 
     w_attn0 = both_cores(second_a0)
-    mod0, mod1, first_e0 = tie(mod0, mod1, first_e0)
-    second_e0 = line_second(first_e0)
-    first_s0 = line_first(after(piece_of(0, 2), first_e0))
     own_f32 = shape((own, model), F32)
     own_bf16 = shape((own, model), BF16)
     blocks = [own_bf16] * count
@@ -709,22 +708,20 @@
             "middle", middle_body, [own_f32, own_f32, own_bf16], parts + [bias, h, mod]
         )
 
-    attn_rows, second_e0, first_s0 = tie(gather(attn_in, "tensor"), second_e0, first_s0)
+    attn_rows, first_e0 = tie(gather(attn_in, "tensor"), first_e0)
+    second_e0 = line_second(first_e0)
+    first_s0 = line_first(after(piece_of(0, 2), first_e0))
+    kept_attn0, parts = attention(attn_rows, w_attn0, biases[0][0])
+    parts, second_e0, first_s0 = tie(parts, second_e0, first_s0)
     second_s0 = line_second(first_s0)
     first_a1 = line_first(after(piece_of(1, 0), first_s0))
-    kept_attn0, parts = attention(attn_rows, w_attn0, biases[0][0])
-    parts, second_s0, first_a1 = tie(parts, second_s0, first_a1)
+    attended0, middle0, mlp_in = middle_of(parts, biases[0][1], h0, mod0)
+    mlp_rows0, second_s0, first_a1 = tie(gather(mlp_in, "tensor"), second_s0, first_a1)
     w_mlp0 = both_cores(second_e0, second_s0)
     second_a1 = line_second(first_a1)
     first_e1 = line_first(after(piece_of(1, 1), first_a1))
-    attended0, middle0, mlp_in = middle_of(parts, biases[0][1], h0, mod0)
-    g_rows1 = gather(after(g_shrunk1, parts), "tensor")
-    mlp_rows0, second_a1, first_e1, g_rows1 = tie(
-        gather(mlp_in, "tensor"), second_a1, first_e1, g_rows1
-    )
-    w_attn1 = both_cores(second_a1)
-    second_e1 = line_second(first_e1)
-    first_s1 = line_first(after(piece_of(1, 2), first_e1))
+    g_rows1 = gather(after(g_shrunk1, mlp_rows0), "tensor")
+    w_mlp0, g_rows1 = tie(w_mlp0, g_rows1)
     outs = kernel(
         "feed_forward",
         mlp_body,
@@ -733,8 +730,10 @@
     )
     mlp_rows0, pre0, hidden0 = outs[:3]
     (parts,) = tie(exchange(outs[3:], "tensor"))
-    parts, second_e1, first_s1 = tie(parts, second_e1, first_s1)
-    second_s1 = line_second(first_s1)
+    parts, second_a1, first_e1 = tie(parts, second_a1, first_e1)
+    w_attn1 = both_cores(second_a1)
+    second_e1 = line_second(first_e1)
+    first_s1 = line_first(after(piece_of(1, 2), first_e1))
     shrunk0, passed, h1, attn_in = kernel(
         "between",
         between_body,
@@ -742,9 +741,13 @@
         parts + [biases[0][3], middle0, mod0, mod1],
     )
 
-    (attn_rows, w_attn1), second_s1 = tie((gather(attn_in, "tensor"), w_attn1), second_s1)
+    (attn_rows, w_attn1), second_e1, first_s1 = tie(
+        (gather(attn_in, "tensor"), w_attn1), second_e1, first_s1
+    )
+    second_s1 = line_second(first_s1)
+    kept_attn1, parts = attention(attn_rows, w_attn1, biases[1][0])
+    parts, second_s1 = tie(parts, second_s1)
     w_mlp1 = both_cores(second_e1, second_s1)
-    kept_attn1, parts = attention(attn_rows, w_attn1, biases[1][0])
     attended1, middle1, mlp_in = middle_of(parts, biases[1][1], h1, mod1)
     outs = kernel(
         "feed_forward_both",
@@ -887,13 +890,11 @@
         [own_bf16, vector, vector],
         y_parts + [biases[1][3], middle1, mod1, g_y1, g_shrunk1],
     )
-    g_rows, near_m0, far_a1 = tie(gather(g_attended, "tensor"), near_m0, far_a1)
+    g_rows, near_m0 = tie(gather(g_attended, "tensor"), near_m0)
     far_m0 = line_far(parts_m0, near_m0)
     (g_rows, g_joint, joint_grad0), parts = attention_back(g_rows, w_attn0, kept_attn0)
-    parts, (parts_a0,) = tie(
-        parts, line_parts(attn_weight_grads(kept_attn0, g_joint, g_rows), 1)
-    )
-    near_a0 = line_near(parts_a0)
+    parts, far_m0, g_joint, g_rows = tie(parts, far_m0, g_joint, g_rows)
+    (parts_a0,) = line_parts(attn_weight_grads(kept_attn0, g_joint, g_rows), 1)
     g_h0, g_shift_attn0, g_scale_attn0 = kernel(
         "finish_back",
         finish_back_body,
@@ -929,8 +930,8 @@
             shrink_grad1,
         ],
     )[0]
-    packed_all, near_a0, far_m0 = tie(gather(packed, "tensor"), near_a0, far_m0)
-    far_a0 = line_far(parts_a0, near_a0)
+    packed_all, parts_a0, far_a1 = tie(gather(packed, "tensor"), parts_a0, far_a1)
+    near_a0 = line_near(parts_a0)
     keep, give = run(
         "grads_sum",
         functools.partial(grads_sum_body, count),
@@ -941,12 +942,13 @@
     joined = run(
         "grads_join",
         grads_join_body,
-        [shape((1, 2 * mods + bias_width), F32)],
+        [shape((1, 2 * mods + bias_width), BF16)],
         [keep, swap(give, "pipe", 1)],
         place,
     )[0]
     joined_all = gather(joined, "dp") if direct else lax.all_gather(joined, "dp", axis=0, tiled=True)
-    joined_all, far_a0 = tie(joined_all, far_a0)
+    joined_all, near_a0 = tie(joined_all, near_a0)
+    far_a0 = line_far(parts_a0, near_a0)
     mlp_grad0 = line_total(parts_m0, near_m0, far_m0)
     mlp_grad1 = jnp.concatenate(
         [line_total(parts_e1, near_e1, far_e1), line_total(parts_s1, near_s1, far_s1)], axis=1
@@ -981,8 +983,8 @@
         act_grad = tree_sum(exchange(outs[3:], "dp"))
     else:
         mod_grads = joined_all[:, : 2 * mods].reshape(line_size * micro, mods)
-        bias_sum = jnp.sum(joined_all[:, 2 * mods :], axis=0, keepdims=True)
-        ada_bias_grad = jnp.sum(mod_grads, axis=0, keepdims=True)
+        bias_sum = jnp.sum(joined_all[:, 2 * mods :].astype(F32), axis=0, keepdims=True)
+        ada_bias_grad = jnp.sum(mod_grads.astype(F32), axis=0, keepdims=True)
         picked = lax.dynamic_slice_in_dim(mod_grads, line * columns, columns, 1).astype(BF16)
         ada_grad = t_dot(activated_all, picked)
         act_partial = dot_t(picked, own_rows).reshape(line_size, micro, -1)

time: 275 us -> 258 us (0.938)
  waiting for transfers between devices: 123 us -> 103 us
  starting transfers between devices: 105 us -> 109 us
    ppermute x104, waiting for transfers between devices: 123 us -> 103 us  [swap(): return lax.ppermute(value, axis, pairs)]
    ppermute x104, starting transfers between devices: 105 us -> 109 us  [swap(): return lax.ppermute(value, axis, pairs)]
  transfers between devices with their start and end apart: 104 -> 104, of which waited for: 64 -> 65; matrix products, arithmetic and copies ran while one was open for 2% -> 1% of each run, Pallas kernels for 6% -> 8%
where the time goes in v9:
time: 258 us
  starting transfers between devices  109 us (42%)
  waiting for transfers between devices  103 us (40%)
  Pallas kernels  35.4 us (14%)
  local copies, waits for them, and re-layouts  6.87 us (3%)
  other arithmetic  2.71 us (1%)
    ppermute x104, starting transfers between devices, swap(): return lax.ppermute(value, axis, pairs)  109 us
    ppermute x104, waiting for transfers between devices, swap(): return lax.ppermute(value, axis, pairs)  103 us
    pallas_call x37, Pallas kernels, run(): pl.pallas_call(body, out_shape=outs, in_specs=specs, out_specs=[pl.BlockS...  33.9 us
  transfers between devices with their start and end apart: 104, of which 65 were waited for; matrix products, arithmetic and copies ran while one was open for 1% of the time, Pallas kernels for 8%

profile of v9, /device:TPU:0, one launch (start us, length us, event | category | flops | bytes accessed | tf_op | source)
XLA Modules:
  0.0 258.0 jit_solution(6244578464942707091)
XLA Ops:
  4.9 5.0 %collective-permute-start.2 = (bf16[2,192]{1,0:T(2,128)(2,1)S(1)}, bf16[2,192]{1,0:T(2,128)(2,1)S(1)}, u32[]{:S(2)}, u32[]{:S(2)}) collective-permute-start(bf16[2,192]{1,0:T(2,128)(2,1)S(1)} %fusion.21.a0), channel_id=1, source_target_pairs={{0,12},{4,8},{8,4},{12,0},{1,13},{5,9},{9,5},{13,1},{2,14},{6,10},... | collective-permute-start | bytes 2312 | tf_op jit(solution)/shard_map/ppermute | solution.py:22
  11.4 2.9 %collective-permute-done.1.a2 = bf16[2,192]{1,0:T(2,128)(2,1)S(1)} collective-permute-done((bf16[2,192]{1,0:T(2,128)(2,1)S(1)}, bf16[2,192]{1,0:T(2,128)(2,1)S(1)}, u32[]{:S(2)}, u32[]{:S(2)}) %collective-permute-start.1) | collective-permute-done | bytes 800 | tf_op jit(solution)/shard_map/ppermute | solution.py:22
  16.5 2.5 collective-permute-start.5
  28.5 2.3 collective-permute-done.8.p1
  40.8 3.1 %collective-permute-done.16 = bf16[192,384]{1,0:T(8,128)(2,1)S(1)} collective-permute-done((bf16[192,384]{1,0:T(8,128)(2,1)S(1)}, bf16[192,384]{1,0:T(8,128)(2,1)S(1)}, u32[]{:S(2)}, u32[]{:S(2)}) %collective-permute-start.16) | collective-permute-done | bytes 147488 | tf_op jit(solution)/shard_map/ppermute | solution.py:22
  53.9 2.9 %collective-permute-done.23 = bf16[192,384]{1,0:T(8,128)(2,1)S(1)} collective-permute-done((bf16[192,384]{1,0:T(8,128)(2,1)S(1)}, bf16[192,384]{1,0:T(8,128)(2,1)S(1)}, u32[]{:S(2)}, u32[]{:S(2)}) %collective-permute-start.23) | collective-permute-done | bytes 147488 | tf_op jit(solution)/shard_map/ppermute | solution.py:22
  64.4 2.8 %collective-permute-done.26.refs_3_ = bf16[64,768]{1,0:T(8,128)(2,1)S(1)} collective-permute-done((bf16[64,768]{1,0:T(8,128)(2,1)S(1)}, bf16[64,768]{1,0:T(8,128)(2,1)S(1)}, u32[]{:S(2)}, u32[]{:S(2)}) %collective-permute-start.26) | collective-permute-done | bytes 98336 | tf_op jit(solution)/shard_map/ppermute | solution.py:22
  75.8 2.9 %collective-permute-done.32.refs_7_ = bf16[64,768]{1,0:T(8,128)(2,1)S(1)} collective-permute-done((bf16[64,768]{1,0:T(8,128)(2,1)S(1)}, bf16[64,768]{1,0:T(8,128)(2,1)S(1)}, u32[]{:S(2)}, u32[]{:S(2)}) %collective-permute-start.32) | collective-permute-done | bytes 98336 | tf_op jit(solution)/shard_map/ppermute | solution.py:22
  95.6 2.2 collective-permute-done.40.refs_3_
  99.8 2.6 %collective-permute-done.38.refs_1_ = bf16[64,768]{1,0:T(8,128)(2,1)S(1)} collective-permute-done((bf16[64,768]{1,0:T(8,128)(2,1)S(1)}, bf16[64,768]{1,0:T(8,128)(2,1)S(1)}, u32[]{:S(2)}, u32[]{:S(2)}) %collective-permute-start.38) | collective-permute-done | bytes 98336 | tf_op jit(solution)/shard_map/ppermute | solution.py:22
  118.5 3.0 %collective-permute-done.50.refs_3_ = bf16[64,768]{1,0:T(8,128)(2,1)S(1)} collective-permute-done((bf16[64,768]{1,0:T(8,128)(2,1)S(1)}, bf16[64,768]{1,0:T(8,128)(2,1)S(1)}, u32[]{:S(2)}, u32[]{:S(2)}) %collective-permute-start.50) | collective-permute-done | bytes 98336 | tf_op jit(solution)/shard_map/ppermute | solution.py:22
  131.8 3.1 %collective-permute-done.53.refs_2_ = bf16[64,768]{1,0:T(8,128)(2,1)S(1)} collective-permute-done((bf16[64,768]{1,0:T(8,128)(2,1)S(1)}, bf16[64,768]{1,0:T(8,128)(2,1)S(1)}, u32[]{:S(2)}, u32[]{:S(2)}) %collective-permute-start.53) | collective-permute-done | bytes 98336 | tf_op jit(solution)/shard_map/ppermute | solution.py:22
  139.4 2.7 %collective-permute-done.62.refs_3_ = bf16[64,768]{1,0:T(8,128)(2,1)S(1)} collective-permute-done((bf16[64,768]{1,0:T(8,128)(2,1)S(1)}, bf16[64,768]{1,0:T(8,128)(2,1)S(1)}, u32[]{:S(2)}, u32[]{:S(2)}) %collective-permute-start.62) | collective-permute-done | bytes 98336 | tf_op jit(solution)/shard_map/ppermute | solution.py:22
  142.6 2.4 attention_back.2
  154.0 3.3 %collective-permute-done.65.refs_2_ = bf16[64,768]{1,0:T(8,128)(2,1)S(1)} collective-permute-done((bf16[64,768]{1,0:T(8,128)(2,1)S(1)}, bf16[64,768]{1,0:T(8,128)(2,1)S(1)}, u32[]{:S(2)}, u32[]{:S(2)}) %collective-permute-start.65) | collective-permute-done | bytes 98336 | tf_op jit(solution)/shard_map/ppermute | solution.py:22
  165.8 2.9 %collective-permute-done.72.refs_3_ = bf16[64,768]{1,0:T(8,128)(2,1)S(1)} collective-permute-done((bf16[64,768]{1,0:T(8,128)(2,1)S(1)}, bf16[64,768]{1,0:T(8,128)(2,1)S(1)}, u32[]{:S(2)}, u32[]{:S(2)}) %collective-permute-start.72) | collective-permute-done | bytes 98336 | tf_op jit(solution)/shard_map/ppermute | solution.py:22
  194.9 2.4 collective-permute-done.81.refs_3_
  200.0 2.7 %collective-permute-start.86 = (bf16[192,768]{1,0:T(8,128)(2,1)S(1)}, bf16[192,768]{1,0:T(8,128)(2,1)S(1)}, u32[]{:S(2)}, u32[]{:S(2)}) collective-permute-start(bf16[192,768]{1,0:T(8,128)(2,1)S(1)} %fusion.2), channel_id=1, source_target_pairs={{0,8},{4,12},{8,0},{12,4},{1,9},{5,13},{9,1},{13,5},{2,10},{6,14},... | collective-permute-start | bytes 884744 | tf_op jit(solution)/shard_map/ppermute | solution.py:22
  202.7 2.4 attention_back.3
  212.5 5.2 %collective-permute-done.86 = bf16[192,768]{1,0:T(8,128)(2,1)S(1)} collective-permute-done((bf16[192,768]{1,0:T(8,128)(2,1)S(1)}, bf16[192,768]{1,0:T(8,128)(2,1)S(1)}, u32[]{:S(2)}, u32[]{:S(2)}) %collective-permute-start.86) | collective-permute-done | bytes 294944 | tf_op jit(solution)/shard_map/ppermute | solution.py:22
  219.6 2.5 collective-permute-start.90
  244.9 2.3 collective-permute-start.100
  247.9 2.3 collective-permute-done.100
  250.9 4.0 %collective-permute-done.101 = bf16[192,384]{1,0:T(8,128)(2,1)S(1)} collective-permute-done((bf16[192,384]{1,0:T(8,128)(2,1)S(1)}, bf16[192,384]{1,0:T(8,128)(2,1)S(1)}, u32[]{:S(2)}, u32[]{:S(2)}) %collective-permute-start.101) | collective-permute-done | bytes 147488 | tf_op jit(solution)/shard_map/ppermute | solution.py:22
  (305 shorter events, 186.1 us)
Async XLA Ops:
  14.3 9.2 %collective-permute-start.7 = (bf16[192,384]{1,0:T(8,128)(2,1)S(1)}, bf16[192,384]{1,0:T(8,128)(2,1)S(1)}, u32[]{:S(2)}, u32[]{:S(2)}) collective-permute-start(bf16[192,384]{1,0:T(8,128)(2,1)S(1)} %get-tuple-element.317), channel_id=1, source_target_pairs={{0,8},{4,12},{8,0},{12,4},{1,9},{5,13},{9,1},{13,5},{2,10},{6,14},... | collective-permute-start | bytes 442376 | tf_op jit(solution)/shard_map/ppermute | solution.py:22
  23.8 10.6 %collective-permute-start.18 = (f32[1,2688]{1,0:T(1,128)S(1)}, f32[1,2688]{1,0:T(1,128)S(1)}, u32[]{:S(2)}, u32[]{:S(2)}) collective-permute-start(f32[1,2688]{1,0:T(1,128)S(1)} %broadcast_in_dim.27), channel_id=1, source_target_pairs={{0,16},{16,0},{1,17},{17,1},{2,18},{18,2},{3,19},{19,3},{4,20},{20... | collective-permute-start | bytes 32264 | tf_op jit(solution)/shard_map/ppermute | solution.py:22
  34.5 9.5 %collective-permute-start.16 = (bf16[192,384]{1,0:T(8,128)(2,1)S(1)}, bf16[192,384]{1,0:T(8,128)(2,1)S(1)}, u32[]{:S(2)}, u32[]{:S(2)}) collective-permute-start(bf16[192,384]{1,0:T(8,128)(2,1)S(1)} %get-tuple-element.338), channel_id=1, source_target_pairs={{0,8},{4,12},{8,0},{12,4},{1,9},{5,13},{9,1},{13,5},{2,10},{6,14},... | collective-permute-start | bytes 442376 | tf_op jit(solution)/shard_map/ppermute | solution.py:22
  36.0 12.2 %collective-permute-start.17 = (bf16[768,384]{1,0:T(8,128)(2,1)S(1)}, bf16[768,384]{1,0:T(8,128)(2,1)S(1)}, u32[]{:S(2)}, u32[]{:S(2)}) collective-permute-start(bf16[768,384]{1,0:T(8,128)(2,1)S(1)} %stack_line.4.refs_4_), channel_id=1, source_target_pairs={{0,16},{16,0},{1,17},{17,1},{2,18},{18,2},{3,19},{19,3},{4,20},{20... | collective-permute-start | bytes 1769480 | tf_op jit(solution)/shard_map/ppermute | solution.py:22
  45.3 12.2 %collective-permute-start.22 = (bf16[2,192,384]{2,1,0:T(8,128)(2,1)S(1)}, bf16[2,192,384]{2,1,0:T(8,128)(2,1)S(1)}, u32[]{:S(2)}, u32[]{:S(2)}) collective-permute-start(bf16[2,192,384]{2,1,0:T(8,128)(2,1)S(1)} %pad_maximum_fusion.1.refs_0_), channel_id=1, source_target_pairs={{0,4},{4,0},{8,12},{12,8},{1,5},{5,1},{9,13},{13,9},{2,6},{6,2},{1... | collective-permute-start | bytes 884744 | tf_op jit(solution)/shard_map/ppermute | solution.py:22
  47.3 9.5 %collective-permute-start.23 = (bf16[192,384]{1,0:T(8,128)(2,1)S(1)}, bf16[192,384]{1,0:T(8,128)(2,1)S(1)}, u32[]{:S(2)}, u32[]{:S(2)}) collective-permute-start(bf16[192,384]{1,0:T(8,128)(2,1)S(1)} %get-tuple-element.348), channel_id=1, source_target_pairs={{0,8},{4,12},{8,0},{12,4},{1,9},{5,13},{9,1},{13,5},{2,10},{6,14},... | collective-permute-start | bytes 442376 | tf_op jit(solution)/shard_map/ppermute | solution.py:22
  58.3 9.6 %collective-permute-start.28 = (bf16[192,384]{1,0:T(8,128)(2,1)S(1)}, bf16[192,384]{1,0:T(8,128)(2,1)S(1)}, u32[]{:S(2)}, u32[]{:S(2)}) collective-permute-start(bf16[192,384]{1,0:T(8,128)(2,1)S(1)} %get-tuple-element.372), channel_id=1, source_target_pairs={{0,8},{4,12},{8,0},{12,4},{1,9},{5,13},{9,1},{13,5},{2,10},{6,14},... | collective-permute-start | bytes 442376 | tf_op jit(solution)/shard_map/ppermute | solution.py:22
  60.3 9.5 %collective-permute-start.27 = (bf16[2,192,384]{2,1,0:T(8,128)(2,1)S(1)}, bf16[2,192,384]{2,1,0:T(8,128)(2,1)S(1)}, u32[]{:S(2)}, u32[]{:S(2)}) collective-permute-start(bf16[2,192,384]{2,1,0:T(8,128)(2,1)S(1)} %pad_maximum_fusion.2.refs_1_), channel_id=1, source_target_pairs={{0,4},{4,0},{8,12},{12,8},{1,5},{5,1},{9,13},{13,9},{2,6},{6,2},{1... | collective-permute-start | bytes 884744 | tf_op jit(solution)/shard_map/ppermute | solution.py:22
  70.5 9.8 %collective-permute-start.29 = (bf16[768,768]{1,0:T(8,128)(2,1)S(1)}, bf16[768,768]{1,0:T(8,128)(2,1)S(1)}, u32[]{:S(2)}, u32[]{:S(2)}) collective-permute-start(bf16[768,768]{1,0:T(8,128)(2,1)S(1)} %stack_line.5.refs_4_), channel_id=1, source_target_pairs={{0,16},{16,0},{1,17},{17,1},{2,18},{18,2},{3,19},{19,3},{4,20},{20... | collective-permute-start | bytes 3538952 | tf_op jit(solution)/shard_map/ppermute | solution.py:22
  70.6 19.2 %collective-permute-start.36 = (bf16[2,192,384]{2,1,0:T(8,128)(2,1)S(1)}, bf16[2,192,384]{2,1,0:T(8,128)(2,1)S(1)}, u32[]{:S(2)}, u32[]{:S(2)}) collective-permute-start(bf16[2,192,384]{2,1,0:T(8,128)(2,1)S(1)} %pad_maximum_fusion.3.refs_0_), channel_id=1, source_target_pairs={{0,4},{4,0},{8,12},{12,8},{1,5},{5,1},{9,13},{13,9},{2,6},{6,2},{1... | collective-permute-start | bytes 884744 | tf_op jit(solution)/shard_map/ppermute | solution.py:22
  78.7 11.1 %collective-permute-start.37 = (bf16[192,384]{1,0:T(8,128)(2,1)S(1)}, bf16[192,384]{1,0:T(8,128)(2,1)S(1)}, u32[]{:S(2)}, u32[]{:S(2)}) collective-permute-start(bf16[192,384]{1,0:T(8,128)(2,1)S(1)} %get-tuple-element.385), channel_id=1, source_target_pairs={{0,8},{4,12},{8,0},{12,4},{1,9},{5,13},{9,1},{13,5},{2,10},{6,14},... | collective-permute-start | bytes 442376 | tf_op jit(solution)/shard_map/ppermute | solution.py:22
  90.4 12.8 %collective-permute-start.41 = (bf16[768,384]{1,0:T(8,128)(2,1)S(1)}, bf16[768,384]{1,0:T(8,128)(2,1)S(1)}, u32[]{:S(2)}, u32[]{:S(2)}) collective-permute-start(bf16[768,384]{1,0:T(8,128)(2,1)S(1)} %stack_line.6.refs_4_), channel_id=1, source_target_pairs={{0,16},{16,0},{1,17},{17,1},{2,18},{18,2},{3,19},{19,3},{4,20},{20... | collective-permute-start | bytes 1769480 | tf_op jit(solution)/shard_map/ppermute | solution.py:22
  90.6 12.6 %collective-permute-start.42 = (bf16[2,192,384]{2,1,0:T(8,128)(2,1)S(1)}, bf16[2,192,384]{2,1,0:T(8,128)(2,1)S(1)}, u32[]{:S(2)}, u32[]{:S(2)}) collective-permute-start(bf16[2,192,384]{2,1,0:T(8,128)(2,1)S(1)} %pad_maximum_fusion.4.refs_0_), channel_id=1, source_target_pairs={{0,4},{4,0},{8,12},{12,8},{1,5},{5,1},{9,13},{13,9},{2,6},{6,2},{1... | collective-permute-start | bytes 884744 | tf_op jit(solution)/shard_map/ppermute | solution.py:22
  92.6 9.9 %collective-permute-start.43 = (bf16[192,384]{1,0:T(8,128)(2,1)S(1)}, bf16[192,384]{1,0:T(8,128)(2,1)S(1)}, u32[]{:S(2)}, u32[]{:S(2)}) collective-permute-start(bf16[192,384]{1,0:T(8,128)(2,1)S(1)} %get-tuple-element.399), channel_id=1, source_target_pairs={{0,8},{4,12},{8,0},{12,4},{1,9},{5,13},{9,1},{13,5},{2,10},{6,14},... | collective-permute-start | bytes 442376 | tf_op jit(solution)/shard_map/ppermute | solution.py:22
  103.2 10.7 %collective-permute-start.47 = (bf16[2,192,384]{2,1,0:T(8,128)(2,1)S(1)}, bf16[2,192,384]{2,1,0:T(8,128)(2,1)S(1)}, u32[]{:S(2)}, u32[]{:S(2)}) collective-permute-start(bf16[2,192,384]{2,1,0:T(8,128)(2,1)S(1)} %pad_maximum_fusion.5.refs_1_), channel_id=1, source_target_pairs={{0,4},{4,0},{8,12},{12,8},{1,5},{5,1},{9,13},{13,9},{2,6},{6,2},{1... | collective-permute-start | bytes 884744 | tf_op jit(solution)/shard_map/ppermute | solution.py:22
  146.3 12.6 %collective-permute-start.69 = (bf16[2,192,384]{2,1,0:T(8,128)(2,1)S(1)}, bf16[2,192,384]{2,1,0:T(8,128)(2,1)S(1)}, u32[]{:S(2)}, u32[]{:S(2)}) collective-permute-start(bf16[2,192,384]{2,1,0:T(8,128)(2,1)S(1)} %get-tuple-element.475), channel_id=1, source_target_pairs={{0,4},{4,0},{8,12},{12,8},{1,5},{5,1},{9,13},{13,9},{2,6},{6,2},{1... | collective-permute-start | bytes 884744 | tf_op jit(solution)/shard_map/ppermute | solution.py:22
  148.0 10.0 %collective-permute-start.68 = (bf16[192,384]{1,0:T(8,128)(2,1)S(1)}, bf16[192,384]{1,0:T(8,128)(2,1)S(1)}, u32[]{:S(2)}, u32[]{:S(2)}) collective-permute-start(bf16[192,384]{1,0:T(8,128)(2,1)S(1)} %fusion.14), channel_id=1, source_target_pairs={{0,8},{4,12},{8,0},{12,4},{1,9},{5,13},{9,1},{13,5},{2,10},{6,14},... | collective-permute-start | bytes 442376 | tf_op jit(solution)/shard_map/ppermute | solution.py:22
  158.9 11.8 %collective-permute-start.73 = (bf16[2,192,384]{2,1,0:T(8,128)(2,1)S(1)}, bf16[2,192,384]{2,1,0:T(8,128)(2,1)S(1)}, u32[]{:S(2)}, u32[]{:S(2)}) collective-permute-start(bf16[2,192,384]{2,1,0:T(8,128)(2,1)S(1)} %get-tuple-element.485), channel_id=1, source_target_pairs={{0,4},{4,0},{8,12},{12,8},{1,5},{5,1},{9,13},{13,9},{2,6},{6,2},{1... | collective-permute-start | bytes 884744 | tf_op jit(solution)/shard_map/ppermute | solution.py:22
  160.7 9.2 %collective-permute-start.74 = (bf16[192,384]{1,0:T(8,128)(2,1)S(1)}, bf16[192,384]{1,0:T(8,128)(2,1)S(1)}, u32[]{:S(2)}, u32[]{:S(2)}) collective-permute-start(bf16[192,384]{1,0:T(8,128)(2,1)S(1)} %fusion.13), channel_id=1, source_target_pairs={{0,8},{4,12},{8,0},{12,4},{1,9},{5,13},{9,1},{13,5},{2,10},{6,14},... | collective-permute-start | bytes 442376 | tf_op jit(solution)/shard_map/ppermute | solution.py:22
  186.9 13.0 %collective-permute-start.82 = (bf16[2,192,768]{2,1,0:T(8,128)(2,1)S(1)}, bf16[2,192,768]{2,1,0:T(8,128)(2,1)S(1)}, u32[]{:S(2)}, u32[]{:S(2)}) collective-permute-start(bf16[2,192,768]{2,1,0:T(8,128)(2,1)S(1)} %get-tuple-element.515), channel_id=1, source_target_pairs={{0,4},{4,0},{8,12},{12,8},{1,5},{5,1},{9,13},{13,9},{2,6},{6,2},{1... | collective-permute-start | bytes 1769480 | tf_op jit(solution)/shard_map/ppermute | solution.py:22
  200.0 17.7 %collective-permute-start.86 = (bf16[192,768]{1,0:T(8,128)(2,1)S(1)}, bf16[192,768]{1,0:T(8,128)(2,1)S(1)}, u32[]{:S(2)}, u32[]{:S(2)}) collective-permute-start(bf16[192,768]{1,0:T(8,128)(2,1)S(1)} %fusion.2), channel_id=1, source_target_pairs={{0,8},{4,12},{8,0},{12,4},{1,9},{5,13},{9,1},{13,5},{2,10},{6,14},... | collective-permute-start | bytes 884744 | tf_op jit(solution)/shard_map/ppermute | solution.py:22
  208.8 15.4 %collective-permute-start.92 = (bf16[192,384]{1,0:T(8,128)(2,1)S(1)}, bf16[192,384]{1,0:T(8,128)(2,1)S(1)}, u32[]{:S(2)}, u32[]{:S(2)}) collective-permute-start(bf16[192,384]{1,0:T(8,128)(2,1)S(1)} %fusion.12), channel_id=1, source_target_pairs={{0,8},{4,12},{8,0},{12,4},{1,9},{5,13},{9,1},{13,5},{2,10},{6,14},... | collective-permute-start | bytes 442376 | tf_op jit(solution)/shard_map/ppermute | solution.py:22
  224.2 10.6 %collective-permute-start.103 = (bf16[192,768]{1,0:T(8,128)(2,1)S(1)}, bf16[192,768]{1,0:T(8,128)(2,1)S(1)}, u32[]{:S(2)}, u32[]{:S(2)}) collective-permute-start(bf16[192,768]{1,0:T(8,128)(2,1)S(1)} %get-tuple-element.614), channel_id=1, source_target_pairs={{0,16},{16,0},{1,17},{17,1},{2,18},{18,2},{3,19},{19,3},{4,20},{20... | collective-permute-start | bytes 884744 | tf_op jit(solution)/shard_map/ppermute | solution.py:22
  227.8 12.5 %collective-permute-start.97 = (bf16[2,192,384]{2,1,0:T(8,128)(2,1)S(1)}, bf16[2,192,384]{2,1,0:T(8,128)(2,1)S(1)}, u32[]{:S(2)}, u32[]{:S(2)}) collective-permute-start(bf16[2,192,384]{2,1,0:T(8,128)(2,1)S(1)} %get-tuple-element.574), channel_id=1, source_target_pairs={{0,4},{4,0},{8,12},{12,8},{1,5},{5,1},{9,13},{13,9},{2,6},{6,2},{1... | collective-permute-start | bytes 884744 | tf_op jit(solution)/shard_map/ppermute | solution.py:22
  (96 other events, 628.1 us)

commit v10 on v9

--- a/solution.py
+++ b/solution.py
@@ -721,13 +721,13 @@
     second_a1 = line_second(first_a1)
     first_e1 = line_first(after(piece_of(1, 1), first_a1))
     g_rows1 = gather(after(g_shrunk1, mlp_rows0), "tensor")
-    w_mlp0, g_rows1 = tie(w_mlp0, g_rows1)
     outs = kernel(
         "feed_forward",
         mlp_body,
         [wide_bf16, shape((rows, hidden), F32), hidden_bf16] + blocks,
         mlp_rows0 + [w_mlp0[0], w_mlp0[1], biases[0][2]],
     )
+    outs, g_rows1 = tie(outs, g_rows1)
     mlp_rows0, pre0, hidden0 = outs[:3]
     (parts,) = tie(exchange(outs[3:], "tensor"))
     parts, second_a1, first_e1 = tie(parts, second_a1, first_e1)
@@ -868,7 +868,6 @@
     g_rows0, near_a1, far_s1, parts_a1 = tie(
         gather(g_shrunk0, "tensor"), near_a1, far_s1, parts_a1
     )
-    far_a1 = line_far(parts_a1, near_a1)
     outs = kernel(
         "feed_forward_back",
         mlp_back_body,
@@ -893,7 +892,8 @@
     g_rows, near_m0 = tie(gather(g_attended, "tensor"), near_m0)
     far_m0 = line_far(parts_m0, near_m0)
     (g_rows, g_joint, joint_grad0), parts = attention_back(g_rows, w_attn0, kept_attn0)
-    parts, far_m0, g_joint, g_rows = tie(parts, far_m0, g_joint, g_rows)
+    parts, far_m0, g_joint, g_rows, near_a1 = tie(parts, far_m0, g_joint, g_rows, near_a1)
+    far_a1 = line_far(parts_a1, near_a1)
     (parts_a0,) = line_parts(attn_weight_grads(kept_attn0, g_joint, g_rows), 1)
     g_h0, g_shift_attn0, g_scale_attn0 = kernel(
         "finish_back",
@@ -930,7 +930,7 @@
             shrink_grad1,
         ],
     )[0]
-    packed_all, parts_a0, far_a1 = tie(gather(packed, "tensor"), parts_a0, far_a1)
+    packed_all, far_a1 = tie(gather(packed, "tensor"), far_a1)
     near_a0 = line_near(parts_a0)
     keep, give = run(
         "grads_sum",
@@ -939,16 +939,17 @@
         packed_all + [joint_grad0, expand_grad0, joint_grad1, expand_grad1],
         place,
     )
+    received, near_a0 = tie(swap(give, "pipe", 1), near_a0)
+    far_a0 = line_far(parts_a0, near_a0)
     joined = run(
         "grads_join",
         grads_join_body,
         [shape((1, 2 * mods + bias_width), BF16)],
-        [keep, swap(give, "pipe", 1)],
+        [keep, received],
         place,
     )[0]
     joined_all = gather(joined, "dp") if direct else lax.all_gather(joined, "dp", axis=0, tiled=True)
-    joined_all, near_a0 = tie(joined_all, near_a0)
-    far_a0 = line_far(parts_a0, near_a0)
+    joined_all, far_a0 = tie(joined_all, far_a0)
     mlp_grad0 = line_total(parts_m0, near_m0, far_m0)
     mlp_grad1 = jnp.concatenate(
         [line_total(parts_e1, near_e1, far_e1), line_total(parts_s1, near_s1, far_s1)], axis=1

time: 258 us -> 254 us (0.984)
  waiting for transfers between devices: 103 us -> 92.7 us
  starting transfers between devices: 109 us -> 114 us
    ppermute x104, waiting for transfers between devices: 103 us -> 92.7 us  [swap(): return lax.ppermute(value, axis, pairs)]
    ppermute x104, starting transfers between devices: 109 us -> 114 us  [swap(): return lax.ppermute(value, axis, pairs)]
  transfers between devices with their start and end apart: 104 -> 104, of which waited for: 65 -> 57; matrix products, arithmetic and copies ran while one was open for 1% -> 2% of each run, Pallas kernels for 8% -> 8%
where the time goes in v10:
time: 254 us; the launch traced here: 253 us
  starting transfers between devices  114 us (45%)
  waiting for transfers between devices  92.7 us (36%)
  Pallas kernels  35.2 us (14%)
  local copies, waits for them, and re-layouts  6.87 us (3%)
  other arithmetic  2.71 us (1%)
    ppermute x104, starting transfers between devices, swap(): return lax.ppermute(value, axis, pairs)  114 us
    ppermute x104, waiting for transfers between devices, swap(): return lax.ppermute(value, axis, pairs)  92.7 us
    pallas_call x37, Pallas kernels, run(): pl.pallas_call(body, out_shape=outs, in_specs=specs, out_specs=[pl.BlockS...  33.7 us
  transfers between devices with their start and end apart: 104, of which 57 were waited for; matrix products, arithmetic and copies ran while one was open for 2% of the time, Pallas kernels for 8%

profile of v10, /device:TPU:0, one launch (start us, length us, event | category | flops | bytes accessed | tf_op | source)
XLA Modules:
  0.0 253.2 jit_solution(14772006001010939789)
XLA Ops:
  4.9 5.0 %collective-permute-start.2 = (bf16[2,192]{1,0:T(2,128)(2,1)S(1)}, bf16[2,192]{1,0:T(2,128)(2,1)S(1)}, u32[]{:S(2)}, u32[]{:S(2)}) collective-permute-start(bf16[2,192]{1,0:T(2,128)(2,1)S(1)} %fusion.21.a0), channel_id=1, source_target_pairs={{0,12},{4,8},{8,4},{12,0},{1,13},{5,9},{9,5},{13,1},{2,14},{6,10},... | collective-permute-start | bytes 2312 | tf_op jit(solution)/shard_map/ppermute | solution.py:22
  11.4 2.9 %collective-permute-done.1.a2 = bf16[2,192]{1,0:T(2,128)(2,1)S(1)} collective-permute-done((bf16[2,192]{1,0:T(2,128)(2,1)S(1)}, bf16[2,192]{1,0:T(2,128)(2,1)S(1)}, u32[]{:S(2)}, u32[]{:S(2)}) %collective-permute-start.1) | collective-permute-done | bytes 800 | tf_op jit(solution)/shard_map/ppermute | solution.py:22
  16.5 2.5 collective-permute-start.5
  28.5 2.3 collective-permute-done.8.p1
  40.8 3.1 %collective-permute-done.16 = bf16[192,384]{1,0:T(8,128)(2,1)S(1)} collective-permute-done((bf16[192,384]{1,0:T(8,128)(2,1)S(1)}, bf16[192,384]{1,0:T(8,128)(2,1)S(1)}, u32[]{:S(2)}, u32[]{:S(2)}) %collective-permute-start.16) | collective-permute-done | bytes 147488 | tf_op jit(solution)/shard_map/ppermute | solution.py:22
  53.9 2.9 %collective-permute-done.23 = bf16[192,384]{1,0:T(8,128)(2,1)S(1)} collective-permute-done((bf16[192,384]{1,0:T(8,128)(2,1)S(1)}, bf16[192,384]{1,0:T(8,128)(2,1)S(1)}, u32[]{:S(2)}, u32[]{:S(2)}) %collective-permute-start.23) | collective-permute-done | bytes 147488 | tf_op jit(solution)/shard_map/ppermute | solution.py:22
  64.4 2.8 %collective-permute-done.26.refs_3_ = bf16[64,768]{1,0:T(8,128)(2,1)S(1)} collective-permute-done((bf16[64,768]{1,0:T(8,128)(2,1)S(1)}, bf16[64,768]{1,0:T(8,128)(2,1)S(1)}, u32[]{:S(2)}, u32[]{:S(2)}) %collective-permute-start.26) | collective-permute-done | bytes 98336 | tf_op jit(solution)/shard_map/ppermute | solution.py:22
  90.7 2.4 collective-permute-start.43
  117.3 3.0 %collective-permute-done.50.refs_3_ = bf16[64,768]{1,0:T(8,128)(2,1)S(1)} collective-permute-done((bf16[64,768]{1,0:T(8,128)(2,1)S(1)}, bf16[64,768]{1,0:T(8,128)(2,1)S(1)}, u32[]{:S(2)}, u32[]{:S(2)}) %collective-permute-start.50) | collective-permute-done | bytes 98336 | tf_op jit(solution)/shard_map/ppermute | solution.py:22
  130.6 3.1 %collective-permute-done.53.refs_2_ = bf16[64,768]{1,0:T(8,128)(2,1)S(1)} collective-permute-done((bf16[64,768]{1,0:T(8,128)(2,1)S(1)}, bf16[64,768]{1,0:T(8,128)(2,1)S(1)}, u32[]{:S(2)}, u32[]{:S(2)}) %collective-permute-start.53) | collective-permute-done | bytes 98336 | tf_op jit(solution)/shard_map/ppermute | solution.py:22
  137.9 2.5 collective-permute-done.62.refs_3_
  141.4 2.4 attention_back.2
  152.8 3.2 %collective-permute-done.65.refs_2_ = bf16[64,768]{1,0:T(8,128)(2,1)S(1)} collective-permute-done((bf16[64,768]{1,0:T(8,128)(2,1)S(1)}, bf16[64,768]{1,0:T(8,128)(2,1)S(1)}, u32[]{:S(2)}, u32[]{:S(2)}) %collective-permute-start.65) | collective-permute-done | bytes 98336 | tf_op jit(solution)/shard_map/ppermute | solution.py:22
  164.6 2.9 %collective-permute-done.72.refs_3_ = bf16[64,768]{1,0:T(8,128)(2,1)S(1)} collective-permute-done((bf16[64,768]{1,0:T(8,128)(2,1)S(1)}, bf16[64,768]{1,0:T(8,128)(2,1)S(1)}, u32[]{:S(2)}, u32[]{:S(2)}) %collective-permute-start.72) | collective-permute-done | bytes 98336 | tf_op jit(solution)/shard_map/ppermute | solution.py:22
  181.1 2.4 collective-permute-start.82
  188.6 3.0 %collective-permute-done.81.refs_3_ = bf16[64,768]{1,0:T(8,128)(2,1)S(1)} collective-permute-done((bf16[64,768]{1,0:T(8,128)(2,1)S(1)}, bf16[64,768]{1,0:T(8,128)(2,1)S(1)}, u32[]{:S(2)}, u32[]{:S(2)}) %collective-permute-start.81) | collective-permute-done | bytes 98336 | tf_op jit(solution)/shard_map/ppermute | solution.py:22
  193.3 2.4 collective-permute-done.82
  197.9 2.4 attention_back.3
  216.5 2.3 collective-permute-start.94
  218.9 5.3 %collective-permute-done.91 = bf16[192,384]{1,0:T(8,128)(2,1)S(1)} collective-permute-done((bf16[192,384]{1,0:T(8,128)(2,1)S(1)}, bf16[192,384]{1,0:T(8,128)(2,1)S(1)}, u32[]{:S(2)}, u32[]{:S(2)}) %collective-permute-start.91) | collective-permute-done | bytes 147488 | tf_op jit(solution)/shard_map/ppermute | solution.py:22
  226.2 2.3 collective-permute-done.94
  236.2 4.6 %collective-permute-done.96.g2 = bf16[1,11904]{1,0:T(2,128)(2,1)S(1)} collective-permute-done((bf16[1,11904]{1,0:T(2,128)(2,1)S(1)}, bf16[1,11904]{1,0:T(2,128)(2,1)S(1)}, u32[]{:S(2)}, u32[]{:S(2)}) %collective-permute-start.96) | collective-permute-done | bytes 23840 | tf_op jit(solution)/shard_map/ppermute | solution.py:22
  243.4 2.3 collective-permute-start.100
  248.5 2.6 %collective-permute-done.101 = f32[2,192]{1,0:T(2,128)S(1)} collective-permute-done((f32[2,192]{1,0:T(2,128)S(1)}, f32[2,192]{1,0:T(2,128)S(1)}, u32[]{:S(2)}, u32[]{:S(2)}) %collective-permute-start.101) | collective-permute-done | bytes 1568 | tf_op jit(solution)/shard_map/ppermute | solution.py:22
  (305 shorter events, 181.0 us)
Async XLA Ops:
  14.3 9.2 %collective-permute-start.7 = (bf16[192,384]{1,0:T(8,128)(2,1)S(1)}, bf16[192,384]{1,0:T(8,128)(2,1)S(1)}, u32[]{:S(2)}, u32[]{:S(2)}) collective-permute-start(bf16[192,384]{1,0:T(8,128)(2,1)S(1)} %get-tuple-element.322), channel_id=1, source_target_pairs={{0,8},{4,12},{8,0},{12,4},{1,9},{5,13},{9,1},{13,5},{2,10},{6,14},... | collective-permute-start | bytes 442376 | tf_op jit(solution)/shard_map/ppermute | solution.py:22
  23.8 10.6 %collective-permute-start.18 = (f32[1,2688]{1,0:T(1,128)S(1)}, f32[1,2688]{1,0:T(1,128)S(1)}, u32[]{:S(2)}, u32[]{:S(2)}) collective-permute-start(f32[1,2688]{1,0:T(1,128)S(1)} %broadcast_in_dim.27), channel_id=1, source_target_pairs={{0,16},{16,0},{1,17},{17,1},{2,18},{18,2},{3,19},{19,3},{4,20},{20... | collective-permute-start | bytes 32264 | tf_op jit(solution)/shard_map/ppermute | solution.py:22
  34.5 9.5 %collective-permute-start.16 = (bf16[192,384]{1,0:T(8,128)(2,1)S(1)}, bf16[192,384]{1,0:T(8,128)(2,1)S(1)}, u32[]{:S(2)}, u32[]{:S(2)}) collective-permute-start(bf16[192,384]{1,0:T(8,128)(2,1)S(1)} %get-tuple-element.343), channel_id=1, source_target_pairs={{0,8},{4,12},{8,0},{12,4},{1,9},{5,13},{9,1},{13,5},{2,10},{6,14},... | collective-permute-start | bytes 442376 | tf_op jit(solution)/shard_map/ppermute | solution.py:22
  36.0 12.2 %collective-permute-start.17 = (bf16[768,384]{1,0:T(8,128)(2,1)S(1)}, bf16[768,384]{1,0:T(8,128)(2,1)S(1)}, u32[]{:S(2)}, u32[]{:S(2)}) collective-permute-start(bf16[768,384]{1,0:T(8,128)(2,1)S(1)} %stack_line.4.refs_4_), channel_id=1, source_target_pairs={{0,16},{16,0},{1,17},{17,1},{2,18},{18,2},{3,19},{19,3},{4,20},{20... | collective-permute-start | bytes 1769480 | tf_op jit(solution)/shard_map/ppermute | solution.py:22
  45.3 12.2 %collective-permute-start.22 = (bf16[2,192,384]{2,1,0:T(8,128)(2,1)S(1)}, bf16[2,192,384]{2,1,0:T(8,128)(2,1)S(1)}, u32[]{:S(2)}, u32[]{:S(2)}) collective-permute-start(bf16[2,192,384]{2,1,0:T(8,128)(2,1)S(1)} %pad_maximum_fusion.1.refs_0_), channel_id=1, source_target_pairs={{0,4},{4,0},{8,12},{12,8},{1,5},{5,1},{9,13},{13,9},{2,6},{6,2},{1... | collective-permute-start | bytes 884744 | tf_op jit(solution)/shard_map/ppermute | solution.py:22
  47.3 9.5 %collective-permute-start.23 = (bf16[192,384]{1,0:T(8,128)(2,1)S(1)}, bf16[192,384]{1,0:T(8,128)(2,1)S(1)}, u32[]{:S(2)}, u32[]{:S(2)}) collective-permute-start(bf16[192,384]{1,0:T(8,128)(2,1)S(1)} %get-tuple-element.353), channel_id=1, source_target_pairs={{0,8},{4,12},{8,0},{12,4},{1,9},{5,13},{9,1},{13,5},{2,10},{6,14},... | collective-permute-start | bytes 442376 | tf_op jit(solution)/shard_map/ppermute | solution.py:22
  58.3 9.6 %collective-permute-start.28 = (bf16[192,384]{1,0:T(8,128)(2,1)S(1)}, bf16[192,384]{1,0:T(8,128)(2,1)S(1)}, u32[]{:S(2)}, u32[]{:S(2)}) collective-permute-start(bf16[192,384]{1,0:T(8,128)(2,1)S(1)} %get-tuple-element.382), channel_id=1, source_target_pairs={{0,8},{4,12},{8,0},{12,4},{1,9},{5,13},{9,1},{13,5},{2,10},{6,14},... | collective-permute-start | bytes 442376 | tf_op jit(solution)/shard_map/ppermute | solution.py:22
  60.3 9.5 %collective-permute-start.27 = (bf16[2,192,384]{2,1,0:T(8,128)(2,1)S(1)}, bf16[2,192,384]{2,1,0:T(8,128)(2,1)S(1)}, u32[]{:S(2)}, u32[]{:S(2)}) collective-permute-start(bf16[2,192,384]{2,1,0:T(8,128)(2,1)S(1)} %pad_maximum_fusion.2.refs_1_), channel_id=1, source_target_pairs={{0,4},{4,0},{8,12},{12,8},{1,5},{5,1},{9,13},{13,9},{2,6},{6,2},{1... | collective-permute-start | bytes 884744 | tf_op jit(solution)/shard_map/ppermute | solution.py:22
  70.6 17.3 %collective-permute-start.36 = (bf16[2,192,384]{2,1,0:T(8,128)(2,1)S(1)}, bf16[2,192,384]{2,1,0:T(8,128)(2,1)S(1)}, u32[]{:S(2)}, u32[]{:S(2)}) collective-permute-start(bf16[2,192,384]{2,1,0:T(8,128)(2,1)S(1)} %pad_maximum_fusion.3.refs_0_), channel_id=1, source_target_pairs={{0,4},{4,0},{8,12},{12,8},{1,5},{5,1},{9,13},{13,9},{2,6},{6,2},{1... | collective-permute-start | bytes 884744 | tf_op jit(solution)/shard_map/ppermute | solution.py:22
  75.8 12.1 %collective-permute-start.37 = (bf16[192,384]{1,0:T(8,128)(2,1)S(1)}, bf16[192,384]{1,0:T(8,128)(2,1)S(1)}, u32[]{:S(2)}, u32[]{:S(2)}) collective-permute-start(bf16[192,384]{1,0:T(8,128)(2,1)S(1)} %get-tuple-element.395), channel_id=1, source_target_pairs={{0,8},{4,12},{8,0},{12,4},{1,9},{5,13},{9,1},{13,5},{2,10},{6,14},... | collective-permute-start | bytes 442376 | tf_op jit(solution)/shard_map/ppermute | solution.py:22
  88.5 12.8 %collective-permute-start.41 = (bf16[768,384]{1,0:T(8,128)(2,1)S(1)}, bf16[768,384]{1,0:T(8,128)(2,1)S(1)}, u32[]{:S(2)}, u32[]{:S(2)}) collective-permute-start(bf16[768,384]{1,0:T(8,128)(2,1)S(1)} %stack_line.6.refs_4_), channel_id=1, source_target_pairs={{0,16},{16,0},{1,17},{17,1},{2,18},{18,2},{3,19},{19,3},{4,20},{20... | collective-permute-start | bytes 1769480 | tf_op jit(solution)/shard_map/ppermute | solution.py:22
  88.6 12.6 %collective-permute-start.42 = (bf16[2,192,384]{2,1,0:T(8,128)(2,1)S(1)}, bf16[2,192,384]{2,1,0:T(8,128)(2,1)S(1)}, u32[]{:S(2)}, u32[]{:S(2)}) collective-permute-start(bf16[2,192,384]{2,1,0:T(8,128)(2,1)S(1)} %pad_maximum_fusion.4.refs_0_), channel_id=1, source_target_pairs={{0,4},{4,0},{8,12},{12,8},{1,5},{5,1},{9,13},{13,9},{2,6},{6,2},{1... | collective-permute-start | bytes 884744 | tf_op jit(solution)/shard_map/ppermute | solution.py:22
  90.7 9.1 %collective-permute-start.43 = (bf16[192,384]{1,0:T(8,128)(2,1)S(1)}, bf16[192,384]{1,0:T(8,128)(2,1)S(1)}, u32[]{:S(2)}, u32[]{:S(2)}) collective-permute-start(bf16[192,384]{1,0:T(8,128)(2,1)S(1)} %get-tuple-element.409), channel_id=1, source_target_pairs={{0,8},{4,12},{8,0},{12,4},{1,9},{5,13},{9,1},{13,5},{2,10},{6,14},... | collective-permute-start | bytes 442376 | tf_op jit(solution)/shard_map/ppermute | solution.py:22
  101.3 11.5 %collective-permute-start.47 = (bf16[2,192,384]{2,1,0:T(8,128)(2,1)S(1)}, bf16[2,192,384]{2,1,0:T(8,128)(2,1)S(1)}, u32[]{:S(2)}, u32[]{:S(2)}) collective-permute-start(bf16[2,192,384]{2,1,0:T(8,128)(2,1)S(1)} %pad_maximum_fusion.5.refs_1_), channel_id=1, source_target_pairs={{0,4},{4,0},{8,12},{12,8},{1,5},{5,1},{9,13},{13,9},{2,6},{6,2},{1... | collective-permute-start | bytes 884744 | tf_op jit(solution)/shard_map/ppermute | solution.py:22
  145.1 12.6 %collective-permute-start.69 = (bf16[2,192,384]{2,1,0:T(8,128)(2,1)S(1)}, bf16[2,192,384]{2,1,0:T(8,128)(2,1)S(1)}, u32[]{:S(2)}, u32[]{:S(2)}) collective-permute-start(bf16[2,192,384]{2,1,0:T(8,128)(2,1)S(1)} %get-tuple-element.485), channel_id=1, source_target_pairs={{0,4},{4,0},{8,12},{12,8},{1,5},{5,1},{9,13},{13,9},{2,6},{6,2},{1... | collective-permute-start | bytes 884744 | tf_op jit(solution)/shard_map/ppermute | solution.py:22
  146.8 10.0 %collective-permute-start.68 = (bf16[192,384]{1,0:T(8,128)(2,1)S(1)}, bf16[192,384]{1,0:T(8,128)(2,1)S(1)}, u32[]{:S(2)}, u32[]{:S(2)}) collective-permute-start(bf16[192,384]{1,0:T(8,128)(2,1)S(1)} %fusion.14), channel_id=1, source_target_pairs={{0,8},{4,12},{8,0},{12,4},{1,9},{5,13},{9,1},{13,5},{2,10},{6,14},... | collective-permute-start | bytes 442376 | tf_op jit(solution)/shard_map/ppermute | solution.py:22
  157.7 11.7 %collective-permute-start.73 = (bf16[2,192,384]{2,1,0:T(8,128)(2,1)S(1)}, bf16[2,192,384]{2,1,0:T(8,128)(2,1)S(1)}, u32[]{:S(2)}, u32[]{:S(2)}) collective-permute-start(bf16[2,192,384]{2,1,0:T(8,128)(2,1)S(1)} %get-tuple-element.495), channel_id=1, source_target_pairs={{0,4},{4,0},{8,12},{12,8},{1,5},{5,1},{9,13},{13,9},{2,6},{6,2},{1... | collective-permute-start | bytes 884744 | tf_op jit(solution)/shard_map/ppermute | solution.py:22
  159.1 9.3 %collective-permute-start.74 = (bf16[192,384]{1,0:T(8,128)(2,1)S(1)}, bf16[192,384]{1,0:T(8,128)(2,1)S(1)}, u32[]{:S(2)}, u32[]{:S(2)}) collective-permute-start(bf16[192,384]{1,0:T(8,128)(2,1)S(1)} %fusion.13), channel_id=1, source_target_pairs={{0,8},{4,12},{8,0},{12,4},{1,9},{5,13},{9,1},{13,5},{2,10},{6,14},... | collective-permute-start | bytes 442376 | tf_op jit(solution)/shard_map/ppermute | solution.py:22
  181.1 14.6 %collective-permute-start.82 = (bf16[2,192,768]{2,1,0:T(8,128)(2,1)S(1)}, bf16[2,192,768]{2,1,0:T(8,128)(2,1)S(1)}, u32[]{:S(2)}, u32[]{:S(2)}) collective-permute-start(bf16[2,192,768]{2,1,0:T(8,128)(2,1)S(1)} %get-tuple-element.525), channel_id=1, source_target_pairs={{0,4},{4,0},{8,12},{12,8},{1,5},{5,1},{9,13},{13,9},{2,6},{6,2},{1... | collective-permute-start | bytes 1769480 | tf_op jit(solution)/shard_map/ppermute | solution.py:22
  195.8 14.3 %collective-permute-start.86 = (bf16[192,768]{1,0:T(8,128)(2,1)S(1)}, bf16[192,768]{1,0:T(8,128)(2,1)S(1)}, u32[]{:S(2)}, u32[]{:S(2)}) collective-permute-start(bf16[192,768]{1,0:T(8,128)(2,1)S(1)} %fusion.2), channel_id=1, source_target_pairs={{0,8},{4,12},{8,0},{12,4},{1,9},{5,13},{9,1},{13,5},{2,10},{6,14},... | collective-permute-start | bytes 884744 | tf_op jit(solution)/shard_map/ppermute | solution.py:22
  216.5 12.0 %collective-permute-start.94 = (bf16[2,192,384]{2,1,0:T(8,128)(2,1)S(1)}, bf16[2,192,384]{2,1,0:T(8,128)(2,1)S(1)}, u32[]{:S(2)}, u32[]{:S(2)}) collective-permute-start(bf16[2,192,384]{2,1,0:T(8,128)(2,1)S(1)} %get-tuple-element.582), channel_id=1, source_target_pairs={{0,4},{4,0},{8,12},{12,8},{1,5},{5,1},{9,13},{13,9},{2,6},{6,2},{1... | collective-permute-start | bytes 884744 | tf_op jit(solution)/shard_map/ppermute | solution.py:22
  228.5 12.3 %collective-permute-start.98 = (bf16[192,384]{1,0:T(8,128)(2,1)S(1)}, bf16[192,384]{1,0:T(8,128)(2,1)S(1)}, u32[]{:S(2)}, u32[]{:S(2)}) collective-permute-start(bf16[192,384]{1,0:T(8,128)(2,1)S(1)} %fusion.11), channel_id=1, source_target_pairs={{0,8},{4,12},{8,0},{12,4},{1,9},{5,13},{9,1},{13,5},{2,10},{6,14},... | collective-permute-start | bytes 442376 | tf_op jit(solution)/shard_map/ppermute | solution.py:22
  231.4 9.4 %collective-permute-start.96 = (bf16[1,11904]{1,0:T(2,128)(2,1)S(1)}, bf16[1,11904]{1,0:T(2,128)(2,1)S(1)}, u32[]{:S(2)}, u32[]{:S(2)}) collective-permute-start(bf16[1,11904]{1,0:T(2,128)(2,1)S(1)} %grads_join.1.g0), channel_id=1, source_target_pairs={{0,8},{4,12},{8,0},{12,4},{1,9},{5,13},{9,1},{13,5},{2,10},{6,14},... | collective-permute-start | bytes 71432 | tf_op jit(solution)/shard_map/ppermute | solution.py:22
  240.9 10.8 %collective-permute-start.102 = (bf16[192,384]{1,0:T(8,128)(2,1)S(1)}, bf16[192,384]{1,0:T(8,128)(2,1)S(1)}, u32[]{:S(2)}, u32[]{:S(2)}) collective-permute-start(bf16[192,384]{1,0:T(8,128)(2,1)S(1)} %get-tuple-element.626), channel_id=1, source_target_pairs={{0,16},{16,0},{1,17},{17,1},{2,18},{18,2},{3,19},{19,3},{4,20},{20... | collective-permute-start | bytes 442376 | tf_op jit(solution)/shard_map/ppermute | solution.py:22
  (96 other events, 638.5 us)

commit v11 on v10

--- a/solution.py
+++ b/solution.py
@@ -930,7 +930,7 @@
             shrink_grad1,
         ],
     )[0]
-    packed_all, far_a1 = tie(gather(packed, "tensor"), far_a1)
+    packed_all = gather(packed, "tensor")
     near_a0 = line_near(parts_a0)
     keep, give = run(
         "grads_sum",
@@ -939,8 +939,7 @@
         packed_all + [joint_grad0, expand_grad0, joint_grad1, expand_grad1],
         place,
     )
-    received, near_a0 = tie(swap(give, "pipe", 1), near_a0)
-    far_a0 = line_far(parts_a0, near_a0)
+    received, far_a1 = tie(swap(give, "pipe", 1), far_a1)
     joined = run(
         "grads_join",
         grads_join_body,
@@ -949,7 +948,8 @@
         place,
     )[0]
     joined_all = gather(joined, "dp") if direct else lax.all_gather(joined, "dp", axis=0, tiled=True)
-    joined_all, far_a0 = tie(joined_all, far_a0)
+    joined_all, near_a0 = tie(joined_all, near_a0)
+    far_a0 = line_far(parts_a0, near_a0)
     mlp_grad0 = line_total(parts_m0, near_m0, far_m0)
     mlp_grad1 = jnp.concatenate(
         [line_total(parts_e1, near_e1, far_e1), line_total(parts_s1, near_s1, far_s1)], axis=1
@@ -981,7 +981,10 @@
             place,
         )
         ada_grad, ada_bias_grad, bias_sum = outs[:3]
-        act_grad = tree_sum(exchange(outs[3:], "dp"))
+        act_parts, joint_w_grad, output_w_grad = tie(
+            exchange(outs[3:], "dp"), joint_w_grad, output_w_grad
+        )
+        act_grad = tree_sum(act_parts)
     else:
         mod_grads = joined_all[:, : 2 * mods].reshape(line_size * micro, mods)
         bias_sum = jnp.sum(joined_all[:, 2 * mods :].astype(F32), axis=0, keepdims=True)

time: 254 us -> 250 us (0.984)
    ppermute x104, waiting for transfers between devices: 92.7 us -> 90.2 us  [swap(): return lax.ppermute(value, axis, pairs)]
  transfers between devices with their start and end apart: 104 -> 104, of which waited for: 57 -> 63; matrix products, arithmetic and copies ran while one was open for 2% -> 2% of each run, Pallas kernels for 8% -> 10%
where the time goes in v11:
time: 250 us
  starting transfers between devices  113 us (45%)
  waiting for transfers between devices  90.2 us (36%)
  Pallas kernels  35.3 us (14%)
  local copies, waits for them, and re-layouts  6.87 us (3%)
  other arithmetic  2.73 us (1%)
    ppermute x104, starting transfers between devices, swap(): return lax.ppermute(value, axis, pairs)  113 us
    ppermute x104, waiting for transfers between devices, swap(): return lax.ppermute(value, axis, pairs)  90.2 us
    pallas_call x37, Pallas kernels, run(): pl.pallas_call(body, out_shape=outs, in_specs=specs, out_specs=[pl.BlockS...  33.9 us
  transfers between devices with their start and end apart: 104, of which 63 were waited for; matrix products, arithmetic and copies ran while one was open for 2% of the time, Pallas kernels for 10%

profile of v11, /device:TPU:0, one launch (start us, length us, event | category | flops | bytes accessed | tf_op | source)
XLA Modules:
  0.0 249.6 jit_solution(9123913369263129043)
XLA Ops:
  4.9 5.0 %collective-permute-start.2 = (bf16[2,192]{1,0:T(2,128)(2,1)S(1)}, bf16[2,192]{1,0:T(2,128)(2,1)S(1)}, u32[]{:S(2)}, u32[]{:S(2)}) collective-permute-start(bf16[2,192]{1,0:T(2,128)(2,1)S(1)} %fusion.21.a0), channel_id=1, source_target_pairs={{0,12},{4,8},{8,4},{12,0},{1,13},{5,9},{9,5},{13,1},{2,14},{6,10},... | collective-permute-start | bytes 2312 | tf_op jit(solution)/shard_map/ppermute | solution.py:22
  11.4 2.9 %collective-permute-done.1.a2 = bf16[2,192]{1,0:T(2,128)(2,1)S(1)} collective-permute-done((bf16[2,192]{1,0:T(2,128)(2,1)S(1)}, bf16[2,192]{1,0:T(2,128)(2,1)S(1)}, u32[]{:S(2)}, u32[]{:S(2)}) %collective-permute-start.1) | collective-permute-done | bytes 800 | tf_op jit(solution)/shard_map/ppermute | solution.py:22
  16.5 2.5 %collective-permute-start.5 = (f32[8,1152]{1,0:T(8,128)S(1)}, f32[8,1152]{1,0:T(8,128)S(1)}, u32[]{:S(2)}, u32[]{:S(2)}) collective-permute-start(f32[8,1152]{1,0:T(8,128)S(1)} %mod_first.1.refs_0_), channel_id=1, source_target_pairs={{0,3},{1,2},{2,1},{3,0},{4,7},{5,6},{6,5},{7,4},{8,11},{9,10},{10,... | collective-permute-start | bytes 110600 | tf_op jit(solution)/shard_map/ppermute | solution.py:22
  28.5 2.3 collective-permute-done.8.p1
  40.8 3.1 %collective-permute-done.16 = bf16[192,384]{1,0:T(8,128)(2,1)S(1)} collective-permute-done((bf16[192,384]{1,0:T(8,128)(2,1)S(1)}, bf16[192,384]{1,0:T(8,128)(2,1)S(1)}, u32[]{:S(2)}, u32[]{:S(2)}) %collective-permute-start.16) | collective-permute-done | bytes 147488 | tf_op jit(solution)/shard_map/ppermute | solution.py:22
  48.2 2.1 attention.2
  53.9 2.9 %collective-permute-done.23 = bf16[192,384]{1,0:T(8,128)(2,1)S(1)} collective-permute-done((bf16[192,384]{1,0:T(8,128)(2,1)S(1)}, bf16[192,384]{1,0:T(8,128)(2,1)S(1)}, u32[]{:S(2)}, u32[]{:S(2)}) %collective-permute-start.23) | collective-permute-done | bytes 147488 | tf_op jit(solution)/shard_map/ppermute | solution.py:22
  64.4 2.8 %collective-permute-done.26.refs_3_ = bf16[64,768]{1,0:T(8,128)(2,1)S(1)} collective-permute-done((bf16[64,768]{1,0:T(8,128)(2,1)S(1)}, bf16[64,768]{1,0:T(8,128)(2,1)S(1)}, u32[]{:S(2)}, u32[]{:S(2)}) %collective-permute-start.26) | collective-permute-done | bytes 98336 | tf_op jit(solution)/shard_map/ppermute | solution.py:22
  90.7 2.4 collective-permute-start.43
  97.8 2.1 collective-permute-done.38.refs_1_
  103.2 2.1 attention.3
  117.3 3.0 %collective-permute-done.50.refs_3_ = bf16[64,768]{1,0:T(8,128)(2,1)S(1)} collective-permute-done((bf16[64,768]{1,0:T(8,128)(2,1)S(1)}, bf16[64,768]{1,0:T(8,128)(2,1)S(1)}, u32[]{:S(2)}, u32[]{:S(2)}) %collective-permute-start.50) | collective-permute-done | bytes 98336 | tf_op jit(solution)/shard_map/ppermute | solution.py:22
  122.0 2.2 feed_forward_both.1
  130.6 3.1 %collective-permute-done.53.refs_2_ = bf16[64,768]{1,0:T(8,128)(2,1)S(1)} collective-permute-done((bf16[64,768]{1,0:T(8,128)(2,1)S(1)}, bf16[64,768]{1,0:T(8,128)(2,1)S(1)}, u32[]{:S(2)}, u32[]{:S(2)}) %collective-permute-start.53) | collective-permute-done | bytes 98336 | tf_op jit(solution)/shard_map/ppermute | solution.py:22
  137.9 2.5 %collective-permute-done.62.refs_3_ = bf16[64,768]{1,0:T(8,128)(2,1)S(1)} collective-permute-done((bf16[64,768]{1,0:T(8,128)(2,1)S(1)}, bf16[64,768]{1,0:T(8,128)(2,1)S(1)}, u32[]{:S(2)}, u32[]{:S(2)}) %collective-permute-start.62) | collective-permute-done | bytes 98336 | tf_op jit(solution)/shard_map/ppermute | solution.py:22
  141.4 2.4 attention_back.2
  152.8 3.2 %collective-permute-done.65.refs_2_ = bf16[64,768]{1,0:T(8,128)(2,1)S(1)} collective-permute-done((bf16[64,768]{1,0:T(8,128)(2,1)S(1)}, bf16[64,768]{1,0:T(8,128)(2,1)S(1)}, u32[]{:S(2)}, u32[]{:S(2)}) %collective-permute-start.65) | collective-permute-done | bytes 98336 | tf_op jit(solution)/shard_map/ppermute | solution.py:22
  164.6 3.0 %collective-permute-done.72.refs_3_ = bf16[64,768]{1,0:T(8,128)(2,1)S(1)} collective-permute-done((bf16[64,768]{1,0:T(8,128)(2,1)S(1)}, bf16[64,768]{1,0:T(8,128)(2,1)S(1)}, u32[]{:S(2)}, u32[]{:S(2)}) %collective-permute-start.72) | collective-permute-done | bytes 98336 | tf_op jit(solution)/shard_map/ppermute | solution.py:22
  185.1 2.5 collective-permute-start.82
  193.6 2.4 collective-permute-done.81.refs_3_
  200.4 2.4 attention_back.3
  210.6 2.1 collective-permute-done.86
  223.5 4.7 %collective-permute-done.92 = bf16[192,384]{1,0:T(8,128)(2,1)S(1)} collective-permute-done((bf16[192,384]{1,0:T(8,128)(2,1)S(1)}, bf16[192,384]{1,0:T(8,128)(2,1)S(1)}, u32[]{:S(2)}, u32[]{:S(2)}) %collective-permute-start.92) | collective-permute-done | bytes 147488 | tf_op jit(solution)/shard_map/ppermute | solution.py:22
  230.8 2.4 collective-permute-start.93
  (305 shorter events, 181.8 us)
Async XLA Ops:
  14.3 9.2 %collective-permute-start.7 = (bf16[192,384]{1,0:T(8,128)(2,1)S(1)}, bf16[192,384]{1,0:T(8,128)(2,1)S(1)}, u32[]{:S(2)}, u32[]{:S(2)}) collective-permute-start(bf16[192,384]{1,0:T(8,128)(2,1)S(1)} %get-tuple-element.323), channel_id=1, source_target_pairs={{0,8},{4,12},{8,0},{12,4},{1,9},{5,13},{9,1},{13,5},{2,10},{6,14},... | collective-permute-start | bytes 442376 | tf_op jit(solution)/shard_map/ppermute | solution.py:22
  23.8 10.6 %collective-permute-start.18 = (f32[1,2688]{1,0:T(1,128)S(1)}, f32[1,2688]{1,0:T(1,128)S(1)}, u32[]{:S(2)}, u32[]{:S(2)}) collective-permute-start(f32[1,2688]{1,0:T(1,128)S(1)} %broadcast_in_dim.27), channel_id=1, source_target_pairs={{0,16},{16,0},{1,17},{17,1},{2,18},{18,2},{3,19},{19,3},{4,20},{20... | collective-permute-start | bytes 32264 | tf_op jit(solution)/shard_map/ppermute | solution.py:22
  34.5 9.5 %collective-permute-start.16 = (bf16[192,384]{1,0:T(8,128)(2,1)S(1)}, bf16[192,384]{1,0:T(8,128)(2,1)S(1)}, u32[]{:S(2)}, u32[]{:S(2)}) collective-permute-start(bf16[192,384]{1,0:T(8,128)(2,1)S(1)} %get-tuple-element.344), channel_id=1, source_target_pairs={{0,8},{4,12},{8,0},{12,4},{1,9},{5,13},{9,1},{13,5},{2,10},{6,14},... | collective-permute-start | bytes 442376 | tf_op jit(solution)/shard_map/ppermute | solution.py:22
  36.0 12.2 %collective-permute-start.17 = (bf16[768,384]{1,0:T(8,128)(2,1)S(1)}, bf16[768,384]{1,0:T(8,128)(2,1)S(1)}, u32[]{:S(2)}, u32[]{:S(2)}) collective-permute-start(bf16[768,384]{1,0:T(8,128)(2,1)S(1)} %stack_line.4.refs_4_), channel_id=1, source_target_pairs={{0,16},{16,0},{1,17},{17,1},{2,18},{18,2},{3,19},{19,3},{4,20},{20... | collective-permute-start | bytes 1769480 | tf_op jit(solution)/shard_map/ppermute | solution.py:22
  45.3 12.2 %collective-permute-start.22 = (bf16[2,192,384]{2,1,0:T(8,128)(2,1)S(1)}, bf16[2,192,384]{2,1,0:T(8,128)(2,1)S(1)}, u32[]{:S(2)}, u32[]{:S(2)}) collective-permute-start(bf16[2,192,384]{2,1,0:T(8,128)(2,1)S(1)} %pad_maximum_fusion.1.refs_0_), channel_id=1, source_target_pairs={{0,4},{4,0},{8,12},{12,8},{1,5},{5,1},{9,13},{13,9},{2,6},{6,2},{1... | collective-permute-start | bytes 884744 | tf_op jit(solution)/shard_map/ppermute | solution.py:22
  47.3 9.5 %collective-permute-start.23 = (bf16[192,384]{1,0:T(8,128)(2,1)S(1)}, bf16[192,384]{1,0:T(8,128)(2,1)S(1)}, u32[]{:S(2)}, u32[]{:S(2)}) collective-permute-start(bf16[192,384]{1,0:T(8,128)(2,1)S(1)} %get-tuple-element.354), channel_id=1, source_target_pairs={{0,8},{4,12},{8,0},{12,4},{1,9},{5,13},{9,1},{13,5},{2,10},{6,14},... | collective-permute-start | bytes 442376 | tf_op jit(solution)/shard_map/ppermute | solution.py:22
  58.3 9.6 %collective-permute-start.28 = (bf16[192,384]{1,0:T(8,128)(2,1)S(1)}, bf16[192,384]{1,0:T(8,128)(2,1)S(1)}, u32[]{:S(2)}, u32[]{:S(2)}) collective-permute-start(bf16[192,384]{1,0:T(8,128)(2,1)S(1)} %get-tuple-element.383), channel_id=1, source_target_pairs={{0,8},{4,12},{8,0},{12,4},{1,9},{5,13},{9,1},{13,5},{2,10},{6,14},... | collective-permute-start | bytes 442376 | tf_op jit(solution)/shard_map/ppermute | solution.py:22
  60.3 9.5 %collective-permute-start.27 = (bf16[2,192,384]{2,1,0:T(8,128)(2,1)S(1)}, bf16[2,192,384]{2,1,0:T(8,128)(2,1)S(1)}, u32[]{:S(2)}, u32[]{:S(2)}) collective-permute-start(bf16[2,192,384]{2,1,0:T(8,128)(2,1)S(1)} %pad_maximum_fusion.2.refs_1_), channel_id=1, source_target_pairs={{0,4},{4,0},{8,12},{12,8},{1,5},{5,1},{9,13},{13,9},{2,6},{6,2},{1... | collective-permute-start | bytes 884744 | tf_op jit(solution)/shard_map/ppermute | solution.py:22
  70.6 17.3 %collective-permute-start.36 = (bf16[2,192,384]{2,1,0:T(8,128)(2,1)S(1)}, bf16[2,192,384]{2,1,0:T(8,128)(2,1)S(1)}, u32[]{:S(2)}, u32[]{:S(2)}) collective-permute-start(bf16[2,192,384]{2,1,0:T(8,128)(2,1)S(1)} %pad_maximum_fusion.3.refs_0_), channel_id=1, source_target_pairs={{0,4},{4,0},{8,12},{12,8},{1,5},{5,1},{9,13},{13,9},{2,6},{6,2},{1... | collective-permute-start | bytes 884744 | tf_op jit(solution)/shard_map/ppermute | solution.py:22
  75.8 12.1 %collective-permute-start.37 = (bf16[192,384]{1,0:T(8,128)(2,1)S(1)}, bf16[192,384]{1,0:T(8,128)(2,1)S(1)}, u32[]{:S(2)}, u32[]{:S(2)}) collective-permute-start(bf16[192,384]{1,0:T(8,128)(2,1)S(1)} %get-tuple-element.396), channel_id=1, source_target_pairs={{0,8},{4,12},{8,0},{12,4},{1,9},{5,13},{9,1},{13,5},{2,10},{6,14},... | collective-permute-start | bytes 442376 | tf_op jit(solution)/shard_map/ppermute | solution.py:22
  88.5 12.8 %collective-permute-start.41 = (bf16[768,384]{1,0:T(8,128)(2,1)S(1)}, bf16[768,384]{1,0:T(8,128)(2,1)S(1)}, u32[]{:S(2)}, u32[]{:S(2)}) collective-permute-start(bf16[768,384]{1,0:T(8,128)(2,1)S(1)} %stack_line.6.refs_4_), channel_id=1, source_target_pairs={{0,16},{16,0},{1,17},{17,1},{2,18},{18,2},{3,19},{19,3},{4,20},{20... | collective-permute-start | bytes 1769480 | tf_op jit(solution)/shard_map/ppermute | solution.py:22
  88.6 12.6 %collective-permute-start.42 = (bf16[2,192,384]{2,1,0:T(8,128)(2,1)S(1)}, bf16[2,192,384]{2,1,0:T(8,128)(2,1)S(1)}, u32[]{:S(2)}, u32[]{:S(2)}) collective-permute-start(bf16[2,192,384]{2,1,0:T(8,128)(2,1)S(1)} %pad_maximum_fusion.4.refs_0_), channel_id=1, source_target_pairs={{0,4},{4,0},{8,12},{12,8},{1,5},{5,1},{9,13},{13,9},{2,6},{6,2},{1... | collective-permute-start | bytes 884744 | tf_op jit(solution)/shard_map/ppermute | solution.py:22
  90.7 9.1 %collective-permute-start.43 = (bf16[192,384]{1,0:T(8,128)(2,1)S(1)}, bf16[192,384]{1,0:T(8,128)(2,1)S(1)}, u32[]{:S(2)}, u32[]{:S(2)}) collective-permute-start(bf16[192,384]{1,0:T(8,128)(2,1)S(1)} %get-tuple-element.410), channel_id=1, source_target_pairs={{0,8},{4,12},{8,0},{12,4},{1,9},{5,13},{9,1},{13,5},{2,10},{6,14},... | collective-permute-start | bytes 442376 | tf_op jit(solution)/shard_map/ppermute | solution.py:22
  101.3 11.5 %collective-permute-start.47 = (bf16[2,192,384]{2,1,0:T(8,128)(2,1)S(1)}, bf16[2,192,384]{2,1,0:T(8,128)(2,1)S(1)}, u32[]{:S(2)}, u32[]{:S(2)}) collective-permute-start(bf16[2,192,384]{2,1,0:T(8,128)(2,1)S(1)} %pad_maximum_fusion.5.refs_1_), channel_id=1, source_target_pairs={{0,4},{4,0},{8,12},{12,8},{1,5},{5,1},{9,13},{13,9},{2,6},{6,2},{1... | collective-permute-start | bytes 884744 | tf_op jit(solution)/shard_map/ppermute | solution.py:22
  145.1 12.6 %collective-permute-start.69 = (bf16[2,192,384]{2,1,0:T(8,128)(2,1)S(1)}, bf16[2,192,384]{2,1,0:T(8,128)(2,1)S(1)}, u32[]{:S(2)}, u32[]{:S(2)}) collective-permute-start(bf16[2,192,384]{2,1,0:T(8,128)(2,1)S(1)} %get-tuple-element.486), channel_id=1, source_target_pairs={{0,4},{4,0},{8,12},{12,8},{1,5},{5,1},{9,13},{13,9},{2,6},{6,2},{1... | collective-permute-start | bytes 884744 | tf_op jit(solution)/shard_map/ppermute | solution.py:22
  146.8 10.0 %collective-permute-start.68 = (bf16[192,384]{1,0:T(8,128)(2,1)S(1)}, bf16[192,384]{1,0:T(8,128)(2,1)S(1)}, u32[]{:S(2)}, u32[]{:S(2)}) collective-permute-start(bf16[192,384]{1,0:T(8,128)(2,1)S(1)} %fusion.14), channel_id=1, source_target_pairs={{0,8},{4,12},{8,0},{12,4},{1,9},{5,13},{9,1},{13,5},{2,10},{6,14},... | collective-permute-start | bytes 442376 | tf_op jit(solution)/shard_map/ppermute | solution.py:22
  157.7 11.7 %collective-permute-start.73 = (bf16[2,192,384]{2,1,0:T(8,128)(2,1)S(1)}, bf16[2,192,384]{2,1,0:T(8,128)(2,1)S(1)}, u32[]{:S(2)}, u32[]{:S(2)}) collective-permute-start(bf16[2,192,384]{2,1,0:T(8,128)(2,1)S(1)} %get-tuple-element.496), channel_id=1, source_target_pairs={{0,4},{4,0},{8,12},{12,8},{1,5},{5,1},{9,13},{13,9},{2,6},{6,2},{1... | collective-permute-start | bytes 884744 | tf_op jit(solution)/shard_map/ppermute | solution.py:22
  159.1 9.2 %collective-permute-start.74 = (bf16[192,384]{1,0:T(8,128)(2,1)S(1)}, bf16[192,384]{1,0:T(8,128)(2,1)S(1)}, u32[]{:S(2)}, u32[]{:S(2)}) collective-permute-start(bf16[192,384]{1,0:T(8,128)(2,1)S(1)} %fusion.13), channel_id=1, source_target_pairs={{0,8},{4,12},{8,0},{12,4},{1,9},{5,13},{9,1},{13,5},{2,10},{6,14},... | collective-permute-start | bytes 442376 | tf_op jit(solution)/shard_map/ppermute | solution.py:22
  171.8 9.2 %collective-permute-start.78 = (bf16[768,768]{1,0:T(8,128)(2,1)S(1)}, bf16[768,768]{1,0:T(8,128)(2,1)S(1)}, u32[]{:S(2)}, u32[]{:S(2)}) collective-permute-start(bf16[768,768]{1,0:T(8,128)(2,1)S(1)} %get-tuple-element.515), channel_id=1, source_target_pairs={{0,16},{16,0},{1,17},{17,1},{2,18},{18,2},{3,19},{19,3},{4,20},{20... | collective-permute-start | bytes 3538952 | tf_op jit(solution)/shard_map/ppermute | solution.py:22
  185.1 13.6 %collective-permute-start.82 = (bf16[2,192,768]{2,1,0:T(8,128)(2,1)S(1)}, bf16[2,192,768]{2,1,0:T(8,128)(2,1)S(1)}, u32[]{:S(2)}, u32[]{:S(2)}) collective-permute-start(bf16[2,192,768]{2,1,0:T(8,128)(2,1)S(1)} %get-tuple-element.526), channel_id=1, source_target_pairs={{0,4},{4,0},{8,12},{12,8},{1,5},{5,1},{9,13},{13,9},{2,6},{6,2},{1... | collective-permute-start | bytes 1769480 | tf_op jit(solution)/shard_map/ppermute | solution.py:22
  198.8 13.9 %collective-permute-start.86 = (bf16[192,768]{1,0:T(8,128)(2,1)S(1)}, bf16[192,768]{1,0:T(8,128)(2,1)S(1)}, u32[]{:S(2)}, u32[]{:S(2)}) collective-permute-start(bf16[192,768]{1,0:T(8,128)(2,1)S(1)} %fusion.2), channel_id=1, source_target_pairs={{0,8},{4,12},{8,0},{12,4},{1,9},{5,13},{9,1},{13,5},{2,10},{6,14},... | collective-permute-start | bytes 884744 | tf_op jit(solution)/shard_map/ppermute | solution.py:22
  219.0 9.2 %collective-permute-start.92 = (bf16[192,384]{1,0:T(8,128)(2,1)S(1)}, bf16[192,384]{1,0:T(8,128)(2,1)S(1)}, u32[]{:S(2)}, u32[]{:S(2)}) collective-permute-start(bf16[192,384]{1,0:T(8,128)(2,1)S(1)} %fusion.12), channel_id=1, source_target_pairs={{0,8},{4,12},{8,0},{12,4},{1,9},{5,13},{9,1},{13,5},{2,10},{6,14},... | collective-permute-start | bytes 442376 | tf_op jit(solution)/shard_map/ppermute | solution.py:22
  219.1 14.8 %collective-permute-start.103 = (bf16[192,768]{1,0:T(8,128)(2,1)S(1)}, bf16[192,768]{1,0:T(8,128)(2,1)S(1)}, u32[]{:S(2)}, u32[]{:S(2)}) collective-permute-start(bf16[192,768]{1,0:T(8,128)(2,1)S(1)} %get-tuple-element.626), channel_id=1, source_target_pairs={{0,16},{16,0},{1,17},{17,1},{2,18},{18,2},{3,19},{19,3},{4,20},{20... | collective-permute-start | bytes 884744 | tf_op jit(solution)/shard_map/ppermute | solution.py:22
  221.4 15.6 %collective-permute-start.97 = (bf16[2,192,384]{2,1,0:T(8,128)(2,1)S(1)}, bf16[2,192,384]{2,1,0:T(8,128)(2,1)S(1)}, u32[]{:S(2)}, u32[]{:S(2)}) collective-permute-start(bf16[2,192,384]{2,1,0:T(8,128)(2,1)S(1)} %get-tuple-element.580), channel_id=1, source_target_pairs={{0,4},{4,0},{8,12},{12,8},{1,5},{5,1},{9,13},{13,9},{2,6},{6,2},{1... | collective-permute-start | bytes 884744 | tf_op jit(solution)/shard_map/ppermute | solution.py:22
  (96 other events, 628.1 us)

commit v12 on v11

--- a/solution.py
+++ b/solution.py
@@ -832,32 +832,23 @@
             place,
         )
 
-    (g_parts, (parts_e1, parts_s1)), y_partial = tie(
-        (
-            exchange(g_partial, "tensor"),
-            line_parts(mlp_weight_grads(mlp_rows1, g_pre1, g_rows1, hidden1), 2),
-        ),
+    g_parts, (parts_m1,), y_partial = tie(
+        exchange(g_partial, "tensor"),
+        line_parts(mlp_weight_grads(mlp_rows1, g_pre1, g_rows1, hidden1), 1),
         y_partial,
     )
-    near_e1 = line_near(parts_e1)
+    near_m1 = line_near(parts_m1)
     g_middle1, g_attended, g_shift_mlp1, g_scale_mlp1, g_gate_attn1, out_grad1 = middle_back(
         g_parts, middle1, mod1, g_y1, attended1
     )
     y_parts = exchange(y_partial, "tensor")
-    g_rows, near_e1, parts_e1, parts_s1 = tie(
-        gather(g_attended, "tensor"), near_e1, parts_e1, parts_s1
-    )
-    far_e1 = line_far(parts_e1, near_e1)
-    near_s1 = line_near(parts_s1)
+    g_rows, near_m1 = tie(gather(g_attended, "tensor"), near_m1)
+    far_m1 = line_far(parts_m1, near_m1)
     (g_rows, g_joint, joint_grad1), parts = attention_back(g_rows, w_attn1, kept_attn1)
-    (parts, (parts_a1,)), far_e1, near_s1, parts_s1 = tie(
-        (parts, line_parts(attn_weight_grads(kept_attn1, g_joint, g_rows), 1)),
-        far_e1,
-        near_s1,
-        parts_s1,
+    parts, (parts_a1,), far_m1 = tie(
+        parts, line_parts(attn_weight_grads(kept_attn1, g_joint, g_rows), 1), far_m1
     )
     near_a1 = line_near(parts_a1)
-    far_s1 = line_far(parts_s1, near_s1)
     g_passed, g_y0, g_shrunk0, g_shift_attn1, g_scale_attn1, g_gate_mlp0, shrink_grad0 = kernel(
         "between_back",
         between_back_body,
@@ -865,9 +856,7 @@
         parts + [h1, mod1, mod0, g_middle1, shrunk0],
     )
 
-    g_rows0, near_a1, far_s1, parts_a1 = tie(
-        gather(g_shrunk0, "tensor"), near_a1, far_s1, parts_a1
-    )
+    g_rows0, near_a1 = tie(gather(g_shrunk0, "tensor"), near_a1)
     outs = kernel(
         "feed_forward_back",
         mlp_back_body,
@@ -939,7 +928,7 @@
         packed_all + [joint_grad0, expand_grad0, joint_grad1, expand_grad1],
         place,
     )
-    received, far_a1 = tie(swap(give, "pipe", 1), far_a1)
+    received = swap(give, "pipe", 1)
     joined = run(
         "grads_join",
         grads_join_body,
@@ -948,12 +937,10 @@
         place,
     )[0]
     joined_all = gather(joined, "dp") if direct else lax.all_gather(joined, "dp", axis=0, tiled=True)
-    joined_all, near_a0 = tie(joined_all, near_a0)
+    joined_all, near_a0, far_a1 = tie(joined_all, near_a0, far_a1)
     far_a0 = line_far(parts_a0, near_a0)
     mlp_grad0 = line_total(parts_m0, near_m0, far_m0)
-    mlp_grad1 = jnp.concatenate(
-        [line_total(parts_e1, near_e1, far_e1), line_total(parts_s1, near_s1, far_s1)], axis=1
-    )
+    mlp_grad1 = line_total(parts_m1, near_m1, far_m1)
     attn_grad0 = line_total(parts_a0, near_a0, far_a0)
     attn_grad1 = line_total(parts_a1, near_a1, far_a1)
     expand_w_grad, shrink_t_grad = run(

time: 250 us -> 255 us (1.020)
  waiting for transfers between devices: 90.2 us -> 102 us
  starting transfers between devices: 113 us -> 106 us
    ppermute x104 -> x102, waiting for transfers between devices: 90.2 us -> 102 us  [swap(): return lax.ppermute(value, axis, pairs)]
    ppermute x104 -> x102, starting transfers between devices: 113 us -> 106 us  [swap(): return lax.ppermute(value, axis, pairs)]
  transfers between devices with their start and end apart: 104 -> 102, of which waited for: 63 -> 59; matrix products, arithmetic and copies ran while one was open for 2% -> 2% of each run, Pallas kernels for 10% -> 9%
where the time goes in v12:
time: 255 us; the launch traced here: 254 us
  starting transfers between devices  106 us (42%)
  waiting for transfers between devices  102 us (40%)
  Pallas kernels  35.4 us (14%)
  local copies, waits for them, and re-layouts  6.87 us (3%)
  other arithmetic  2.58 us (1%)
    ppermute x102, starting transfers between devices, swap(): return lax.ppermute(value, axis, pairs)  106 us
    ppermute x102, waiting for transfers between devices, swap(): return lax.ppermute(value, axis, pairs)  102 us
    pallas_call x37, Pallas kernels, run(): pl.pallas_call(body, out_shape=outs, in_specs=specs, out_specs=[pl.BlockS...  33.9 us
  transfers between devices with their start and end apart: 102, of which 59 were waited for; matrix products, arithmetic and copies ran while one was open for 2% of the time, Pallas kernels for 9%

profile of v12, /device:TPU:0, one launch (start us, length us, event | category | flops | bytes accessed | tf_op | source)
XLA Modules:
  0.0 254.3 jit_solution(4189707678989185408)
XLA Ops:
  4.9 5.0 %collective-permute-start.2 = (bf16[2,192]{1,0:T(2,128)(2,1)S(1)}, bf16[2,192]{1,0:T(2,128)(2,1)S(1)}, u32[]{:S(2)}, u32[]{:S(2)}) collective-permute-start(bf16[2,192]{1,0:T(2,128)(2,1)S(1)} %fusion.18.a0), channel_id=1, source_target_pairs={{0,12},{4,8},{8,4},{12,0},{1,13},{5,9},{9,5},{13,1},{2,14},{6,10},... | collective-permute-start | bytes 2312 | tf_op jit(solution)/shard_map/ppermute | solution.py:22
  11.4 2.9 %collective-permute-done.1.a2 = bf16[2,192]{1,0:T(2,128)(2,1)S(1)} collective-permute-done((bf16[2,192]{1,0:T(2,128)(2,1)S(1)}, bf16[2,192]{1,0:T(2,128)(2,1)S(1)}, u32[]{:S(2)}, u32[]{:S(2)}) %collective-permute-start.1) | collective-permute-done | bytes 800 | tf_op jit(solution)/shard_map/ppermute | solution.py:22
  16.5 2.5 collective-permute-start.5
  28.5 2.3 collective-permute-done.8.p1
  40.8 3.1 %collective-permute-done.16 = bf16[192,384]{1,0:T(8,128)(2,1)S(1)} collective-permute-done((bf16[192,384]{1,0:T(8,128)(2,1)S(1)}, bf16[192,384]{1,0:T(8,128)(2,1)S(1)}, u32[]{:S(2)}, u32[]{:S(2)}) %collective-permute-start.16) | collective-permute-done | bytes 147488 | tf_op jit(solution)/shard_map/ppermute | solution.py:22
  48.2 2.1 attention.2
  53.9 2.9 %collective-permute-done.23 = bf16[192,384]{1,0:T(8,128)(2,1)S(1)} collective-permute-done((bf16[192,384]{1,0:T(8,128)(2,1)S(1)}, bf16[192,384]{1,0:T(8,128)(2,1)S(1)}, u32[]{:S(2)}, u32[]{:S(2)}) %collective-permute-start.23) | collective-permute-done | bytes 147488 | tf_op jit(solution)/shard_map/ppermute | solution.py:22
  64.4 2.8 %collective-permute-done.26.refs_3_ = bf16[64,768]{1,0:T(8,128)(2,1)S(1)} collective-permute-done((bf16[64,768]{1,0:T(8,128)(2,1)S(1)}, bf16[64,768]{1,0:T(8,128)(2,1)S(1)}, u32[]{:S(2)}, u32[]{:S(2)}) %collective-permute-start.26) | collective-permute-done | bytes 98336 | tf_op jit(solution)/shard_map/ppermute | solution.py:22
  90.7 2.4 collective-permute-start.43
  117.3 3.0 %collective-permute-done.50.refs_3_ = bf16[64,768]{1,0:T(8,128)(2,1)S(1)} collective-permute-done((bf16[64,768]{1,0:T(8,128)(2,1)S(1)}, bf16[64,768]{1,0:T(8,128)(2,1)S(1)}, u32[]{:S(2)}, u32[]{:S(2)}) %collective-permute-start.50) | collective-permute-done | bytes 98336 | tf_op jit(solution)/shard_map/ppermute | solution.py:22
  122.0 2.2 feed_forward_both.1
  130.6 3.1 %collective-permute-done.53.refs_2_ = bf16[64,768]{1,0:T(8,128)(2,1)S(1)} collective-permute-done((bf16[64,768]{1,0:T(8,128)(2,1)S(1)}, bf16[64,768]{1,0:T(8,128)(2,1)S(1)}, u32[]{:S(2)}, u32[]{:S(2)}) %collective-permute-start.53) | collective-permute-done | bytes 98336 | tf_op jit(solution)/shard_map/ppermute | solution.py:22
  137.9 2.5 collective-permute-done.62.refs_3_
  141.4 6.1 %collective-permute-done.63 = bf16[2,192,768]{2,1,0:T(8,128)(2,1)S(1)} collective-permute-done((bf16[2,192,768]{2,1,0:T(8,128)(2,1)S(1)}, bf16[2,192,768]{2,1,0:T(8,128)(2,1)S(1)}, u32[]{:S(2)}, u32[]{:S(2)}) %collective-permute-start.63) | collective-permute-done | bytes 589856 | tf_op jit(solution)/shard_map/ppermute | solution.py:22
  147.5 2.4 attention_back.2
  157.6 3.1 %collective-permute-done.65.refs_2_ = bf16[64,768]{1,0:T(8,128)(2,1)S(1)} collective-permute-done((bf16[64,768]{1,0:T(8,128)(2,1)S(1)}, bf16[64,768]{1,0:T(8,128)(2,1)S(1)}, u32[]{:S(2)}, u32[]{:S(2)}) %collective-permute-start.65) | collective-permute-done | bytes 98336 | tf_op jit(solution)/shard_map/ppermute | solution.py:22
  160.7 7.2 %collective-permute-done.68 = bf16[192,768]{1,0:T(8,128)(2,1)S(1)} collective-permute-done((bf16[192,768]{1,0:T(8,128)(2,1)S(1)}, bf16[192,768]{1,0:T(8,128)(2,1)S(1)}, u32[]{:S(2)}, u32[]{:S(2)}) %collective-permute-start.68) | collective-permute-done | bytes 294944 | tf_op jit(solution)/shard_map/ppermute | solution.py:22
  171.9 2.5 collective-permute-done.71.refs_3_
  184.6 3.1 %collective-permute-done.74.refs_2_ = bf16[64,768]{1,0:T(8,128)(2,1)S(1)} collective-permute-done((bf16[64,768]{1,0:T(8,128)(2,1)S(1)}, bf16[64,768]{1,0:T(8,128)(2,1)S(1)}, u32[]{:S(2)}, u32[]{:S(2)}) %collective-permute-start.74) | collective-permute-done | bytes 98336 | tf_op jit(solution)/shard_map/ppermute | solution.py:22
  204.5 2.4 attention_back.3
  214.3 2.5 collective-permute-done.84
  235.7 5.2 %collective-permute-done.90.g1 = bf16[1,11904]{1,0:T(2,128)(2,1)S(1)} collective-permute-done((bf16[1,11904]{1,0:T(2,128)(2,1)S(1)}, bf16[1,11904]{1,0:T(2,128)(2,1)S(1)}, u32[]{:S(2)}, u32[]{:S(2)}) %collective-permute-start.90) | collective-permute-done | bytes 23840 | tf_op jit(solution)/shard_map/ppermute | solution.py:22
  245.2 2.5 collective-permute-start.96
  247.7 2.3 collective-permute-start.98
  (298 shorter events, 176.5 us)
Async XLA Ops:
  14.3 9.2 %collective-permute-start.7 = (bf16[192,384]{1,0:T(8,128)(2,1)S(1)}, bf16[192,384]{1,0:T(8,128)(2,1)S(1)}, u32[]{:S(2)}, u32[]{:S(2)}) collective-permute-start(bf16[192,384]{1,0:T(8,128)(2,1)S(1)} %get-tuple-element.305), channel_id=1, source_target_pairs={{0,8},{4,12},{8,0},{12,4},{1,9},{5,13},{9,1},{13,5},{2,10},{6,14},... | collective-permute-start | bytes 442376 | tf_op jit(solution)/shard_map/ppermute | solution.py:22
  23.8 10.6 %collective-permute-start.18 = (f32[1,2688]{1,0:T(1,128)S(1)}, f32[1,2688]{1,0:T(1,128)S(1)}, u32[]{:S(2)}, u32[]{:S(2)}) collective-permute-start(f32[1,2688]{1,0:T(1,128)S(1)} %broadcast_in_dim.27), channel_id=1, source_target_pairs={{0,16},{16,0},{1,17},{17,1},{2,18},{18,2},{3,19},{19,3},{4,20},{20... | collective-permute-start | bytes 32264 | tf_op jit(solution)/shard_map/ppermute | solution.py:22
  34.5 9.5 %collective-permute-start.16 = (bf16[192,384]{1,0:T(8,128)(2,1)S(1)}, bf16[192,384]{1,0:T(8,128)(2,1)S(1)}, u32[]{:S(2)}, u32[]{:S(2)}) collective-permute-start(bf16[192,384]{1,0:T(8,128)(2,1)S(1)} %get-tuple-element.326), channel_id=1, source_target_pairs={{0,8},{4,12},{8,0},{12,4},{1,9},{5,13},{9,1},{13,5},{2,10},{6,14},... | collective-permute-start | bytes 442376 | tf_op jit(solution)/shard_map/ppermute | solution.py:22
  36.0 12.2 %collective-permute-start.17 = (bf16[768,384]{1,0:T(8,128)(2,1)S(1)}, bf16[768,384]{1,0:T(8,128)(2,1)S(1)}, u32[]{:S(2)}, u32[]{:S(2)}) collective-permute-start(bf16[768,384]{1,0:T(8,128)(2,1)S(1)} %stack_line.4.refs_4_), channel_id=1, source_target_pairs={{0,16},{16,0},{1,17},{17,1},{2,18},{18,2},{3,19},{19,3},{4,20},{20... | collective-permute-start | bytes 1769480 | tf_op jit(solution)/shard_map/ppermute | solution.py:22
  45.3 12.2 %collective-permute-start.22 = (bf16[2,192,384]{2,1,0:T(8,128)(2,1)S(1)}, bf16[2,192,384]{2,1,0:T(8,128)(2,1)S(1)}, u32[]{:S(2)}, u32[]{:S(2)}) collective-permute-start(bf16[2,192,384]{2,1,0:T(8,128)(2,1)S(1)} %pad_maximum_fusion.1.refs_0_), channel_id=1, source_target_pairs={{0,4},{4,0},{8,12},{12,8},{1,5},{5,1},{9,13},{13,9},{2,6},{6,2},{1... | collective-permute-start | bytes 884744 | tf_op jit(solution)/shard_map/ppermute | solution.py:22
  47.3 9.5 %collective-permute-start.23 = (bf16[192,384]{1,0:T(8,128)(2,1)S(1)}, bf16[192,384]{1,0:T(8,128)(2,1)S(1)}, u32[]{:S(2)}, u32[]{:S(2)}) collective-permute-start(bf16[192,384]{1,0:T(8,128)(2,1)S(1)} %get-tuple-element.336), channel_id=1, source_target_pairs={{0,8},{4,12},{8,0},{12,4},{1,9},{5,13},{9,1},{13,5},{2,10},{6,14},... | collective-permute-start | bytes 442376 | tf_op jit(solution)/shard_map/ppermute | solution.py:22
  58.3 9.6 %collective-permute-start.28 = (bf16[192,384]{1,0:T(8,128)(2,1)S(1)}, bf16[192,384]{1,0:T(8,128)(2,1)S(1)}, u32[]{:S(2)}, u32[]{:S(2)}) collective-permute-start(bf16[192,384]{1,0:T(8,128)(2,1)S(1)} %get-tuple-element.365), channel_id=1, source_target_pairs={{0,8},{4,12},{8,0},{12,4},{1,9},{5,13},{9,1},{13,5},{2,10},{6,14},... | collective-permute-start | bytes 442376 | tf_op jit(solution)/shard_map/ppermute | solution.py:22
  60.3 9.5 %collective-permute-start.27 = (bf16[2,192,384]{2,1,0:T(8,128)(2,1)S(1)}, bf16[2,192,384]{2,1,0:T(8,128)(2,1)S(1)}, u32[]{:S(2)}, u32[]{:S(2)}) collective-permute-start(bf16[2,192,384]{2,1,0:T(8,128)(2,1)S(1)} %pad_maximum_fusion.2.refs_1_), channel_id=1, source_target_pairs={{0,4},{4,0},{8,12},{12,8},{1,5},{5,1},{9,13},{13,9},{2,6},{6,2},{1... | collective-permute-start | bytes 884744 | tf_op jit(solution)/shard_map/ppermute | solution.py:22
  70.6 17.3 %collective-permute-start.36 = (bf16[2,192,384]{2,1,0:T(8,128)(2,1)S(1)}, bf16[2,192,384]{2,1,0:T(8,128)(2,1)S(1)}, u32[]{:S(2)}, u32[]{:S(2)}) collective-permute-start(bf16[2,192,384]{2,1,0:T(8,128)(2,1)S(1)} %pad_maximum_fusion.3.refs_0_), channel_id=1, source_target_pairs={{0,4},{4,0},{8,12},{12,8},{1,5},{5,1},{9,13},{13,9},{2,6},{6,2},{1... | collective-permute-start | bytes 884744 | tf_op jit(solution)/shard_map/ppermute | solution.py:22
  75.8 12.1 %collective-permute-start.37 = (bf16[192,384]{1,0:T(8,128)(2,1)S(1)}, bf16[192,384]{1,0:T(8,128)(2,1)S(1)}, u32[]{:S(2)}, u32[]{:S(2)}) collective-permute-start(bf16[192,384]{1,0:T(8,128)(2,1)S(1)} %get-tuple-element.378), channel_id=1, source_target_pairs={{0,8},{4,12},{8,0},{12,4},{1,9},{5,13},{9,1},{13,5},{2,10},{6,14},... | collective-permute-start | bytes 442376 | tf_op jit(solution)/shard_map/ppermute | solution.py:22
  88.5 12.8 %collective-permute-start.41 = (bf16[768,384]{1,0:T(8,128)(2,1)S(1)}, bf16[768,384]{1,0:T(8,128)(2,1)S(1)}, u32[]{:S(2)}, u32[]{:S(2)}) collective-permute-start(bf16[768,384]{1,0:T(8,128)(2,1)S(1)} %stack_line.6.refs_4_), channel_id=1, source_target_pairs={{0,16},{16,0},{1,17},{17,1},{2,18},{18,2},{3,19},{19,3},{4,20},{20... | collective-permute-start | bytes 1769480 | tf_op jit(solution)/shard_map/ppermute | solution.py:22
  88.6 12.6 %collective-permute-start.42 = (bf16[2,192,384]{2,1,0:T(8,128)(2,1)S(1)}, bf16[2,192,384]{2,1,0:T(8,128)(2,1)S(1)}, u32[]{:S(2)}, u32[]{:S(2)}) collective-permute-start(bf16[2,192,384]{2,1,0:T(8,128)(2,1)S(1)} %pad_maximum_fusion.4.refs_0_), channel_id=1, source_target_pairs={{0,4},{4,0},{8,12},{12,8},{1,5},{5,1},{9,13},{13,9},{2,6},{6,2},{1... | collective-permute-start | bytes 884744 | tf_op jit(solution)/shard_map/ppermute | solution.py:22
  90.7 9.1 %collective-permute-start.43 = (bf16[192,384]{1,0:T(8,128)(2,1)S(1)}, bf16[192,384]{1,0:T(8,128)(2,1)S(1)}, u32[]{:S(2)}, u32[]{:S(2)}) collective-permute-start(bf16[192,384]{1,0:T(8,128)(2,1)S(1)} %get-tuple-element.392), channel_id=1, source_target_pairs={{0,8},{4,12},{8,0},{12,4},{1,9},{5,13},{9,1},{13,5},{2,10},{6,14},... | collective-permute-start | bytes 442376 | tf_op jit(solution)/shard_map/ppermute | solution.py:22
  101.3 11.5 %collective-permute-start.47 = (bf16[2,192,384]{2,1,0:T(8,128)(2,1)S(1)}, bf16[2,192,384]{2,1,0:T(8,128)(2,1)S(1)}, u32[]{:S(2)}, u32[]{:S(2)}) collective-permute-start(bf16[2,192,384]{2,1,0:T(8,128)(2,1)S(1)} %pad_maximum_fusion.5.refs_1_), channel_id=1, source_target_pairs={{0,4},{4,0},{8,12},{12,8},{1,5},{5,1},{9,13},{13,9},{2,6},{6,2},{1... | collective-permute-start | bytes 884744 | tf_op jit(solution)/shard_map/ppermute | solution.py:22
  133.6 13.9 %collective-permute-start.63 = (bf16[2,192,768]{2,1,0:T(8,128)(2,1)S(1)}, bf16[2,192,768]{2,1,0:T(8,128)(2,1)S(1)}, u32[]{:S(2)}, u32[]{:S(2)}) collective-permute-start(bf16[2,192,768]{2,1,0:T(8,128)(2,1)S(1)} %get-tuple-element.438), channel_id=1, source_target_pairs={{0,4},{4,0},{8,12},{12,8},{1,5},{5,1},{9,13},{13,9},{2,6},{6,2},{1... | collective-permute-start | bytes 1769480 | tf_op jit(solution)/shard_map/ppermute | solution.py:22
  151.3 16.6 %collective-permute-start.68 = (bf16[192,768]{1,0:T(8,128)(2,1)S(1)}, bf16[192,768]{1,0:T(8,128)(2,1)S(1)}, u32[]{:S(2)}, u32[]{:S(2)}) collective-permute-start(bf16[192,768]{1,0:T(8,128)(2,1)S(1)} %fusion.5), channel_id=1, source_target_pairs={{0,8},{4,12},{8,0},{12,4},{1,9},{5,13},{9,1},{13,5},{2,10},{6,14},... | collective-permute-start | bytes 884744 | tf_op jit(solution)/shard_map/ppermute | solution.py:22
  167.9 9.0 %collective-permute-start.72 = (bf16[2,192,384]{2,1,0:T(8,128)(2,1)S(1)}, bf16[2,192,384]{2,1,0:T(8,128)(2,1)S(1)}, u32[]{:S(2)}, u32[]{:S(2)}) collective-permute-start(bf16[2,192,384]{2,1,0:T(8,128)(2,1)S(1)} %get-tuple-element.467), channel_id=1, source_target_pairs={{0,4},{4,0},{8,12},{12,8},{1,5},{5,1},{9,13},{13,9},{2,6},{6,2},{1... | collective-permute-start | bytes 884744 | tf_op jit(solution)/shard_map/ppermute | solution.py:22
  187.7 16.1 %collective-permute-start.80 = (bf16[2,192,768]{2,1,0:T(8,128)(2,1)S(1)}, bf16[2,192,768]{2,1,0:T(8,128)(2,1)S(1)}, u32[]{:S(2)}, u32[]{:S(2)}) collective-permute-start(bf16[2,192,768]{2,1,0:T(8,128)(2,1)S(1)} %get-tuple-element.493), channel_id=1, source_target_pairs={{0,4},{4,0},{8,12},{12,8},{1,5},{5,1},{9,13},{13,9},{2,6},{6,2},{1... | collective-permute-start | bytes 1769480 | tf_op jit(solution)/shard_map/ppermute | solution.py:22
  203.9 12.9 %collective-permute-start.84 = (bf16[192,768]{1,0:T(8,128)(2,1)S(1)}, bf16[192,768]{1,0:T(8,128)(2,1)S(1)}, u32[]{:S(2)}, u32[]{:S(2)}) collective-permute-start(bf16[192,768]{1,0:T(8,128)(2,1)S(1)} %fusion.4), channel_id=1, source_target_pairs={{0,8},{4,12},{8,0},{12,4},{1,9},{5,13},{9,1},{13,5},{2,10},{6,14},... | collective-permute-start | bytes 884744 | tf_op jit(solution)/shard_map/ppermute | solution.py:22
  220.7 9.0 %collective-permute-start.85 = (bf16[64,768]{1,0:T(8,128)(2,1)S(1)}, bf16[64,768]{1,0:T(8,128)(2,1)S(1)}, u32[]{:S(2)}, u32[]{:S(2)}) collective-permute-start(bf16[64,768]{1,0:T(8,128)(2,1)S(1)} %broadcast_select_fusion.6), channel_id=1, source_target_pairs={{0,16},{16,0},{1,17},{17,1},{2,18},{18,2},{3,19},{19,3},{4,20},{20... | collective-permute-start | bytes 294920 | tf_op jit(solution)/shard_map/ppermute | solution.py:22
  223.1 17.8 %collective-permute-start.95 = (bf16[192,384]{1,0:T(8,128)(2,1)S(1)}, bf16[192,384]{1,0:T(8,128)(2,1)S(1)}, u32[]{:S(2)}, u32[]{:S(2)}) collective-permute-start(bf16[192,384]{1,0:T(8,128)(2,1)S(1)} %fusion.11), channel_id=1, source_target_pairs={{0,8},{4,12},{8,0},{12,4},{1,9},{5,13},{9,1},{13,5},{2,10},{6,14},... | collective-permute-start | bytes 442376 | tf_op jit(solution)/shard_map/ppermute | solution.py:22
  229.7 11.2 %collective-permute-start.94 = (bf16[2,192,384]{2,1,0:T(8,128)(2,1)S(1)}, bf16[2,192,384]{2,1,0:T(8,128)(2,1)S(1)}, u32[]{:S(2)}, u32[]{:S(2)}) collective-permute-start(bf16[2,192,384]{2,1,0:T(8,128)(2,1)S(1)} %get-tuple-element.544), channel_id=1, source_target_pairs={{0,4},{4,0},{8,12},{12,8},{1,5},{5,1},{9,13},{13,9},{2,6},{6,2},{1... | collective-permute-start | bytes 884744 | tf_op jit(solution)/shard_map/ppermute | solution.py:22
  231.8 9.1 %collective-permute-start.90 = (bf16[1,11904]{1,0:T(2,128)(2,1)S(1)}, bf16[1,11904]{1,0:T(2,128)(2,1)S(1)}, u32[]{:S(2)}, u32[]{:S(2)}) collective-permute-start(bf16[1,11904]{1,0:T(2,128)(2,1)S(1)} %grads_join.1.g0), channel_id=1, source_target_pairs={{0,4},{4,0},{8,12},{12,8},{1,5},{5,1},{9,13},{13,9},{2,6},{6,2},{1... | collective-permute-start | bytes 71432 | tf_op jit(solution)/shard_map/ppermute | solution.py:22
  241.0 9.6 %collective-permute-start.99 = (bf16[192,384]{1,0:T(8,128)(2,1)S(1)}, bf16[192,384]{1,0:T(8,128)(2,1)S(1)}, u32[]{:S(2)}, u32[]{:S(2)}) collective-permute-start(bf16[192,384]{1,0:T(8,128)(2,1)S(1)} %fusion.8), channel_id=1, source_target_pairs={{0,8},{4,12},{8,0},{12,4},{1,9},{5,13},{9,1},{13,5},{2,10},{6,14},... | collective-permute-start | bytes 442376 | tf_op jit(solution)/shard_map/ppermute | solution.py:22
  (94 other events, 612.0 us)
